TPU v7x, 128 devices: a whole 4x4x4 slice. The times are simulated.
128 devices in a mesh: row: 16 (over z, y_lo, core), col: 8 (over y_hi, x).
Axes of the slice: x: 4, y: 4 (y_hi: 2, y_lo: 2; y = y_hi * 2 + y_lo), z: 4, core: 2. Of those that a mesh axis runs over, the one named last changes fastest.
Arguments:
- tokens: bfloat16 [16384, 1536], P(('row', 'col')), may hold values from -6 to 6
- segments: int32 [16384], P(('row', 'col')), may hold values from 0 to 2, as said below
- routes: int32 [16384, 6], P(('row', 'col')), may hold values from 0 to 63, all different within a row; in each aligned block of 128 rows (0 to 127, 128 to 255, ...) at most 24 rows name the same one
- norm1_gain: bfloat16 [1536], P(('row', 'col')), may hold values from 0.5 to 1.5
- w_query: bfloat16 [1536, 1536], P(('row', 'col')), may hold values from -0.15625 to 0.15625
- key_value_weight: bfloat16 [1536, 1024], P(('row', 'col')), may hold values from -0.15625 to 0.15625
- w_output: bfloat16 [1536, 1536], P(None, ('row', 'col')), may hold values from -0.625 to 0.625
- norm2_gain: bfloat16 [1536], P(('row', 'col')), may hold values from 0.5 to 1.5
- w_router: bfloat16 [1536, 64], P(('row', 'col')), may hold values from -0.078125 to 0.078125
- w_shgate: bfloat16 [1536, 1024], P(('row', 'col')), may hold values from -0.15625 to 0.15625
- w_shup: bfloat16 [1536, 1024], P(('row', 'col')), may hold values from -0.15625 to 0.15625
- w_shdown: bfloat16 [1024, 1536], P(None, ('row', 'col')), may hold values from -0.1875 to 0.1875
- w_exgate: bfloat16 [128, 1536, 256], P(('row', 'col')), may hold values from -0.15625 to 0.15625
- w_exup: bfloat16 [128, 1536, 256], P(('row', 'col')), may hold values from -0.15625 to 0.15625
- w_exdown: bfloat16 [128, 256, 1536], P(('row', 'col')), may hold values from -0.5 to 0.5
- cotangent: bfloat16 [16384, 1536], P(('row', 'col')), may hold values from -24 to 24
Outputs:
- block_out: bfloat16 [16384, 1536], P(('row', 'col'))
- grad_tokens: float32 [16384, 1536], P(('row', 'col'))
- grad_norm1_gain: float32 [1536], P(('row', 'col'))
- grad_w_query: float32 [1536, 1536], P(('row', 'col'))
- grad_w_keyval: float32 [1536, 1024], P(('row', 'col'))
- grad_w_output: float32 [1536, 1536], P(None, ('row', 'col'))
- grad_norm2_gain: float32 [1536], P(('row', 'col'))
- grad_w_router: float32 [1536, 64], P(('row', 'col'))
- grad_w_shgate: float32 [1536, 1024], P(('row', 'col'))
- grad_w_shup: float32 [1536, 1024], P(('row', 'col'))
- grad_w_shdown: float32 [1024, 1536], P(None, ('row', 'col'))
- grad_w_exgate: float32 [128, 1536, 256], P(('row', 'col'))
- grad_w_exup: float32 [128, 1536, 256], P(('row', 'col'))
- grad_w_exdown: float32 [128, 256, 1536], P(('row', 'col'))
Inputs may be any that keep to these rules, and one draw needn't show every extreme that they name: `routes`: each row names 6 different experts. Among the rows of one device no expert is named more than 24 times, and in every draw some expert is named exactly 24 times by the rows of some device. `segments`: each sequence of 1024 tokens holds three documents numbered 0, 1, 2 in order: the first and the last of 96 to 127 tokens each, the middle one all tokens between them, so that it holds tokens of every index of col.
All inputs are finite; a program needn't handle non-finite values.
Results may differ from a plain program's by a relative error of at most 0.02.
Values may be sent and summed in bfloat16 or wider, within the bound.
A program may use at most 320 MiB of HBM per device.

v0:
```python
import jax
import jax.numpy as jnp
from jax import lax
from jax.sharding import PartitionSpec as P

QUERY_HEADS = 12
KEY_VALUE_HEADS = 4
HEAD_SIZE = 128
EXPERTS = 64
TOPK = 6
CAP = 24


EPSILON = 1e-05


def inverse_rms(residual):
    return lax.rsqrt(jnp.mean(residual * residual, axis=-1, keepdims=True) + EPSILON)


def contract(left_side, right_side, left_dim, right_dim):
    return lax.dot_general(
        left_side,
        right_side,
        (((left_dim,), (right_dim,)), ((), ())),
        preferred_element_type=jnp.float32,
    )


def gated_unit(gate_pre, up_pre):
    return jax.nn.silu(gate_pre) * up_pre


def norm_backward(residual, norm_scale, gain_row, grad_normed):
    weighted = grad_normed * gain_row
    inner_sum = jnp.mean(weighted * residual, axis=-1, keepdims=True)
    grad_residual = (
        norm_scale * weighted - residual * norm_scale * norm_scale * norm_scale * inner_sum
    )
    grad_gain = jnp.sum(grad_normed * residual * norm_scale, axis=0)
    return (grad_residual, grad_gain)


def route_slots(routes):
    flat_routes = routes.reshape(-1)
    onehot = (flat_routes[:, None] == jnp.arange(EXPERTS, dtype=jnp.int32)[None, :]).astype(
        jnp.int32
    )
    slot_rank = jnp.sum((jnp.cumsum(onehot, axis=0) - 1) * onehot, axis=1)
    target = flat_routes * CAP + slot_rank
    route_ids = jnp.arange(flat_routes.shape[0], dtype=jnp.int32)
    slot_route = (
        jnp.full((EXPERTS * CAP,), flat_routes.shape[0], jnp.int32).at[target].set(route_ids)
    )
    return (target, slot_route)


def shards(
    tokens,
    segments,
    routes,
    norm1_gain,
    w_query,
    key_value_weight,
    w_output,
    norm2_gain,
    w_router,
    w_shgate,
    w_shup,
    w_shdown,
    w_exgate,
    w_exup,
    w_exdown,
    cotangent,
):
    local_rows = tokens.shape[0]
    feature_count = tokens.shape[1]
    col_count = lax.axis_size("col")
    col_place = lax.axis_index("col")
    sequence_length = local_rows * col_count
    heads_per_group = QUERY_HEADS // KEY_VALUE_HEADS
    key_value_width = KEY_VALUE_HEADS * HEAD_SIZE
    score_scale = HEAD_SIZE ** (-0.5)
    gains_first, query_w, keyval_w, output_w, gains_second, router_w, shgate_w, shup_w, shdown_w = (
        lax.all_gather(norm1_gain, ("row", "col"), axis=0, tiled=True),
        lax.all_gather(w_query, ("row", "col"), axis=0, tiled=True),
        lax.all_gather(key_value_weight, ("row", "col"), axis=0, tiled=True),
        lax.all_gather(w_output, ("row", "col"), axis=1, tiled=True),
        lax.all_gather(norm2_gain, ("row", "col"), axis=0, tiled=True),
        lax.all_gather(w_router, ("row", "col"), axis=0, tiled=True),
        lax.all_gather(w_shgate, ("row", "col"), axis=0, tiled=True),
        lax.all_gather(w_shup, ("row", "col"), axis=0, tiled=True),
        lax.all_gather(w_shdown, ("row", "col"), axis=1, tiled=True),
    )
    gain_first = gains_first.astype(jnp.float32)
    gain_second = gains_second.astype(jnp.float32)
    residual0 = tokens.astype(jnp.float32)
    scale_first = inverse_rms(residual0)
    first_normed = (residual0 * scale_first * gain_first).astype(jnp.bfloat16)
    query_rows = jnp.dot(first_normed, query_w, preferred_element_type=jnp.float32).astype(
        jnp.bfloat16
    )
    key_value_rows = jnp.dot(first_normed, keyval_w, preferred_element_type=jnp.float32).astype(
        jnp.bfloat16
    )
    own_segments = segments.astype(jnp.bfloat16)
    every_key_value, all_segments = (
        lax.all_gather(key_value_rows, "col", axis=0, tiled=True),
        lax.all_gather(own_segments, "col", axis=0, tiled=True),
    )
    key_matrix = every_key_value[:, :key_value_width].reshape(
        sequence_length, KEY_VALUE_HEADS, HEAD_SIZE
    )
    value_matrix = every_key_value[:, key_value_width:].reshape(
        sequence_length, KEY_VALUE_HEADS, HEAD_SIZE
    )
    query_head_count = query_rows.reshape(local_rows, KEY_VALUE_HEADS, heads_per_group, HEAD_SIZE)
    query_place = col_place * local_rows + jnp.arange(local_rows, dtype=jnp.int32)
    key_place = jnp.arange(sequence_length, dtype=jnp.int32)
    allowed = (key_place[None, :] <= query_place[:, None]) & (
        all_segments[None, :] == own_segments[:, None]
    )

    def masked_scores():
        raw_scores = (
            jnp.einsum(
                "tkgd,skd->kgts", query_head_count, key_matrix, preferred_element_type=jnp.float32
            )
            * score_scale
        )
        return jnp.where(allowed, raw_scores, -1e30)

    scores = masked_scores()
    row_max = jnp.max(scores, axis=-1, keepdims=True)
    shifted = jnp.exp(scores - row_max)
    row_total = jnp.sum(shifted, axis=-1, keepdims=True)
    log_total = row_max + jnp.log(row_total)
    weights_low = (shifted / row_total).astype(jnp.bfloat16)
    attended_rows = jnp.einsum(
        "kgts,skd->tkgd", weights_low, value_matrix, preferred_element_type=jnp.float32
    )
    attended_rows = attended_rows.reshape(local_rows, QUERY_HEADS * HEAD_SIZE).astype(jnp.bfloat16)
    residual1 = residual0 + jnp.dot(attended_rows, output_w, preferred_element_type=jnp.float32)
    scale_second = inverse_rms(residual1)
    second_normed = (residual1 * scale_second * gain_second).astype(jnp.bfloat16)
    logits = jnp.dot(second_normed, router_w, preferred_element_type=jnp.float32)
    chosen = jnp.take_along_axis(logits, routes, axis=1)
    chosen_exp = jnp.exp(chosen - jnp.max(chosen, axis=1, keepdims=True))
    gate_probs = chosen_exp / jnp.sum(chosen_exp, axis=1, keepdims=True)
    shared_gate = jnp.dot(second_normed, shgate_w, preferred_element_type=jnp.float32)
    shared_up = jnp.dot(second_normed, shup_w, preferred_element_type=jnp.float32)
    shared_hidden = gated_unit(shared_gate, shared_up).astype(jnp.bfloat16)
    shared_out = jnp.dot(shared_hidden, shdown_w, preferred_element_type=jnp.float32)
    target, slot_route = route_slots(routes)
    slot_token = slot_route // TOPK
    rows_padded = jnp.concatenate(
        [second_normed, jnp.zeros((1, feature_count), jnp.bfloat16)], axis=0
    )
    outgoing = jnp.repeat(rows_padded[slot_token].reshape(EXPERTS, CAP, feature_count), 2, axis=0)
    received = lax.all_to_all(outgoing, ("row", "col"), split_axis=0, concat_axis=1, tiled=True)
    gate_units = jnp.einsum("urd,udh->urh", received, w_exgate, preferred_element_type=jnp.float32)
    up_units = jnp.einsum("urd,udh->urh", received, w_exup, preferred_element_type=jnp.float32)
    hidden_units = gated_unit(gate_units, up_units).astype(jnp.bfloat16)
    half_out = jnp.einsum(
        "urh,uhd->urd", hidden_units, w_exdown, preferred_element_type=jnp.float32
    ).astype(jnp.bfloat16)
    returned = lax.all_to_all(half_out, ("row", "col"), split_axis=1, concat_axis=0, tiled=True)
    expert_slots = jnp.sum(
        returned.reshape(EXPERTS, 2, CAP, feature_count).astype(jnp.float32), axis=1
    ).reshape(EXPERTS * CAP, feature_count)
    route_out = expert_slots[target].reshape(local_rows, TOPK, feature_count)
    expert_mix = jnp.sum(route_out * gate_probs[:, :, None], axis=1)
    residual2 = residual1 + shared_out + expert_mix
    block_out = residual2.astype(jnp.bfloat16)
    grad_residual2 = cotangent.astype(jnp.float32)
    grad_shdown = contract(shared_hidden, cotangent, 0, 0)
    grad_shared_hidden = contract(cotangent, shdown_w, 1, 1)
    unused_shared, pull_shared = jax.vjp(gated_unit, shared_gate, shared_up)
    grad_shared_gate, grad_shared_up = pull_shared(grad_shared_hidden)
    grad_shared_gate = grad_shared_gate.astype(jnp.bfloat16)
    grad_shared_up = grad_shared_up.astype(jnp.bfloat16)
    grad_shgate = contract(second_normed, grad_shared_gate, 0, 0)
    grad_shup = contract(second_normed, grad_shared_up, 0, 0)
    grad_second = contract(grad_shared_gate, shgate_w, 1, 1) + contract(
        grad_shared_up, shup_w, 1, 1
    )
    gates_padded = jnp.concatenate([gate_probs.reshape(-1), jnp.zeros((1,), jnp.float32)], axis=0)
    cotangent_padded = jnp.concatenate(
        [grad_residual2, jnp.zeros((1, feature_count), jnp.float32)], axis=0
    )
    grad_slots = (cotangent_padded[slot_token] * gates_padded[slot_route][:, None]).astype(
        jnp.bfloat16
    )
    outgoing_grads = jnp.repeat(grad_slots.reshape(EXPERTS, CAP, feature_count), 2, axis=0)
    grad_received = lax.all_to_all(
        outgoing_grads, ("row", "col"), split_axis=0, concat_axis=1, tiled=True
    )
    grad_hidden_units = jnp.einsum(
        "urd,uhd->urh", grad_received, w_exdown, preferred_element_type=jnp.float32
    )
    grad_exdown = jnp.einsum(
        "urh,urd->uhd", hidden_units, grad_received, preferred_element_type=jnp.float32
    )
    unused_units, pull_units = jax.vjp(gated_unit, gate_units, up_units)
    grad_gate_units, grad_up_units = pull_units(grad_hidden_units)
    grad_gate_low = grad_gate_units.astype(jnp.bfloat16)
    grad_up_low = grad_up_units.astype(jnp.bfloat16)
    grad_exgate = jnp.einsum(
        "urd,urh->udh", received, grad_gate_low, preferred_element_type=jnp.float32
    )
    grad_exup = jnp.einsum(
        "urd,urh->udh", received, grad_up_low, preferred_element_type=jnp.float32
    )
    grad_rows = jnp.einsum(
        "urh,udh->urd", grad_gate_low, w_exgate, preferred_element_type=jnp.float32
    )
    grad_rows = (
        grad_rows
        + jnp.einsum("urh,udh->urd", grad_up_low, w_exup, preferred_element_type=jnp.float32)
    ).astype(jnp.bfloat16)
    grad_returned = lax.all_to_all(
        grad_rows, ("row", "col"), split_axis=1, concat_axis=0, tiled=True
    )
    grad_slot_rows = jnp.sum(
        grad_returned.reshape(EXPERTS, 2, CAP, feature_count).astype(jnp.float32), axis=1
    ).reshape(EXPERTS * CAP, feature_count)
    grad_second = grad_second + jnp.sum(
        grad_slot_rows[target].reshape(local_rows, TOPK, feature_count), axis=1
    )
    grad_gates = jnp.sum(route_out * grad_residual2[:, None, :], axis=2)
    grad_chosen = gate_probs * (
        grad_gates - jnp.sum(gate_probs * grad_gates, axis=1, keepdims=True)
    )
    expert_match = (
        routes[:, :, None] == jnp.arange(EXPERTS, dtype=jnp.int32)[None, None, :]
    ).astype(jnp.float32)
    grad_logits = jnp.sum(grad_chosen[:, :, None] * expert_match, axis=1).astype(jnp.bfloat16)
    grad_router = contract(second_normed, grad_logits, 0, 0)
    grad_second = grad_second + contract(grad_logits, router_w, 1, 1)
    grad_norm_second, grad_gain_second = norm_backward(
        residual1, scale_second, gain_second, grad_second
    )
    grad_residual1 = grad_residual2 + grad_norm_second
    grad_attn_low = grad_residual1.astype(jnp.bfloat16)
    grad_output = contract(attended_rows, grad_attn_low, 0, 0)
    attended_gradient = contract(grad_attn_low, output_w, 1, 1).astype(jnp.bfloat16)
    weights_again = jnp.exp(masked_scores() - log_total)
    heads_gradient = attended_gradient.reshape(
        local_rows, KEY_VALUE_HEADS, heads_per_group, HEAD_SIZE
    )
    grad_weights = jnp.einsum(
        "tkgd,skd->kgts", heads_gradient, value_matrix, preferred_element_type=jnp.float32
    )
    inner_sum = jnp.sum(weights_again * grad_weights, axis=-1, keepdims=True)
    grad_scores = (weights_again * (grad_weights - inner_sum)).astype(jnp.bfloat16)
    grad_queries = (
        jnp.einsum("kgts,skd->tkgd", grad_scores, key_matrix, preferred_element_type=jnp.float32)
        * score_scale
    )
    grad_queries = grad_queries.reshape(local_rows, QUERY_HEADS * HEAD_SIZE).astype(jnp.bfloat16)
    grad_keys = (
        jnp.einsum(
            "kgts,tkgd->skd", grad_scores, query_head_count, preferred_element_type=jnp.float32
        )
        * score_scale
    )
    grad_values = jnp.einsum(
        "kgts,tkgd->skd",
        weights_again.astype(jnp.bfloat16),
        heads_gradient,
        preferred_element_type=jnp.float32,
    )
    partial_keyvals = jnp.concatenate(
        [
            grad_keys.reshape(sequence_length, key_value_width),
            grad_values.reshape(sequence_length, key_value_width),
        ],
        axis=1,
    )
    grad_keyvals = lax.psum_scatter(
        partial_keyvals.astype(jnp.bfloat16), "col", scatter_dimension=0, tiled=True
    )
    grad_query = contract(first_normed, grad_queries, 0, 0)
    grad_keyval = contract(first_normed, grad_keyvals, 0, 0)
    grad_first = contract(grad_queries, query_w, 1, 1) + contract(grad_keyvals, keyval_w, 1, 1)
    grad_norm_first, grad_gain_first = norm_backward(residual0, scale_first, gain_first, grad_first)
    grad_tokens = grad_residual1 + grad_norm_first
    (
        sum_gain1,
        sum_query,
        sum_keyval,
        sum_output,
        sum_gain2,
        sum_router,
        sum_shgate,
        sum_shup,
        sum_shdown,
    ) = (
        lax.psum_scatter(grad_gain_first, ("row", "col"), scatter_dimension=0, tiled=True),
        lax.psum_scatter(grad_query, ("row", "col"), scatter_dimension=0, tiled=True),
        lax.psum_scatter(grad_keyval, ("row", "col"), scatter_dimension=0, tiled=True),
        lax.psum_scatter(grad_output, ("row", "col"), scatter_dimension=1, tiled=True),
        lax.psum_scatter(grad_gain_second, ("row", "col"), scatter_dimension=0, tiled=True),
        lax.psum_scatter(grad_router, ("row", "col"), scatter_dimension=0, tiled=True),
        lax.psum_scatter(grad_shgate, ("row", "col"), scatter_dimension=0, tiled=True),
        lax.psum_scatter(grad_shup, ("row", "col"), scatter_dimension=0, tiled=True),
        lax.psum_scatter(grad_shdown, ("row", "col"), scatter_dimension=1, tiled=True),
    )
    return (
        block_out,
        grad_tokens,
        sum_gain1,
        sum_query,
        sum_keyval,
        sum_output,
        sum_gain2,
        sum_router,
        sum_shgate,
        sum_shup,
        sum_shdown,
        grad_exgate,
        grad_exup,
        grad_exdown,
    )


def solution(mesh):
    in_specs = (
        P(("row", "col"), None),
        P(("row", "col")),
        P(("row", "col"), None),
        P(("row", "col")),
        P(("row", "col"), None),
        P(("row", "col"), None),
        P(None, ("row", "col")),
        P(("row", "col")),
        P(("row", "col"), None),
        P(("row", "col"), None),
        P(("row", "col"), None),
        P(None, ("row", "col")),
        P(("row", "col"), None, None),
        P(("row", "col"), None, None),
        P(("row", "col"), None, None),
        P(("row", "col"), None),
    )
    out_specs = (
        P(("row", "col"), None),
        P(("row", "col"), None),
        P(("row", "col")),
        P(("row", "col"), None),
        P(("row", "col"), None),
        P(None, ("row", "col")),
        P(("row", "col")),
        P(("row", "col"), None),
        P(("row", "col"), None),
        P(("row", "col"), None),
        P(None, ("row", "col")),
        P(("row", "col"), None, None),
        P(("row", "col"), None, None),
        P(("row", "col"), None, None),
    )
    return jax.shard_map(shards, mesh=mesh, in_specs=in_specs, out_specs=out_specs, check_vma=False)
```

profile of v0, /device:TPU:3, one launch (start us, length us, event | category | flops | bytes accessed | tf_op | source)
XLA Modules:
  0.0 4848.2 jit_solution(7134141497252804764)
XLA Ops:
  11.2 67.1 %all-reduce.21 = (bf16[1536]{0:T(1024)(128)(2,1)S(1)}, bf16[1536]{0:T(1024)(128)(2,1)S(1)}) all-reduce(bf16[1536]{0:T(1024)(128)(2,1)S(1)} %dynamic-update-slice, bf16[1536]{0:T(1024)(128)(2,1)S(1)} %dynamic-update-slice.1), channel_id=1, replica_groups=mesh['row'=16,'col'=8] {'row','col'}, use_global_device_ids=true, to_apply=%add.2 | all-reduce | flops 3072 | bytes 12288
  79.5 237.6 %all-gather.18.cloned.1.call-done = bf16[128,12,1024]{2,1,0:T(8,128)(2,1)} async-done(((bf16[1,12,1024]{2,1,0:T(8,128)(2,1)}), bf16[128,12,1024]{2,1,0:T(8,128)(2,1)}) %all-gather.18.cloned.1.call-update) | async-done | bytes 3145744 | tf_op jit(solution)/shard_map/all_gather | solution.py:87
  356.2 271.9 %all-gather.20.cloned.1.call-done = bf16[128,12,1536]{2,1,0:T(8,128)(2,1)} async-done(((bf16[1,12,1536]{2,1,0:T(8,128)(2,1)}), bf16[128,12,1536]{2,1,0:T(8,128)(2,1)}) %all-gather.20.cloned.1.call-update) | async-done | bytes 4718608 | tf_op jit(solution)/shard_map/all_gather | solution.py:86
  640.4 302.1 %all-gather.22.cloned.1.call-done = bf16[128,12,1536]{2,1,0:T(8,128)(2,1)} async-done(((bf16[1,12,1536]{2,1,0:T(8,128)(2,1)}), bf16[128,12,1536]{2,1,0:T(8,128)(2,1)}) %all-gather.22.cloned.1.call-update) | async-done | bytes 4718608 | tf_op jit(solution)/shard_map/all_gather | solution.py:88
  950.7 48.2 all-gather.16.cloned.1.call-done
  1039.1 402.1 %all-gather.7 = bf16[128,12,64]{2,1,0:T(8,128)(2,1)S(1)} all-gather(bf16[1,12,64]{2,1,0:T(8,128)(2,1)S(1)} %bitcast.215), channel_id=1, replica_groups=mesh['row'=16,'col'=8] {'row','col'}, dimensions={0}, use_global_device_ids=true | all-gather | bytes 198144 | tf_op jit(solution)/shard_map/all_gather | solution.py:90
  1514.9 99.5 %all-to-all-done.2 = bf16[128,24,1536]{2,1,0:T(8,128)(2,1)} async-done(((bf16[128,24,1536]{2,1,0:T(8,128)(2,1)}), bf16[128,24,1536]{2,1,0:T(8,128)(2,1)}, u32[]{:S(2)}, u32[]{:S(2)}) %all-to-all-start.2) | async-done | bytes 9437216 | tf_op jit(solution)/shard_map/all_to_all | solution.py:195
  1627.9 103.4 %copy.196 = bf16[1,3072,1536]{2,0,1:T(2,128)(2,1)} copy(bf16[1,3072,1536]{2,1,0:T(8,128)(2,1)S(1)} %fusion.7) | data formatting | bytes 18874368 | tf_op jit(solution)/shard_map/convert_element_type | solution.py:166
  1731.8 61.3 %reduce.9 = bf16[3072,1536]{1,0:T(8,128)(2,1)} reduce(bf16[3072,1,1536]{2,1,0:T(2,128)(2,1)} %bitcast.180, bf16[]{:T(256)} %broadcast.252), dimensions={1}, to_apply=%bitcast.171.reduce_sub_computation | reduce | bytes 18874370
  1863.0 61.5 %reduce.10 = bf16[3072,1536]{1,0:T(8,128)(2,1)} reduce(bf16[3072,1,1536]{2,1,0:T(2,128)(2,1)} %bitcast.181, bf16[]{:T(256)} %broadcast.252), dimensions={1}, to_apply=%bitcast.170.reduce_sub_computation | reduce | bytes 18874370
  1963.7 364.0 %all-gather.26.cloned.1.call-done = bf16[128,12,1024]{2,1,0:T(8,128)(2,1)} async-done(((bf16[1,12,1024]{2,1,0:T(8,128)(2,1)}), bf16[128,12,1024]{2,1,0:T(8,128)(2,1)}) %all-gather.26.cloned.1.call-update) | async-done | bytes 3145744 | tf_op jit(solution)/shard_map/all_gather | solution.py:92
  2333.8 303.5 %all-gather.28.cloned.1.call-done = bf16[128,12,1024]{2,1,0:T(8,128)(2,1)} async-done(((bf16[1,12,1024]{2,1,0:T(8,128)(2,1)}), bf16[128,12,1024]{2,1,0:T(8,128)(2,1)}) %all-gather.28.cloned.1.call-update) | async-done | bytes 3145744 | tf_op jit(solution)/shard_map/all_gather | solution.py:93
  2654.6 39.4 reshape.456
  2743.5 39.4 reshape.458
  2852.0 359.4 %fusion.6 = f32[1024,16]{0,1:T(8,128)} fusion(f32[1024,1536]{0,1:T(8,128)} %fusion.91), kind=kCustom, calls=%all-reduce-scatter.6 | all-reduce-scatter fusion | flops 2097153 | bytes 6356992
  3225.6 29.3 collective-permute-start.219
  3343.1 557.5 %fusion.81 = (f32[16,1536]{1,0:T(8,128)S(1)}, f32[16,1024]{1,0:T(8,128)S(1)}, f32[1536,16]{0,1:T(8,128)S(1)}, f32[16,64]{1,0:T(8,128)S(1)}, f32[16,1024]{1,0:T(8,128)S(1)}, /*index=5*/f32[16,1024]{1,0:T(8,128)S(1)}) fusion(f32[1536,1536]{1,0:T(8,128)} %fusion.77, f32[1536,1024]{1,0:T(8,128)} %fusion.75, f32[1536,1536]{0,1:T(8,128)} %fusion.61, ...), kind=kCustom, calls=%all-reduce-scatter.7 | all-reduce-scatter fusion | flops 12713985 | bytes 38539264
  4234.5 50.5 %concatenate.26 = f32[1024,524]{0,1:T(8,128)} concatenate(f32[1024,12]{0,1:T(8,128)} %copy-done.128, f32[1024,16]{0,1:T(8,128)} %copy-done.127, f32[1024,16]{0,1:T(8,128)} %copy-done.129, f32[1024,16]{0,1:T(8,128)} %copy-done.130, f32[1024,16]{0,1:T(8,128)} %copy-done.131, f32[1024,16]{0,1:T(8,128)} %copy-done.132, f32[1024,16]{0,1:T(8,128)} %copy-done.135, ...), dimensions={1} | concatenate | bytes 4292608
  4429.2 65.2 %all-reduce.20 = (f32[1536]{0:T(1024)S(1)}, f32[1536]{0:T(1024)S(1)}) all-reduce(f32[1536]{0:T(1024)} %get-tuple-element.18, f32[1536]{0:T(1024)} %get-tuple-element.16), channel_id=3, replica_groups=mesh['row'=16,'col'=8] {'row','col'}, use_global_device_ids=true, to_apply=%region_22.23.clone | all-reduce | flops 3072 | bytes 24576
  4542.7 49.4 %concatenate.21 = f32[524,1024]{1,0:T(8,128)} concatenate(f32[12,1024]{1,0:T(8,128)S(1)} %copy-done.134, f32[16,1024]{1,0:T(8,128)S(1)} %copy-done.121, f32[16,1024]{1,0:T(8,128)S(1)} %copy-done.123, f32[16,1024]{1,0:T(8,128)S(1)} %copy-done.137, f32[16,1024]{1,0:T(8,128)S(1)} %copy-done.140, f32[16,1024]{1,0:T(8,128)} %copy-done.142, f32[16,1024]{1,0:T(8,128)} %copy-done.144, ...), dimensions={0} | concatenate | bytes 4292608
  4592.3 49.6 %concatenate.24 = f32[524,1024]{1,0:T(8,128)} concatenate(f32[12,1024]{1,0:T(8,128)S(1)} %copy-done.126, f32[16,1024]{1,0:T(8,128)} %copy-done.187, f32[16,1024]{1,0:T(8,128)} %copy-done.188, f32[16,1024]{1,0:T(8,128)} %copy-done.189, f32[16,1024]{1,0:T(8,128)} %copy-done.190, f32[16,1024]{1,0:T(8,128)} %copy-done.191, f32[16,1024]{1,0:T(8,128)} %collective-permute-done.153, ...), dimensions={0} | concatenate | bytes 4292608
  4641.8 29.5 concatenate.25
  4715.2 53.4 %concatenate.20 = f32[524,1536]{1,0:T(8,128)} concatenate(f32[12,1536]{1,0:T(8,128)} %copy-done.58, f32[16,1536]{1,0:T(8,128)S(1)} %copy-done.55, f32[16,1536]{1,0:T(8,128)S(1)} %copy-done.57, f32[16,1536]{1,0:T(8,128)} %copy-done.59, f32[16,1536]{1,0:T(8,128)} %copy-done.60, f32[16,1536]{1,0:T(8,128)} %copy-done.61, f32[16,1536]{1,0:T(8,128)} %copy-done.62, ...), dimensions={0} | concatenate | bytes 6438912
  4789.0 50.4 %concatenate.22 = f32[1536,524]{0,1:T(8,128)} concatenate(f32[1536,12]{0,1:T(8,128)S(1)} %copy-done.53, f32[1536,16]{0,1:T(8,128)S(1)} %copy-done.82, f32[1536,16]{0,1:T(8,128)S(1)} %copy-done.85, f32[1536,16]{0,1:T(8,128)S(1)} %copy-done.88, f32[1536,16]{0,1:T(8,128)S(1)} %copy-done.91, f32[1536,16]{0,1:T(8,128)S(1)} %copy-done.93, f32[1536,16]{0,1:T(8,128)S(1)} %copy-done.95, ...), dimensions={1} | concatenate | bytes 6438912
  (1119 shorter events, 1132.0 us)
Async XLA Ops:
  7.2 309.9 %all-gather.18.cloned.1.call-start = ((), (), s32[]{:S(2)}) async-start(), calls=%async_computation.6 | async-start | bytes 4227072 | tf_op jit(solution)/shard_map/all_gather | solution.py:87
  7.9 620.1 %all-gather.20.cloned.1.call-start = ((), (), s32[]{:S(2)}) async-start(), calls=%async_computation.7 | async-start | bytes 6340608 | tf_op jit(solution)/shard_map/all_gather | solution.py:86
  8.7 933.7 %all-gather.22.cloned.1.call-start = ((), (), s32[]{:S(2)}) async-start(), calls=%async_computation.8 | async-start | bytes 6340608 | tf_op jit(solution)/shard_map/all_gather | solution.py:88
  9.4 989.5 %all-gather.16.cloned.1.call-start = ((), (), s32[]{:S(2)}) async-start(), calls=%async_computation.5 | async-start | bytes 2359296 | tf_op jit(solution)/shard_map/all_gather | solution.py:108
  1028.8 438.3 %all-to-all-start = ((bf16[128,24,1536]{2,1,0:T(8,128)(2,1)}), bf16[128,24,1536]{2,1,0:T(8,128)(2,1)}, u32[]{:S(2)}, u32[]{:S(2)}) async-start(bf16[128,24,1536]{2,1,0:T(8,128)(2,1)} %bitcast.190), calls=%async_computation | async-start | bytes 18874368 | tf_op jit(solution)/shard_map/all_to_all | solution.py:160
  1473.8 140.6 %all-to-all-start.2 = ((bf16[128,24,1536]{2,1,0:T(8,128)(2,1)}), bf16[128,24,1536]{2,1,0:T(8,128)(2,1)}, u32[]{:S(2)}, u32[]{:S(2)}) async-start(bf16[128,24,1536]{2,1,0:T(8,128)(2,1)} %bitcast.191), calls=%async_computation.2 | async-start | bytes 18874368 | tf_op jit(solution)/shard_map/all_to_all | solution.py:195
  1498.3 459.0 %all-gather.24.cloned.1.call-start = ((), (), s32[]{:S(2)}) async-start(), calls=%async_computation.9 | async-start | bytes 4227072 | tf_op jit(solution)/shard_map/all_gather | solution.py:91
  1814.8 131.4 %all-to-all-start.1 = ((bf16[128,2,18432]{2,1,0:T(2,128)(2,1)}), bf16[128,2,18432]{2,1,0:T(2,128)(2,1)}, u32[]{:S(2)}, u32[]{:S(2)}) async-start(bf16[128,2,18432]{2,1,0:T(2,128)(2,1)} %reshape.455), calls=%async_computation.1 | async-start | bytes 18874368 | tf_op jit(solution)/shard_map/all_to_all | solution.py:167
  1825.6 502.0 %all-gather.26.cloned.1.call-start = ((), (), s32[]{:S(2)}) async-start(), calls=%async_computation.10 | async-start | bytes 4227072 | tf_op jit(solution)/shard_map/all_gather | solution.py:92
  1946.2 797.3 %all-to-all-start.3 = ((bf16[128,2,18432]{2,1,0:T(2,128)(2,1)}), bf16[128,2,18432]{2,1,0:T(2,128)(2,1)}, u32[]{:S(2)}, u32[]{:S(2)}) async-start(bf16[128,2,18432]{2,1,0:T(2,128)(2,1)} %reshape.457), calls=%async_computation.3 | async-start | bytes 18874368 | tf_op jit(solution)/shard_map/all_to_all | solution.py:221
  1956.4 680.9 %all-gather.28.cloned.1.call-start = ((), (), s32[]{:S(2)}) async-start(), calls=%async_computation.11 | async-start | bytes 4227072 | tf_op jit(solution)/shard_map/all_gather | solution.py:93
  1957.2 1365.2 %reduce-scatter.18.cloned.1.call-start = ((), (), s32[]{:S(2)}) async-start(), calls=%async_computation.12 | async-start | bytes 2359296
  3327.1 573.5 %collective-permute-start.196 = (f32[1024,16]{0,1:T(8,128)}, f32[1024,16]{0,1:T(8,128)}, u32[]{:S(2)}, u32[]{:S(2)}) collective-permute-start(f32[1024,16]{0,1:T(8,128)} %fusion.6), channel_id=1, source_target_pairs={{0,5},{1,6},{2,7},{3,8},{4,9},{5,10},{6,11},{7,12},{8,13},{9,14},{... | collective-permute-start | bytes 196616
  3332.6 569.5 %collective-permute-start.195 = (f32[1024,16]{0,1:T(8,128)}, f32[1024,16]{0,1:T(8,128)}, u32[]{:S(2)}, u32[]{:S(2)}) collective-permute-start(f32[1024,16]{0,1:T(8,128)} %fusion.6), channel_id=1, source_target_pairs={{0,4},{1,5},{2,6},{3,7},{4,8},{5,9},{6,10},{7,11},{8,12},{9,13},{1... | collective-permute-start | bytes 196616
  3334.6 568.8 %collective-permute-start.194 = (f32[1024,16]{0,1:T(8,128)}, f32[1024,16]{0,1:T(8,128)}, u32[]{:S(2)}, u32[]{:S(2)}) collective-permute-start(f32[1024,16]{0,1:T(8,128)} %fusion.6), channel_id=1, source_target_pairs={{0,3},{1,4},{2,5},{3,6},{4,7},{5,8},{6,9},{7,10},{8,11},{9,12},{10... | collective-permute-start | bytes 196616
  3337.4 567.3 %collective-permute-start.193 = (f32[1024,16]{0,1:T(8,128)}, f32[1024,16]{0,1:T(8,128)}, u32[]{:S(2)}, u32[]{:S(2)}) collective-permute-start(f32[1024,16]{0,1:T(8,128)} %fusion.6), channel_id=1, source_target_pairs={{0,2},{1,3},{2,4},{3,5},{4,6},{5,7},{6,8},{7,9},{8,10},{9,11},{10,... | collective-permute-start | bytes 196616
  3339.7 576.6 %collective-permute-start.192 = (f32[1024,16]{0,1:T(8,128)}, f32[1024,16]{0,1:T(8,128)}, u32[]{:S(2)}, u32[]{:S(2)}) collective-permute-start(f32[1024,16]{0,1:T(8,128)} %fusion.6), channel_id=1, source_target_pairs={{0,1},{1,2},{2,3},{3,4},{4,5},{5,6},{6,7},{7,8},{8,9},{9,10},{10,1... | collective-permute-start | bytes 196616
  4420.7 110.2 %collective-permute-start.90 = (f32[1536,16]{0,1:T(8,128)S(1)}, f32[1536,16]{0,1:T(8,128)S(1)}, u32[]{:S(2)}, u32[]{:S(2)}) collective-permute-start(f32[1536,16]{0,1:T(8,128)S(1)} %get-tuple-element.32), channel_id=1, source_target_pairs={{0,27},{1,28},{2,29},{3,30},{4,31},{5,32},{6,33},{7,34},{8,35},{9,... | collective-permute-start | bytes 294920
  4422.2 113.7 %collective-permute-start.89 = (f32[1536,16]{0,1:T(8,128)S(1)}, f32[1536,16]{0,1:T(8,128)S(1)}, u32[]{:S(2)}, u32[]{:S(2)}) collective-permute-start(f32[1536,16]{0,1:T(8,128)S(1)} %get-tuple-element.32), channel_id=1, source_target_pairs={{0,26},{1,27},{2,28},{3,29},{4,30},{5,31},{6,32},{7,33},{8,34},{9,... | collective-permute-start | bytes 294920
  4520.3 151.1 %collective-permute-start.88 = (f32[1536,16]{0,1:T(8,128)S(1)}, f32[1536,16]{0,1:T(8,128)S(1)}, u32[]{:S(2)}, u32[]{:S(2)}) collective-permute-start(f32[1536,16]{0,1:T(8,128)S(1)} %get-tuple-element.32), channel_id=1, source_target_pairs={{0,25},{1,26},{2,27},{3,28},{4,29},{5,30},{6,31},{7,32},{8,33},{9,... | collective-permute-start | bytes 294920
  4523.3 151.0 %collective-permute-start.87 = (f32[1536,16]{0,1:T(8,128)S(1)}, f32[1536,16]{0,1:T(8,128)}, u32[]{:S(2)}, u32[]{:S(2)}) collective-permute-start(f32[1536,16]{0,1:T(8,128)S(1)} %get-tuple-element.32), channel_id=1, source_target_pairs={{0,24},{1,25},{2,26},{3,27},{4,28},{5,29},{6,30},{7,31},{8,32},{9,... | collective-permute-start | bytes 294920
  4527.1 148.7 %collective-permute-start.86 = (f32[1536,16]{0,1:T(8,128)S(1)}, f32[1536,16]{0,1:T(8,128)}, u32[]{:S(2)}, u32[]{:S(2)}) collective-permute-start(f32[1536,16]{0,1:T(8,128)S(1)} %get-tuple-element.32), channel_id=1, source_target_pairs={{0,23},{1,24},{2,25},{3,26},{4,27},{5,28},{6,29},{7,30},{8,31},{9,... | collective-permute-start | bytes 294920
  4531.0 146.5 %collective-permute-start.85 = (f32[1536,16]{0,1:T(8,128)S(1)}, f32[1536,16]{0,1:T(8,128)}, u32[]{:S(2)}, u32[]{:S(2)}) collective-permute-start(f32[1536,16]{0,1:T(8,128)S(1)} %get-tuple-element.32), channel_id=1, source_target_pairs={{0,22},{1,23},{2,24},{3,25},{4,26},{5,27},{6,28},{7,29},{8,30},{9,... | collective-permute-start | bytes 294920
  4535.9 144.4 %collective-permute-start.84 = (f32[1536,16]{0,1:T(8,128)S(1)}, f32[1536,16]{0,1:T(8,128)}, u32[]{:S(2)}, u32[]{:S(2)}) collective-permute-start(f32[1536,16]{0,1:T(8,128)S(1)} %get-tuple-element.32), channel_id=1, source_target_pairs={{0,21},{1,22},{2,23},{3,24},{4,25},{5,26},{6,27},{7,28},{8,29},{9,... | collective-permute-start | bytes 294920
  (460 other events, 25226.8 us)
Sparse Core Ops, SparseCore 0:
  9.7 307.3 all-gather.17
  318.8 309.2 all-gather.19
  629.8 312.6 all-gather.21
  945.2 53.6 all-gather.15
  1500.5 442.5 all-gather.23
  1944.7 382.9 all-gather.25
  2329.3 307.9 all-gather.27
  2852.1 79.0 reduce-scatter.17
where the time goes:
time: 4880 us; the launch traced here: 4850 us
  waiting for transfers between devices  1630 us (33%)
  blocking collectives  1470 us (30%)
  local copies, waits for them, and re-layouts  734 us (15%)
  starting transfers between devices  678 us (14%)
  other arithmetic  171 us (4%)
  matrix products  135 us (3%)
    unnamed x4, blocking collectives  1050 us
    unnamed x225, starting transfers between devices  622 us
    unnamed x539, local copies, waits for them, and re-layouts  531 us
    all_gather x1, blocking collectives, shards(): lax.all_gather(w_router, ('row', 'col'), axis=0, tiled=True)  402 us
    all_gather x1, waiting for transfers between devices, shards(): lax.all_gather(w_shup, ('row', 'col'), axis=0, tiled=True)  364 us
    all_gather x1, waiting for transfers between devices, shards(): lax.all_gather(w_shdown, ('row', 'col'), axis=1, tiled=True)  304 us
    all_gather x1, waiting for transfers between devices, shards(): lax.all_gather(w_output, ('row', 'col'), axis=1, tiled=True)  302 us
    all_gather x1, waiting for transfers between devices, shards(): lax.all_gather(w_query, ('row', 'col'), axis=0, tiled=True)  272 us
  transfers between devices with their start and end apart: 236, of which 10 were waited for; matrix products, arithmetic and copies ran while one was open for 36% of the time, Pallas kernels for 0%

commit v1 on v0

v1 whole, which is shorter than its diff:
```python
import functools

import jax
import jax.numpy as jnp
from jax import lax
from jax.experimental import pallas as pl
from jax.experimental.pallas import tpu as pltpu
from jax.sharding import Mesh
from jax.sharding import PartitionSpec as P

QUERY_HEADS = 12
KEY_VALUE_HEADS = 4
HEAD_SIZE = 128
EXPERTS = 64
TOPK = 6
CAP = 24
EPSILON = 1e-05

F32 = jnp.float32
BF16 = jnp.bfloat16
MESH_ID = pl.DeviceIdType.MESH
AXES = ("z", "yl", "core", "yh", "xh", "xl")
SIZES = (4, 2, 2, 2, 2, 2)
EXPERT_AXES = ("z", "yl", "core", "yh", "xh")
COL_AXES = ("yh", "xh", "xl")

PARTS = (
    ("qkv", 2560, "yz"),
    ("outt", 1536, "yzx"),
    ("shgu", 2048, "zy"),
    ("shdt", 1024, "zy"),
    ("misc", 128, "yz"),
)
TOTAL = sum(part[1] for part in PARTS)


def rem(value, size):
    return lax.rem(value, jnp.int32(size))


def place():
    at = {name: lax.axis_index(name) for name in AXES}
    return {
        "x": at["xh"] * 2 + at["xl"],
        "y": at["yh"] * 2 + at["yl"],
        "z": at["z"],
        "core": at["core"],
    }


def device(axis, value):
    if axis == "x":
        return {"xh": value // 2, "xl": rem(value, 2)}
    if axis == "y":
        return {"yh": value // 2, "yl": rem(value, 2)}
    return {axis: value}


def greet(targets):
    barrier = pltpu.get_barrier_semaphore()
    for target in targets:
        pl.semaphore_signal(barrier, inc=1, device_id=target, device_id_type=MESH_ID)
    pl.semaphore_wait(barrier, len(targets))


class Wires:
    def __init__(self, send_sems, recv_sems, local_sems):
        self.send, self.recv, self.local = send_sems, recv_sems, local_sems
        self.used, self.used_local, self.started, self.kept = 0, 0, [], []

    def remote(self, source, target, where):
        copy = pltpu.make_async_remote_copy(
            src_ref=source,
            dst_ref=target,
            send_sem=self.send.at[self.used],
            recv_sem=self.recv.at[self.used],
            device_id=where,
            device_id_type=MESH_ID,
        )
        self.used += 1
        copy.start()
        self.started.append(copy)
        return copy

    def copy(self, source, target):
        copy = pltpu.make_async_copy(source, target, self.local.at[self.used_local])
        self.used_local += 1
        copy.start()
        return copy

    def finish(self):
        for copy in self.started:
            copy.wait_send()


def halves(width):
    first = width // 256 * 128 if width > 128 else width
    return first, width - first


def spread_rows(shape, swap):
    dense = lax.broadcasted_iota(jnp.int32, shape, 1 if swap else 0)
    padded = lax.broadcasted_iota(jnp.int32, shape, 0 if swap else 1)
    shift = jnp.zeros(shape, jnp.int32)
    for edge in (12, 24, 36):
        shift = shift + jnp.where(dense >= edge, 4, 0)
    return dense + shift == padded


def block_ref(ref, axes, me, axis, value, columns):
    spot = dict(me)
    spot[axis] = value
    z = slice(None) if "z" in axes else spot["z"]
    yl = slice(None) if "y" in axes else rem(spot["y"], 2)
    yh = slice(None) if "y" in axes else spot["y"] // 2
    return ref.at[z, yl, me["core"], yh, :, columns]


def gather_kernel(shard_ref, *rest):
    count = len(PARTS)
    outs = rest[:count]
    landed = rest[count]
    stages = rest[count + 1 : count + 1 + count]
    send_sems, recv_sems, local_sems = rest[count + 1 + count :]
    me = place()
    nxt = {axis: rem(me[axis] + 1, 4) for axis in "xyz"}
    opp = {axis: rem(me[axis] + 2, 4) for axis in "xyz"}
    prv = {axis: rem(me[axis] + 3, 4) for axis in "xyz"}
    sibling = {"core": 1 - me["core"]}
    greet(
        [device("x", nxt["x"]), device("x", opp["x"]), device("x", prv["x"])]
        + [device("y", nxt["y"]), device("y", prv["y"])]
        + [device("z", nxt["z"]), device("z", prv["z"]), sibling]
    )
    wires = Wires(send_sems, recv_sems, local_sems)
    first = [
        wires.remote(shard_ref, landed.at[me["x"]], device("x", where["x"]))
        for where in (nxt, prv, opp)
    ]
    own = wires.copy(shard_ref, landed.at[me["x"]])
    own.wait()
    for copy in first:
        copy.wait_recv()
    pick = spread_rows((48, 64), False).astype(BF16)
    runs, start = [], 0
    for index, (name, width, order) in enumerate(PARTS):
        for left in range(0, width, 512):
            size = min(512, width - left)
            piece = landed[:, :, start + left : start + left + size].reshape(64, size)
            stages[index][:, left : left + size] = jnp.dot(
                pick, piece, preferred_element_type=F32
            ).astype(BF16)
        start += width
        if len(order) == 3:
            quarter = width // 4
            columns = pl.ds(pl.multiple_of(me["x"] * quarter, 128), quarter)
        else:
            quarter, columns = width, pl.ds(0, width)
        runs.append(
            {
                "out": outs[index],
                "order": order,
                "width": quarter,
                "base": me["x"] * quarter if len(order) == 3 else 0,
                "columns": columns,
                "done": "",
                "stage": stages[index],
                "index": index,
            }
        )
        runs[-1]["own"] = wires.copy(
            stages[index].at[:, columns],
            outs[index].at[me["z"], rem(me["y"], 2), me["core"], me["y"] // 2, :, columns],
        )

    def part_columns(run, axis, value, which):
        if axis == "x":
            base = value * run["width"]
        else:
            base = run["base"]
        left, size = 0, run["width"]
        if which is not None:
            first_half, second_half = halves(run["width"])
            left, size = (0, first_half) if which == 0 else (first_half, second_half)
        if isinstance(base, int):
            return pl.ds(base + left, size)
        return pl.ds(pl.multiple_of(base + left, 128), size)

    def blocks(run, axis, value, which=None):
        columns = part_columns(run, axis, value, which)
        return block_ref(run["out"], run["done"], me, axis, value, columns)

    def begin(run, axis):
        target = blocks(run, axis, me[axis])
        run["forth"] = wires.remote(target, target, device(axis, nxt[axis]))
        run["back"] = wires.remote(target, target, device(axis, prv[axis]))

    def forward(run, axis):
        run["forth"].wait_recv()
        source = blocks(run, axis, prv[axis], 0)
        run["more"] = [wires.remote(source, source, device(axis, nxt[axis]))]
        run["back"].wait_recv()
        if halves(run["width"])[1] > 0:
            source = blocks(run, axis, nxt[axis], 1)
            run["more"].append(wires.remote(source, source, device(axis, prv[axis])))

    def share(run, axis, value):
        source = blocks(run, axis, value)
        run["shared"].append(wires.remote(source, source, sibling))

    for run in runs:
        run["own"].wait()
        begin(run, run["order"][0])
    most = max(len(run["order"]) for run in runs)
    for step in range(most):
        active = [run for run in runs if step < len(run["order"])]
        for run in active:
            forward(run, run["order"][step])
            if step == len(run["order"]) - 1:
                axis = run["order"][step]
                share(run, axis, prv[axis])
                share(run, axis, nxt[axis])
        for run in active:
            axis = run["order"][step]
            for copy in run["more"]:
                copy.wait_recv()
            if step < len(run["order"]) - 1:
                run["done"] = run["done"] + axis
                following = run["order"][step + 1]
                begin(run, following)
                if step + 1 == len(run["order"]) - 1:
                    run["shared"] = []
                    share(run, following, me[following])
            else:
                share(run, axis, opp[axis])
    for run in runs:
        for copy in run["shared"]:
            copy.wait_recv()
    wires.finish()


def gather_weights(shard):
    shapes = [jax.ShapeDtypeStruct((4, 2, 2, 2, 48, width), BF16) for _, width, _ in PARTS]
    copies = 160
    return pl.pallas_call(
        gather_kernel,
        out_shape=shapes,
        in_specs=[pl.BlockSpec(memory_space=pltpu.VMEM)],
        out_specs=[pl.BlockSpec(memory_space=pl.ANY)] * len(PARTS),
        scratch_shapes=[pltpu.VMEM((4, 16, TOTAL), BF16)]
        + [pltpu.VMEM((48, width), BF16) for _, width, _ in PARTS]
        + [
            pltpu.SemaphoreType.DMA((copies,)),
            pltpu.SemaphoreType.DMA((copies,)),
            pltpu.SemaphoreType.DMA((16,)),
        ],
        compiler_params=pltpu.CompilerParams(
            collective_id=0, has_side_effects=True, vmem_limit_bytes=16 * 1024 * 1024
        ),
    )(shard)


def sum_kernel(*refs):
    count = len(PARTS)
    grads = refs[:count]
    outs = refs[count : 2 * count]
    rest = refs[2 * count :]
    own = rest[:count]
    theirs = rest[count : 2 * count]
    near1 = rest[2 * count : 3 * count]
    near2 = rest[3 * count : 4 * count]
    ends = rest[4 * count : 5 * count]
    arrived = rest[5 * count : 6 * count]
    send_sems, recv_sems, local_sems = rest[6 * count :]
    me = place()
    core = me["core"]
    nxt = {axis: rem(me[axis] + 1, 4) for axis in "xyz"}
    opp = {axis: rem(me[axis] + 2, 4) for axis in "xyz"}
    prv = {axis: rem(me[axis] + 3, 4) for axis in "xyz"}
    sibling = {"core": 1 - core}
    greet(
        [device("x", nxt["x"]), device("x", opp["x"]), device("x", prv["x"])]
        + [device("y", nxt["y"]), device("y", prv["y"])]
        + [device("z", nxt["z"]), device("z", prv["z"]), sibling]
    )
    wires = Wires(send_sems, recv_sems, local_sems)

    def spot(left_axes, axis, value, with_core):
        at = dict(me)
        if axis is not None:
            at[axis] = value
        whole = [name for name in left_axes if name != axis]
        z = slice(None) if "z" in whole else at["z"]
        yl = slice(None) if "y" in whole else rem(at["y"], 2)
        yh = slice(None) if "y" in whole else at["y"] // 2
        return (z, yl) + (() if with_core is None else (with_core,)) + (yh,)

    def lead(left_axes, axis):
        dims = []
        for name in ("z", "y"):
            if name in left_axes and name != axis:
                dims += [4] if name == "z" else [2, 2]
        return dims

    def loop_over(dims, body):
        total = 1
        for size in dims:
            total *= size

        def step(flat, carry):
            index, rest_flat = [], flat
            for size in reversed(dims):
                index.append(rem(rest_flat, size))
                rest_flat = rest_flat // size
            body(tuple(reversed(index)))
            return carry

        if total == 1:
            body(())
        else:
            lax.fori_loop(0, total, step, 0)

    def add_into(target, sources, dims):
        def body(index):
            for row in range(0, 48, 16):
                at = index + (pl.ds(row, 16),)
                value = target[at].astype(F32)
                for source in sources:
                    value = value + source[at].astype(F32)
                target[at] = value.astype(target.dtype)

        loop_over(dims, body)

    runs = []
    for index, (name, width, order) in enumerate(PARTS):
        quarter = width // 4 if len(order) == 3 else width
        runs.append(
            {
                "index": index,
                "name": name,
                "order": order[::-1],
                "width": quarter,
                "full": width,
                "left": "zy",
                "turn": 0,
            }
        )

    def columns_of(run, axis, value, which):
        if len(run["order"]) == 3:
            base = (value if axis == "x" else me["x"]) * run["width"]
        else:
            base = 0
        left, size = 0, run["width"]
        if which is not None:
            first_half, second_half = halves(run["width"])
            left, size = (0, first_half) if which == 0 else (first_half, second_half)
        if isinstance(base, int):
            return pl.ds(base + left, size)
        return pl.ds(pl.multiple_of(base + left, 128), size)

    def chunk(run, axis, value, which=None, ref=None, with_core=None):
        ref = own[run["index"]] if ref is None else ref
        columns = columns_of(run, axis, value, which)
        return ref.at[spot(run["left"], axis, value, with_core) + (slice(None), columns)]

    def pair(run, axis, value):
        index = run["index"]
        give = wires.remote(
            chunk(run, axis, value, None, grads[index], 1 - core),
            chunk(run, axis, value, None, theirs[index]),
            sibling,
        )
        keep = wires.copy(
            chunk(run, axis, value, None, grads[index], core), chunk(run, axis, value)
        )
        return give, keep

    def join(run, axis, value, copies):
        copies[0].wait_recv()
        copies[1].wait()
        add_into(
            chunk(run, axis, value),
            [chunk(run, axis, value, None, theirs[run["index"]])],
            lead(run["left"], axis),
        )

    def slots(run, axis):
        dims = lead(run["left"], axis)
        phase = run["turn"]
        ref = (near1 if phase == 0 else near2)[run["index"]]
        if phase == 2:
            ref = ends[run["index"]]
        if not dims:
            ref = ref.at[:, pl.ds(0, 48)]
        return ref.at[0], ref.at[1], ref.at[2], dims

    def part(ref, run, which, dims):
        first_half, second_half = halves(run["width"])
        columns = pl.ds(0, first_half) if which == 0 else pl.ds(first_half, second_half)
        return ref.at[(slice(None),) * len(dims) + (slice(None), columns)]

    def ring_open(run, axis):
        from_prv, from_nxt, passing, dims = slots(run, axis)
        run["passing"] = [
            wires.remote(
                chunk(run, axis, opp[axis], 0), part(passing, run, 0, dims), device(axis, nxt[axis])
            )
        ]
        if halves(run["width"])[1]:
            run["passing"].append(
                wires.remote(
                    chunk(run, axis, opp[axis], 1),
                    part(passing, run, 1, dims),
                    device(axis, prv[axis]),
                )
            )

    def ring_near(run, axis):
        from_prv, from_nxt, passing, dims = slots(run, axis)
        run["near"] = []
        if halves(run["width"])[1]:
            run["near"].append(
                wires.remote(
                    chunk(run, axis, nxt[axis], 1),
                    part(from_prv, run, 1, dims),
                    device(axis, nxt[axis]),
                )
            )
        run["near"].append(
            wires.remote(
                chunk(run, axis, prv[axis], 0), part(from_nxt, run, 0, dims), device(axis, prv[axis])
            )
        )

    def ring_pass(run, axis):
        from_prv, from_nxt, passing, dims = slots(run, axis)
        run["passing"][0].wait_recv()
        add_into(chunk(run, axis, nxt[axis], 0), [part(passing, run, 0, dims)], dims)
        run["near"].append(
            wires.remote(
                chunk(run, axis, nxt[axis], 0), part(from_prv, run, 0, dims), device(axis, nxt[axis])
            )
        )
        if halves(run["width"])[1]:
            run["passing"][1].wait_recv()
            add_into(chunk(run, axis, prv[axis], 1), [part(passing, run, 1, dims)], dims)
            run["near"].append(
                wires.remote(
                    chunk(run, axis, prv[axis], 1),
                    part(from_nxt, run, 1, dims),
                    device(axis, prv[axis]),
                )
            )

    def ring_close(run, axis):
        from_prv, from_nxt, passing, dims = slots(run, axis)
        for copy in run["near"]:
            copy.wait_recv()
        if halves(run["width"])[1]:
            add_into(chunk(run, axis, me[axis]), [from_prv, from_nxt], dims)
        else:
            add_into(chunk(run, axis, me[axis]), [from_prv, from_nxt], dims)
        run["left"] = run["left"].replace(axis, "")
        run["turn"] += 1

    begun = []
    for where in (opp, nxt, prv, me):
        begun.append([pair(run, run["order"][0], where[run["order"][0]]) for run in runs])
    for run, copies in zip(runs, begun[0]):
        axis = run["order"][0]
        join(run, axis, opp[axis], copies)
        ring_open(run, axis)
    for run, nexts, prevs in zip(runs, begun[1], begun[2]):
        axis = run["order"][0]
        join(run, axis, nxt[axis], nexts)
        join(run, axis, prv[axis], prevs)
        ring_near(run, axis)
    for run, copies in zip(runs, begun[3]):
        axis = run["order"][0]
        join(run, axis, me[axis], copies)
    for run in runs:
        ring_pass(run, run["order"][0])
    for run in runs:
        ring_close(run, run["order"][0])
        following = run["order"][1]
        ring_open(run, following)
        ring_near(run, following)
    for run in runs:
        ring_pass(run, run["order"][1])
    for run in runs:
        ring_close(run, run["order"][1])
        if len(run["order"]) == 3:
            following = run["order"][2]
            ring_open(run, following)
            ring_near(run, following)
    for run in runs:
        if len(run["order"]) == 3:
            ring_pass(run, run["order"][2])
            ring_close(run, run["order"][2])
    lasts = []
    for run in runs:
        index, width = run["index"], run["width"]
        summed = own[index].at[me["z"], rem(me["y"], 2), me["y"] // 2]
        exact = lax.Precision.HIGHEST if summed.dtype == F32 else None
        pick = spread_rows((64, 48), True).astype(summed.dtype)
        target = arrived[index]
        staging = ends[index].at[3] if len(run["order"]) == 3 else near2[index].at[3]
        base = me["x"] * width if len(run["order"]) == 3 else 0
        for left in range(0, width, 512):
            size = min(512, width - left)
            if isinstance(base, int):
                columns = pl.ds(left, size)
            else:
                columns = pl.ds(pl.multiple_of(base + left, 128), size)
            staging[:, left : left + size] = jnp.dot(
                pick, summed[:, columns], preferred_element_type=F32, precision=exact
            ).astype(staging.dtype)
        if len(run["order"]) == 3:
            columns = pl.ds(pl.multiple_of(base, 128), width)
            lands = target.at[:, columns]
        else:
            lands = target.at[me["x"]]
        run["copies"] = []
        for where in (nxt, opp, prv):
            row = pl.ds(pl.multiple_of(where["x"] * 16, 16), 16)
            run["copies"].append(
                wires.remote(staging.at[row], lands, device("x", where["x"]))
            )
        row = pl.ds(pl.multiple_of(me["x"] * 16, 16), 16)
        run["keep"] = wires.copy(staging.at[row], lands)
    for run in runs:
        index = run["index"]
        run["keep"].wait()
        for copy in run["copies"]:
            copy.wait_recv()
        if len(run["order"]) == 3:
            outs[index][...] = arrived[index][...].astype(F32)
        else:
            value = arrived[index][0].astype(F32)
            for place_x in range(1, 4):
                value = value + arrived[index][place_x].astype(F32)
            outs[index][...] = value
    wires.finish()


def sum_gradients(grads):
    scratch_own, scratch_theirs, near1, near2, ends, arrived = [], [], [], [], [], []
    for name, width, order in PARTS:
        kind = F32 if name == "misc" else BF16
        scratch_own.append(pltpu.VMEM((4, 2, 2, 48, width), kind))
        scratch_theirs.append(pltpu.VMEM((4, 2, 2, 48, width), kind))
        if order == "yz":
            near1.append(pltpu.VMEM((3, 2, 2, 48, width), kind))
            near2.append(pltpu.VMEM((4, 64, width), kind))
        elif order == "zy":
            near1.append(pltpu.VMEM((3, 4, 48, width), kind))
            near2.append(pltpu.VMEM((4, 64, width), kind))
        else:
            quarter = width // 4
            near1.append(pltpu.VMEM((3, 4, 2, 2, 48, quarter), kind))
            near2.append(pltpu.VMEM((3, 2, 2, 48, quarter), kind))
        ends.append(pltpu.VMEM((4, 64, width // 4 if len(order) == 3 else 128), kind))
        arrived.append(pltpu.VMEM((16, width) if len(order) == 3 else (4, 16, width), kind))
    copies = 160
    return pl.pallas_call(
        sum_kernel,
        out_shape=[jax.ShapeDtypeStruct((16, width), F32) for _, width, _ in PARTS],
        in_specs=[pl.BlockSpec(memory_space=pl.ANY)] * len(PARTS),
        out_specs=[pl.BlockSpec(memory_space=pltpu.VMEM)] * len(PARTS),
        scratch_shapes=scratch_own
        + scratch_theirs
        + near1
        + near2
        + ends
        + arrived
        + [
            pltpu.SemaphoreType.DMA((copies,)),
            pltpu.SemaphoreType.DMA((copies,)),
            pltpu.SemaphoreType.DMA((48,)),
        ],
        compiler_params=pltpu.CompilerParams(
            collective_id=1, has_side_effects=True, vmem_limit_bytes=56 * 1024 * 1024
        ),
    )(*grads)


def col_device(col):
    return {"yh": col // 4, "xh": rem(col // 2, 2), "xl": rem(col, 2)}


def col_index():
    return lax.axis_index("yh") * 4 + lax.axis_index("xh") * 2 + lax.axis_index("xl")


def later_kernel(own_ref, out_ref, send_sems, recv_sems, local_sem):
    me = col_index()
    greet([col_device(rem(me + far, 8)) for far in range(1, 8)])

    def copy(far):
        return pltpu.make_async_remote_copy(
            src_ref=own_ref,
            dst_ref=out_ref.at[me],
            send_sem=send_sems.at[far],
            recv_sem=recv_sems.at[far],
            device_id=col_device(rem(me + far, 8)),
            device_id_type=MESH_ID,
        )

    for far in range(7, 0, -1):

        @pl.when(me + far < 8)
        def _():
            copy(far).start()

    keep = pltpu.make_async_copy(own_ref, out_ref.at[me], local_sem)
    keep.start()
    for far in range(1, 8):

        @pl.when(me + far < 8)
        def _():
            out_ref[me + far] = jnp.zeros(own_ref.shape, own_ref.dtype)

    keep.wait()
    for far in range(1, 8):

        @pl.when(me >= far)
        def _():
            copy(far).wait_recv()

        @pl.when(me + far < 8)
        def _():
            copy(far).wait_send()


def to_later(rows):
    return pl.pallas_call(
        later_kernel,
        out_shape=jax.ShapeDtypeStruct((8,) + rows.shape, rows.dtype),
        in_specs=[pl.BlockSpec(memory_space=pltpu.VMEM)],
        out_specs=pl.BlockSpec(memory_space=pltpu.VMEM),
        scratch_shapes=[
            pltpu.SemaphoreType.DMA((8,)),
            pltpu.SemaphoreType.DMA((8,)),
            pltpu.SemaphoreType.DMA,
        ],
        compiler_params=pltpu.CompilerParams(
            collective_id=2, has_side_effects=True, vmem_limit_bytes=16 * 1024 * 1024
        ),
    )(rows)


def earlier_kernel(blocks_ref, out_ref, landed, send_sems, recv_sems):
    me = col_index()
    greet([col_device(rem(me + far, 8)) for far in range(1, 8)])

    def copy(far):
        return pltpu.make_async_remote_copy(
            src_ref=blocks_ref.at[rem(me + 8 - far, 8)],
            dst_ref=landed.at[far],
            send_sem=send_sems.at[far],
            recv_sem=recv_sems.at[far],
            device_id=col_device(rem(me + 8 - far, 8)),
            device_id_type=MESH_ID,
        )

    for far in range(7, 0, -1):

        @pl.when(me >= far)
        def _():
            copy(far).start()

    for far in range(1, 8):

        @pl.when(me + far < 8)
        def _():
            copy(far).wait_recv()

        @pl.when(me + far >= 8)
        def _():
            landed[far] = jnp.zeros(landed.shape[1:], landed.dtype)

    rows = out_ref.shape[0]
    for row in range(0, rows, 16):
        at = pl.ds(row, 16)
        value = blocks_ref[me, at].astype(F32)
        for far in range(1, 8):
            value = value + landed[far, at].astype(F32)
        out_ref[at] = value.astype(out_ref.dtype)
    for far in range(1, 8):

        @pl.when(me >= far)
        def _():
            copy(far).wait_send()


def sum_earlier(blocks):
    return pl.pallas_call(
        earlier_kernel,
        out_shape=jax.ShapeDtypeStruct(blocks.shape[1:], blocks.dtype),
        in_specs=[pl.BlockSpec(memory_space=pltpu.VMEM)],
        out_specs=pl.BlockSpec(memory_space=pltpu.VMEM),
        scratch_shapes=[
            pltpu.VMEM(blocks.shape, blocks.dtype),
            pltpu.SemaphoreType.DMA((8,)),
            pltpu.SemaphoreType.DMA((8,)),
        ],
        compiler_params=pltpu.CompilerParams(
            collective_id=3, has_side_effects=True, vmem_limit_bytes=16 * 1024 * 1024
        ),
    )(blocks)


def inverse_rms(residual):
    return lax.rsqrt(jnp.mean(residual * residual, axis=-1, keepdims=True) + EPSILON)


def contract(left_side, right_side, left_dim, right_dim):
    return lax.dot_general(
        left_side,
        right_side,
        (((left_dim,), (right_dim,)), ((), ())),
        preferred_element_type=F32,
    )


def gated_unit(gate_pre, up_pre):
    return jax.nn.silu(gate_pre) * up_pre


def norm_backward(residual, norm_scale, gain_row, grad_normed):
    weighted = grad_normed * gain_row
    inner_sum = jnp.mean(weighted * residual, axis=-1, keepdims=True)
    grad_residual = (
        norm_scale * weighted - residual * norm_scale * norm_scale * norm_scale * inner_sum
    )
    grad_gain = jnp.sum(grad_normed * residual * norm_scale, axis=0)
    return (grad_residual, grad_gain)


def to_experts(rows):
    return lax.all_to_all(rows, EXPERT_AXES, split_axis=0, concat_axis=0, tiled=True)


def swap_halves(block):
    return lax.ppermute(block, "xl", [(0, 1), (1, 0)])


def shards(
    tokens,
    segments,
    routes,
    norm1_gain,
    w_query,
    key_value_weight,
    w_output,
    norm2_gain,
    w_router,
    w_shgate,
    w_shup,
    w_shdown,
    w_exgate,
    w_exup,
    w_exdown,
    cotangent,
):
    local_rows, feature_count = tokens.shape
    sequence_length = local_rows * 8
    heads_per_group = QUERY_HEADS // KEY_VALUE_HEADS
    key_value_width = KEY_VALUE_HEADS * HEAD_SIZE
    score_scale = HEAD_SIZE ** (-0.5)

    own_gate, own_up, own_down = w_exgate[0], w_exup[0], w_exdown[0]
    other_gate, other_up, other_down = (
        swap_halves(own_gate),
        swap_halves(own_up),
        swap_halves(own_down),
    )

    shard = jnp.concatenate(
        [
            w_query,
            key_value_weight,
            w_output.T,
            w_shgate,
            w_shup,
            w_shdown.T,
            w_router,
            norm1_gain[:, None],
            norm2_gain[:, None],
            jnp.zeros((12, 62), BF16),
        ],
        axis=1,
    )
    shard = jnp.concatenate([shard, jnp.zeros((4, TOTAL), BF16)], axis=0)
    qkv_w, outt_w, shgu_w, shdt_w, misc_w = [
        gathered.reshape(feature_count, gathered.shape[-1]) for gathered in gather_weights(shard)
    ]
    router_w = misc_w[:, :EXPERTS]
    gain_first = misc_w[:, EXPERTS].astype(F32)
    gain_second = misc_w[:, EXPERTS + 1].astype(F32)

    residual0 = tokens.astype(F32)
    scale_first = inverse_rms(residual0)
    first_normed = (residual0 * scale_first * gain_first).astype(BF16)
    qkv_rows = jnp.dot(first_normed, qkv_w, preferred_element_type=F32).astype(BF16)
    query_rows = qkv_rows[:, : QUERY_HEADS * HEAD_SIZE]
    own_segments = segments.astype(BF16)
    key_value_rows = jnp.concatenate(
        [
            qkv_rows[:, QUERY_HEADS * HEAD_SIZE :],
            jnp.broadcast_to(own_segments[:, None], (local_rows, 128)),
        ],
        axis=1,
    )
    every = to_later(key_value_rows).reshape(sequence_length, 2 * key_value_width + 128)
    all_segments = every[:, 2 * key_value_width]
    key_matrix = every[:, :key_value_width].reshape(sequence_length, KEY_VALUE_HEADS, HEAD_SIZE)
    value_matrix = every[:, key_value_width : 2 * key_value_width].reshape(
        sequence_length, KEY_VALUE_HEADS, HEAD_SIZE
    )
    query_head_count = query_rows.reshape(local_rows, KEY_VALUE_HEADS, heads_per_group, HEAD_SIZE)
    query_place = col_index() * local_rows + jnp.arange(local_rows, dtype=jnp.int32)
    key_place = jnp.arange(sequence_length, dtype=jnp.int32)
    allowed = (key_place[None, :] <= query_place[:, None]) & (
        all_segments[None, :] == own_segments[:, None]
    )

    def masked_scores():
        raw_scores = (
            jnp.einsum("tkgd,skd->kgts", query_head_count, key_matrix, preferred_element_type=F32)
            * score_scale
        )
        return jnp.where(allowed, raw_scores, -1e30)

    scores = masked_scores()
    row_max = jnp.max(scores, axis=-1, keepdims=True)
    shifted = jnp.exp(scores - row_max)
    row_total = jnp.sum(shifted, axis=-1, keepdims=True)
    log_total = row_max + jnp.log(row_total)
    weights_low = (shifted / row_total).astype(BF16)
    attended_rows = jnp.einsum(
        "kgts,skd->tkgd", weights_low, value_matrix, preferred_element_type=F32
    )
    attended_rows = attended_rows.reshape(local_rows, QUERY_HEADS * HEAD_SIZE).astype(BF16)
    residual1 = residual0 + contract(attended_rows, outt_w, 1, 1)
    scale_second = inverse_rms(residual1)
    second_normed = (residual1 * scale_second * gain_second).astype(BF16)

    logits = jnp.dot(second_normed, router_w, preferred_element_type=F32)
    expert_ids = jnp.arange(EXPERTS, dtype=jnp.int32)
    named = jnp.any(routes[:, :, None] == expert_ids[None, None, :], axis=1)
    named_low = named.astype(BF16)
    chosen = jnp.where(named, logits, -jnp.inf)
    chosen_exp = jnp.where(named, jnp.exp(chosen - jnp.max(chosen, axis=1, keepdims=True)), 0.0)
    gates = chosen_exp / jnp.sum(chosen_exp, axis=1, keepdims=True)
    token_ids = jnp.arange(local_rows, dtype=jnp.int32)
    before = (token_ids[None, :] <= token_ids[:, None]).astype(BF16)
    rank = jnp.dot(before, named_low, preferred_element_type=F32) * named.astype(F32)
    slot_count = EXPERTS * CAP
    slot_ids = jnp.arange(slot_count, dtype=jnp.int32)
    widen = (slot_ids[None, :] // CAP == expert_ids[:, None]).astype(BF16)
    rank_wide = jnp.dot(rank.astype(BF16), widen, preferred_element_type=F32)
    slots = rank_wide == (slot_ids % CAP + 1).astype(F32)[None, :]
    slots_low = slots.astype(BF16)
    gates_wide = jnp.dot(
        gates, widen.astype(F32), precision=lax.Precision.HIGHEST, preferred_element_type=F32
    )
    slot_gates = jnp.where(slots, gates_wide, 0.0)

    def dispatch(rows):
        return rows.reshape(EXPERTS, CAP, feature_count)

    received = to_experts(dispatch(contract(slots_low, second_normed, 0, 0).astype(BF16)))
    gate_column = jnp.sum(slot_gates, axis=0)[:, None]
    sent_grads = (gate_column * contract(slots_low, cotangent, 0, 0)).astype(BF16)
    grad_received = to_experts(dispatch(sent_grads))
    received = received.reshape(slot_count, feature_count)
    grad_received = grad_received.reshape(slot_count, feature_count)

    shared_pre = jnp.dot(second_normed, shgu_w, preferred_element_type=F32)
    shared_gate, shared_up = shared_pre[:, :1024], shared_pre[:, 1024:]
    shared_hidden = gated_unit(shared_gate, shared_up).astype(BF16)
    shared_out = contract(shared_hidden, shdt_w, 1, 1)
    grad_shdt = contract(cotangent, shared_hidden, 0, 0).astype(BF16)
    grad_shared_hidden = jnp.dot(cotangent, shdt_w, preferred_element_type=F32)
    unused_shared, pull_shared = jax.vjp(gated_unit, shared_gate, shared_up)
    grad_shared_gate, grad_shared_up = pull_shared(grad_shared_hidden)
    grad_shared = jnp.concatenate(
        [grad_shared_gate.astype(BF16), grad_shared_up.astype(BF16)], axis=1
    )
    grad_shgu = contract(second_normed, grad_shared, 0, 0).astype(BF16)
    grad_second = contract(grad_shared, shgu_w, 1, 1)

    def units(first, second):
        left = jnp.dot(received, first, preferred_element_type=F32)
        right = jnp.dot(received, second, preferred_element_type=F32)
        return left, right

    sums = []
    half_out = None
    grad_rows = None
    for gate_w, up_w, down_w in (
        (own_gate, own_up, own_down),
        (other_gate, other_up, other_down),
    ):
        gate_units, up_units = units(gate_w, up_w)
        hidden = gated_unit(gate_units, up_units).astype(BF16)
        part_out = jnp.dot(hidden, down_w, preferred_element_type=F32)
        half_out = part_out if half_out is None else half_out + part_out
        grad_hidden = contract(grad_received, down_w, 1, 1)
        unused_units, pull_units = jax.vjp(gated_unit, gate_units, up_units)
        grad_gate_units, grad_up_units = pull_units(grad_hidden)
        grad_gate_low = grad_gate_units.astype(BF16)
        grad_up_low = grad_up_units.astype(BF16)
        part_rows = contract(grad_gate_low, gate_w, 1, 1) + contract(grad_up_low, up_w, 1, 1)
        grad_rows = part_rows if grad_rows is None else grad_rows + part_rows
        sums.append(
            (
                contract(received, grad_gate_low, 0, 0),
                contract(received, grad_up_low, 0, 0),
                contract(hidden, grad_received, 0, 0),
            )
        )
    returned = to_experts(dispatch(half_out.astype(BF16))).reshape(slot_count, feature_count)
    grad_returned = to_experts(dispatch(grad_rows.astype(BF16))).reshape(slot_count, feature_count)
    grad_exgate, grad_exup, grad_exdown = [
        (mine + swap_halves(theirs.astype(BF16)).astype(F32))[None]
        for mine, theirs in zip(sums[0], sums[1])
    ]

    gates_high = slot_gates.astype(BF16)
    gates_rest = (slot_gates - gates_high.astype(F32)).astype(BF16)
    expert_mix = jnp.dot(gates_high, returned, preferred_element_type=F32) + jnp.dot(
        gates_rest, returned, preferred_element_type=F32
    )
    block_out = (residual1 + shared_out + expert_mix).astype(BF16)
    along = jnp.where(slots, contract(cotangent, returned, 1, 1), 0.0)
    grad_gates = jnp.dot(
        along, widen.T.astype(F32), precision=lax.Precision.HIGHEST, preferred_element_type=F32
    )
    grad_logits = (
        gates * (grad_gates - jnp.sum(gates * grad_gates, axis=1, keepdims=True))
    ).astype(BF16)
    grad_router = contract(second_normed, grad_logits, 0, 0)
    grad_second = grad_second + contract(grad_logits, router_w, 1, 1)
    grad_second = grad_second + jnp.dot(slots_low, grad_returned, preferred_element_type=F32)
    grad_norm_second, grad_gain_second = norm_backward(
        residual1, scale_second, gain_second, grad_second
    )
    grad_residual1 = cotangent.astype(F32) + grad_norm_second
    grad_attn_low = grad_residual1.astype(BF16)
    grad_outt = contract(grad_attn_low, attended_rows, 0, 0).astype(BF16)
    attended_gradient = jnp.dot(grad_attn_low, outt_w, preferred_element_type=F32).astype(BF16)
    weights_again = jnp.exp(masked_scores() - log_total)
    heads_gradient = attended_gradient.reshape(
        local_rows, KEY_VALUE_HEADS, heads_per_group, HEAD_SIZE
    )
    grad_weights = jnp.einsum(
        "tkgd,skd->kgts", heads_gradient, value_matrix, preferred_element_type=F32
    )
    inner_sum = jnp.sum(weights_again * grad_weights, axis=-1, keepdims=True)
    grad_scores = (weights_again * (grad_weights - inner_sum)).astype(BF16)
    grad_queries = (
        jnp.einsum("kgts,skd->tkgd", grad_scores, key_matrix, preferred_element_type=F32)
        * score_scale
    )
    grad_queries = grad_queries.reshape(local_rows, QUERY_HEADS * HEAD_SIZE).astype(BF16)
    grad_keys = (
        jnp.einsum("kgts,tkgd->skd", grad_scores, query_head_count, preferred_element_type=F32)
        * score_scale
    )
    grad_values = jnp.einsum(
        "kgts,tkgd->skd",
        weights_again.astype(BF16),
        heads_gradient,
        preferred_element_type=F32,
    )
    partial_keyvals = jnp.concatenate(
        [
            grad_keys.reshape(sequence_length, key_value_width),
            grad_values.reshape(sequence_length, key_value_width),
        ],
        axis=1,
    ).astype(BF16)
    grad_keyvals = sum_earlier(partial_keyvals.reshape(8, local_rows, 2 * key_value_width))
    grad_qkv_rows = jnp.concatenate([grad_queries, grad_keyvals], axis=1)
    grad_qkv = contract(first_normed, grad_qkv_rows, 0, 0).astype(BF16)
    grad_first = contract(grad_qkv_rows, qkv_w, 1, 1)
    grad_norm_first, grad_gain_first = norm_backward(residual0, scale_first, gain_first, grad_first)
    grad_tokens = grad_residual1 + grad_norm_first
    grad_misc = jnp.concatenate(
        [
            grad_router,
            grad_gain_first[:, None],
            grad_gain_second[:, None],
            jnp.zeros((feature_count, 62), F32),
        ],
        axis=1,
    )
    summed = sum_gradients(
        [
            grad.reshape(4, 2, 2, 2, 48, grad.shape[-1])
            for grad in (grad_qkv, grad_outt, grad_shgu, grad_shdt, grad_misc)
        ]
    )
    sum_qkv, sum_outt, sum_shgu, sum_shdt, sum_misc = [piece[:12] for piece in summed]
    return (
        block_out,
        grad_tokens,
        sum_misc[:, EXPERTS],
        sum_qkv[:, :1536],
        sum_qkv[:, 1536:],
        sum_outt.T,
        sum_misc[:, EXPERTS + 1],
        sum_misc[:, :EXPERTS],
        sum_shgu[:, :1024],
        sum_shgu[:, 1024:],
        sum_shdt.T,
        grad_exgate,
        grad_exup,
        grad_exdown,
    )


def solution(mesh):
    fine = Mesh(mesh.devices.reshape(SIZES), AXES)
    rows = P(AXES, None)
    columns = P(None, AXES)
    flat = P(AXES)
    blocks = P(AXES, None, None)
    in_specs = (
        rows,
        flat,
        rows,
        flat,
        rows,
        rows,
        columns,
        flat,
        rows,
        rows,
        rows,
        columns,
        blocks,
        blocks,
        blocks,
        rows,
    )
    out_specs = (
        rows,
        rows,
        flat,
        rows,
        rows,
        columns,
        flat,
        rows,
        rows,
        rows,
        columns,
        blocks,
        blocks,
        blocks,
    )
    return jax.shard_map(shards, mesh=fine, in_specs=in_specs, out_specs=out_specs, check_vma=False)
```

time: 4880 us -> 755 us (0.15)
  blocking collectives: 1470 us -> 0 us
  waiting for transfers between devices: 1630 us -> 239 us
  local copies, waits for them, and re-layouts: 734 us -> 42.7 us
  starting transfers between devices: 678 us -> 53.2 us
  Pallas kernels: 0 us -> 246 us
  other arithmetic: 171 us -> 9.32 us
    all_gather x7 -> x0, waiting for transfers between devices: 1530 us -> none  [the longest x1 364 us: shards(): lax.all_gather(w_shup, ('row', 'col'), axis=0, tiled=True)]
    unnamed x4 -> x0, blocking collectives: 1050 us -> none
    unnamed x225 -> x0, starting transfers between devices: 622 us -> none
    unnamed x539 -> x138, local copies, waits for them, and re-layouts: 531 us -> 16.8 us
    all_gather x2 -> x0, blocking collectives: 425 us -> none  [the longest x1 402 us: shards(): lax.all_gather(w_router, ('row', 'col'), axis=0, tiled=True)]
    pallas_call x0 -> x4, Pallas kernels: none -> 246 us  [the longest x1 95.9 us: gather_weights(): pl.pallas_call(gather_kernel, out_shape=shapes, in_specs=[pl.BlockSpec(me...]
    ppermute x0 -> x6, waiting for transfers between devices: none -> 148 us  [swap_halves(): return lax.ppermute(block, 'xl', [(0, 1), (1, 0)])]
    unnamed x7 -> x3, other arithmetic: 123 us -> 0.01 us
  transfers between devices with their start and end apart: 236 -> 10, of which waited for: 10 -> 8; matrix products, arithmetic and copies ran while one was open for 36% -> 13% of each run, Pallas kernels for 0% -> 0%
where the time goes in v1:
time: 755 us; the launch traced here: 747 us
  Pallas kernels  246 us (33%)
  waiting for transfers between devices  239 us (32%)
  matrix products  155 us (21%)
  starting transfers between devices  53.2 us (7%)
  local copies, waits for them, and re-layouts  42.7 us (6%)
  other arithmetic  9.32 us (1%)
    ppermute x6, waiting for transfers between devices, swap_halves(): return lax.ppermute(block, 'xl', [(0, 1), (1, 0)])  148 us
    pallas_call x1, Pallas kernels, gather_weights(): pl.pallas_call(gather_kernel, out_shape=shapes, in_specs=[pl.BlockSpec(me...  95.9 us
    dot_general x25, matrix products, contract(): lax.dot_general(left_side, right_side, (((left_dim,), (right_dim,)), ((),...  93.4 us
    all_to_all x4, waiting for transfers between devices, to_experts(): lax.all_to_all(rows, EXPERT_AXES, split_axis=0, concat_axis=0, tiled=True)  90.9 us
    pallas_call x1, Pallas kernels, sum_gradients(): pl.pallas_call(sum_kernel, out_shape=[jax.ShapeDtypeStruct((16, width), F...  84.3 us
    all_to_all x4, starting transfers between devices, to_experts(): lax.all_to_all(rows, EXPERT_AXES, split_axis=0, concat_axis=0, tiled=True)  45.5 us
    pallas_call x1, Pallas kernels, to_later(): pl.pallas_call(later_kernel, out_shape=jax.ShapeDtypeStruct((8,) + rows.s...  39.5 us
    pallas_call x1, Pallas kernels, sum_earlier(): pl.pallas_call(earlier_kernel, out_shape=jax.ShapeDtypeStruct(blocks.shap...  26.3 us
  transfers between devices with their start and end apart: 10, of which 8 were waited for; matrix products, arithmetic and copies ran while one was open for 13% of the time, Pallas kernels for 0%

profile of v1, /device:TPU:3, one launch (start us, length us, event | category | flops | bytes accessed | tf_op | source)
XLA Modules:
  0.0 747.4 jit_solution(6008418266627372671)
XLA Ops:
  3.2 95.9 %shard_map.263 = (bf16[4,2,2,2,48,2560]{5,4,3,2,1,0:T(8,128)(2,1)S(1)}, bf16[4,2,2,2,48,1536]{5,4,3,2,1,0:T(8,128)(2,1)S(1)}, bf16[4,2,2,2,48,2048]{5,4,3,2,1,0:...) custom-call(bf16[16,7296]{1,0:T(8,128)(2,1)S(1)} %concatenate.35.shard_ref), custom_call_target="tpu_custom_call" | custom-call | tf_op jit(solution)/shard_map/pallas_call | solution.py:245
  115.9 39.5 %shard_map.264 = bf16[8,128,1152]{2,1,0:T(8,128)(2,1)S(1)} custom-call(bf16[128,1152]{1,0:T(8,128)(2,1)S(1)} %pad_maximum_fusion.7.own_ref), custom_call_target="tpu_custom_call" | custom-call | tf_op jit(solution)/shard_map/pallas_call | solution.py:637
  172.6 8.4 %all-to-all-start = ((bf16[64,24,1536]{2,1,0:T(8,128)(2,1)}), bf16[64,24,1536]{2,1,0:T(8,128)(2,1)}, u32[]{:S(2)}, u32[]{:S(2)}) async-start(bf16[64,24,1536]{2,1,0:T(8,128)(2,1)} %bitcast.209), calls=%async_computation | async-start | bytes 9437184 | tf_op jit(solution)/shard_map/all_to_all | solution.py:742
  186.5 54.7 %all-to-all-done = bf16[64,24,1536]{2,1,0:T(8,128)(2,1)} async-done(((bf16[64,24,1536]{2,1,0:T(8,128)(2,1)}), bf16[64,24,1536]{2,1,0:T(8,128)(2,1)}, u32[]{:S(2)}, u32[]{:S(2)}) %all-to-all-start) | async-done | bytes 4718624 | tf_op jit(solution)/shard_map/all_to_all | solution.py:742
  241.2 7.7 %all-to-all-start.2 = ((bf16[64,24,1536]{2,1,0:T(8,128)(2,1)}), bf16[64,24,1536]{2,1,0:T(8,128)(2,1)}, u32[]{:S(2)}, u32[]{:S(2)}) async-start(bf16[64,24,1536]{2,1,0:T(8,128)(2,1)} %bitcast.208), calls=%async_computation.2 | async-start | bytes 9437184 | tf_op jit(solution)/shard_map/all_to_all | solution.py:742
  250.8 5.1 fusion.85
  255.9 5.1 fusion.89
  261.0 59.1 %collective-permute-done.2 = bf16[256,1536]{1,0:T(8,128)(2,1)} collective-permute-done((bf16[256,1536]{1,0:T(8,128)(2,1)S(1)}, bf16[256,1536]{1,0:T(8,128)(2,1)}, u32[]{:S(2)}, u32[]{:S(2)}) %collective-permute-start.2) | collective-permute-done | bytes 786464 | tf_op jit(solution)/shard_map/ppermute | solution.py:746
  324.3 5.3 multiply_convert_fusion.1
  329.5 7.4 collective-permute-done.1
  342.3 11.5 %collective-permute-done = bf16[1536,256]{1,0:T(8,128)(2,1)} collective-permute-done((bf16[1536,256]{1,0:T(8,128)(2,1)}, bf16[1536,256]{1,0:T(8,128)(2,1)}, u32[]{:S(2)}, u32[]{:S(2)}) %collective-permute-start) | collective-permute-done | bytes 786464 | tf_op jit(solution)/shard_map/ppermute | solution.py:746
  353.8 5.7 fusion.26
  364.5 22.1 %all-to-all-start.1 = ((bf16[64,24,1536]{2,1,0:T(8,128)(2,1)}), bf16[64,24,1536]{2,1,0:T(8,128)(2,1)}, u32[]{:S(2)}, u32[]{:S(2)}) async-start(bf16[64,24,1536]{2,1,0:T(8,128)(2,1)} %bitcast.211), calls=%async_computation.1 | async-start | bytes 9437184 | tf_op jit(solution)/shard_map/all_to_all | solution.py:742
  405.4 5.1 fusion.1
  410.5 36.2 %all-to-all-done.1 = bf16[64,24,1536]{2,1,0:T(8,128)(2,1)} async-done(((bf16[64,24,1536]{2,1,0:T(8,128)(2,1)}), bf16[64,24,1536]{2,1,0:T(8,128)(2,1)}, u32[]{:S(2)}, u32[]{:S(2)}) %all-to-all-start.1) | async-done | bytes 4718624 | tf_op jit(solution)/shard_map/all_to_all | solution.py:742
  446.8 7.4 all-to-all-start.3
  459.0 5.9 fusion.52
  482.0 46.4 %collective-permute-done.5 = bf16[256,1536]{1,0:T(8,128)(2,1)S(1)} collective-permute-done((bf16[256,1536]{1,0:T(8,128)(2,1)S(1)}, bf16[256,1536]{1,0:T(8,128)(2,1)S(1)}, u32[]{:S(2)}, u32[]{:S(2)}) %collective-permute-start.5) | collective-permute-done | bytes 786464 | tf_op jit(solution)/shard_map/ppermute | solution.py:746
  533.4 12.0 %collective-permute-done.4 = bf16[1536,256]{1,0:T(8,128)(2,1)S(1)} collective-permute-done((bf16[1536,256]{1,0:T(8,128)(2,1)S(1)}, bf16[1536,256]{1,0:T(8,128)(2,1)S(1)}, u32[]{:S(2)}, u32[]{:S(2)}) %collective-permute-start.4) | collective-permute-done | bytes 786464 | tf_op jit(solution)/shard_map/ppermute | solution.py:746
  550.3 11.9 %collective-permute-done.3 = bf16[1536,256]{1,0:T(8,128)(2,1)S(1)} collective-permute-done((bf16[1536,256]{1,0:T(8,128)(2,1)S(1)}, bf16[1536,256]{1,0:T(8,128)(2,1)S(1)}, u32[]{:S(2)}, u32[]{:S(2)}) %collective-permute-start.3) | collective-permute-done | bytes 786464 | tf_op jit(solution)/shard_map/ppermute | solution.py:746
  600.8 26.3 %shard_map.265 = bf16[128,1024]{1,0:T(8,128)(2,1)S(1)} custom-call(bf16[8,128,1024]{2,1,0:T(8,128)(2,1)S(1)} %pad_maximum_fusion.blocks_ref), custom_call_target="tpu_custom_call" | custom-call | tf_op jit(solution)/shard_map/pallas_call | solution.py:698
  627.3 6.1 fusion.42
  633.4 5.4 convolution_convert_fusion
  643.4 84.3 %shard_map.266 = (f32[16,2560]{1,0:T(8,128)}, f32[16,1536]{1,0:T(8,128)}, f32[16,2048]{1,0:T(8,128)}, f32[16,1024]{1,0:T(8,128)}, f32[16,128]{1,0:T(8,128)}) custom-call(bf16[4,2,2,2,48,2560]{5,4,3,2,1,0:T(8,128)(2,1)} %bitcast.205, bf16[4,2,2,2,48,1536]{5,4,3,2,1,0:T(8,128)(2,1)} %bitcast.207, bf16[4,2,2,2,48,2048]{5,4,3,2,1,0:T(8,128)(2,1)} %bitcast.206, ...), custom_call_target="tpu_custom_call" | custom-call | tf_op jit(solution)/shard_map/pallas_call | solution.py:566
  (240 shorter events, 171.1 us)
Async XLA Ops:
  168.1 409.9 %copy-start.8 = (f32[128,1536]{1,0:T(8,128)}, f32[128,1536]{1,0:T(8,128)S(1)}, u32[]{:S(2)}) copy-start(f32[128,1536]{1,0:T(8,128)S(1)} %get-tuple-element.58) | copy-start | bytes 2359300
  169.0 13.8 %copy-start.20 = (pred[128,1536]{1,0:T(32,128)(4,1)}, pred[128,1536]{1,0:T(32,128)(4,1)S(1)}, u32[]{:S(2)}) copy-start(pred[128,1536]{1,0:T(32,128)(4,1)S(1)} %convolution_compare_fusion) | copy-start | bytes 589828
  172.6 68.6 %all-to-all-start = ((bf16[64,24,1536]{2,1,0:T(8,128)(2,1)}), bf16[64,24,1536]{2,1,0:T(8,128)(2,1)}, u32[]{:S(2)}, u32[]{:S(2)}) async-start(bf16[64,24,1536]{2,1,0:T(8,128)(2,1)} %bitcast.209), calls=%async_computation | async-start | bytes 9437184 | tf_op jit(solution)/shard_map/all_to_all | solution.py:742
  241.2 78.9 %all-to-all-start.2 = ((bf16[64,24,1536]{2,1,0:T(8,128)(2,1)}), bf16[64,24,1536]{2,1,0:T(8,128)(2,1)}, u32[]{:S(2)}, u32[]{:S(2)}) async-start(bf16[64,24,1536]{2,1,0:T(8,128)(2,1)} %bitcast.208), calls=%async_computation.2 | async-start | bytes 9437184 | tf_op jit(solution)/shard_map/all_to_all | solution.py:742
  248.9 71.2 %collective-permute-start.2 = (bf16[256,1536]{1,0:T(8,128)(2,1)S(1)}, bf16[256,1536]{1,0:T(8,128)(2,1)}, u32[]{:S(2)}, u32[]{:S(2)}) collective-permute-start(bf16[256,1536]{1,0:T(8,128)(2,1)S(1)} %bitcast.230), channel_id=1, source_target_pairs={{0,1},{1,0},{2,3},{3,2},{4,5},{5,4},{6,7},{7,6},{8,9},{9,8},{10,11... | collective-permute-start | bytes 2359304 | tf_op jit(solution)/shard_map/ppermute | solution.py:746
  249.4 87.6 %collective-permute-start.1 = (bf16[1536,256]{1,0:T(8,128)(2,1)}, bf16[1536,256]{1,0:T(8,128)(2,1)}, u32[]{:S(2)}, u32[]{:S(2)}) collective-permute-start(bf16[1536,256]{1,0:T(8,128)(2,1)} %bitcast.231), channel_id=1, source_target_pairs={{0,1},{1,0},{2,3},{3,2},{4,5},{5,4},{6,7},{7,6},{8,9},{9,8},{10,11... | collective-permute-start | bytes 2359304 | tf_op jit(solution)/shard_map/ppermute | solution.py:746
  250.4 103.3 %collective-permute-start = (bf16[1536,256]{1,0:T(8,128)(2,1)}, bf16[1536,256]{1,0:T(8,128)(2,1)}, u32[]{:S(2)}, u32[]{:S(2)}) collective-permute-start(bf16[1536,256]{1,0:T(8,128)(2,1)} %bitcast.21), channel_id=1, source_target_pairs={{0,1},{1,0},{2,3},{3,2},{4,5},{5,4},{6,7},{7,6},{8,9},{9,8},{10,11... | collective-permute-start | bytes 2359304 | tf_op jit(solution)/shard_map/ppermute | solution.py:746
  329.5 12.8 %copy-start.15 = (bf16[1536,256]{1,0:T(8,128)(2,1)}, bf16[1536,256]{1,0:T(8,128)(2,1)S(1)}, u32[]{:S(2)}) copy-start(bf16[1536,256]{1,0:T(8,128)(2,1)S(1)} %get-tuple-element.45) | copy-start | bytes 2359300
  329.5 69.1 %copy-start.35 = (bf16[1536,256]{1,0:T(8,128)(2,1)}, bf16[1536,256]{1,0:T(8,128)(2,1)S(1)}, u32[]{:S(2)}) copy-start(bf16[1536,256]{1,0:T(8,128)(2,1)S(1)} %get-tuple-element.44) | copy-start | bytes 2359300
  364.5 82.3 %all-to-all-start.1 = ((bf16[64,24,1536]{2,1,0:T(8,128)(2,1)}), bf16[64,24,1536]{2,1,0:T(8,128)(2,1)}, u32[]{:S(2)}, u32[]{:S(2)}) async-start(bf16[64,24,1536]{2,1,0:T(8,128)(2,1)} %bitcast.211), calls=%async_computation.1 | async-start | bytes 9437184 | tf_op jit(solution)/shard_map/all_to_all | solution.py:742
  446.8 126.3 %all-to-all-start.3 = ((bf16[64,24,1536]{2,1,0:T(8,128)(2,1)}), bf16[64,24,1536]{2,1,0:T(8,128)(2,1)}, u32[]{:S(2)}, u32[]{:S(2)}) async-start(bf16[64,24,1536]{2,1,0:T(8,128)(2,1)} %bitcast.210), calls=%async_computation.3 | async-start | bytes 9437184 | tf_op jit(solution)/shard_map/all_to_all | solution.py:742
  468.7 59.8 %collective-permute-start.5 = (bf16[256,1536]{1,0:T(8,128)(2,1)S(1)}, bf16[256,1536]{1,0:T(8,128)(2,1)S(1)}, u32[]{:S(2)}, u32[]{:S(2)}) collective-permute-start(bf16[256,1536]{1,0:T(8,128)(2,1)S(1)} %convolution_convert_fusion.6), channel_id=1, source_target_pairs={{0,1},{1,0},{2,3},{3,2},{4,5},{5,4},{6,7},{7,6},{8,9},{9,8},{10,11... | collective-permute-start | bytes 2359304 | tf_op jit(solution)/shard_map/ppermute | solution.py:746
  476.2 52.3 %copy-start.16 = (bf16[1536,256]{1,0:T(8,128)(2,1)S(1)}, bf16[1536,256]{1,0:T(8,128)(2,1)}, u32[]{:S(2)}) copy-start(bf16[1536,256]{1,0:T(8,128)(2,1)} %copy-done.15) | copy-start | bytes 2359300
  476.2 69.1 %collective-permute-start.4 = (bf16[1536,256]{1,0:T(8,128)(2,1)S(1)}, bf16[1536,256]{1,0:T(8,128)(2,1)S(1)}, u32[]{:S(2)}, u32[]{:S(2)}) collective-permute-start(bf16[1536,256]{1,0:T(8,128)(2,1)S(1)} %convolution_convert_fusion.7), channel_id=1, source_target_pairs={{0,1},{1,0},{2,3},{3,2},{4,5},{5,4},{6,7},{7,6},{8,9},{9,8},{10,11... | collective-permute-start | bytes 2359304 | tf_op jit(solution)/shard_map/ppermute | solution.py:746
  480.2 65.1 %copy-start.31 = (bf16[1536,256]{1,0:T(8,128)(2,1)S(1)}, bf16[1536,256]{1,0:T(8,128)(2,1)}, u32[]{:S(2)}) copy-start(bf16[1536,256]{1,0:T(8,128)(2,1)} %get-tuple-element.43) | copy-start | bytes 2359300
  480.2 82.0 %collective-permute-start.3 = (bf16[1536,256]{1,0:T(8,128)(2,1)S(1)}, bf16[1536,256]{1,0:T(8,128)(2,1)S(1)}, u32[]{:S(2)}, u32[]{:S(2)}) collective-permute-start(bf16[1536,256]{1,0:T(8,128)(2,1)S(1)} %convolution_convert_fusion.8), channel_id=1, source_target_pairs={{0,1},{1,0},{2,3},{3,2},{4,5},{5,4},{6,7},{7,6},{8,9},{9,8},{10,11... | collective-permute-start | bytes 2359304 | tf_op jit(solution)/shard_map/ppermute | solution.py:746
  533.4 28.8 %copy-start.36 = (bf16[1536,256]{1,0:T(8,128)(2,1)S(1)}, bf16[1536,256]{1,0:T(8,128)(2,1)}, u32[]{:S(2)}) copy-start(bf16[1536,256]{1,0:T(8,128)(2,1)} %copy-done.35) | copy-start | bytes 2359300
  550.3 16.9 %copy-start.19 = (bf16[128,1536]{1,0:T(8,128)(2,1)S(1)}, bf16[128,1536]{1,0:T(8,128)(2,1)}, u32[]{:S(2)}) copy-start(bf16[128,1536]{1,0:T(8,128)(2,1)} %param.31) | copy-start | bytes 1179652
  550.3 16.9 %copy-start.21 = (pred[128,1536]{1,0:T(32,128)(4,1)S(1)}, pred[128,1536]{1,0:T(32,128)(4,1)}, u32[]{:S(2)}) copy-start(pred[128,1536]{1,0:T(32,128)(4,1)} %copy-done.20) | copy-start | bytes 589828
  567.1 12.1 %slice-start.2 = ((s8[4718592]{0:T(1024)(128)(4,1)}), s8[524288]{0:T(1024)(128)(4,1)S(1)}, s32[]{:S(2)}) async-start(s8[4718592]{0:T(1024)(128)(4,1)} %bitcast.193), calls=%async_computation.6 | async-start | bytes 1048576
  598.6 28.7 %copy-start.28 = (bf16[4,128,3,128]{3,1,2,0:T(8,128)(2,1)S(1)}, bf16[4,128,3,128]{3,1,2,0:T(8,128)(2,1)}, u32[]{:S(2)}) copy-start(bf16[4,128,3,128]{3,1,2,0:T(8,128)(2,1)} %fusion.29) | copy-start | bytes 1179652
  598.6 28.7 %copy-start.52 = (f32[1536]{0:T(1024)S(1)}, f32[1536]{0:T(1024)}, u32[]{:S(2)}) copy-start(f32[1536]{0:T(1024)} %copy-done.51) | copy-start | bytes 18436
  598.7 28.7 %copy-start.55 = (f32[128]{0:T(128)S(1)}, f32[128]{0:T(128)}, u32[]{:S(2)}) copy-start(f32[128]{0:T(128)} %copy-done.54) | copy-start | bytes 1540
  643.4 93.3 %copy-start.17 = (f32[128,1536]{1,0:T(8,128)S(1)}, f32[128,1536]{1,0:T(8,128)}, u32[]{:S(2)}) copy-start(f32[128,1536]{1,0:T(8,128)} %get-tuple-element.62) | copy-start | bytes 2359300
  (52 other events, 213.9 us)

commit v2 on v1

v2 whole, which is shorter than its diff:
```python
import functools

import jax
import jax.numpy as jnp
from jax import lax
from jax.experimental import pallas as pl
from jax.experimental.pallas import tpu as pltpu
from jax.sharding import Mesh
from jax.sharding import PartitionSpec as P

QUERY_HEADS = 12
KEY_VALUE_HEADS = 4
HEAD_SIZE = 128
EXPERTS = 64
TOPK = 6
CAP = 24
EPSILON = 1e-05

F32 = jnp.float32
BF16 = jnp.bfloat16
MESH_ID = pl.DeviceIdType.MESH
AXES = ("z", "yl", "core", "yh", "xh", "xl")
SIZES = (4, 2, 2, 2, 2, 2)
EXPERT_AXES = ("z", "yl", "yh", "xh", "xl")
COL_AXES = ("yh", "xh", "xl")

PARTS = (
    ("outt", 1536, "yzx"),
    ("misc", 128, "yz"),
    ("qkv", 2560, "yz"),
    ("shgu", 2048, "zy"),
    ("shdt", 1024, "zy"),
)
HALF = 256
EXPERT_SEM = 156
TOTAL = sum(part[1] for part in PARTS)


def rem(value, size):
    return lax.rem(value, jnp.int32(size))


def place():
    at = {name: lax.axis_index(name) for name in AXES}
    return {
        "x": at["xh"] * 2 + at["xl"],
        "y": at["yh"] * 2 + at["yl"],
        "z": at["z"],
        "core": at["core"],
    }


def device(axis, value):
    if axis == "x":
        return {"xh": value // 2, "xl": rem(value, 2)}
    if axis == "y":
        return {"yh": value // 2, "yl": rem(value, 2)}
    return {axis: value}


def greet(targets):
    barrier = pltpu.get_barrier_semaphore()
    for target in targets:
        pl.semaphore_signal(barrier, inc=1, device_id=target, device_id_type=MESH_ID)
    pl.semaphore_wait(barrier, len(targets))


class Wires:
    def __init__(self, send_sems, recv_sems, local_sems):
        self.send, self.recv, self.local = send_sems, recv_sems, local_sems
        self.used, self.used_local, self.started, self.kept = 0, 0, [], []

    def remote(self, source, target, where):
        copy = pltpu.make_async_remote_copy(
            src_ref=source,
            dst_ref=target,
            send_sem=self.send.at[self.used],
            recv_sem=self.recv.at[self.used],
            device_id=where,
            device_id_type=MESH_ID,
        )
        self.used += 1
        copy.start()
        self.started.append(copy)
        return copy

    def copy(self, source, target):
        copy = pltpu.make_async_copy(source, target, self.local.at[self.used_local])
        self.used_local += 1
        copy.start()
        return copy

    def finish(self):
        for copy in self.started:
            copy.wait_send()


def balanced_offsets():
    left = [(x, y, z) for x in range(4) for y in range(4) for z in range(4) if x + y + z > 0]
    load, order = [0] * 6, []

    def uses(offset):
        used = [0] * 6
        for axis, hops in enumerate(offset):
            used[2 * axis] += hops in (1, 2)
            used[2 * axis + 1] += hops in (2, 3)
        return used

    def cost(offset):
        used = uses(offset)
        after = [a + b for a, b in zip(load, used)]
        mean = sum(after) / 6
        return (max(after), sum((a - mean) ** 2 for a in after), -sum(used))

    while left:
        best = min(left, key=cost)
        load = [a + b for a, b in zip(load, uses(best))]
        left.remove(best)
        order.append(best)
    return order


OFFSETS = balanced_offsets()


def chip_at(me, offset, sign=1):
    x, y, z = [rem(me[axis] + (sign * hops) % 4, 4) for axis, hops in zip("xyz", offset)]
    where = {"z": z, "yh": y // 2, "yl": rem(y, 2), "xh": x // 2, "xl": rem(x, 2)}
    return where, z * 16 + rem(y, 2) * 8 + (y // 2) * 4 + x


def halves(width):
    first = width // 256 * 128 if width > 128 else width
    return first, width - first


def spread_rows(shape, swap):
    dense = lax.broadcasted_iota(jnp.int32, shape, 1 if swap else 0)
    padded = lax.broadcasted_iota(jnp.int32, shape, 0 if swap else 1)
    shift = jnp.zeros(shape, jnp.int32)
    for edge in (12, 24, 36):
        shift = shift + jnp.where(dense >= edge, 4, 0)
    return dense + shift == padded


def block_ref(ref, axes, me, axis, value, columns):
    spot = dict(me)
    spot[axis] = value
    z = slice(None) if "z" in axes else spot["z"]
    yl = slice(None) if "y" in axes else rem(spot["y"], 2)
    yh = slice(None) if "y" in axes else spot["y"] // 2
    return ref.at[z, yl, me["core"], yh, :, columns]


def gather_kernel(shard_ref, gate_ref, up_ref, down_ref, *rest):
    count = len(PARTS)
    outs = rest[:count]
    expert_in, expert_out, landed = rest[count : count + 3]
    stages = rest[count + 3 : 2 * count + 3]
    send_sems, recv_sems, local_sems = rest[2 * count + 3 :]
    me = place()
    nxt = {axis: rem(me[axis] + 1, 4) for axis in "xyz"}
    opp = {axis: rem(me[axis] + 2, 4) for axis in "xyz"}
    prv = {axis: rem(me[axis] + 3, 4) for axis in "xyz"}
    sibling = {"core": 1 - me["core"]}
    partner = {"core": 1 - me["core"], "xl": 1 - lax.axis_index("xl")}
    crossed = me["core"] != lax.axis_index("xl")
    greet(
        [device("x", nxt["x"]), device("x", opp["x"]), device("x", prv["x"])]
        + [device("y", nxt["y"]), device("y", prv["y"])]
        + [device("z", nxt["z"]), device("z", prv["z"]), sibling, partner]
    )
    wires = Wires(send_sems, recv_sems, local_sems)
    runs, start = [], 0
    for index, (name, width, order) in enumerate(PARTS):
        last_x = len(order) == 3
        quarter = width // 4 if last_x else width
        run = {
            "out": outs[index],
            "order": order,
            "width": quarter,
            "done": "",
            "stage": stages[index],
            "start": start,
            "landed": landed.at[:, :, pl.ds(start, quarter)],
            "base": me["x"] * quarter if last_x else 0,
            "first": [],
            "shared": [],
        }

        def piece(x):
            if last_x:
                return shard_ref.at[:, pl.ds(pl.multiple_of(start + x * quarter, 128), quarter)]
            return shard_ref.at[:, pl.ds(start, quarter)]

        for where in (nxt, prv, opp):
            run["first"].append(
                wires.remote(piece(where["x"]), run["landed"].at[me["x"]], device("x", where["x"]))
            )
        run["bring"] = wires.copy(piece(me["x"]), run["landed"].at[me["x"]])
        runs.append(run)
        start += width

    whole = [
        (gate_ref, expert_in.at[:, pl.ds(0, HALF)]),
        (up_ref, expert_in.at[:, pl.ds(HALF, HALF)]),
        (down_ref, expert_out.at[pl.ds(0, HALF)]),
    ]

    def moved(slot):
        source, target = whole[slot]
        return pltpu.make_async_remote_copy(
            src_ref=source,
            dst_ref=target,
            send_sem=send_sems.at[EXPERT_SEM + slot],
            recv_sem=recv_sems.at[EXPERT_SEM + slot],
            device_id=partner,
            device_id_type=MESH_ID,
        )

    def kept(slot):
        source, target = whole[slot]
        return pltpu.make_async_copy(source, target, local_sems.at[20 + slot])

    @pl.when(crossed)
    def _():
        for slot in range(3):
            moved(slot).start()

    @pl.when(jnp.logical_not(crossed))
    def _():
        for slot in range(3):
            kept(slot).start()

    def part_columns(run, axis, value, which):
        base = value * run["width"] if axis == "x" else run["base"]
        left, size = 0, run["width"]
        if which is not None:
            first_half, second_half = halves(run["width"])
            left, size = (0, first_half) if which == 0 else (first_half, second_half)
        if isinstance(base, int):
            return pl.ds(base + left, size)
        return pl.ds(pl.multiple_of(base + left, 128), size)

    def blocks(run, axis, value, which=None):
        columns = part_columns(run, axis, value, which)
        return block_ref(run["out"], run["done"], me, axis, value, columns)

    def begin(run, axis, source=None):
        target = blocks(run, axis, me[axis])
        source = target if source is None else source
        run["forth"] = wires.remote(source, target, device(axis, nxt[axis]))
        run["back"] = wires.remote(source, target, device(axis, prv[axis]))

    pick = spread_rows((48, 64), False).astype(BF16)
    for run in runs:
        run["bring"].wait()
        for copy in run["first"]:
            copy.wait_recv()
        for left in range(0, run["width"], 512):
            size = min(512, run["width"] - left)
            left_in = run["start"] + left
            piece_rows = landed[:, :, left_in : left_in + size].reshape(64, size)
            run["stage"][:, left : left + size] = jnp.dot(
                pick, piece_rows, preferred_element_type=F32
            ).astype(BF16)
        axis = run["order"][0]
        begin(run, axis, run["stage"])
        run["own"] = wires.copy(run["stage"], blocks(run, axis, me[axis]))

    def forward(run, axis):
        run["forth"].wait_recv()
        source = blocks(run, axis, prv[axis], 0)
        run["more"] = [wires.remote(source, source, device(axis, nxt[axis]))]
        run["back"].wait_recv()
        if halves(run["width"])[1] > 0:
            source = blocks(run, axis, nxt[axis], 1)
            run["more"].append(wires.remote(source, source, device(axis, prv[axis])))

    def share(run, axis, value):
        source = blocks(run, axis, value)
        run["shared"].append(wires.remote(source, source, sibling))

    def advance(run, step):
        axis = run["order"][step]
        for copy in run["more"]:
            copy.wait_recv()
        if step == len(run["order"]) - 1:
            share(run, axis, opp[axis])
            return
        if step == 0:
            run["own"].wait()
        run["done"] = run["done"] + axis
        following = run["order"][step + 1]
        begin(run, following)
        if step + 1 == len(run["order"]) - 1:
            share(run, following, me[following])

    def last_forward(run):
        axis = run["order"][-1]
        forward(run, axis)
        share(run, axis, prv[axis])
        share(run, axis, nxt[axis])

    threes = [run for run in runs if len(run["order"]) == 3]
    twos = [run for run in runs if len(run["order"]) == 2]
    for run in runs:
        forward(run, run["order"][0])
    for run in runs:
        advance(run, 0)
    for run in threes:
        forward(run, run["order"][1])
    for run in threes:
        advance(run, 1)
    for run in twos:
        last_forward(run)
    for run in threes:
        last_forward(run)

    @pl.when(crossed)
    def _():
        for slot in range(3):
            moved(slot).wait_recv()

    @pl.when(jnp.logical_not(crossed))
    def _():
        for slot in range(3):
            kept(slot).wait()

    handed = [
        wires.remote(
            expert_in.at[:, pl.ds(0, 2 * HALF)], expert_in.at[:, pl.ds(2 * HALF, 2 * HALF)], sibling
        ),
        wires.remote(expert_out.at[pl.ds(0, HALF)], expert_out.at[pl.ds(HALF, HALF)], sibling),
    ]
    for run in twos + threes:
        advance(run, len(run["order"]) - 1)
    for run in runs:
        for copy in run["shared"]:
            copy.wait_recv()
    for copy in handed:
        copy.wait_recv()
    wires.finish()

    @pl.when(crossed)
    def _():
        for slot in range(3):
            moved(slot).wait_send()


def gather_weights(shard, gate_w, up_w, down_w):
    shapes = [jax.ShapeDtypeStruct((4, 2, 2, 2, 48, width), BF16) for _, width, _ in PARTS]
    shapes += [
        jax.ShapeDtypeStruct((gate_w.shape[0], 4 * HALF), BF16),
        jax.ShapeDtypeStruct((2 * HALF, down_w.shape[1]), BF16),
    ]
    copies = 160
    anywhere = pl.BlockSpec(memory_space=pl.ANY)
    return pl.pallas_call(
        gather_kernel,
        out_shape=shapes,
        in_specs=[pl.BlockSpec(memory_space=pltpu.VMEM)] + [anywhere] * 3,
        out_specs=[anywhere] * (len(PARTS) + 2),
        scratch_shapes=[pltpu.VMEM((4, 16, TOTAL), BF16)]
        + [
            pltpu.VMEM((48, width // 4 if len(order) == 3 else width), BF16)
            for _, width, order in PARTS
        ]
        + [
            pltpu.SemaphoreType.DMA((copies,)),
            pltpu.SemaphoreType.DMA((copies,)),
            pltpu.SemaphoreType.DMA((24,)),
        ],
        compiler_params=pltpu.CompilerParams(
            collective_id=0, has_side_effects=True, vmem_limit_bytes=16 * 1024 * 1024
        ),
        cost_estimate=pl.CostEstimate(flops=0, bytes_accessed=200_000_000, transcendentals=0),
    )(shard, gate_w, up_w, down_w)


def sum_kernel(*refs):
    count = len(PARTS)
    grads = refs[:count]
    expert_from = refs[count : count + 2]
    outs = refs[count + 2 : 2 * count + 2]
    expert_to = refs[2 * count + 2 : 2 * count + 4]
    rest = refs[2 * count + 4 :]
    own = rest[:count]
    theirs = rest[count : 2 * count]
    near1 = rest[2 * count : 3 * count]
    near2 = rest[3 * count : 4 * count]
    ends = rest[4 * count : 5 * count]
    arrived = rest[5 * count : 6 * count]
    send_sems, recv_sems, local_sems = rest[6 * count :]
    me = place()
    core = me["core"]
    nxt = {axis: rem(me[axis] + 1, 4) for axis in "xyz"}
    opp = {axis: rem(me[axis] + 2, 4) for axis in "xyz"}
    prv = {axis: rem(me[axis] + 3, 4) for axis in "xyz"}
    sibling = {"core": 1 - core}
    partner = {"core": 1 - core, "xl": 1 - lax.axis_index("xl")}
    crossed = core != lax.axis_index("xl")
    greet(
        [device("x", nxt["x"]), device("x", opp["x"]), device("x", prv["x"])]
        + [device("y", nxt["y"]), device("y", prv["y"])]
        + [device("z", nxt["z"]), device("z", prv["z"]), sibling, partner]
    )

    def moved(slot):
        return pltpu.make_async_remote_copy(
            src_ref=expert_from[slot],
            dst_ref=expert_to[slot],
            send_sem=send_sems.at[EXPERT_SEM + slot],
            recv_sem=recv_sems.at[EXPERT_SEM + slot],
            device_id=partner,
            device_id_type=MESH_ID,
        )

    def kept(slot):
        return pltpu.make_async_copy(
            expert_from[slot], expert_to[slot], local_sems.at[44 + slot]
        )

    wires = Wires(send_sems, recv_sems, local_sems)

    def spot(left_axes, axis, value, with_core):
        at = dict(me)
        if axis is not None:
            at[axis] = value
        whole = [name for name in left_axes if name != axis]
        z = slice(None) if "z" in whole else at["z"]
        yl = slice(None) if "y" in whole else rem(at["y"], 2)
        yh = slice(None) if "y" in whole else at["y"] // 2
        return (z, yl) + (() if with_core is None else (with_core,)) + (yh,)

    def lead(left_axes, axis):
        dims = []
        for name in ("z", "y"):
            if name in left_axes and name != axis:
                dims += [4] if name == "z" else [2, 2]
        return dims

    def loop_over(dims, body):
        total = 1
        for size in dims:
            total *= size

        def step(flat, carry):
            index, rest_flat = [], flat
            for size in reversed(dims):
                index.append(rem(rest_flat, size))
                rest_flat = rest_flat // size
            body(tuple(reversed(index)))
            return carry

        if total == 1:
            body(())
        else:
            lax.fori_loop(0, total, step, 0)

    def add_into(target, sources, dims):
        def body(index):
            for row in range(0, 48, 16):
                at = index + (pl.ds(row, 16),)
                value = target[at].astype(F32)
                for source in sources:
                    value = value + source[at].astype(F32)
                target[at] = value.astype(target.dtype)

        loop_over(dims, body)

    runs = []
    for index, (name, width, order) in enumerate(PARTS):
        quarter = width // 4 if len(order) == 3 else width
        runs.append(
            {
                "index": index,
                "name": name,
                "order": order[::-1],
                "width": quarter,
                "full": width,
                "left": "zy",
                "turn": 0,
            }
        )

    def columns_of(run, axis, value, which):
        if len(run["order"]) == 3:
            base = (value if axis == "x" else me["x"]) * run["width"]
        else:
            base = 0
        left, size = 0, run["width"]
        if which is not None:
            first_half, second_half = halves(run["width"])
            left, size = (0, first_half) if which == 0 else (first_half, second_half)
        if isinstance(base, int):
            return pl.ds(base + left, size)
        return pl.ds(pl.multiple_of(base + left, 128), size)

    def chunk(run, axis, value, which=None, ref=None, with_core=None):
        ref = own[run["index"]] if ref is None else ref
        columns = columns_of(run, axis, value, which)
        return ref.at[spot(run["left"], axis, value, with_core) + (slice(None), columns)]

    def pair(run, axis, value):
        index = run["index"]
        give = wires.remote(
            chunk(run, axis, value, None, grads[index], 1 - core),
            chunk(run, axis, value, None, theirs[index]),
            sibling,
        )
        keep = wires.copy(
            chunk(run, axis, value, None, grads[index], core), chunk(run, axis, value)
        )
        return give, keep

    def join(run, axis, value, copies):
        copies[0].wait_recv()
        copies[1].wait()
        add_into(
            chunk(run, axis, value),
            [chunk(run, axis, value, None, theirs[run["index"]])],
            lead(run["left"], axis),
        )

    def slots(run, axis):
        dims = lead(run["left"], axis)
        phase = run["turn"]
        ref = (near1 if phase == 0 else near2)[run["index"]]
        if phase == 2:
            ref = ends[run["index"]]
        if not dims:
            ref = ref.at[:, pl.ds(0, 48)]
        return ref.at[0], ref.at[1], ref.at[2], dims

    def part(ref, run, which, dims):
        first_half, second_half = halves(run["width"])
        columns = pl.ds(0, first_half) if which == 0 else pl.ds(first_half, second_half)
        return ref.at[(slice(None),) * len(dims) + (slice(None), columns)]

    def ring_open(run, axis):
        from_prv, from_nxt, passing, dims = slots(run, axis)
        run["passing"] = [
            wires.remote(
                chunk(run, axis, opp[axis], 0), part(passing, run, 0, dims), device(axis, nxt[axis])
            )
        ]
        if halves(run["width"])[1]:
            run["passing"].append(
                wires.remote(
                    chunk(run, axis, opp[axis], 1),
                    part(passing, run, 1, dims),
                    device(axis, prv[axis]),
                )
            )

    def ring_near(run, axis):
        from_prv, from_nxt, passing, dims = slots(run, axis)
        run["near"] = []
        if halves(run["width"])[1]:
            run["near"].append(
                wires.remote(
                    chunk(run, axis, nxt[axis], 1),
                    part(from_prv, run, 1, dims),
                    device(axis, nxt[axis]),
                )
            )
        run["near"].append(
            wires.remote(
                chunk(run, axis, prv[axis], 0), part(from_nxt, run, 0, dims), device(axis, prv[axis])
            )
        )

    def ring_pass(run, axis):
        from_prv, from_nxt, passing, dims = slots(run, axis)
        run["passing"][0].wait_recv()
        add_into(chunk(run, axis, nxt[axis], 0), [part(passing, run, 0, dims)], dims)
        run["near"].append(
            wires.remote(
                chunk(run, axis, nxt[axis], 0), part(from_prv, run, 0, dims), device(axis, nxt[axis])
            )
        )
        if halves(run["width"])[1]:
            run["passing"][1].wait_recv()
            add_into(chunk(run, axis, prv[axis], 1), [part(passing, run, 1, dims)], dims)
            run["near"].append(
                wires.remote(
                    chunk(run, axis, prv[axis], 1),
                    part(from_nxt, run, 1, dims),
                    device(axis, prv[axis]),
                )
            )

    def ring_close(run, axis):
        from_prv, from_nxt, passing, dims = slots(run, axis)
        for copy in run["near"]:
            copy.wait_recv()
        if halves(run["width"])[1]:
            add_into(chunk(run, axis, me[axis]), [from_prv, from_nxt], dims)
        else:
            add_into(chunk(run, axis, me[axis]), [from_prv, from_nxt], dims)
        run["left"] = run["left"].replace(axis, "")
        run["turn"] += 1

    threes = [run for run in runs if len(run["order"]) == 3]
    twos = [run for run in runs if len(run["order"]) == 2]
    begun = []
    for where in (opp, nxt, prv, me):
        begun.append([pair(run, run["order"][0], where[run["order"][0]]) for run in runs])

    @pl.when(crossed)
    def _():
        for slot in range(2):
            moved(slot).start()

    @pl.when(jnp.logical_not(crossed))
    def _():
        for slot in range(2):
            kept(slot).start()

    for run, copies in zip(runs, begun[0]):
        axis = run["order"][0]
        join(run, axis, opp[axis], copies)
        ring_open(run, axis)
    for run, nexts, prevs in zip(runs, begun[1], begun[2]):
        axis = run["order"][0]
        join(run, axis, nxt[axis], nexts)
        join(run, axis, prv[axis], prevs)
        ring_near(run, axis)
    for run in threes:
        ring_pass(run, run["order"][0])
    for run, copies in zip(runs, begun[3]):
        axis = run["order"][0]
        join(run, axis, me[axis], copies)
    for run in twos:
        ring_pass(run, run["order"][0])

    def turn(run):
        ring_close(run, run["order"][run["turn"]])
        following = run["order"][run["turn"]]
        ring_open(run, following)
        ring_near(run, following)

    for run in threes:
        turn(run)
    for run in threes:
        ring_pass(run, run["order"][1])
    for run in twos:
        turn(run)
    for run in threes:
        turn(run)
    for run in twos:
        ring_pass(run, run["order"][1])
    for run in threes:
        ring_pass(run, run["order"][2])
    for run in twos:
        ring_close(run, run["order"][1])
    for run in threes:
        ring_close(run, run["order"][2])
    lasts = []
    for run in runs:
        index, width = run["index"], run["width"]
        summed = own[index].at[me["z"], rem(me["y"], 2), me["y"] // 2]
        exact = lax.Precision.HIGHEST if summed.dtype == F32 else None
        pick = spread_rows((64, 48), True).astype(summed.dtype)
        target = arrived[index]
        staging = ends[index].at[3] if len(run["order"]) == 3 else near2[index].at[3]
        base = me["x"] * width if len(run["order"]) == 3 else 0
        for left in range(0, width, 512):
            size = min(512, width - left)
            if isinstance(base, int):
                columns = pl.ds(left, size)
            else:
                columns = pl.ds(pl.multiple_of(base + left, 128), size)
            staging[:, left : left + size] = jnp.dot(
                pick, summed[:, columns], preferred_element_type=F32, precision=exact
            ).astype(staging.dtype)
        if len(run["order"]) == 3:
            columns = pl.ds(pl.multiple_of(base, 128), width)
            lands = target.at[:, columns]
        else:
            lands = target.at[me["x"]]
        run["copies"] = []
        for where in (nxt, opp, prv):
            row = pl.ds(pl.multiple_of(where["x"] * 16, 16), 16)
            run["copies"].append(
                wires.remote(staging.at[row], lands, device("x", where["x"]))
            )
        row = pl.ds(pl.multiple_of(me["x"] * 16, 16), 16)
        run["keep"] = wires.copy(staging.at[row], lands)
    for run in runs:
        index = run["index"]
        run["keep"].wait()
        for copy in run["copies"]:
            copy.wait_recv()
        if len(run["order"]) == 3:
            outs[index][...] = arrived[index][...].astype(F32)
        else:
            value = arrived[index][0].astype(F32)
            for place_x in range(1, 4):
                value = value + arrived[index][place_x].astype(F32)
            outs[index][...] = value
    wires.finish()

    @pl.when(crossed)
    def _():
        for slot in range(2):
            moved(slot).wait_recv()
            moved(slot).wait_send()

    @pl.when(jnp.logical_not(crossed))
    def _():
        for slot in range(2):
            kept(slot).wait()


def sum_gradients(grads, expert_grads):
    scratch_own, scratch_theirs, near1, near2, ends, arrived = [], [], [], [], [], []
    for name, width, order in PARTS:
        kind = F32 if name == "misc" else BF16
        scratch_own.append(pltpu.VMEM((4, 2, 2, 48, width), kind))
        scratch_theirs.append(pltpu.VMEM((4, 2, 2, 48, width), kind))
        if order == "yz":
            near1.append(pltpu.VMEM((3, 2, 2, 48, width), kind))
            near2.append(pltpu.VMEM((4, 64, width), kind))
        elif order == "zy":
            near1.append(pltpu.VMEM((3, 4, 48, width), kind))
            near2.append(pltpu.VMEM((4, 64, width), kind))
        else:
            quarter = width // 4
            near1.append(pltpu.VMEM((3, 4, 2, 2, 48, quarter), kind))
            near2.append(pltpu.VMEM((3, 2, 2, 48, quarter), kind))
        ends.append(pltpu.VMEM((4, 64, width // 4 if len(order) == 3 else 128), kind))
        arrived.append(pltpu.VMEM((16, width) if len(order) == 3 else (4, 16, width), kind))
    copies = 160
    anywhere = pl.BlockSpec(memory_space=pl.ANY)
    return pl.pallas_call(
        sum_kernel,
        out_shape=[jax.ShapeDtypeStruct((16, width), F32) for _, width, _ in PARTS]
        + [jax.ShapeDtypeStruct(grad.shape, grad.dtype) for grad in expert_grads],
        in_specs=[anywhere] * (len(PARTS) + 2),
        out_specs=[pl.BlockSpec(memory_space=pltpu.VMEM)] * len(PARTS) + [anywhere] * 2,
        scratch_shapes=scratch_own
        + scratch_theirs
        + near1
        + near2
        + ends
        + arrived
        + [
            pltpu.SemaphoreType.DMA((copies,)),
            pltpu.SemaphoreType.DMA((copies,)),
            pltpu.SemaphoreType.DMA((48,)),
        ],
        compiler_params=pltpu.CompilerParams(
            collective_id=1, has_side_effects=True, vmem_limit_bytes=56 * 1024 * 1024
        ),
    )(*grads, *expert_grads)


def col_device(col):
    return {"yh": col // 4, "xh": rem(col // 2, 2), "xl": rem(col, 2)}


def col_index():
    return lax.axis_index("yh") * 4 + lax.axis_index("xh") * 2 + lax.axis_index("xl")


def later_kernel(own_ref, marks_ref, out_ref, marks_out, send_sems, recv_sems, local_sem):
    me = col_index()
    rows = own_ref.shape[0]
    tail = marks_ref.shape[0]
    late = pl.ds(rows - tail, tail)
    greet([col_device(rem(me + far, 8)) for far in range(1, 8)])

    def copies(far, first):
        there = col_device(rem(me + far, 8))
        pairs = [(own_ref, out_ref.at[me])]
        if first:
            pairs = [(own_ref.at[late], out_ref.at[0, late]), (marks_ref, marks_out)]
        return [
            pltpu.make_async_remote_copy(
                src_ref=source,
                dst_ref=target,
                send_sem=send_sems.at[far, number],
                recv_sem=recv_sems.at[far, number],
                device_id=there,
                device_id_type=MESH_ID,
            )
            for number, (source, target) in enumerate(pairs)
        ]

    def each(far, first, condition, act):
        @pl.when(condition)
        def _():
            for copy in copies(far, first):
                act(copy)

    for far in range(7, 0, -1):
        each(far, False, (me > 0) & (me + far < 8), lambda copy: copy.start())
        each(far, True, me == 0, lambda copy: copy.start())
    keep = pltpu.make_async_copy(own_ref, out_ref.at[me], local_sem)
    keep.start()

    @pl.when(me == 0)
    def _():
        marks_out[...] = marks_ref[...]

    @pl.when(me > 0)
    def _():
        out_ref[0, : rows - tail] = jnp.zeros((rows - tail, own_ref.shape[1]), own_ref.dtype)

    for far in range(1, 8):

        @pl.when(me + far < 8)
        def _():
            out_ref[me + far] = jnp.zeros(own_ref.shape, own_ref.dtype)

    keep.wait()
    for far in range(1, 8):
        each(far, False, me > far, lambda copy: copy.wait_recv())
        each(far, True, me == far, lambda copy: copy.wait_recv())
        each(far, False, (me > 0) & (me + far < 8), lambda copy: copy.wait_send())
        each(far, True, me == 0, lambda copy: copy.wait_send())


def to_later(rows, marks):
    vmem = pl.BlockSpec(memory_space=pltpu.VMEM)
    return pl.pallas_call(
        later_kernel,
        out_shape=[
            jax.ShapeDtypeStruct((8,) + rows.shape, rows.dtype),
            jax.ShapeDtypeStruct(marks.shape, marks.dtype),
        ],
        in_specs=[vmem, vmem],
        out_specs=[vmem, vmem],
        scratch_shapes=[
            pltpu.SemaphoreType.DMA((8, 2)),
            pltpu.SemaphoreType.DMA((8, 2)),
            pltpu.SemaphoreType.DMA,
        ],
        compiler_params=pltpu.CompilerParams(
            collective_id=2, has_side_effects=True, vmem_limit_bytes=16 * 1024 * 1024
        ),
        cost_estimate=pl.CostEstimate(flops=0, bytes_accessed=70_000_000, transcendentals=0),
    )(rows, marks)


def earlier_kernel(
    tail,
    blocks_ref,
    in_ref,
    down_ref,
    rows_ref,
    out_ref,
    in_out,
    down_out,
    rows_out,
    landed,
    send_sems,
    recv_sems,
    local_sem,
):
    me = col_index()
    spot = place()
    chips = [chip_at(spot, offset) for offset in OFFSETS]
    mine = chip_at(spot, (0, 0, 0))[1]
    rows = out_ref.shape[0]
    late = pl.ds(rows - tail, tail)
    sibling = {"core": 1 - lax.axis_index("core")}
    greet([where for where, _ in chips] + [sibling])

    def remote(source, target, number, where):
        return pltpu.make_async_remote_copy(
            src_ref=source,
            dst_ref=target,
            send_sem=send_sems.at[number],
            recv_sem=recv_sems.at[number],
            device_id=where,
            device_id_type=MESH_ID,
        )

    def copy(far, first):
        block = rem(me + 8 - far, 8)
        there = col_device(block)
        if first:
            return remote(blocks_ref.at[0, late], landed.at[far, late], far, there)
        return remote(blocks_ref.at[block], landed.at[far], far, there)

    def each(far, first, condition, act):
        @pl.when(condition)
        def _():
            act(copy(far, first))

    for far in range(7, 0, -1):
        each(far, False, me > far, lambda moved: moved.start())
        each(far, True, me == far, lambda moved: moved.start())
    halves_sent = [
        remote(in_ref, in_out, 8, sibling),
        remote(down_ref, down_out, 9, sibling),
    ]
    for sent in halves_sent:
        sent.start()
    rows_sent = [
        remote(rows_ref.at[holder], rows_out.at[mine], 10 + number, where)
        for number, (where, holder) in enumerate(chips)
    ]
    for sent in rows_sent:
        sent.start()
    kept = pltpu.make_async_copy(rows_ref.at[mine], rows_out.at[mine], local_sem)
    kept.start()

    @pl.when(me == 0)
    def _():
        for far in range(1, 8):
            landed[far, : rows - tail] = jnp.zeros(
                (rows - tail, landed.shape[2]), landed.dtype
            )

    for far in range(1, 8):

        @pl.when(me + far >= 8)
        def _():
            landed[far] = jnp.zeros(landed.shape[1:], landed.dtype)

    for far in range(1, 8):
        each(far, False, (me > 0) & (me + far < 8), lambda moved: moved.wait_recv())
        each(far, True, me == 0, lambda moved: moved.wait_recv())

    for row in range(0, rows, 16):
        at = pl.ds(row, 16)
        value = blocks_ref[me, at].astype(F32)
        for far in range(1, 8):
            value = value + landed[far, at].astype(F32)
        out_ref[at] = value.astype(out_ref.dtype)
    for far in range(1, 8):
        each(far, False, me > far, lambda moved: moved.wait_send())
        each(far, True, me == far, lambda moved: moved.wait_send())
    for sent in halves_sent + rows_sent:
        sent.wait()
    kept.wait()


def sum_earlier(blocks, tail, expert_in, expert_down, rows):
    vmem = pl.BlockSpec(memory_space=pltpu.VMEM)
    anywhere = pl.BlockSpec(memory_space=pl.ANY)
    return pl.pallas_call(
        functools.partial(earlier_kernel, tail),
        out_shape=[
            jax.ShapeDtypeStruct(blocks.shape[1:], blocks.dtype),
            jax.ShapeDtypeStruct(expert_in.shape, expert_in.dtype),
            jax.ShapeDtypeStruct(expert_down.shape, expert_down.dtype),
            jax.ShapeDtypeStruct(rows.shape, rows.dtype),
        ],
        in_specs=[vmem, anywhere, anywhere, anywhere],
        out_specs=[vmem, anywhere, anywhere, anywhere],
        scratch_shapes=[
            pltpu.VMEM(blocks.shape, blocks.dtype),
            pltpu.SemaphoreType.DMA((73,)),
            pltpu.SemaphoreType.DMA((73,)),
            pltpu.SemaphoreType.DMA,
        ],
        compiler_params=pltpu.CompilerParams(
            collective_id=3, has_side_effects=True, vmem_limit_bytes=16 * 1024 * 1024
        ),
        cost_estimate=pl.CostEstimate(flops=0, bytes_accessed=70_000_000, transcendentals=0),
    )(blocks, expert_in, expert_down, rows)


VMEM_SPEC = pl.BlockSpec(memory_space=pltpu.VMEM)
GROUP = QUERY_HEADS // KEY_VALUE_HEADS
EXTRA = 128


def dot(left, right, left_dim=1, right_dim=0):
    return lax.dot_general(
        left, right, (((left_dim,), (right_dim,)), ((), ())), preferred_element_type=F32
    )


def rounded_parts(value):
    first = value.astype(BF16)
    left = value - first.astype(F32)
    second = left.astype(BF16)
    return [first, second, (left - second.astype(F32)).astype(BF16)]


def lane_column(index):
    return (lax.broadcasted_iota(jnp.int32, (16, 128), 1) == index).astype(BF16)


def gain_row(misc_ref, index):
    return dot(lane_column(index), misc_ref[...], 1, 1)[:1]


def allowed_pairs(marks_ref, segments_ref, rows, keys):
    me = col_index()
    shape = (rows, keys)
    own = segments_ref[:, :1]
    first_length = jnp.where(
        me == 0,
        jnp.sum((own == 0.0).astype(F32), axis=0, keepdims=True),
        marks_ref[:1, :1].astype(F32),
    )
    last_start = (me * rows).astype(F32) + jnp.sum(
        (own < 2.0).astype(F32), axis=0, keepdims=True
    )
    lowest = jnp.where(own == 0.0, 0.0, jnp.where(own == 1.0, first_length, last_start))
    key = lax.broadcasted_iota(jnp.int32, shape, 1)
    query = lax.broadcasted_iota(jnp.int32, shape, 0) + me * rows
    return (key <= query) & (key.astype(F32) >= lowest)


def head_columns(ref, group):
    width = GROUP * HEAD_SIZE
    return jnp.concatenate(
        [
            ref[:, group * width + head * HEAD_SIZE : group * width + (head + 1) * HEAD_SIZE]
            for head in range(GROUP)
        ],
        axis=0,
    )


def head_weights(queries, keys, allowed):
    scores = dot(queries, keys, 1, 1) * (HEAD_SIZE ** (-0.5))
    scores = jnp.where(allowed, scores, -1e30)
    shifted = jnp.exp(scores - jnp.max(scores, axis=1, keepdims=True))
    return shifted / jnp.sum(shifted, axis=1, keepdims=True)


def middle_kernel(
    qkv_ref,
    every_ref,
    marks_ref,
    segments_ref,
    tokens_ref,
    outt_ref,
    misc_ref,
    named_ref,
    slots_ref,
    owner_ref,
    attended_ref,
    residual_ref,
    normed_ref,
    gates_ref,
    outgoing_ref,
):
    rows, features = tokens_ref.shape
    width = KEY_VALUE_HEADS * HEAD_SIZE
    keys_count = 8 * rows
    allowed = allowed_pairs(marks_ref, segments_ref, rows, keys_count)
    allowed = jnp.concatenate([allowed.astype(F32)] * GROUP, axis=0) > 0.5
    for group in range(KEY_VALUE_HEADS):
        queries = head_columns(qkv_ref, group)
        columns = pl.ds(group * HEAD_SIZE, HEAD_SIZE)
        keys = every_ref[:, :, columns].reshape(keys_count, HEAD_SIZE)
        values = every_ref[:, :, pl.ds(width + group * HEAD_SIZE, HEAD_SIZE)].reshape(
            keys_count, HEAD_SIZE
        )
        weights = head_weights(queries, keys, allowed)
        mixed = dot(weights.astype(BF16), values).astype(BF16)
        for head in range(GROUP):
            at = (group * GROUP + head) * HEAD_SIZE
            attended_ref[:, at : at + HEAD_SIZE] = mixed[head * rows : (head + 1) * rows]
    attended = attended_ref[...]
    total = jnp.zeros((rows, 1), F32)
    for left in range(0, features, 512):
        piece = tokens_ref[:, left : left + 512].astype(F32) + dot(
            attended, outt_ref[left : left + 512], 1, 1
        )
        residual_ref[:, left : left + 512] = piece
        total = total + jnp.sum(piece * piece, axis=1, keepdims=True)
    scale = lax.rsqrt(total / features + EPSILON)
    normed_ref[...] = (residual_ref[...] * scale * gain_row(misc_ref, EXPERTS + 1)).astype(BF16)
    normed = normed_ref[...]
    logits = dot(normed, misc_ref[...])
    named = named_ref[...] > 0.5
    chosen = jnp.where(named, logits, -1e30)
    chosen_exp = jnp.where(named, jnp.exp(chosen - jnp.max(chosen, axis=1, keepdims=True)), 0.0)
    gates = chosen_exp / jnp.sum(chosen_exp, axis=1, keepdims=True)
    gates_ref[...] = gates
    parts = jnp.concatenate(rounded_parts(gates), axis=1)

    def send_rows(step, carry):
        at = pl.ds(pl.multiple_of(step * 256, 256), 256)
        slots = slots_ref[at]
        outgoing_ref[at, :features] = dot(slots, normed).astype(BF16)
        gate_parts = dot(slots, parts)
        owner = owner_ref[at].astype(F32)
        lane = lax.broadcasted_iota(jnp.int32, (256, EXTRA), 1)
        extra = jnp.zeros((256, EXTRA), F32)
        for part in range(3):
            column = jnp.sum(
                gate_parts[:, part * 128 : (part + 1) * 128] * owner, axis=1, keepdims=True
            )
            extra = jnp.where(lane == part, column, extra)
        outgoing_ref[at, features:] = extra.astype(BF16)
        return carry

    lax.fori_loop(0, slots_ref.shape[0] // 256, send_rows, 0)


def middle(qkv, every, marks, segments, tokens, outt, misc, named, slots, owner):
    rows, features = tokens.shape
    return pl.pallas_call(
        middle_kernel,
        out_shape=[
            jax.ShapeDtypeStruct((rows, features), BF16),
            jax.ShapeDtypeStruct((rows, features), F32),
            jax.ShapeDtypeStruct((rows, features), BF16),
            jax.ShapeDtypeStruct((rows, 128), F32),
            jax.ShapeDtypeStruct((slots.shape[0], features + EXTRA), BF16),
        ],
        in_specs=[VMEM_SPEC] * 10,
        out_specs=[VMEM_SPEC] * 5,
        compiler_params=pltpu.CompilerParams(vmem_limit_bytes=48 * 1024 * 1024),
        cost_estimate=pl.CostEstimate(
            flops=6_000_000_000, bytes_accessed=20_000_000, transcendentals=2_000_000
        ),
    )(qkv, every, marks, segments, tokens, outt, misc, named, slots, owner)


def expert_kernel(
    arrived_ref, cotangent_ref, weight_ref, down_ref, back_ref, grads_ref, hidden_ref, gated_ref
):
    rows, features = cotangent_ref.shape
    extra = arrived_ref[:, features:].astype(F32)
    gate = extra[:, :1] + extra[:, 1:2] + extra[:, 2:3]
    pre = dot(arrived_ref[:, :features], weight_ref[...])
    grad_hidden = dot(cotangent_ref[...], down_ref[...], 1, 1)
    along = jnp.zeros((rows, 1), F32)
    for part in range(2):
        base = part * 2 * HALF
        gate_pre, up_pre = pre[:, base : base + HALF], pre[:, base + HALF : base + 2 * HALF]
        grad_part = grad_hidden[:, part * HALF : (part + 1) * HALF]
        sigmoid = 1.0 / (1.0 + jnp.exp(-gate_pre))
        silu = gate_pre * sigmoid
        hidden = silu * up_pre
        along = along + jnp.sum(hidden * grad_part, axis=1, keepdims=True)
        gated_grad = grad_part * gate
        grads_ref[:, base : base + HALF] = (
            gated_grad * up_pre * sigmoid * (1.0 + gate_pre * (1.0 - sigmoid))
        ).astype(BF16)
        grads_ref[:, base + HALF : base + 2 * HALF] = (gated_grad * silu).astype(BF16)
        hidden_ref[:, part * HALF : (part + 1) * HALF] = hidden.astype(BF16)
        gated_ref[:, part * HALF : (part + 1) * HALF] = (hidden * gate).astype(BF16)
    back_ref[:, :features] = dot(grads_ref[...], weight_ref[...], 1, 1).astype(BF16)
    lane = lax.broadcasted_iota(jnp.int32, (rows, EXTRA), 1)
    value = jnp.zeros((rows, EXTRA), F32)
    for part, column in enumerate(rounded_parts(along)):
        value = jnp.where(lane == part, column.astype(F32), value)
    back_ref[:, features:] = value.astype(BF16)


def expert(arrived, grad_received, weight, down):
    count, features = grad_received.shape
    tile = 256

    def rows_of(width):
        return pl.BlockSpec((tile, width), lambda step: (step, 0))

    def whole(array):
        return pl.BlockSpec(array.shape, lambda step: (0, 0))

    return pl.pallas_call(
        expert_kernel,
        grid=(count // tile,),
        out_shape=[
            jax.ShapeDtypeStruct((count, features + EXTRA), BF16),
            jax.ShapeDtypeStruct((count, 4 * HALF), BF16),
            jax.ShapeDtypeStruct((count, 2 * HALF), BF16),
            jax.ShapeDtypeStruct((count, 2 * HALF), BF16),
        ],
        in_specs=[rows_of(features + EXTRA), rows_of(features), whole(weight), whole(down)],
        out_specs=[rows_of(features + EXTRA), rows_of(4 * HALF), rows_of(2 * HALF), rows_of(2 * HALF)],
        compiler_params=pltpu.CompilerParams(vmem_limit_bytes=48 * 1024 * 1024),
        cost_estimate=pl.CostEstimate(
            flops=12_000_000_000, bytes_accessed=25_000_000, transcendentals=1_000_000
        ),
    )(arrived, grad_received, weight, down)


def back_kernel(
    grad_back_ref,
    slots_ref,
    owner_ref,
    gates_ref,
    cotangent_ref,
    residual_ref,
    partial_ref,
    misc_ref,
    outt_ref,
    qkv_ref,
    every_ref,
    marks_ref,
    segments_ref,
    grad_residual_ref,
    grad_low_ref,
    grad_logits_ref,
    grad_gain_ref,
    grad_queries_ref,
    partial_keyvals_ref,
    grad_attended,
):
    rows, features = cotangent_ref.shape
    width = KEY_VALUE_HEADS * HEAD_SIZE
    keys_count = 8 * rows
    score_scale = HEAD_SIZE ** (-0.5)
    slots = slots_ref[...]
    extra = grad_back_ref[:, features:].astype(F32)
    owner = owner_ref[...].astype(F32)
    grad_gates = jnp.zeros((rows, 128), F32)
    for part in range(3):
        grad_gates = grad_gates + dot(slots, (owner * extra[:, part : part + 1]).astype(BF16))
    gates = gates_ref[...]
    grad_logits = (
        gates * (grad_gates - jnp.sum(gates * grad_gates, axis=1, keepdims=True))
    ).astype(BF16)
    grad_logits_ref[...] = grad_logits
    gain = gain_row(misc_ref, EXPERTS + 1)
    square, inner = jnp.zeros((rows, 1), F32), jnp.zeros((rows, 1), F32)
    for left in range(0, features, 512):
        columns = pl.ds(left, 512)
        piece = (
            partial_ref[:, columns]
            + dot(slots, grad_back_ref[:, columns])
            + dot(grad_logits, misc_ref[columns], 1, 1)
        )
        grad_residual_ref[:, columns] = piece
        residual = residual_ref[:, columns]
        square = square + jnp.sum(residual * residual, axis=1, keepdims=True)
        inner = inner + jnp.sum(
            piece * gain[:, left : left + 512] * residual, axis=1, keepdims=True
        )
    scale = lax.rsqrt(square / features + EPSILON)
    cubed = scale * scale * scale * (inner / features)
    for left in range(0, features, 512):
        columns = pl.ds(left, 512)
        piece = grad_residual_ref[:, columns]
        residual = residual_ref[:, columns]
        grad_gain_ref[:, columns] = jnp.broadcast_to(
            jnp.sum(piece * residual * scale, axis=0, keepdims=True), (8, 512)
        )
        value = (
            cotangent_ref[:, columns].astype(F32)
            + scale * piece * gain[:, left : left + 512]
            - residual * cubed
        )
        grad_residual_ref[:, columns] = value
        grad_low_ref[:, columns] = value.astype(BF16)
    grad_low = grad_low_ref[...]
    for left in range(0, features, 512):
        columns = pl.ds(left, 512)
        grad_attended[:, columns] = dot(grad_low, outt_ref[:, columns]).astype(BF16)
    allowed = allowed_pairs(marks_ref, segments_ref, rows, keys_count)
    allowed = jnp.concatenate([allowed.astype(F32)] * GROUP, axis=0) > 0.5
    for group in range(KEY_VALUE_HEADS):
        queries = head_columns(qkv_ref, group)
        heads_gradient = head_columns(grad_attended, group)
        key_columns = pl.ds(group * HEAD_SIZE, HEAD_SIZE)
        value_columns = pl.ds(width + group * HEAD_SIZE, HEAD_SIZE)
        keys = every_ref[:, :, key_columns].reshape(keys_count, HEAD_SIZE)
        values = every_ref[:, :, value_columns].reshape(keys_count, HEAD_SIZE)
        weights = head_weights(queries, keys, allowed)
        grad_weights = dot(heads_gradient, values, 1, 1)
        inner_sum = jnp.sum(weights * grad_weights, axis=1, keepdims=True)
        grad_scores = (weights * (grad_weights - inner_sum)).astype(BF16)
        grad_queries = (dot(grad_scores, keys) * score_scale).astype(BF16)
        for head in range(GROUP):
            at = (group * GROUP + head) * HEAD_SIZE
            grad_queries_ref[:, at : at + HEAD_SIZE] = grad_queries[
                head * rows : (head + 1) * rows
            ]
        partial_keyvals_ref[:, :, key_columns] = (
            (dot(grad_scores, queries, 0, 0) * score_scale)
            .astype(BF16)
            .reshape(8, rows, HEAD_SIZE)
        )
        partial_keyvals_ref[:, :, value_columns] = (
            dot(weights.astype(BF16), heads_gradient, 0, 0)
            .astype(BF16)
            .reshape(8, rows, HEAD_SIZE)
        )


def back(
    grad_back,
    slots,
    owner,
    gates,
    cotangent,
    residual1,
    partial,
    misc,
    outt,
    qkv,
    every,
    marks,
    segments,
):
    rows, features = cotangent.shape
    return pl.pallas_call(
        back_kernel,
        out_shape=[
            jax.ShapeDtypeStruct((rows, features), F32),
            jax.ShapeDtypeStruct((rows, features), BF16),
            jax.ShapeDtypeStruct((rows, 128), BF16),
            jax.ShapeDtypeStruct((8, features), F32),
            jax.ShapeDtypeStruct((rows, features), BF16),
            jax.ShapeDtypeStruct(every.shape, BF16),
        ],
        in_specs=[VMEM_SPEC] * 13,
        out_specs=[VMEM_SPEC] * 6,
        scratch_shapes=[pltpu.VMEM((rows, features), BF16)],
        compiler_params=pltpu.CompilerParams(vmem_limit_bytes=48 * 1024 * 1024),
        cost_estimate=pl.CostEstimate(
            flops=10_000_000_000, bytes_accessed=30_000_000, transcendentals=2_000_000
        ),
    )(
        grad_back,
        slots,
        owner,
        gates,
        cotangent,
        residual1,
        partial,
        misc,
        outt,
        qkv,
        every,
        marks,
        segments,
    )


def inverse_rms(residual):
    return lax.rsqrt(jnp.mean(residual * residual, axis=-1, keepdims=True) + EPSILON)


def contract(left_side, right_side, left_dim, right_dim):
    return lax.dot_general(
        left_side,
        right_side,
        (((left_dim,), (right_dim,)), ((), ())),
        preferred_element_type=F32,
    )


def gated_unit(gate_pre, up_pre):
    return jax.nn.silu(gate_pre) * up_pre


def norm_backward(residual, norm_scale, gain_row, grad_normed):
    weighted = grad_normed * gain_row
    inner_sum = jnp.mean(weighted * residual, axis=-1, keepdims=True)
    grad_residual = (
        norm_scale * weighted - residual * norm_scale * norm_scale * norm_scale * inner_sum
    )
    grad_gain = jnp.sum(grad_normed * residual * norm_scale, axis=0)
    return (grad_residual, grad_gain)


def to_experts(rows):
    return lax.all_to_all(rows, EXPERT_AXES, split_axis=0, concat_axis=0, tiled=True)


def shards(
    tokens,
    segments,
    routes,
    norm1_gain,
    w_query,
    key_value_weight,
    w_output,
    norm2_gain,
    w_router,
    w_shgate,
    w_shup,
    w_shdown,
    w_exgate,
    w_exup,
    w_exdown,
    cotangent,
):
    local_rows, feature_count = tokens.shape
    sequence_length = local_rows * 8
    shard = jnp.concatenate(
        [
            w_output.T,
            w_router,
            norm1_gain[:, None],
            norm2_gain[:, None],
            jnp.zeros((12, 62), BF16),
            w_query,
            key_value_weight,
            w_shgate,
            w_shup,
            w_shdown.T,
        ],
        axis=1,
    )
    shard = jnp.concatenate([shard, jnp.zeros((4, TOTAL), BF16)], axis=0)
    *dense, expert_w, expert_down = gather_weights(shard, w_exgate[0], w_exup[0], w_exdown[0])
    outt_w, misc_w, qkv_w, shgu_w, shdt_w = [
        gathered.reshape(feature_count, gathered.shape[-1]) for gathered in dense
    ]
    gain_first = misc_w[:, EXPERTS].astype(F32)

    expert_ids = jnp.arange(128, dtype=jnp.int32)
    named = jnp.any(routes[:, :, None] == expert_ids[None, None, :], axis=1)
    named_low = named.astype(BF16)
    token_ids = jnp.arange(local_rows, dtype=jnp.int32)
    before = (token_ids[None, :] <= token_ids[:, None]).astype(BF16)
    rank = jnp.dot(before, named_low, preferred_element_type=F32) * named.astype(F32)
    slot_count = EXPERTS * CAP
    slot_ids = jnp.arange(slot_count, dtype=jnp.int32)
    holder = slot_ids // CAP
    slot_expert = (holder // 8) * 8 + (holder % 2) * 4 + holder // 2 % 4
    owner = (slot_expert[:, None] == expert_ids[None, :]).astype(BF16)
    rank_wide = contract(rank.astype(BF16), owner, 1, 1)
    slots = (rank_wide == (slot_ids % CAP + 1).astype(F32)[None, :]).astype(BF16)
    slots_down = (
        contract(owner, rank.astype(BF16), 1, 1) == (slot_ids % CAP + 1).astype(F32)[:, None]
    ).astype(BF16)

    def dispatch(rows):
        return rows.reshape(EXPERTS, CAP, rows.shape[-1])

    sent_cotangent = dispatch(jnp.dot(slots_down, cotangent, preferred_element_type=F32).astype(BF16))
    sent_cotangent, qkv_w = lax.optimization_barrier((sent_cotangent, qkv_w))
    grad_received = to_experts(sent_cotangent).reshape(slot_count, feature_count)

    residual0 = tokens.astype(F32)
    scale_first = inverse_rms(residual0)
    first_normed = (residual0 * scale_first * gain_first).astype(BF16)
    qkv_rows = jnp.dot(first_normed, qkv_w, preferred_element_type=F32).astype(BF16)
    own_segments = segments.astype(F32)
    tail = 32
    first_length = jnp.sum((segments == 0).astype(F32)).astype(BF16)
    every, marks = to_later(
        qkv_rows[:, QUERY_HEADS * HEAD_SIZE :], jnp.broadcast_to(first_length, (tail, 128))
    )
    segment_tile = jnp.broadcast_to(own_segments[:, None], (local_rows, 128))
    attended_rows, residual1, second_normed, gates, outgoing = middle(
        qkv_rows,
        every,
        marks,
        segment_tile,
        tokens,
        outt_w,
        misc_w,
        named.astype(F32),
        slots_down,
        owner,
    )
    outgoing, grad_received = lax.optimization_barrier((outgoing, grad_received))
    arrived = to_experts(dispatch(outgoing)).reshape(slot_count, feature_count + EXTRA)

    shared_pre = jnp.dot(second_normed, shgu_w, preferred_element_type=F32)
    shared_gate, shared_up = shared_pre[:, :1024], shared_pre[:, 1024:]
    shared_hidden = gated_unit(shared_gate, shared_up).astype(BF16)
    shared_out = contract(shared_hidden, shdt_w, 1, 1)
    grad_shdt = contract(cotangent, shared_hidden, 0, 0).astype(BF16)
    grad_shared_hidden = jnp.dot(cotangent, shdt_w, preferred_element_type=F32)
    unused_shared, pull_shared = jax.vjp(gated_unit, shared_gate, shared_up)
    grad_shared_gate, grad_shared_up = pull_shared(grad_shared_hidden)
    grad_shared = jnp.concatenate(
        [grad_shared_gate.astype(BF16), grad_shared_up.astype(BF16)], axis=1
    )
    grad_shgu = contract(second_normed, grad_shared, 0, 0).astype(BF16)
    grad_second = contract(grad_shared, shgu_w, 1, 1)

    forward_rows = residual1 + shared_out
    arrived, grad_shdt, grad_shgu, grad_second, forward_rows = lax.optimization_barrier(
        (arrived, grad_shdt, grad_shgu, grad_second, forward_rows)
    )
    grad_rows, grads_pre, hidden, gated_hidden = expert(
        arrived, grad_received, expert_w, expert_down
    )
    grad_back = to_experts(dispatch(grad_rows)).reshape(slot_count, feature_count + EXTRA)
    half_out = jnp.dot(hidden, expert_down, preferred_element_type=F32).astype(BF16)
    received = arrived[:, :feature_count]
    own_in = contract(received, grads_pre[:, : 2 * HALF], 0, 0)
    other_in = contract(received, grads_pre[:, 2 * HALF :], 0, 0).astype(BF16)
    own_down = contract(gated_hidden[:, :HALF], grad_received, 0, 0)
    other_down = contract(gated_hidden[:, HALF:], grad_received, 0, 0).astype(BF16)
    grad_back, half_out, own_in, other_in, own_down, other_down = lax.optimization_barrier(
        (grad_back, half_out, own_in, other_in, own_down, other_down)
    )
    (
        grad_residual1,
        grad_attn_low,
        grad_logits,
        grad_gain_second,
        grad_queries,
        partial_keyvals,
    ) = back(
        grad_back,
        slots,
        owner,
        gates,
        cotangent,
        residual1,
        grad_second,
        misc_w,
        outt_w,
        qkv_rows,
        every,
        marks,
        segment_tile,
    )
    grad_gain_second = grad_gain_second[0]
    grad_router = contract(second_normed, grad_logits, 0, 0)
    grad_outt = contract(grad_attn_low, attended_rows, 0, 0).astype(BF16)
    grad_keyvals, their_in, their_down, returned = sum_earlier(
        partial_keyvals, tail, other_in, other_down, dispatch(half_out)
    )
    returned = returned.reshape(slot_count, feature_count)
    half_in = (own_in + their_in.astype(F32)).astype(BF16)
    half_down = (own_down + their_down.astype(F32)).astype(BF16)
    grad_qkv_rows = jnp.concatenate([grad_queries, grad_keyvals], axis=1)
    grad_qkv = contract(first_normed, grad_qkv_rows, 0, 0).astype(BF16)
    grad_first = contract(grad_qkv_rows, qkv_w, 1, 1)
    grad_norm_first, grad_gain_first = norm_backward(residual0, scale_first, gain_first, grad_first)
    grad_tokens = grad_residual1 + grad_norm_first
    grad_misc = jnp.concatenate(
        [
            grad_router[:, :EXPERTS],
            grad_gain_first[:, None],
            grad_gain_second[:, None],
            jnp.zeros((feature_count, 62), F32),
        ],
        axis=1,
    )
    slot_gates = slots.astype(F32) * jnp.dot(
        gates, owner.T.astype(F32), precision=lax.Precision.HIGHEST, preferred_element_type=F32
    )
    gates_high = lax.reduce_precision(slot_gates, exponent_bits=8, mantissa_bits=7)
    expert_mix = jnp.dot(
        gates_high.astype(BF16), returned, preferred_element_type=F32
    ) + jnp.dot((slot_gates - gates_high).astype(BF16), returned, preferred_element_type=F32)
    block_out = (forward_rows + expert_mix).astype(BF16)
    grad_misc, block_out = lax.optimization_barrier((grad_misc, block_out))
    *summed, half_in, half_down = sum_gradients(
        [
            grad.reshape(4, 2, 2, 2, 48, grad.shape[-1])
            for grad in (grad_outt, grad_misc, grad_qkv, grad_shgu, grad_shdt)
        ],
        [half_in, half_down],
    )
    sum_outt, sum_misc, sum_qkv, sum_shgu, sum_shdt = [piece[:12] for piece in summed]
    return (
        block_out,
        grad_tokens,
        sum_misc[:, EXPERTS],
        sum_qkv[:, :1536],
        sum_qkv[:, 1536:],
        sum_outt.T,
        sum_misc[:, EXPERTS + 1],
        sum_misc[:, :EXPERTS],
        sum_shgu[:, :1024],
        sum_shgu[:, 1024:],
        sum_shdt.T,
        half_in[None, :, :HALF].astype(F32),
        half_in[None, :, HALF:].astype(F32),
        half_down[None].astype(F32),
    )


def solution(mesh):
    fine = Mesh(mesh.devices.reshape(SIZES), AXES)
    rows = P(AXES, None)
    columns = P(None, AXES)
    flat = P(AXES)
    blocks = P(AXES, None, None)
    in_specs = (
        rows,
        flat,
        rows,
        flat,
        rows,
        rows,
        columns,
        flat,
        rows,
        rows,
        rows,
        columns,
        blocks,
        blocks,
        blocks,
        rows,
    )
    out_specs = (
        rows,
        rows,
        flat,
        rows,
        rows,
        columns,
        flat,
        rows,
        rows,
        rows,
        columns,
        blocks,
        blocks,
        blocks,
    )
    return jax.shard_map(shards, mesh=fine, in_specs=in_specs, out_specs=out_specs, check_vma=False)
```

time: 755 us -> 628 us (0.83)
  waiting for transfers between devices: 239 us -> 75.2 us
  Pallas kernels: 246 us -> 371 us
  matrix products: 155 us -> 70.6 us
  starting transfers between devices: 53.2 us -> 40.8 us
    ppermute x6 -> x0, waiting for transfers between devices: 148 us -> none  [swap_halves(): return lax.ppermute(block, 'xl', [(0, 1), (1, 0)])]
    pallas_call x2 -> x5, Pallas kernels: 65.8 us -> 209 us  [the longest x1 96.4 us: sum_earlier(): pl.pallas_call(functools.partial(earlier_kernel, tail), out_shape=[jax.Sh...]
    dot_general x25 -> x14, matrix products: 93.4 us -> 48.9 us  [contract(): lax.dot_general(left_side, right_side, (((left_dim,), (right_dim,)), ((),...]
    dot_general x20 -> x6, matrix products: 52.3 us -> 12.3 us  [the longest x1 4.66 us: shards(): jnp.dot(hidden, expert_down, preferred_element_type=F32).astype(BF16)]
    pallas_call x1, Pallas kernels: 95.9 us -> 80 us  [gather_weights(): pl.pallas_call(gather_kernel, out_shape=shapes, in_specs=[pl.BlockSpec(me...]
    all_to_all x4 -> x3, waiting for transfers between devices: 90.9 us -> 75.2 us  [to_experts(): lax.all_to_all(rows, EXPERT_AXES, split_axis=0, concat_axis=0, tiled=True)]
    unnamed x138 -> x134, local copies, waits for them, and re-layouts: 16.8 us -> 26.7 us
    convert_element_type x5 -> x7, other arithmetic: 1.49 us -> 9.39 us  [the longest x1 3.37 us: shards(): half_in[None, :, HALF:].astype(F32)]
  transfers between devices with their start and end apart: 10 -> 3, of which waited for: 8 -> 2; matrix products, arithmetic and copies ran while one was open for 13% -> 9% of each run, Pallas kernels for 0% -> 13%
where the time goes in v2:
time: 628 us; the launch traced here: 616 us
  Pallas kernels  371 us (59%)
  waiting for transfers between devices  75.2 us (12%)
  matrix products  70.6 us (11%)
  local copies, waits for them, and re-layouts  43.3 us (7%)
  starting transfers between devices  40.8 us (6%)
  other arithmetic  13.6 us (2%)
    pallas_call x1, Pallas kernels, sum_earlier(): pl.pallas_call(functools.partial(earlier_kernel, tail), out_shape=[jax.Sh...  96.4 us
    pallas_call x1, Pallas kernels, sum_gradients(): pl.pallas_call(sum_kernel, out_shape=[jax.ShapeDtypeStruct((16, width), F...  82.1 us
    pallas_call x1, Pallas kernels, gather_weights(): pl.pallas_call(gather_kernel, out_shape=shapes, in_specs=[pl.BlockSpec(me...  80 us
    all_to_all x3, waiting for transfers between devices, to_experts(): lax.all_to_all(rows, EXPERT_AXES, split_axis=0, concat_axis=0, tiled=True)  75.2 us
    pallas_call x1, Pallas kernels, to_later(): pl.pallas_call(later_kernel, out_shape=[jax.ShapeDtypeStruct((8,) + rows....  67.2 us
    dot_general x14, matrix products, contract(): lax.dot_general(left_side, right_side, (((left_dim,), (right_dim,)), ((),...  48.9 us
    all_to_all x3, starting transfers between devices, to_experts(): lax.all_to_all(rows, EXPERT_AXES, split_axis=0, concat_axis=0, tiled=True)  40.8 us
    unnamed x134, local copies, waits for them, and re-layouts  26.7 us
  transfers between devices with their start and end apart: 3, of which 2 were waited for; matrix products, arithmetic and copies ran while one was open for 9% of the time, Pallas kernels for 13%

profile of v2, /device:TPU:3, one launch (start us, length us, event | category | flops | bytes accessed | tf_op | source)
XLA Modules:
  0.0 616.3 jit_solution(7069479791433494794)
XLA Ops:
  6.3 3.5 convolution_convert_fusion.4
  9.8 80.0 %shard_map.263 = (bf16[4,2,2,2,48,1536]{5,4,3,2,1,0:T(8,128)(2,1)S(1)}, bf16[4,2,2,2,48,128]{5,4,3,2,1,0:T(8,128)(2,1)S(1)}, bf16[4,2,2,2,48,2560]{5,4,3,2,1,0:T...) custom-call(bf16[16,7296]{1,0:T(8,128)(2,1)S(1)} %concatenate.16.sha, ...), custom_call_target="tpu_custom_call" | custom-call | bytes 200000000 | tf_op jit(solution)/shard_map/pallas_call | solution.py:359
  102.4 11.3 %all-to-all-start = ((bf16[64,24,1536]{2,1,0:T(8,128)(2,1)}), bf16[64,24,1536]{2,1,0:T(8,128)(2,1)}, u32[]{:S(2)}, u32[]{:S(2)}) async-start(bf16[64,24,1536]{2,1,0:T(8,128)(2,1)} %bitcast.99), calls=%async_computation | async-start | bytes 9437184 | tf_op jit(solution)/shard_map/all_to_all | solution.py:1364
  114.2 4.6 convolution_convert_fusion.6.qkv_ref
  120.1 67.2 %shard_map.264 = (bf16[8,128,1024]{2,1,0:T(8,128)(2,1)S(1)}, bf16[32,128]{1,0:T(8,128)(2,1)S(1)}) custom-call(bf16[128,1024]{1,0:T(8,128)(2,1)S(1)} %slice.100.own_ref, bf16[32,128]{1,0:T(8,128)(2,1)S(1)} %broadcast_in_dim.17.marks_ref), custom_call_target="tpu_custom_call" | custom-call | bytes 70000000 | tf_op jit(solution)/shard_map/pallas_call | solution.py:828
  187.7 12.9 %shard_map.265 = (bf16[128,1536]{1,0:T(8,128)(2,1)S(1)}, f32[128,1536]{1,0:T(8,128)S(1)}, bf16[128,1536]{1,0:T(8,128)(2,1)S(1)}, f32[128,128]{1,0:T(8,128)S(1)}, bf16[1536,1664]{1,0:T(8,128)(2,1)}) custom-call(bf16[128,2560]{1,0:T(8,128)(2,1)S(1)} %convolution_convert_fusion.6.qkv_ref, bf16[8,128,1024]{2,1,0:T(8,128)(2,1)S(1)} %get-tuple-element.69.every_ref, ...), custom_call_target="tpu_custom_call" | custom-call | flops 6000000000 | bytes 20000000 | tf_op jit(solution)/shard_map/pallas_call | solution.py:1105
  202.7 14.6 %all-to-all-start.1 = ((bf16[64,24,1664]{2,1,0:T(8,128)(2,1)}), bf16[64,24,1664]{2,1,0:T(8,128)(2,1)}, u32[]{:S(2)}, u32[]{:S(2)}) async-start(bf16[64,24,1664]{2,1,0:T(8,128)(2,1)} %bitcast.102), calls=%async_computation.1 | async-start | bytes 10223616 | tf_op jit(solution)/shard_map/all_to_all | solution.py:1364
  217.3 3.9 fusion.67
  226.8 4.5 convolution_convert_fusion.2
  234.4 45.8 %all-to-all-done.1 = bf16[64,24,1664]{2,1,0:T(8,128)(2,1)} async-done(((bf16[64,24,1664]{2,1,0:T(8,128)(2,1)}), bf16[64,24,1664]{2,1,0:T(8,128)(2,1)}, u32[]{:S(2)}, u32[]{:S(2)}) %all-to-all-start.1) | async-done | bytes 5111840 | tf_op jit(solution)/shard_map/all_to_all | solution.py:1364
  280.2 18.1 %shard_map.266 = (bf16[1536,1664]{1,0:T(8,128)(2,1)}, bf16[1536,1024]{1,0:T(8,128)(2,1)}, bf16[1536,512]{1,0:T(8,128)(2,1)S(1)}, bf16[1536,512]{1,0:T(8,128)(2,1)S(1)}) custom-call(bf16[1536,1664]{1,0:T(8,128)(2,1)} %bitcast.13.arrived_ref, bf16[1536,1536]{1,0:T(8,128)(2,1)} %bitcast.11.cotangent_ref, bf16[1536,1024]{1,0:T(8,128)(2,1)} %copy-done.29, ...), custom_call_target="tpu_custom_call" | custom-call | flops 12000000000 | bytes 25000000 | tf_op jit(solution)/shard_map/pallas_call | solution.py:1165
  300.6 14.9 %all-to-all-start.2 = ((bf16[64,24,1664]{2,1,0:T(8,128)(2,1)}), bf16[64,24,1664]{2,1,0:T(8,128)(2,1)}, u32[]{:S(2)}, u32[]{:S(2)}) async-start(bf16[64,24,1664]{2,1,0:T(8,128)(2,1)} %bitcast.103), calls=%async_computation.2 | async-start | bytes 10223616 | tf_op jit(solution)/shard_map/all_to_all | solution.py:1364
  318.1 4.7 copy.46
  322.8 5.0 convolution_convert_fusion.7.down_ref
  327.8 5.0 fusion.27
  332.8 4.7 convolution_convert_fusion.1
  337.5 6.7 %fusion.2 = f32[1536,512]{1,0:T(8,128)} fusion(bf16[1536,1664]{1,0:T(8,128)(2,1)} %bitcast.13.arrived_ref, bf16[1536,1024]{1,0:T(8,128)(2,1)S(1)} %copy-done.59), kind=kOutput, calls=%fused_computation.7 | convolution fusion | flops 2415919104 | bytes 9437184 | tf_op jit(solution)/shard_map/dot_general | solution.py:1341
  344.1 5.0 fusion.5.in_ref
  349.1 29.4 %all-to-all-done.2 = bf16[64,24,1664]{2,1,0:T(8,128)(2,1)} async-done(((bf16[64,24,1664]{2,1,0:T(8,128)(2,1)}), bf16[64,24,1664]{2,1,0:T(8,128)(2,1)}, u32[]{:S(2)}, u32[]{:S(2)}) %all-to-all-start.2) | async-done | bytes 5111840 | tf_op jit(solution)/shard_map/all_to_all | solution.py:1364
  384.2 14.8 %shard_map.267 = (f32[128,1536]{1,0:T(8,128)S(1)}, bf16[128,1536]{1,0:T(8,128)(2,1)S(1)}, bf16[128,128]{1,0:T(8,128)(2,1)S(1)}, f32[8,1536]{1,0:T(8,128)S(1)}, b...) custom-call(bf16[1536,1664]{1,0:T(8,128)(2,1)} %bitcast.19.grad_back_ref, bf16[128,1536]{1,0:T(8,128)(2,1)S(1)} %copy-done.23, ...), custom_call_target="tpu_custom_call" | custom-call | flops 10000000000 | bytes 30000000 | tf_op jit(solution)/shard_map/pallas_call | solution.py:1302
  401.0 96.4 %shard_map.268 = (bf16[128,1024]{1,0:T(8,128)(2,1)S(1)}, bf16[1536,512]{1,0:T(8,128)(2,1)S(1)}, bf16[256,1536]{1,0:T(8,128)(2,1)S(1)}, bf16[64,24,1536]{2,1,0:T(8,128)(2,1)S(1)}) custom-call(bf16[8,128,1024]{2,1,0:T(8,128)(2,1)S(1)} %copy-done.5, bf16[1536,512]{1,0:T(8,128)(2,1)S(1)} %fusion.5.in_ref, bf16[256,1536]{1,0:T(8,128)(2,1)S(1)} %copy-done.14, ...), custom_call_target="tpu_custom_call" | custom-call | bytes 70000000 | tf_op jit(solution)/shard_map/pallas_call | solution.py:946
  498.6 5.4 convolution_convert_fusion
  518.1 3.6 convolution_convert_fusion.3
  521.7 82.1 %shard_map.269 = (f32[16,1536]{1,0:T(8,128)}, f32[16,128]{1,0:T(8,128)}, f32[16,2560]{1,0:T(8,128)}, f32[16,2048]{1,0:T(8,128)}, f32[16,1024]{1,0:T(8,128)}, /*i...) custom-call(bf16[4,2,2,2,48,1536]{5,4,3,2,1,0:T(8,128)(2,1)} %bitcast.100, f32[4,2,2,2,48,128]{5,4,3,2,1,0:T(8,128)} %bitcast.104, ...), custom_call_target="tpu_custom_call" | custom-call | tf_op jit(solution)/shard_map/pallas_call | solution.py:737
  (186 shorter events, 71.1 us)
Async XLA Ops:
  0.7 9.1 %copy-start.52 = (f32[1536]{0:T(1024)}, f32[1536]{0:T(1024)S(1)}, u32[]{:S(2)}) copy-start(f32[1536]{0:T(1024)S(1)} %get-tuple-element.133) | copy-start | bytes 18436
  0.7 186.6 %copy-start.45 = (s32[1536]{0:T(1024)}, s32[1536]{0:T(1024)S(1)}, u32[]{:S(2)}) copy-start(s32[1536]{0:T(1024)S(1)} %get-tuple-element.132) | copy-start | bytes 18436
  1.8 8.1 %copy-start.57 = (bf16[128,128]{1,0:T(8,128)(2,1)}, bf16[128,128]{1,0:T(8,128)(2,1)S(1)}, u32[]{:S(2)}) copy-start(bf16[128,128]{1,0:T(8,128)(2,1)S(1)} %fusion.13) | copy-start | bytes 98308
  102.3 85.3 %copy-start.24 = (bf16[4,2,2,2,48,128]{5,4,3,2,1,0:T(8,128)(2,1)}, bf16[4,2,2,2,48,128]{5,4,3,2,1,0:T(8,128)(2,1)S(1)}, u32[]{:S(2)}) copy-start(bf16[4,2,2,2,48,128]{5,4,3,2,1,0:T(8,128)(2,1)S(1)} %get-tuple-element.66) | copy-start | bytes 1179652
  102.3 11.7 %copy-start.2 = (bf16[128,1536]{1,0:T(8,128)(2,1)S(1)}, bf16[128,1536]{1,0:T(8,128)(2,1)}, u32[]{:S(2)}) copy-start(bf16[128,1536]{1,0:T(8,128)(2,1)} %tokens_ref.1) | copy-start | bytes 1179652
  102.4 100.3 %all-to-all-start = ((bf16[64,24,1536]{2,1,0:T(8,128)(2,1)}), bf16[64,24,1536]{2,1,0:T(8,128)(2,1)}, u32[]{:S(2)}, u32[]{:S(2)}) async-start(bf16[64,24,1536]{2,1,0:T(8,128)(2,1)} %bitcast.99), calls=%async_computation | async-start | bytes 9437184 | tf_op jit(solution)/shard_map/all_to_all | solution.py:1364
  114.2 73.4 %copy-start.36 = (bf16[1536,128]{1,0:T(8,128)(2,1)S(1)}, bf16[1536,128]{1,0:T(8,128)(2,1)}, u32[]{:S(2)}) copy-start(bf16[1536,128]{1,0:T(8,128)(2,1)} %get-tuple-element.129.slots_ref) | copy-start | bytes 1179652
  187.6 13.0 %copy-start.26 = (bf16[1536,128]{1,0:T(8,128)(2,1)}, bf16[1536,128]{1,0:T(8,128)(2,1)S(1)}, u32[]{:S(2)}) copy-start(bf16[1536,128]{1,0:T(8,128)(2,1)S(1)} %fusion.29.owner_ref) | copy-start | bytes 1179652
  202.7 22.1 %copy-start.11 = (f32[128,1536]{1,0:T(8,128)}, f32[128,1536]{1,0:T(8,128)S(1)}, u32[]{:S(2)}) copy-start(f32[128,1536]{1,0:T(8,128)S(1)} %get-tuple-element.78.residual_ref) | copy-start | bytes 2359300
  202.7 77.5 %all-to-all-start.1 = ((bf16[64,24,1664]{2,1,0:T(8,128)(2,1)}), bf16[64,24,1664]{2,1,0:T(8,128)(2,1)}, u32[]{:S(2)}, u32[]{:S(2)}) async-start(bf16[64,24,1664]{2,1,0:T(8,128)(2,1)} %bitcast.102), calls=%async_computation.1 | async-start | bytes 10223616 | tf_op jit(solution)/shard_map/all_to_all | solution.py:1364
  231.3 48.9 %copy-start.32 = (bf16[512,1536]{1,0:T(8,128)(2,1)S(1)}, bf16[512,1536]{1,0:T(8,128)(2,1)}, u32[]{:S(2)}) copy-start(bf16[512,1536]{1,0:T(8,128)(2,1)} %copy-done.31) | copy-start | bytes 4718596
  300.6 15.5 %copy-start.46 = (s32[1536]{0:T(1024)S(1)}, s32[1536]{0:T(1024)}, u32[]{:S(2)}) copy-start(s32[1536]{0:T(1024)} %copy-done.45) | copy-start | bytes 18436
  300.6 15.5 %copy-start.53 = (f32[1536]{0:T(1024)S(1)}, f32[1536]{0:T(1024)}, u32[]{:S(2)}) copy-start(f32[1536]{0:T(1024)} %copy-done.52) | copy-start | bytes 18436
  300.6 15.5 %copy-start.58 = (bf16[128,128]{1,0:T(8,128)(2,1)S(1)}, bf16[128,128]{1,0:T(8,128)(2,1)}, u32[]{:S(2)}) copy-start(bf16[128,128]{1,0:T(8,128)(2,1)} %copy-done.57) | copy-start | bytes 98308
  300.6 78.0 %all-to-all-start.2 = ((bf16[64,24,1664]{2,1,0:T(8,128)(2,1)}), bf16[64,24,1664]{2,1,0:T(8,128)(2,1)}, u32[]{:S(2)}, u32[]{:S(2)}) async-start(bf16[64,24,1664]{2,1,0:T(8,128)(2,1)} %bitcast.103), calls=%async_computation.2 | async-start | bytes 10223616 | tf_op jit(solution)/shard_map/all_to_all | solution.py:1364
  378.5 20.5 %slice-start.4 = ((s8[4718592]{0:T(1024)(128)(4,1)}), s8[4194304]{0:T(1024)(128)(4,1)S(1)}, s32[]{:S(2)}) async-start(s8[4718592]{0:T(1024)(128)(4,1)} %bitcast.84), calls=%async_computation.7 | async-start | bytes 8388608
  384.1 14.8 %slice-start.5 = ((s8[4718592]{0:T(1024)(128)(4,1)}), s8[524288]{0:T(1024)(128)(4,1)S(1)}, s32[]{:S(2)}) async-start(s8[4718592]{0:T(1024)(128)(4,1)} %bitcast.84), calls=%async_computation.8 | async-start | bytes 1048576
  384.1 14.9 %copy-start.14 = (bf16[256,1536]{1,0:T(8,128)(2,1)S(1)}, bf16[256,1536]{1,0:T(8,128)(2,1)}, u32[]{:S(2)}) copy-start(bf16[256,1536]{1,0:T(8,128)(2,1)} %convolution_convert_fusion.7.down_ref) | copy-start | bytes 2359300
  398.9 98.4 %copy-start.9 = (bf16[128,1536]{1,0:T(8,128)(2,1)}, bf16[128,1536]{1,0:T(8,128)(2,1)S(1)}, u32[]{:S(2)}) copy-start(bf16[128,1536]{1,0:T(8,128)(2,1)S(1)} %get-tuple-element.102) | copy-start | bytes 1179652
  398.9 98.4 %copy-start.18 = (f32[128,1536]{1,0:T(8,128)}, f32[128,1536]{1,0:T(8,128)S(1)}, u32[]{:S(2)}) copy-start(f32[128,1536]{1,0:T(8,128)S(1)} %get-tuple-element.101) | copy-start | bytes 2359300
  401.0 97.6 %copy-start.50 = (f32[128]{0:T(128)S(1)}, f32[128]{0:T(128)}, u32[]{:S(2)}) copy-start(f32[128]{0:T(128)} %copy-done.49) | copy-start | bytes 1540
  401.0 103.0 %slice-start = ((s8[7864320]{0:T(1024)(128)(4,1)}), s8[4194304]{0:T(1024)(128)(4,1)S(1)}, s32[]{:S(2)}) async-start(s8[7864320]{0:T(1024)(128)(4,1)} %bitcast.75), calls=%async_computation.3 | async-start | bytes 8388608
  606.9 7.4 %copy-start.55 = (f32[128]{0:T(128)S(1)}, f32[128]{0:T(128)}, u32[]{:S(2)}) copy-start(f32[128]{0:T(128)} %get-tuple-element.118) | copy-start | bytes 1540
  606.9 7.4 %copy-start.19 = (f32[128,1536]{1,0:T(8,128)S(1)}, f32[128,1536]{1,0:T(8,128)}, u32[]{:S(2)}) copy-start(f32[128,1536]{1,0:T(8,128)} %copy-done.18) | copy-start | bytes 2359300
  (45 other events, 152.6 us)

commit v3 on v2

v3 whole, which is shorter than its diff:
```python
import functools

import jax
import jax.numpy as jnp
from jax import lax
from jax.experimental import pallas as pl
from jax.experimental.pallas import tpu as pltpu
from jax.sharding import Mesh
from jax.sharding import PartitionSpec as P

QUERY_HEADS = 12
KEY_VALUE_HEADS = 4
HEAD_SIZE = 128
EXPERTS = 64
TOPK = 6
CAP = 24
EPSILON = 1e-05

F32 = jnp.float32
BF16 = jnp.bfloat16
MESH_ID = pl.DeviceIdType.MESH
AXES = ("z", "yl", "core", "yh", "xh", "xl")
SIZES = (4, 2, 2, 2, 2, 2)
EXPERT_AXES = ("z", "yl", "yh", "xh", "xl")
COL_AXES = ("yh", "xh", "xl")

PARTS = (
    ("outt", 1536, "yzx", "zy"),
    ("misc", 128, "yz", "yz"),
    ("q", 1536, "yz", "yz"),
    ("kv", 1024, "zy", "yz"),
    ("shg", 1024, "yz", "yz"),
    ("shu", 1024, "zy", "zy"),
    ("shdt", 1024, "zy", "yz"),
)
GATHERED = tuple((name, width, order) for name, width, order, _ in PARTS)
SUMMED = tuple((name, width, order) for name, width, _, order in PARTS)
TOTAL = sum(part[1] for part in PARTS)
HALF = 256
EXPERT_SEM = 200
TOTAL = sum(part[1] for part in PARTS)


def rem(value, size):
    return lax.rem(value, jnp.int32(size))


def place():
    at = {name: lax.axis_index(name) for name in AXES}
    return {
        "x": at["xh"] * 2 + at["xl"],
        "y": at["yh"] * 2 + at["yl"],
        "z": at["z"],
        "core": at["core"],
    }


def device(axis, value):
    if axis == "x":
        return {"xh": value // 2, "xl": rem(value, 2)}
    if axis == "y":
        return {"yh": value // 2, "yl": rem(value, 2)}
    return {axis: value}


def greet(targets):
    barrier = pltpu.get_barrier_semaphore()
    for target in targets:
        pl.semaphore_signal(barrier, inc=1, device_id=target, device_id_type=MESH_ID)
    pl.semaphore_wait(barrier, len(targets))


def ring_neighbours(me):
    near = [device("x", rem(me["x"] + hops, 4)) for hops in (1, 2, 3)]
    near += [device("y", rem(me["y"] + hops, 4)) for hops in (1, 3)]
    near += [device("z", rem(me["z"] + hops, 4)) for hops in (1, 3)]
    return near + [{"core": 1 - me["core"]}]


class Wires:
    def __init__(self, send_sems, recv_sems, local_sems):
        self.send, self.recv, self.local = send_sems, recv_sems, local_sems
        self.used, self.used_local, self.started, self.kept = 0, 0, [], []

    def remote(self, source, target, where):
        copy = pltpu.make_async_remote_copy(
            src_ref=source,
            dst_ref=target,
            send_sem=self.send.at[self.used],
            recv_sem=self.recv.at[self.used],
            device_id=where,
            device_id_type=MESH_ID,
        )
        self.used += 1
        copy.start()
        self.started.append(copy)
        return copy

    def copy(self, source, target):
        copy = pltpu.make_async_copy(source, target, self.local.at[self.used_local])
        self.used_local += 1
        copy.start()
        return copy

    def finish(self):
        for copy in self.started:
            copy.wait_send()


def balanced_offsets():
    left = [(x, y, z) for x in range(4) for y in range(4) for z in range(4) if x + y + z > 0]
    load, order = [0] * 6, []

    def uses(offset):
        used = [0] * 6
        for axis, hops in enumerate(offset):
            used[2 * axis] += hops in (1, 2)
            used[2 * axis + 1] += hops in (2, 3)
        return used

    def cost(offset):
        used = uses(offset)
        after = [a + b for a, b in zip(load, used)]
        mean = sum(after) / 6
        return (max(after), sum((a - mean) ** 2 for a in after), -sum(used))

    while left:
        best = min(left, key=cost)
        load = [a + b for a, b in zip(load, uses(best))]
        left.remove(best)
        order.append(best)
    return order


OFFSETS = balanced_offsets()


def chip_at(me, offset, sign=1):
    x, y, z = [rem(me[axis] + (sign * hops) % 4, 4) for axis, hops in zip("xyz", offset)]
    where = {"z": z, "yh": y // 2, "yl": rem(y, 2), "xh": x // 2, "xl": rem(x, 2)}
    return where, z * 16 + rem(y, 2) * 8 + (y // 2) * 4 + x


def halves(width):
    first = width // 256 * 128 if width > 128 else width
    return first, width - first


def spread_rows(shape, swap):
    dense = lax.broadcasted_iota(jnp.int32, shape, 1 if swap else 0)
    padded = lax.broadcasted_iota(jnp.int32, shape, 0 if swap else 1)
    shift = jnp.zeros(shape, jnp.int32)
    for edge in (12, 24, 36):
        shift = shift + jnp.where(dense >= edge, 4, 0)
    return dense + shift == padded


def block_ref(ref, axes, me, axis, value, columns):
    spot = dict(me)
    spot[axis] = value
    z = slice(None) if "z" in axes else spot["z"]
    yl = slice(None) if "y" in axes else rem(spot["y"], 2)
    yh = slice(None) if "y" in axes else spot["y"] // 2
    return ref.at[z, yl, me["core"], yh, :, columns]


def gather_kernel(shard_ref, gate_ref, up_ref, down_ref, *rest):
    count = len(GATHERED)
    outs = rest[:count]
    expert_in, expert_out, landed = rest[count : count + 3]
    stages = rest[count + 3 : 2 * count + 3]
    send_sems, recv_sems, local_sems = rest[2 * count + 3 :]
    me = place()
    nxt = {axis: rem(me[axis] + 1, 4) for axis in "xyz"}
    opp = {axis: rem(me[axis] + 2, 4) for axis in "xyz"}
    prv = {axis: rem(me[axis] + 3, 4) for axis in "xyz"}
    sibling = {"core": 1 - me["core"]}
    partner = {"core": 1 - me["core"], "xl": 1 - lax.axis_index("xl")}
    crossed = me["core"] != lax.axis_index("xl")
    greet(
        [device("x", nxt["x"]), device("x", opp["x"]), device("x", prv["x"])]
        + [device("y", nxt["y"]), device("y", prv["y"])]
        + [device("z", nxt["z"]), device("z", prv["z"]), sibling, partner]
    )
    wires = Wires(send_sems, recv_sems, local_sems)
    runs, start = [], 0
    for index, (name, width, order) in enumerate(GATHERED):
        last_x = len(order) == 3
        quarter = width // 4 if last_x else width
        run = {
            "out": outs[index],
            "order": order,
            "width": quarter,
            "done": "",
            "stage": stages[index],
            "start": start,
            "landed": landed.at[:, :, pl.ds(start, quarter)],
            "base": me["x"] * quarter if last_x else 0,
            "first": [],
            "shared": [],
        }

        def piece(x):
            if last_x:
                return shard_ref.at[:, pl.ds(pl.multiple_of(start + x * quarter, 128), quarter)]
            return shard_ref.at[:, pl.ds(start, quarter)]

        for where in (nxt, prv, opp):
            run["first"].append(
                wires.remote(piece(where["x"]), run["landed"].at[me["x"]], device("x", where["x"]))
            )
        run["bring"] = wires.copy(piece(me["x"]), run["landed"].at[me["x"]])
        runs.append(run)
        start += width

    whole = [
        (gate_ref, expert_in.at[:, pl.ds(0, HALF)]),
        (up_ref, expert_in.at[:, pl.ds(HALF, HALF)]),
        (down_ref, expert_out.at[pl.ds(0, HALF)]),
    ]

    def moved(slot):
        source, target = whole[slot]
        return pltpu.make_async_remote_copy(
            src_ref=source,
            dst_ref=target,
            send_sem=send_sems.at[EXPERT_SEM + slot],
            recv_sem=recv_sems.at[EXPERT_SEM + slot],
            device_id=partner,
            device_id_type=MESH_ID,
        )

    def kept(slot):
        source, target = whole[slot]
        return pltpu.make_async_copy(source, target, local_sems.at[20 + slot])

    @pl.when(crossed)
    def _():
        for slot in range(3):
            moved(slot).start()

    @pl.when(jnp.logical_not(crossed))
    def _():
        for slot in range(3):
            kept(slot).start()

    def part_columns(run, axis, value, which):
        base = value * run["width"] if axis == "x" else run["base"]
        left, size = 0, run["width"]
        if which is not None:
            first_half, second_half = halves(run["width"])
            left, size = (0, first_half) if which == 0 else (first_half, second_half)
        if isinstance(base, int):
            return pl.ds(base + left, size)
        return pl.ds(pl.multiple_of(base + left, 128), size)

    def blocks(run, axis, value, which=None):
        columns = part_columns(run, axis, value, which)
        return block_ref(run["out"], run["done"], me, axis, value, columns)

    def begin(run, axis, source=None):
        target = blocks(run, axis, me[axis])
        source = target if source is None else source
        run["forth"] = wires.remote(source, target, device(axis, nxt[axis]))
        run["back"] = wires.remote(source, target, device(axis, prv[axis]))

    pick = spread_rows((48, 64), False).astype(BF16)
    for run in runs:
        run["bring"].wait()
        for copy in run["first"]:
            copy.wait_recv()
        for left in range(0, run["width"], 512):
            size = min(512, run["width"] - left)
            left_in = run["start"] + left
            piece_rows = landed[:, :, left_in : left_in + size].reshape(64, size)
            run["stage"][:, left : left + size] = jnp.dot(
                pick, piece_rows, preferred_element_type=F32
            ).astype(BF16)
        axis = run["order"][0]
        begin(run, axis, run["stage"])
        run["own"] = wires.copy(run["stage"], blocks(run, axis, me[axis]))

    def forward(run, axis):
        run["forth"].wait_recv()
        source = blocks(run, axis, prv[axis], 0)
        run["more"] = [wires.remote(source, source, device(axis, nxt[axis]))]
        run["back"].wait_recv()
        if halves(run["width"])[1] > 0:
            source = blocks(run, axis, nxt[axis], 1)
            run["more"].append(wires.remote(source, source, device(axis, prv[axis])))

    def share(run, axis, value):
        source = blocks(run, axis, value)
        run["shared"].append(wires.remote(source, source, sibling))

    def advance(run, step):
        axis = run["order"][step]
        for copy in run["more"]:
            copy.wait_recv()
        if step == len(run["order"]) - 1:
            share(run, axis, opp[axis])
            return
        if step == 0:
            run["own"].wait()
        run["done"] = run["done"] + axis
        following = run["order"][step + 1]
        begin(run, following)
        if step + 1 == len(run["order"]) - 1:
            share(run, following, me[following])

    def last_forward(run):
        axis = run["order"][-1]
        forward(run, axis)
        share(run, axis, prv[axis])
        share(run, axis, nxt[axis])

    threes = [run for run in runs if len(run["order"]) == 3]
    twos = [run for run in runs if len(run["order"]) == 2]
    for run in runs:
        forward(run, run["order"][0])
    for run in runs:
        advance(run, 0)
    for run in threes:
        forward(run, run["order"][1])
    for run in threes:
        advance(run, 1)
    for run in twos:
        last_forward(run)
    for run in threes:
        last_forward(run)

    @pl.when(crossed)
    def _():
        for slot in range(3):
            moved(slot).wait_recv()

    @pl.when(jnp.logical_not(crossed))
    def _():
        for slot in range(3):
            kept(slot).wait()

    handed = [
        wires.remote(
            expert_in.at[:, pl.ds(0, 2 * HALF)], expert_in.at[:, pl.ds(2 * HALF, 2 * HALF)], sibling
        ),
        wires.remote(expert_out.at[pl.ds(0, HALF)], expert_out.at[pl.ds(HALF, HALF)], sibling),
    ]
    for run in twos + threes:
        advance(run, len(run["order"]) - 1)
    for run in runs:
        for copy in run["shared"]:
            copy.wait_recv()
    for copy in handed:
        copy.wait_recv()
    wires.finish()

    @pl.when(crossed)
    def _():
        for slot in range(3):
            moved(slot).wait_send()


def gather_weights(shard, gate_w, up_w, down_w):
    shapes = [jax.ShapeDtypeStruct((4, 2, 2, 2, 48, width), BF16) for _, width, _ in GATHERED]
    shapes += [
        jax.ShapeDtypeStruct((gate_w.shape[0], 4 * HALF), BF16),
        jax.ShapeDtypeStruct((2 * HALF, down_w.shape[1]), BF16),
    ]
    anywhere = pl.BlockSpec(memory_space=pl.ANY)
    return pl.pallas_call(
        gather_kernel,
        out_shape=shapes,
        in_specs=[pl.BlockSpec(memory_space=pltpu.VMEM)] + [anywhere] * 3,
        out_specs=[anywhere] * (len(GATHERED) + 2),
        scratch_shapes=[pltpu.VMEM((4, 16, TOTAL), BF16)]
        + [
            pltpu.VMEM((48, width // 4 if len(order) == 3 else width), BF16)
            for _, width, order in GATHERED
        ]
        + [
            pltpu.SemaphoreType.DMA((EXPERT_SEM + 4,)),
            pltpu.SemaphoreType.DMA((EXPERT_SEM + 4,)),
            pltpu.SemaphoreType.DMA((24,)),
        ],
        compiler_params=pltpu.CompilerParams(
            collective_id=0, has_side_effects=True, vmem_limit_bytes=16 * 1024 * 1024
        ),
        cost_estimate=pl.CostEstimate(flops=0, bytes_accessed=200_000_000, transcendentals=0),
    )(shard, gate_w, up_w, down_w)


class Summing:
    def __init__(self, wires, me, parts, grads, outs, scratch):
        self.wires, self.me = wires, me
        self.next = {axis: rem(me[axis] + 1, 4) for axis in "xyz"}
        self.opposite = {axis: rem(me[axis] + 2, 4) for axis in "xyz"}
        self.previous = {axis: rem(me[axis] + 3, 4) for axis in "xyz"}
        self.sibling = {"core": 1 - me["core"]}
        count = len(parts)
        self.runs = []
        for index, (name, width, order) in enumerate(parts):
            self.runs.append(
                {
                    "order": order[::-1],
                    "width": width // 4 if len(order) == 3 else width,
                    "left": "zy",
                    "turn": 0,
                    "grads": grads[index],
                    "out": outs[index],
                    "own": scratch[index],
                    "theirs": scratch[count + index],
                    "near1": scratch[2 * count + index],
                    "near2": scratch[3 * count + index],
                    "ends": scratch[4 * count + index],
                    "arrived": scratch[5 * count + index],
                }
            )

    def spot(self, left_axes, axis, value, with_core):
        at = dict(self.me)
        if axis is not None:
            at[axis] = value
        whole = [name for name in left_axes if name != axis]
        z = slice(None) if "z" in whole else at["z"]
        yl = slice(None) if "y" in whole else rem(at["y"], 2)
        yh = slice(None) if "y" in whole else at["y"] // 2
        return (z, yl) + (() if with_core is None else (with_core,)) + (yh,)

    def lead(self, left_axes, axis):
        dims = []
        for name in ("z", "y"):
            if name in left_axes and name != axis:
                dims += [4] if name == "z" else [2, 2]
        return dims

    def add_into(self, target, sources, dims):
        total = 1
        for size in dims:
            total *= size

        def body(index):
            for row in range(0, 48, 16):
                at = index + (pl.ds(row, 16),)
                value = target[at].astype(F32)
                for source in sources:
                    value = value + source[at].astype(F32)
                target[at] = value.astype(target.dtype)

        def step(flat, carry):
            index, rest_flat = [], flat
            for size in reversed(dims):
                index.append(rem(rest_flat, size))
                rest_flat = rest_flat // size
            body(tuple(reversed(index)))
            return carry

        if total == 1:
            body(())
        else:
            lax.fori_loop(0, total, step, 0)

    def columns_of(self, run, axis, value, which):
        base = 0
        if len(run["order"]) == 3:
            base = (value if axis == "x" else self.me["x"]) * run["width"]
        left, size = 0, run["width"]
        if which is not None:
            first_half, second_half = halves(run["width"])
            left, size = (0, first_half) if which == 0 else (first_half, second_half)
        if isinstance(base, int):
            return pl.ds(base + left, size)
        return pl.ds(pl.multiple_of(base + left, 128), size)

    def chunk(self, run, axis, value, which=None, ref=None, with_core=None):
        ref = run["own"] if ref is None else ref
        columns = self.columns_of(run, axis, value, which)
        return ref.at[self.spot(run["left"], axis, value, with_core) + (slice(None), columns)]

    def pair(self, run, axis, value):
        core = self.me["core"]
        give = self.wires.remote(
            self.chunk(run, axis, value, None, run["grads"], 1 - core),
            self.chunk(run, axis, value, None, run["theirs"]),
            self.sibling,
        )
        keep = self.wires.copy(
            self.chunk(run, axis, value, None, run["grads"], core), self.chunk(run, axis, value)
        )
        return give, keep

    def join(self, run, axis, value, copies):
        copies[0].wait_recv()
        copies[1].wait()
        self.add_into(
            self.chunk(run, axis, value),
            [self.chunk(run, axis, value, None, run["theirs"])],
            self.lead(run["left"], axis),
        )

    def slots(self, run, axis):
        dims = self.lead(run["left"], axis)
        ref = (run["near1"], run["near2"], run["ends"])[run["turn"]]
        if not dims:
            ref = ref.at[:, pl.ds(0, 48)]
        return ref.at[0], ref.at[1], ref.at[2], dims

    def part(self, ref, run, which, dims):
        first_half, second_half = halves(run["width"])
        columns = pl.ds(0, first_half) if which == 0 else pl.ds(first_half, second_half)
        return ref.at[(slice(None),) * len(dims) + (slice(None), columns)]

    def ring_open(self, run):
        axis = run["order"][run["turn"]]
        _, _, passing, dims = self.slots(run, axis)
        far = self.opposite[axis]
        run["passing"] = [
            self.wires.remote(
                self.chunk(run, axis, far, 0),
                self.part(passing, run, 0, dims),
                device(axis, self.next[axis]),
            )
        ]
        if halves(run["width"])[1]:
            run["passing"].append(
                self.wires.remote(
                    self.chunk(run, axis, far, 1),
                    self.part(passing, run, 1, dims),
                    device(axis, self.previous[axis]),
                )
            )

    def ring_near(self, run):
        axis = run["order"][run["turn"]]
        from_prv, from_nxt, _, dims = self.slots(run, axis)
        nxt, prv = self.next[axis], self.previous[axis]
        run["near"] = []
        if halves(run["width"])[1]:
            run["near"].append(
                self.wires.remote(
                    self.chunk(run, axis, nxt, 1),
                    self.part(from_prv, run, 1, dims),
                    device(axis, nxt),
                )
            )
        run["near"].append(
            self.wires.remote(
                self.chunk(run, axis, prv, 0), self.part(from_nxt, run, 0, dims), device(axis, prv)
            )
        )

    def ring_pass(self, run):
        axis = run["order"][run["turn"]]
        from_prv, from_nxt, passing, dims = self.slots(run, axis)
        nxt, prv = self.next[axis], self.previous[axis]
        run["passing"][0].wait_recv()
        self.add_into(self.chunk(run, axis, nxt, 0), [self.part(passing, run, 0, dims)], dims)
        run["near"].append(
            self.wires.remote(
                self.chunk(run, axis, nxt, 0), self.part(from_prv, run, 0, dims), device(axis, nxt)
            )
        )
        if halves(run["width"])[1]:
            run["passing"][1].wait_recv()
            self.add_into(self.chunk(run, axis, prv, 1), [self.part(passing, run, 1, dims)], dims)
            run["near"].append(
                self.wires.remote(
                    self.chunk(run, axis, prv, 1),
                    self.part(from_nxt, run, 1, dims),
                    device(axis, prv),
                )
            )

    def ring_close(self, run):
        axis = run["order"][run["turn"]]
        from_prv, from_nxt, _, dims = self.slots(run, axis)
        for copy in run["near"]:
            copy.wait_recv()
        self.add_into(self.chunk(run, axis, self.me[axis]), [from_prv, from_nxt], dims)
        run["left"] = run["left"].replace(axis, "")
        run["turn"] += 1

    def turn(self, run):
        self.ring_close(run)
        self.ring_open(run)
        self.ring_near(run)

    def spread(self, run):
        me, width = self.me, run["width"]
        third = len(run["order"]) == 3
        summed = run["own"].at[me["z"], rem(me["y"], 2), me["y"] // 2]
        exact = lax.Precision.HIGHEST if summed.dtype == F32 else None
        pick = spread_rows((64, 48), True).astype(summed.dtype)
        staging = run["ends"].at[3] if third else run["near2"].at[3]
        base = me["x"] * width if third else 0
        for left in range(0, width, 512):
            size = min(512, width - left)
            columns = pl.ds(left, size)
            if third:
                columns = pl.ds(pl.multiple_of(base + left, 128), size)
            staging[:, left : left + size] = jnp.dot(
                pick, summed[:, columns], preferred_element_type=F32, precision=exact
            ).astype(staging.dtype)
        if third:
            lands = run["arrived"].at[:, pl.ds(pl.multiple_of(base, 128), width)]
        else:
            lands = run["arrived"].at[me["x"]]
        run["copies"] = []
        for where in (self.next, self.opposite, self.previous):
            row = pl.ds(pl.multiple_of(where["x"] * 16, 16), 16)
            run["copies"].append(
                self.wires.remote(staging.at[row], lands, device("x", where["x"]))
            )
        row = pl.ds(pl.multiple_of(me["x"] * 16, 16), 16)
        run["keep"] = self.wires.copy(staging.at[row], lands)

    def deliver(self, run):
        run["keep"].wait()
        for copy in run["copies"]:
            copy.wait_recv()
        if len(run["order"]) == 3:
            run["out"][...] = run["arrived"][...].astype(F32)
        else:
            value = run["arrived"][0].astype(F32)
            for place_x in range(1, 4):
                value = value + run["arrived"][place_x].astype(F32)
            run["out"][...] = value

    def stages(self):
        runs = self.runs
        threes = [run for run in runs if len(run["order"]) == 3]
        twos = [run for run in runs if len(run["order"]) == 2]
        begun = []
        for where in (self.opposite, self.next, self.previous, self.me):
            begun.append([self.pair(run, run["order"][0], where[run["order"][0]]) for run in runs])
        yield
        for run, copies in zip(runs, begun[0]):
            axis = run["order"][0]
            self.join(run, axis, self.opposite[axis], copies)
            self.ring_open(run)
        for run, nexts, prevs in zip(runs, begun[1], begun[2]):
            axis = run["order"][0]
            self.join(run, axis, self.next[axis], nexts)
            self.join(run, axis, self.previous[axis], prevs)
            self.ring_near(run)
        yield
        for run in threes:
            self.ring_pass(run)
        for run, copies in zip(runs, begun[3]):
            axis = run["order"][0]
            self.join(run, axis, self.me[axis], copies)
        for run in twos:
            self.ring_pass(run)
        yield
        for run in threes:
            self.turn(run)
        for run in threes:
            self.ring_pass(run)
        for run in twos:
            self.turn(run)
        yield
        for run in threes:
            self.turn(run)
        for run in twos:
            self.ring_pass(run)
        for run in threes:
            self.ring_pass(run)
        yield
        for run in twos:
            self.ring_close(run)
            self.spread(run)
        for run in threes:
            self.ring_close(run)
            self.spread(run)
        yield
        for run in runs:
            self.deliver(run)
        yield


def summing_scratch(parts):
    own, theirs, near1, near2, ends, arrived = [], [], [], [], [], []
    for name, width, order in parts:
        kind = F32 if name == "misc" else BF16
        own.append(pltpu.VMEM((4, 2, 2, 48, width), kind))
        theirs.append(pltpu.VMEM((4, 2, 2, 48, width), kind))
        if len(order) == 3:
            quarter = width // 4
            near1.append(pltpu.VMEM((3, 4, 2, 2, 48, quarter), kind))
            near2.append(pltpu.VMEM((3, 2, 2, 48, quarter), kind))
            ends.append(pltpu.VMEM((4, 64, quarter), kind))
            arrived.append(pltpu.VMEM((16, width), kind))
        else:
            near1.append(pltpu.VMEM((3, 2, 2, 48, width) if order == "yz" else (3, 4, 48, width), kind))
            near2.append(pltpu.VMEM((4, 64, width), kind))
            ends.append(pltpu.VMEM((16, 128), kind))
            arrived.append(pltpu.VMEM((4, 16, width), kind))
    return own + theirs + near1 + near2 + ends + arrived


SHARED_PARTS = [part for part in SUMMED if part[0].startswith("sh")]
LAST_PARTS = [part for part in SUMMED if not part[0].startswith("sh")]

def last_kernel(*refs):
    count = len(LAST_PARTS)
    grads = refs[:count]
    expert_from = refs[count : count + 2]
    outs = refs[count + 2 : 2 * count + 2]
    expert_to = refs[2 * count + 2 : 2 * count + 4]
    scratch = refs[2 * count + 4 : 8 * count + 4]
    swap_send, swap_recv, swap_local, send_sems, recv_sems, local_sems = refs[8 * count + 4 :]
    me = place()
    partner = {"core": 1 - me["core"], "xl": 1 - lax.axis_index("xl")}
    crossed = me["core"] != lax.axis_index("xl")
    greet(ring_neighbours(me) + [partner])

    def moved(slot):
        return pltpu.make_async_remote_copy(
            src_ref=expert_from[slot],
            dst_ref=expert_to[slot],
            send_sem=swap_send.at[slot],
            recv_sem=swap_recv.at[slot],
            device_id=partner,
            device_id_type=MESH_ID,
        )

    def kept(slot):
        return pltpu.make_async_copy(expert_from[slot], expert_to[slot], swap_local.at[slot])

    wires = Wires(send_sems, recv_sems, local_sems)
    stages = Summing(wires, me, LAST_PARTS, grads, outs, scratch).stages()
    next(stages)
    next(stages)

    @pl.when(crossed)
    def _():
        for slot in range(2):
            moved(slot).start()

    @pl.when(jnp.logical_not(crossed))
    def _():
        for slot in range(2):
            kept(slot).start()

    for _ in stages:
        pass
    wires.finish()

    @pl.when(crossed)
    def _():
        for slot in range(2):
            moved(slot).wait_recv()
            moved(slot).wait_send()

    @pl.when(jnp.logical_not(crossed))
    def _():
        for slot in range(2):
            kept(slot).wait()


def sum_last(grads, expert_grads):
    anywhere = pl.BlockSpec(memory_space=pl.ANY)
    vmem = pl.BlockSpec(memory_space=pltpu.VMEM)
    count = len(LAST_PARTS)
    return pl.pallas_call(
        last_kernel,
        out_shape=[jax.ShapeDtypeStruct((16, width), F32) for _, width, _ in LAST_PARTS]
        + [jax.ShapeDtypeStruct(grad.shape, grad.dtype) for grad in expert_grads],
        in_specs=[anywhere] * (count + 2),
        out_specs=[vmem] * count + [anywhere] * 2,
        scratch_shapes=summing_scratch(LAST_PARTS)
        + [
            pltpu.SemaphoreType.DMA((2,)),
            pltpu.SemaphoreType.DMA((2,)),
            pltpu.SemaphoreType.DMA((2,)),
            pltpu.SemaphoreType.DMA((140,)),
            pltpu.SemaphoreType.DMA((140,)),
            pltpu.SemaphoreType.DMA((32,)),
        ],
        compiler_params=pltpu.CompilerParams(
            collective_id=1, has_side_effects=True, vmem_limit_bytes=56 * 1024 * 1024
        ),
        cost_estimate=pl.CostEstimate(
            flops=1_000_000_000, bytes_accessed=200_000_000, transcendentals=0
        ),
    )(*grads, *expert_grads)


def col_device(col):
    return {"yh": col // 4, "xh": rem(col // 2, 2), "xl": rem(col, 2)}


def col_index():
    return lax.axis_index("yh") * 4 + lax.axis_index("xh") * 2 + lax.axis_index("xl")


def later_kernel(own_ref, marks_ref, out_ref, marks_out, send_sems, recv_sems, local_sem):
    me = col_index()
    rows = own_ref.shape[0]
    tail = marks_ref.shape[0]
    late = pl.ds(rows - tail, tail)
    greet([col_device(rem(me + far, 8)) for far in range(1, 8)])

    def copies(far, first):
        there = col_device(rem(me + far, 8))
        pairs = [(own_ref, out_ref.at[me])]
        if first:
            pairs = [(own_ref.at[late], out_ref.at[0, late]), (marks_ref, marks_out)]
        return [
            pltpu.make_async_remote_copy(
                src_ref=source,
                dst_ref=target,
                send_sem=send_sems.at[far, number],
                recv_sem=recv_sems.at[far, number],
                device_id=there,
                device_id_type=MESH_ID,
            )
            for number, (source, target) in enumerate(pairs)
        ]

    def each(far, first, condition, act):
        @pl.when(condition)
        def _():
            for copy in copies(far, first):
                act(copy)

    for far in range(7, 0, -1):
        each(far, False, (me > 0) & (me + far < 8), lambda copy: copy.start())
        each(far, True, me == 0, lambda copy: copy.start())
    keep = pltpu.make_async_copy(own_ref, out_ref.at[me], local_sem)
    keep.start()

    @pl.when(me == 0)
    def _():
        marks_out[...] = marks_ref[...]

    @pl.when(me > 0)
    def _():
        out_ref[0, : rows - tail] = jnp.zeros((rows - tail, own_ref.shape[1]), own_ref.dtype)

    for far in range(1, 8):

        @pl.when(me + far < 8)
        def _():
            out_ref[me + far] = jnp.zeros(own_ref.shape, own_ref.dtype)

    keep.wait()
    for far in range(1, 8):
        each(far, False, me > far, lambda copy: copy.wait_recv())
        each(far, True, me == far, lambda copy: copy.wait_recv())
        each(far, False, (me > 0) & (me + far < 8), lambda copy: copy.wait_send())
        each(far, True, me == 0, lambda copy: copy.wait_send())


def to_later(rows, marks):
    vmem = pl.BlockSpec(memory_space=pltpu.VMEM)
    return pl.pallas_call(
        later_kernel,
        out_shape=[
            jax.ShapeDtypeStruct((8,) + rows.shape, rows.dtype),
            jax.ShapeDtypeStruct(marks.shape, marks.dtype),
        ],
        in_specs=[vmem, vmem],
        out_specs=[vmem, vmem],
        scratch_shapes=[
            pltpu.SemaphoreType.DMA((8, 2)),
            pltpu.SemaphoreType.DMA((8, 2)),
            pltpu.SemaphoreType.DMA,
        ],
        compiler_params=pltpu.CompilerParams(
            collective_id=2, has_side_effects=True, vmem_limit_bytes=16 * 1024 * 1024
        ),
        cost_estimate=pl.CostEstimate(flops=0, bytes_accessed=70_000_000, transcendentals=0),
    )(rows, marks)


VMEM_SPEC = pl.BlockSpec(memory_space=pltpu.VMEM)
GROUP = QUERY_HEADS // KEY_VALUE_HEADS
EXTRA = 128


def dot(left, right, left_dim=1, right_dim=0):
    return lax.dot_general(
        left, right, (((left_dim,), (right_dim,)), ((), ())), preferred_element_type=F32
    )


def rounded_parts(value):
    first = value.astype(BF16)
    left = value - first.astype(F32)
    second = left.astype(BF16)
    return [first, second, (left - second.astype(F32)).astype(BF16)]


def lane_column(index):
    return (lax.broadcasted_iota(jnp.int32, (16, 128), 1) == index).astype(BF16)


def gain_row(misc_ref, index):
    return dot(lane_column(index), misc_ref[...], 1, 1)[:1]


def allowed_pairs(marks_ref, segments_ref, rows, keys):
    me = col_index()
    shape = (rows, keys)
    own = segments_ref[:, :1]
    first_length = jnp.where(
        me == 0,
        jnp.sum((own == 0.0).astype(F32), axis=0, keepdims=True),
        marks_ref[:1, :1].astype(F32),
    )
    last_start = (me * rows).astype(F32) + jnp.sum(
        (own < 2.0).astype(F32), axis=0, keepdims=True
    )
    lowest = jnp.where(own == 0.0, 0.0, jnp.where(own == 1.0, first_length, last_start))
    key = lax.broadcasted_iota(jnp.int32, shape, 1)
    query = lax.broadcasted_iota(jnp.int32, shape, 0) + me * rows
    return (key <= query) & (key.astype(F32) >= lowest)


def head_columns(ref, group):
    width = GROUP * HEAD_SIZE
    return jnp.concatenate(
        [
            ref[:, group * width + head * HEAD_SIZE : group * width + (head + 1) * HEAD_SIZE]
            for head in range(GROUP)
        ],
        axis=0,
    )


def head_weights(queries, keys, allowed):
    scores = dot(queries, keys, 1, 1) * (HEAD_SIZE ** (-0.5))
    scores = jnp.where(allowed, scores, -1e30)
    shifted = jnp.exp(scores - jnp.max(scores, axis=1, keepdims=True))
    return shifted / jnp.sum(shifted, axis=1, keepdims=True)


def middle_kernel(
    qkv_ref,
    every_ref,
    marks_ref,
    segments_ref,
    tokens_ref,
    outt_ref,
    misc_ref,
    named_ref,
    slots_ref,
    owner_ref,
    attended_ref,
    residual_ref,
    normed_ref,
    gates_ref,
    outgoing_ref,
):
    rows, features = tokens_ref.shape
    width = KEY_VALUE_HEADS * HEAD_SIZE
    keys_count = 8 * rows
    allowed = allowed_pairs(marks_ref, segments_ref, rows, keys_count)
    allowed = jnp.concatenate([allowed.astype(F32)] * GROUP, axis=0) > 0.5
    for group in range(KEY_VALUE_HEADS):
        queries = head_columns(qkv_ref, group)
        columns = pl.ds(group * HEAD_SIZE, HEAD_SIZE)
        keys = every_ref[:, :, columns].reshape(keys_count, HEAD_SIZE)
        values = every_ref[:, :, pl.ds(width + group * HEAD_SIZE, HEAD_SIZE)].reshape(
            keys_count, HEAD_SIZE
        )
        weights = head_weights(queries, keys, allowed)
        mixed = dot(weights.astype(BF16), values).astype(BF16)
        for head in range(GROUP):
            at = (group * GROUP + head) * HEAD_SIZE
            attended_ref[:, at : at + HEAD_SIZE] = mixed[head * rows : (head + 1) * rows]
    attended = attended_ref[...]
    total = jnp.zeros((rows, 1), F32)
    for left in range(0, features, 512):
        piece = tokens_ref[:, left : left + 512].astype(F32) + dot(
            attended, outt_ref[left : left + 512], 1, 1
        )
        residual_ref[:, left : left + 512] = piece
        total = total + jnp.sum(piece * piece, axis=1, keepdims=True)
    scale = lax.rsqrt(total / features + EPSILON)
    normed_ref[...] = (residual_ref[...] * scale * gain_row(misc_ref, EXPERTS + 1)).astype(BF16)
    normed = normed_ref[...]
    logits = dot(normed, misc_ref[...])
    named = named_ref[...] > 0.5
    chosen = jnp.where(named, logits, -1e30)
    chosen_exp = jnp.where(named, jnp.exp(chosen - jnp.max(chosen, axis=1, keepdims=True)), 0.0)
    gates = chosen_exp / jnp.sum(chosen_exp, axis=1, keepdims=True)
    gates_ref[...] = gates
    parts = jnp.concatenate(rounded_parts(gates), axis=1)

    def send_rows(step, carry):
        at = pl.ds(pl.multiple_of(step * 256, 256), 256)
        slots = slots_ref[at]
        outgoing_ref[at, :features] = dot(slots, normed).astype(BF16)
        gate_parts = dot(slots, parts)
        owner = owner_ref[at].astype(F32)
        lane = lax.broadcasted_iota(jnp.int32, (256, EXTRA), 1)
        extra = jnp.zeros((256, EXTRA), F32)
        for part in range(3):
            column = jnp.sum(
                gate_parts[:, part * 128 : (part + 1) * 128] * owner, axis=1, keepdims=True
            )
            extra = jnp.where(lane == part, column, extra)
        outgoing_ref[at, features:] = extra.astype(BF16)
        return carry

    lax.fori_loop(0, slots_ref.shape[0] // 256, send_rows, 0)


def middle(qkv, every, marks, segments, tokens, outt, misc, named, slots, owner):
    rows, features = tokens.shape
    return pl.pallas_call(
        middle_kernel,
        out_shape=[
            jax.ShapeDtypeStruct((rows, features), BF16),
            jax.ShapeDtypeStruct((rows, features), F32),
            jax.ShapeDtypeStruct((rows, features), BF16),
            jax.ShapeDtypeStruct((rows, 128), F32),
            jax.ShapeDtypeStruct((slots.shape[0], features + EXTRA), BF16),
        ],
        in_specs=[VMEM_SPEC] * 10,
        out_specs=[VMEM_SPEC] * 5,
        compiler_params=pltpu.CompilerParams(vmem_limit_bytes=48 * 1024 * 1024),
        cost_estimate=pl.CostEstimate(
            flops=6_000_000_000, bytes_accessed=20_000_000, transcendentals=2_000_000
        ),
    )(qkv, every, marks, segments, tokens, outt, misc, named, slots, owner)


GROUP_BLOCKS = 16


def expert_kernel(
    outgoing_ref,
    cotangent_in,
    weight_ref,
    down_ref,
    returned_ref,
    rows_out,
    own_in_ref,
    other_in_ref,
    own_down_ref,
    other_down_ref,
    landed,
    cotangents,
    back,
    grads,
    hiddens,
    gated,
    rows_staged,
    other_in,
    other_down,
    send_sems,
    recv_sems,
    local_sems,
):
    features = cotangent_in.shape[2]
    spot = place()
    chips = [chip_at(spot, offset) for offset in OFFSETS]
    sources = [chip_at(spot, offset, -1) for offset in OFFSETS]
    mine = chip_at(spot, (0, 0, 0))[1]
    greet([where for where, _ in chips])
    wires = Wires(send_sems, recv_sems, local_sems)
    rows_in = [wires.copy(outgoing_ref.at[mine], landed.at[0])]
    for number, (where, holder) in enumerate(chips):
        rows_in.append(wires.remote(outgoing_ref.at[holder], landed.at[number + 1], where))
    holders = [mine] + [holder for _, holder in sources]
    brought = [
        wires.copy(cotangent_in.at[holder], cotangents.at[number])
        for number, holder in enumerate(holders)
    ]
    count = len(holders)
    tile = GROUP_BLOCKS * CAP
    returning = []

    def flat(ref, first, columns):
        blocks = ref[first : first + GROUP_BLOCKS, :, columns].astype(F32)
        return blocks.reshape(tile, blocks.shape[-1]).astype(BF16)

    def blocks_of(value):
        return value.reshape(GROUP_BLOCKS, CAP, value.shape[-1]).astype(BF16)

    for first in range(0, count, GROUP_BLOCKS):
        for number in range(first, first + GROUP_BLOCKS):
            brought[number].wait()
            if number == 0:
                rows_in[number].wait()
            else:
                rows_in[number].wait_recv()
        at = pl.ds(first * CAP, tile)
        extra = flat(landed, first, pl.ds(features, EXTRA)).astype(F32)
        gate = extra[:, :1] + extra[:, 1:2] + extra[:, 2:3]
        everything = pl.ds(0, features)
        pre = dot(flat(landed, first, everything), weight_ref[...])
        grad_hidden = dot(flat(cotangents, first, everything), down_ref[...], 1, 1)
        along = jnp.zeros((tile, 1), F32)
        for part in range(2):
            base = part * 2 * HALF
            gate_pre, up_pre = pre[:, base : base + HALF], pre[:, base + HALF : base + 2 * HALF]
            grad_part = grad_hidden[:, part * HALF : (part + 1) * HALF]
            sigmoid = 1.0 / (1.0 + jnp.exp(-gate_pre))
            silu = gate_pre * sigmoid
            hidden = silu * up_pre
            along = along + jnp.sum(hidden * grad_part, axis=1, keepdims=True)
            gated_grad = grad_part * gate
            grads[at, base : base + HALF] = (
                gated_grad * up_pre * sigmoid * (1.0 + gate_pre * (1.0 - sigmoid))
            ).astype(BF16)
            grads[at, base + HALF : base + 2 * HALF] = (gated_grad * silu).astype(BF16)
            hiddens[at, part * HALF : (part + 1) * HALF] = hidden.astype(BF16)
            gated[at, part * HALF : (part + 1) * HALF] = (hidden * gate).astype(BF16)
        group_grads = grads[at]
        for left in range(0, features, 512):
            back[first : first + GROUP_BLOCKS, :, left : left + 512] = blocks_of(
                dot(group_grads, weight_ref[left : left + 512], 1, 1)
            )
        lane = lax.broadcasted_iota(jnp.int32, (tile, EXTRA), 1)
        value = jnp.zeros((tile, EXTRA), F32)
        for part, column in enumerate(rounded_parts(along)):
            value = jnp.where(lane == part, column.astype(F32), value)
        back[first : first + GROUP_BLOCKS, :, features:] = blocks_of(value)
        for number in range(first, first + GROUP_BLOCKS):
            if number == 0:
                kept = wires.copy(back.at[0], returned_ref.at[mine])
            else:
                returning.append(
                    wires.remote(back.at[number], returned_ref.at[mine], sources[number - 1][0])
                )
    staged = []
    for index, first in enumerate(range(0, count, GROUP_BLOCKS)):
        at = pl.ds(first * CAP, tile)
        group_hidden = hiddens[at]
        slot = index % 2
        if index >= 2:
            for copy in staged[index - 2]:
                copy.wait()
        for left in range(0, features, 512):
            columns = pl.ds(left, 512)
            rows_staged[slot, :, :, left : left + 512] = blocks_of(
                dot(group_hidden, down_ref[:, columns])
            )
        staged.append(
            [
                wires.copy(rows_staged.at[slot, number], rows_out.at[holders[first + number]])
                for number in range(GROUP_BLOCKS)
            ]
        )
        for left in range(0, features, 512):
            columns = pl.ds(left, 512)
            rows = flat(landed, first, columns)
            own = dot(rows, grads[at, : 2 * HALF], 0, 0)
            other = dot(rows, grads[at, 2 * HALF :], 0, 0)
            rows = flat(cotangents, first, columns)
            own_down = dot(gated[at, :HALF], rows, 0, 0)
            other_part = dot(gated[at, HALF:], rows, 0, 0)
            if index > 0:
                own = own + own_in_ref[columns]
                other = other + other_in[columns]
                own_down = own_down + own_down_ref[:, columns]
                other_part = other_part + other_down[:, columns]
            own_in_ref[columns] = own
            own_down_ref[:, columns] = own_down
            if first + GROUP_BLOCKS == count:
                other_in_ref[columns] = other.astype(BF16)
                other_down_ref[:, columns] = other_part.astype(BF16)
            else:
                other_in[columns] = other
                other_down[:, columns] = other_part
    for copies in staged[-2:]:
        for copy in copies:
            copy.wait()
    kept.wait()
    for copy in returning:
        copy.wait_recv()
    wires.finish()


def expert(outgoing, grad_received, weight, down):
    count, cap, features = grad_received.shape
    anywhere = pl.BlockSpec(memory_space=pl.ANY)
    return pl.pallas_call(
        expert_kernel,
        out_shape=[
            jax.ShapeDtypeStruct(outgoing.shape, BF16),
            jax.ShapeDtypeStruct(grad_received.shape, BF16),
            jax.ShapeDtypeStruct((features, 2 * HALF), F32),
            jax.ShapeDtypeStruct((features, 2 * HALF), BF16),
            jax.ShapeDtypeStruct((HALF, features), F32),
            jax.ShapeDtypeStruct((HALF, features), BF16),
        ],
        in_specs=[anywhere, anywhere, VMEM_SPEC, VMEM_SPEC],
        out_specs=[anywhere, anywhere] + [VMEM_SPEC] * 4,
        scratch_shapes=[
            pltpu.VMEM(outgoing.shape, BF16),
            pltpu.VMEM(grad_received.shape, BF16),
            pltpu.VMEM(outgoing.shape, BF16),
            pltpu.VMEM((count * cap, 4 * HALF), BF16),
            pltpu.VMEM((count * cap, 2 * HALF), BF16),
            pltpu.VMEM((count * cap, 2 * HALF), BF16),
            pltpu.VMEM((2, GROUP_BLOCKS, cap, features), BF16),
            pltpu.VMEM((features, 2 * HALF), F32),
            pltpu.VMEM((HALF, features), F32),
            pltpu.SemaphoreType.DMA((128,)),
            pltpu.SemaphoreType.DMA((128,)),
            pltpu.SemaphoreType.DMA((136,)),
        ],
        compiler_params=pltpu.CompilerParams(
            collective_id=4, has_side_effects=True, vmem_limit_bytes=58 * 1024 * 1024
        ),
        cost_estimate=pl.CostEstimate(
            flops=22_000_000_000, bytes_accessed=300_000_000, transcendentals=1_000_000
        ),
    )(outgoing, grad_received, weight, down)


def back_to_residual(
    grad_back_ref,
    slots_ref,
    owner_ref,
    gates_ref,
    cotangent_ref,
    residual_ref,
    partial_ref,
    misc_ref,
    outt_ref,
    grad_residual_ref,
    grad_low_ref,
    grad_logits_ref,
    grad_gain_ref,
    grad_attended,
):
    rows, features = cotangent_ref.shape
    slots = slots_ref[...]
    extra = grad_back_ref[:, features:].astype(F32)
    owner = owner_ref[...].astype(F32)
    grad_gates = jnp.zeros((rows, 128), F32)
    for part in range(3):
        grad_gates = grad_gates + dot(slots, (owner * extra[:, part : part + 1]).astype(BF16))
    gates = gates_ref[...]
    grad_logits = (
        gates * (grad_gates - jnp.sum(gates * grad_gates, axis=1, keepdims=True))
    ).astype(BF16)
    grad_logits_ref[...] = grad_logits
    gain = gain_row(misc_ref, EXPERTS + 1)
    square, inner = jnp.zeros((rows, 1), F32), jnp.zeros((rows, 1), F32)
    for left in range(0, features, 512):
        columns = pl.ds(left, 512)
        piece = (
            partial_ref[:, columns]
            + dot(slots, grad_back_ref[:, columns])
            + dot(grad_logits, misc_ref[columns], 1, 1)
        )
        grad_residual_ref[:, columns] = piece
        residual = residual_ref[:, columns]
        square = square + jnp.sum(residual * residual, axis=1, keepdims=True)
        inner = inner + jnp.sum(
            piece * gain[:, left : left + 512] * residual, axis=1, keepdims=True
        )
    scale = lax.rsqrt(square / features + EPSILON)
    cubed = scale * scale * scale * (inner / features)
    for left in range(0, features, 512):
        columns = pl.ds(left, 512)
        piece = grad_residual_ref[:, columns]
        residual = residual_ref[:, columns]
        grad_gain_ref[:, columns] = jnp.broadcast_to(
            jnp.sum(piece * residual * scale, axis=0, keepdims=True), (8, 512)
        )
        value = (
            cotangent_ref[:, columns].astype(F32)
            + scale * piece * gain[:, left : left + 512]
            - residual * cubed
        )
        grad_residual_ref[:, columns] = value
        grad_low_ref[:, columns] = value.astype(BF16)
    grad_low = grad_low_ref[...]
    for left in range(0, features, 512):
        columns = pl.ds(left, 512)
        grad_attended[:, columns] = dot(grad_low, outt_ref[:, columns]).astype(BF16)


def back_heads(
    group, allowed, qkv_ref, every_ref, grad_attended, grad_queries_ref, partial_keyvals
):
    rows = qkv_ref.shape[0]
    width = KEY_VALUE_HEADS * HEAD_SIZE
    keys_count = 8 * rows
    score_scale = HEAD_SIZE ** (-0.5)
    queries = head_columns(qkv_ref, group)
    heads_gradient = head_columns(grad_attended, group)
    key_columns = pl.ds(group * HEAD_SIZE, HEAD_SIZE)
    value_columns = pl.ds(width + group * HEAD_SIZE, HEAD_SIZE)
    keys = every_ref[:, :, key_columns].reshape(keys_count, HEAD_SIZE)
    values = every_ref[:, :, value_columns].reshape(keys_count, HEAD_SIZE)
    weights = head_weights(queries, keys, allowed)
    grad_weights = dot(heads_gradient, values, 1, 1)
    inner_sum = jnp.sum(weights * grad_weights, axis=1, keepdims=True)
    grad_scores = (weights * (grad_weights - inner_sum)).astype(BF16)
    grad_queries = (dot(grad_scores, keys) * score_scale).astype(BF16)
    for head in range(GROUP):
        at = (group * GROUP + head) * HEAD_SIZE
        grad_queries_ref[:, at : at + HEAD_SIZE] = grad_queries[head * rows : (head + 1) * rows]
    partial_keyvals[:, :, key_columns] = (
        (dot(grad_scores, queries, 0, 0) * score_scale).astype(BF16).reshape(8, rows, HEAD_SIZE)
    )
    partial_keyvals[:, :, value_columns] = (
        dot(weights.astype(BF16), heads_gradient, 0, 0).astype(BF16).reshape(8, rows, HEAD_SIZE)
    )


def rear_kernel(tail, *refs):
    count = len(SHARED_PARTS)
    (
        grad_back_ref,
        slots_ref,
        owner_ref,
        gates_ref,
        cotangent_ref,
        residual_ref,
        partial_ref,
        misc_ref,
        outt_ref,
        qkv_ref,
        every_ref,
        marks_ref,
        segments_ref,
        in_ref,
        down_ref,
    ) = refs[:15]
    grads = refs[15 : 15 + count]
    (
        grad_residual_ref,
        grad_low_ref,
        grad_logits_ref,
        grad_gain_ref,
        grad_queries_ref,
        grad_keyvals_ref,
        in_out,
        down_out,
    ) = refs[15 + count : 23 + count]
    outs = refs[23 + count : 23 + 2 * count]
    scratch = refs[23 + 2 * count : 23 + 8 * count]
    (
        grad_attended,
        blocks_ref,
        landed,
        sequence_send,
        sequence_recv,
        send_sems,
        recv_sems,
        local_sems,
    ) = refs[23 + 8 * count :]
    me = col_index()
    spot = place()
    rows = cotangent_ref.shape[0]
    late = pl.ds(rows - tail, tail)
    sibling = {"core": 1 - spot["core"]}
    distant = [col_device(rem(me + far, 8)) for far in range(1, 8)]
    greet(ring_neighbours(spot) + distant)
    wires = Wires(send_sems, recv_sems, local_sems)
    stages = Summing(wires, spot, SHARED_PARTS, grads, outs, scratch).stages()
    next(stages)
    arriving = [
        wires.remote(in_ref, in_out, sibling),
        wires.remote(down_ref, down_out, sibling),
    ]
    back_to_residual(
        grad_back_ref,
        slots_ref,
        owner_ref,
        gates_ref,
        cotangent_ref,
        residual_ref,
        partial_ref,
        misc_ref,
        outt_ref,
        grad_residual_ref,
        grad_low_ref,
        grad_logits_ref,
        grad_gain_ref,
        grad_attended,
    )
    next(stages)
    allowed = allowed_pairs(marks_ref, segments_ref, rows, 8 * rows)
    allowed = jnp.concatenate([allowed.astype(F32)] * GROUP, axis=0) > 0.5

    def heads(group):
        back_heads(
            group, allowed, qkv_ref, every_ref, grad_attended, grad_queries_ref, blocks_ref
        )

    for group in range(KEY_VALUE_HEADS):
        heads(group)

    def copy(far, first):
        block = rem(me + 8 - far, 8)
        source, target = blocks_ref.at[block], landed.at[far]
        if first:
            source, target = blocks_ref.at[0, late], landed.at[far, late]
        return pltpu.make_async_remote_copy(
            src_ref=source,
            dst_ref=target,
            send_sem=sequence_send.at[far],
            recv_sem=sequence_recv.at[far],
            device_id=col_device(block),
            device_id_type=MESH_ID,
        )

    def each(far, first, condition, act):
        @pl.when(condition)
        def _():
            act(copy(far, first))

    for far in range(7, 0, -1):
        each(far, False, me > far, lambda moved: moved.start())
        each(far, True, me == far, lambda moved: moved.start())

    @pl.when(me == 0)
    def _():
        for far in range(1, 8):
            landed[far, : rows - tail] = jnp.zeros((rows - tail, landed.shape[2]), landed.dtype)

    for far in range(1, 8):

        @pl.when(me + far >= 8)
        def _():
            landed[far] = jnp.zeros(landed.shape[1:], landed.dtype)

    next(stages)
    next(stages)
    for far in range(1, 8):
        each(far, False, (me > 0) & (me + far < 8), lambda moved: moved.wait_recv())
        each(far, True, me == 0, lambda moved: moved.wait_recv())
    for row in range(0, rows, 16):
        at = pl.ds(row, 16)
        value = blocks_ref[me, at].astype(F32)
        for far in range(1, 8):
            value = value + landed[far, at].astype(F32)
        grad_keyvals_ref[at] = value.astype(BF16)
    next(stages)
    next(stages)
    next(stages)
    for far in range(1, 8):
        each(far, False, me > far, lambda moved: moved.wait_send())
        each(far, True, me == far, lambda moved: moved.wait_send())
    for moved in arriving:
        moved.wait_recv()
    wires.finish()


def rear(tail, grad_back, slots, owner, gates, cotangent, residual1, partial, misc, outt, qkv, every,
         marks, segments, expert_in, expert_down, grads):
    rows, features = cotangent.shape
    anywhere = pl.BlockSpec(memory_space=pl.ANY)
    inputs = (grad_back, slots, owner, gates, cotangent, residual1, partial, misc, outt, qkv, every,
              marks, segments)
    return pl.pallas_call(
        functools.partial(rear_kernel, tail),
        out_shape=[
            jax.ShapeDtypeStruct((rows, features), F32),
            jax.ShapeDtypeStruct((rows, features), BF16),
            jax.ShapeDtypeStruct((rows, 128), BF16),
            jax.ShapeDtypeStruct((8, features), F32),
            jax.ShapeDtypeStruct((rows, features), BF16),
            jax.ShapeDtypeStruct(every.shape[1:], BF16),
            jax.ShapeDtypeStruct(expert_in.shape, BF16),
            jax.ShapeDtypeStruct(expert_down.shape, BF16),
        ]
        + [jax.ShapeDtypeStruct((16, width), F32) for _, width, _ in SHARED_PARTS],
        in_specs=[VMEM_SPEC] * 13 + [anywhere] * (2 + len(SHARED_PARTS)),
        out_specs=[VMEM_SPEC] * 6 + [anywhere] * 2 + [VMEM_SPEC] * len(SHARED_PARTS),
        scratch_shapes=summing_scratch(SHARED_PARTS)
        + [
            pltpu.VMEM((rows, features), BF16),
            pltpu.VMEM(every.shape, BF16),
            pltpu.VMEM(every.shape, BF16),
            pltpu.SemaphoreType.DMA((8,)),
            pltpu.SemaphoreType.DMA((8,)),
            pltpu.SemaphoreType.DMA((140,)),
            pltpu.SemaphoreType.DMA((140,)),
            pltpu.SemaphoreType.DMA((32,)),
        ],
        compiler_params=pltpu.CompilerParams(
            collective_id=3, has_side_effects=True, vmem_limit_bytes=56 * 1024 * 1024
        ),
        cost_estimate=pl.CostEstimate(
            flops=10_000_000_000, bytes_accessed=150_000_000, transcendentals=2_000_000
        ),
    )(*inputs, expert_in, expert_down, *grads)


def inverse_rms(residual):
    return lax.rsqrt(jnp.mean(residual * residual, axis=-1, keepdims=True) + EPSILON)


def contract(left_side, right_side, left_dim, right_dim):
    return lax.dot_general(
        left_side,
        right_side,
        (((left_dim,), (right_dim,)), ((), ())),
        preferred_element_type=F32,
    )


def gated_unit(gate_pre, up_pre):
    return jax.nn.silu(gate_pre) * up_pre


def norm_backward(residual, norm_scale, gain_row, grad_normed):
    weighted = grad_normed * gain_row
    inner_sum = jnp.mean(weighted * residual, axis=-1, keepdims=True)
    grad_residual = (
        norm_scale * weighted - residual * norm_scale * norm_scale * norm_scale * inner_sum
    )
    grad_gain = jnp.sum(grad_normed * residual * norm_scale, axis=0)
    return (grad_residual, grad_gain)


def expert_of(holder):
    return (holder // 8) * 8 + (holder % 2) * 4 + holder // 2 % 4


def packed(grad):
    return grad.reshape(4, 2, 2, 2, 48, grad.shape[-1])


def to_experts(rows):
    return lax.all_to_all(rows, EXPERT_AXES, split_axis=0, concat_axis=0, tiled=True)


def shards(
    tokens,
    segments,
    routes,
    norm1_gain,
    w_query,
    key_value_weight,
    w_output,
    norm2_gain,
    w_router,
    w_shgate,
    w_shup,
    w_shdown,
    w_exgate,
    w_exup,
    w_exdown,
    cotangent,
):
    local_rows, feature_count = tokens.shape
    sequence_length = local_rows * 8
    shard = jnp.concatenate(
        [
            w_output.T,
            w_router,
            norm1_gain[:, None],
            norm2_gain[:, None],
            jnp.zeros((12, 62), BF16),
            w_query,
            key_value_weight,
            w_shgate,
            w_shup,
            w_shdown.T,
        ],
        axis=1,
    )
    shard = jnp.concatenate([shard, jnp.zeros((4, TOTAL), BF16)], axis=0)
    *dense, expert_w, expert_down = gather_weights(shard, w_exgate[0], w_exup[0], w_exdown[0])
    outt_w, misc_w, query_w, keyval_w, shgate_w, shup_w, shdt_w = [
        gathered.reshape(feature_count, gathered.shape[-1]) for gathered in dense
    ]
    gain_first = misc_w[:, EXPERTS].astype(F32)

    expert_ids = jnp.arange(128, dtype=jnp.int32)
    named = jnp.any(routes[:, :, None] == expert_ids[None, None, :], axis=1)
    named_low = named.astype(BF16)
    token_ids = jnp.arange(local_rows, dtype=jnp.int32)
    before = (token_ids[None, :] <= token_ids[:, None]).astype(BF16)
    rank = jnp.dot(before, named_low, preferred_element_type=F32) * named.astype(F32)
    slot_count = EXPERTS * CAP
    slot_ids = jnp.arange(slot_count, dtype=jnp.int32)
    holder = slot_ids // CAP
    slot_expert = expert_of(holder)
    owner = (slot_expert[:, None] == expert_ids[None, :]).astype(BF16)
    rank_wide = contract(rank.astype(BF16), owner, 1, 1)
    slots = (rank_wide == (slot_ids % CAP + 1).astype(F32)[None, :]).astype(BF16)
    slots_down = (
        contract(owner, rank.astype(BF16), 1, 1) == (slot_ids % CAP + 1).astype(F32)[:, None]
    ).astype(BF16)

    def dispatch(rows):
        return rows.reshape(EXPERTS, CAP, rows.shape[-1])

    sent_cotangent = dispatch(jnp.dot(slots_down, cotangent, preferred_element_type=F32).astype(BF16))
    residual0 = tokens.astype(F32)
    scale_first = inverse_rms(residual0)
    first_normed = (residual0 * scale_first * gain_first).astype(BF16)
    query_rows = jnp.dot(first_normed, query_w, preferred_element_type=F32).astype(BF16)
    keyval_rows = jnp.dot(first_normed, keyval_w, preferred_element_type=F32).astype(BF16)
    own_segments = segments.astype(F32)
    tail = 32
    first_length = jnp.sum((segments == 0).astype(F32)).astype(BF16)
    every, marks = to_later(
        keyval_rows, jnp.broadcast_to(first_length, (tail, 128))
    )
    sent_cotangent, every = lax.optimization_barrier((sent_cotangent, every))
    grad_received = to_experts(sent_cotangent)
    segment_tile = jnp.broadcast_to(own_segments[:, None], (local_rows, 128))
    attended_rows, residual1, second_normed, gates, outgoing = middle(
        query_rows,
        every,
        marks,
        segment_tile,
        tokens,
        outt_w,
        misc_w,
        named.astype(F32),
        slots_down,
        owner,
    )
    shared_gate = jnp.dot(second_normed, shgate_w, preferred_element_type=F32)
    shared_up = jnp.dot(second_normed, shup_w, preferred_element_type=F32)
    shared_hidden = gated_unit(shared_gate, shared_up).astype(BF16)
    shared_out = contract(shared_hidden, shdt_w, 1, 1)
    grad_shdt = contract(cotangent, shared_hidden, 0, 0).astype(BF16)
    grad_shared_hidden = jnp.dot(cotangent, shdt_w, preferred_element_type=F32)
    unused_shared, pull_shared = jax.vjp(gated_unit, shared_gate, shared_up)
    grad_shared_gate, grad_shared_up = pull_shared(grad_shared_hidden)
    grad_shared_gate = grad_shared_gate.astype(BF16)
    grad_shared_up = grad_shared_up.astype(BF16)
    grad_shgate = contract(second_normed, grad_shared_gate, 0, 0).astype(BF16)
    grad_shup = contract(second_normed, grad_shared_up, 0, 0).astype(BF16)
    grad_second = contract(grad_shared_gate, shgate_w, 1, 1) + contract(
        grad_shared_up, shup_w, 1, 1
    )

    forward_rows = residual1 + shared_out
    slot_gates = slots.astype(F32) * lax.dot_general(
        gates,
        owner.astype(F32),
        (((1,), (1,)), ((), ())),
        precision=lax.Precision.HIGHEST,
        preferred_element_type=F32,
    )
    gates_high = lax.reduce_precision(slot_gates, exponent_bits=8, mantissa_bits=7)
    (
        outgoing,
        grad_shdt,
        grad_shgate,
        grad_shup,
        grad_second,
        forward_rows,
        slot_gates,
        gates_high,
    ) = lax.optimization_barrier(
        (
            outgoing,
            grad_shdt,
            grad_shgate,
            grad_shup,
            grad_second,
            forward_rows,
            slot_gates,
            gates_high,
        )
    )
    grad_back, half_out, own_in, other_in, own_down, other_down = expert(
        dispatch(outgoing), grad_received, expert_w, expert_down
    )
    grad_back = grad_back.reshape(slot_count, feature_count + EXTRA)
    (
        grad_residual1,
        grad_attn_low,
        grad_logits,
        grad_gain_second,
        grad_queries,
        grad_keyvals,
        their_in,
        their_down,
        sum_shgate,
        sum_shup,
        sum_shdt,
    ) = rear(
        tail,
        grad_back,
        slots,
        owner,
        gates,
        cotangent,
        residual1,
        grad_second,
        misc_w,
        outt_w,
        query_rows,
        every,
        marks,
        segment_tile,
        other_in,
        other_down,
        [packed(grad_shgate), packed(grad_shup), packed(grad_shdt)],
    )
    half_out, grad_keyvals = lax.optimization_barrier((half_out, grad_keyvals))
    returned = to_experts(half_out).reshape(slot_count, feature_count)
    grad_gain_second = grad_gain_second[0]
    grad_router = contract(second_normed, grad_logits, 0, 0)
    grad_outt = contract(grad_attn_low, attended_rows, 0, 0).astype(BF16)
    half_in = (own_in + their_in.astype(F32)).astype(BF16)
    half_down = (own_down + their_down.astype(F32)).astype(BF16)
    grad_query = contract(first_normed, grad_queries, 0, 0).astype(BF16)
    grad_keyval = contract(first_normed, grad_keyvals, 0, 0).astype(BF16)
    grad_first = contract(grad_queries, query_w, 1, 1) + contract(grad_keyvals, keyval_w, 1, 1)
    grad_norm_first, grad_gain_first = norm_backward(residual0, scale_first, gain_first, grad_first)
    grad_tokens = grad_residual1 + grad_norm_first
    grad_misc = jnp.concatenate(
        [
            grad_router[:, :EXPERTS],
            grad_gain_first[:, None],
            grad_gain_second[:, None],
            jnp.zeros((feature_count, 62), F32),
        ],
        axis=1,
    )
    expert_mix = jnp.dot(
        gates_high.astype(BF16), returned, preferred_element_type=F32
    ) + jnp.dot((slot_gates - gates_high).astype(BF16), returned, preferred_element_type=F32)
    block_out = (forward_rows + expert_mix).astype(BF16)
    grad_misc, block_out = lax.optimization_barrier((grad_misc, block_out))
    *summed, half_in, half_down = sum_last(
        [packed(grad) for grad in (grad_outt, grad_misc, grad_query, grad_keyval)],
        [half_in, half_down],
    )
    sum_outt, sum_misc, sum_query, sum_keyval, sum_shgate, sum_shup, sum_shdt = [
        piece[:12] for piece in (*summed, sum_shgate, sum_shup, sum_shdt)
    ]
    return (
        block_out,
        grad_tokens,
        sum_misc[:, EXPERTS],
        sum_query,
        sum_keyval,
        sum_outt.T,
        sum_misc[:, EXPERTS + 1],
        sum_misc[:, :EXPERTS],
        sum_shgate,
        sum_shup,
        sum_shdt.T,
        half_in[None, :, :HALF].astype(F32),
        half_in[None, :, HALF:].astype(F32),
        half_down[None].astype(F32),
    )


def solution(mesh):
    fine = Mesh(mesh.devices.reshape(SIZES), AXES)
    rows = P(AXES, None)
    columns = P(None, AXES)
    flat = P(AXES)
    blocks = P(AXES, None, None)
    in_specs = (
        rows,
        flat,
        rows,
        flat,
        rows,
        rows,
        columns,
        flat,
        rows,
        rows,
        rows,
        columns,
        blocks,
        blocks,
        blocks,
        rows,
    )
    out_specs = (
        rows,
        rows,
        flat,
        rows,
        rows,
        columns,
        flat,
        rows,
        rows,
        rows,
        columns,
        blocks,
        blocks,
        blocks,
    )
    return jax.shard_map(shards, mesh=fine, in_specs=in_specs, out_specs=out_specs, check_vma=False)
```

time: 628 us -> 601 us (0.957)
  Pallas kernels: 371 us -> 421 us
  waiting for transfers between devices: 75.2 us -> 51.5 us
  matrix products: 70.6 us -> 50.1 us
  starting transfers between devices: 40.8 us -> 23.5 us
  local copies, waits for them, and re-layouts: 43.3 us -> 32.7 us
    pallas_call x4 -> x3, Pallas kernels: 211 us -> 305 us  [the longest x1 141 us: expert(): pl.pallas_call(expert_kernel, out_shape=[jax.ShapeDtypeStruct(outgoing.sh...]
    pallas_call x1, Pallas kernels: 67.2 us -> 23.8 us  [to_later(): pl.pallas_call(later_kernel, out_shape=[jax.ShapeDtypeStruct((8,) + rows....]
    all_to_all x3 -> x2, waiting for transfers between devices: 75.2 us -> 51.5 us  [to_experts(): lax.all_to_all(rows, EXPERT_AXES, split_axis=0, concat_axis=0, tiled=True)]
    dot_general x14, matrix products: 48.9 us -> 31.5 us  [contract(): lax.dot_general(left_side, right_side, (((left_dim,), (right_dim,)), ((),...]
    all_to_all x3 -> x2, starting transfers between devices: 40.8 us -> 23.5 us  [to_experts(): lax.all_to_all(rows, EXPERT_AXES, split_axis=0, concat_axis=0, tiled=True)]
    dot_general x4 -> x5, matrix products: 14.7 us -> 6.97 us  [the longest x1 3.33 us: shards(): jnp.dot(first_normed, query_w, preferred_element_type=F32).astype(BF16)]
    unnamed x134 -> x137, local copies, waits for them, and re-layouts: 26.7 us -> 19.7 us
  transfers between devices with their start and end apart: 3 -> 2, of which waited for: 2 -> 2; matrix products, arithmetic and copies ran while one was open for 9% -> 8% of each run, Pallas kernels for 13% -> 2%
where the time goes in v3:
time: 601 us; the launch traced here: 592 us
  Pallas kernels  421 us (70%)
  waiting for transfers between devices  51.5 us (9%)
  matrix products  50.1 us (8%)
  local copies, waits for them, and re-layouts  32.7 us (5%)
  starting transfers between devices  23.5 us (4%)
  other arithmetic  10.9 us (2%)
    pallas_call x1, Pallas kernels, expert(): pl.pallas_call(expert_kernel, out_shape=[jax.ShapeDtypeStruct(outgoing.sh...  141 us
    pallas_call x1, Pallas kernels, sum_last(): pl.pallas_call(last_kernel, out_shape=[jax.ShapeDtypeStruct((16, width),...  90.8 us
    pallas_call x1, Pallas kernels, gather_weights(): pl.pallas_call(gather_kernel, out_shape=shapes, in_specs=[pl.BlockSpec(me...  79.3 us
    pallas_call x1, Pallas kernels, rear(): pl.pallas_call(functools.partial(rear_kernel, tail), out_shape=[jax.Shape...  73.5 us
    all_to_all x2, waiting for transfers between devices, to_experts(): lax.all_to_all(rows, EXPERT_AXES, split_axis=0, concat_axis=0, tiled=True)  51.5 us
    dot_general x14, matrix products, contract(): lax.dot_general(left_side, right_side, (((left_dim,), (right_dim,)), ((),...  31.5 us
    pallas_call x1, Pallas kernels, to_later(): pl.pallas_call(later_kernel, out_shape=[jax.ShapeDtypeStruct((8,) + rows....  23.8 us
    all_to_all x2, starting transfers between devices, to_experts(): lax.all_to_all(rows, EXPERT_AXES, split_axis=0, concat_axis=0, tiled=True)  23.5 us
  transfers between devices with their start and end apart: 2, of which 2 were waited for; matrix products, arithmetic and copies ran while one was open for 8% of the time, Pallas kernels for 2%

profile of v3, /device:TPU:3, one launch (start us, length us, event | category | flops | bytes accessed | tf_op | source)
XLA Modules:
  0.0 591.8 jit_solution(6753923231263912512)
XLA Ops:
  7.2 79.3 %shard_map.263 = (bf16[4,2,2,2,48,1536]{5,4,3,2,1,0:T(8,128)(2,1)S(1)}, bf16[4,2,2,2,48,128]{5,4,3,2,1,0:T(8,128)(2,1)S(1)}, bf16[4,2,2,2,48,1536]{5,4,3,2,1,0:T...) custom-call(bf16[16,7296]{1,0:T(8,128)(2,1)S(1)} %concatenate.10.sha, ...), custom_call_target="tpu_custom_call" | custom-call | bytes 200000000 | tf_op jit(solution)/shard_map/pallas_call | solution.py:370
  91.5 2.1 copy-done.22
  99.1 23.8 %shard_map.264 = (bf16[8,128,1024]{2,1,0:T(8,128)(2,1)S(1)}, bf16[32,128]{1,0:T(8,128)(2,1)S(1)}) custom-call(bf16[128,1024]{1,0:T(8,128)(2,1)S(1)} %convolution_convert_fusion.8.own_ref, bf16[32,128]{1,0:T(8,128)(2,1)S(1)} %broadcast_in_dim.17.marks_ref), custom_call_target="tpu_custom_call" | custom-call | bytes 70000000 | tf_op jit(solution)/shard_map/pallas_call | solution.py:856
  126.3 3.5 convolution_convert_fusion.2
  129.8 13.2 %all-to-all-start = ((bf16[64,24,1536]{2,1,0:T(8,128)(2,1)}), bf16[64,24,1536]{2,1,0:T(8,128)(2,1)}, u32[]{:S(2)}, u32[]{:S(2)}) async-start(bf16[64,24,1536]{2,1,0:T(8,128)(2,1)} %bitcast.104), calls=%async_computation | async-start | bytes 9437184 | tf_op jit(solution)/shard_map/all_to_all | solution.py:1527
  143.2 3.3 convolution_convert_fusion.7.qkv_ref.refs_9_
  147.5 13.3 %shard_map.265 = (bf16[128,1536]{1,0:T(8,128)(2,1)S(1)}, f32[128,1536]{1,0:T(8,128)S(1)}, bf16[128,1536]{1,0:T(8,128)(2,1)S(1)}, f32[128,128]{1,0:T(8,128)S(1)}, bf16[1536,1664]{1,0:T(8,128)(2,1)}) custom-call(bf16[128,1536]{1,0:T(8,128)(2,1)S(1)} %convolution_convert_fusion.7.qkv_ref.refs_9_, bf16[8,128,1024]{2,1,0:T(8,128)(2,1)S(1)} %copy-done.25, ...), custom_call_target="tpu_custom_call" | custom-call | flops 6000000000 | bytes 20000000 | tf_op jit(solution)/shard_map/pallas_call | solution.py:1012
  165.9 2.6 convolution_convert_fusion.4
  168.5 2.6 convolution_convert_fusion.5
  171.1 2.6 fusion
  179.1 5.0 copy.45
  184.8 15.9 %all-to-all-done.cotangent_in = bf16[64,24,1536]{2,1,0:T(8,128)(2,1)} async-done(((bf16[64,24,1536]{2,1,0:T(8,128)(2,1)}), bf16[64,24,1536]{2,1,0:T(8,128)(2,1)}, u32[]{:S(2)}, u32[]{:S(2)}) %all-to-all-start) | async-done | bytes 4718624 | tf_op jit(solution)/shard_map/all_to_all | solution.py:1527
  200.6 140.6 %shard_map.266 = (bf16[64,24,1664]{2,1,0:T(8,128)(2,1)}, bf16[64,24,1536]{2,1,0:T(8,128)(2,1)}, f32[1536,512]{1,0:T(8,128)}, bf16[1536,512]{1,0:T(8,128)(2,1)}, ...) custom-call(bf16[64,24,1664]{2,1,0:T(8,128)(2,1)} %bitcast.121, bf16[64,24,1536]{2,1,0:T(8,128)(2,1)} %all-to-all-done.cotangent_in, ...), custom_call_target="tpu_custom_call" | custom-call | flops 22000001024 | bytes 300000000 | tf_op jit(solution)/shard_map/pallas_call | solution.py:1181
  341.2 73.5 %shard_map.267 = (f32[128,1536]{1,0:T(8,128)}, bf16[128,1536]{1,0:T(8,128)(2,1)}, bf16[128,128]{1,0:T(8,128)(2,1)}, f32[8,1536]{1,0:T(8,128)}, bf16[128,1536]{1,...) custom-call(bf16[1536,1664]{1,0:T(8,128)(2,1)} %bitcast.122, ...), custom_call_target="tpu_custom_call" | custom-call | flops 10000000000 | bytes 150000000 | tf_op jit(solution)/shard_map/pallas_call | solution.py:1456
  414.8 10.3 %all-to-all-start.1 = ((bf16[64,24,1536]{2,1,0:T(8,128)(2,1)}), bf16[64,24,1536]{2,1,0:T(8,128)(2,1)}, u32[]{:S(2)}, u32[]{:S(2)}) async-start(bf16[64,24,1536]{2,1,0:T(8,128)(2,1)} %get-tuple-element.100), calls=%async_computation.1 | async-start | bytes 9437184 | tf_op jit(solution)/shard_map/all_to_all | solution.py:1527
  425.1 4.1 fusion.56
  431.6 2.8 convolution_convert_fusion.3
  434.4 3.6 convolution_convert_fusion.1
  438.0 3.7 convolution_convert_fusion
  447.5 35.7 %all-to-all-done.1 = bf16[64,24,1536]{2,1,0:T(8,128)(2,1)} async-done(((bf16[64,24,1536]{2,1,0:T(8,128)(2,1)}), bf16[64,24,1536]{2,1,0:T(8,128)(2,1)}, u32[]{:S(2)}, u32[]{:S(2)}) %all-to-all-start.1) | async-done | bytes 4718624 | tf_op jit(solution)/shard_map/all_to_all | solution.py:1527
  483.2 3.2 fusion.21
  486.5 3.9 fusion.2
  491.5 90.8 %shard_map.268 = (f32[16,1536]{1,0:T(8,128)}, f32[16,128]{1,0:T(8,128)}, f32[16,1536]{1,0:T(8,128)}, f32[16,1024]{1,0:T(8,128)}, bf16[1536,512]{1,0:T(8,128)(2,1)}, /*index=5*/bf16[256,1536]{1,0:T(8,128)(2,1)}) custom-call(bf16[4,2,2,2,48,1536]{5,4,3,2,1,0:T(8,128)(2,1)} %bitcast.105, f32[4,2,2,2,48,128]{5,4,3,2,1,0:T(8,128)} %bitcast.111, ...), custom_call_target="tpu_custom_call" | custom-call | flops 1000000000 | bytes 200000000 | tf_op jit(solution)/shard_map/pallas_call | solution.py:764
  582.4 3.4 bitcast_convert_fusion.1
  (179 shorter events, 47.1 us)
Async XLA Ops:
  0.6 96.0 %copy-start = (bf16[128,1536]{1,0:T(8,128)(2,1)S(1)}, bf16[128,1536]{1,0:T(8,128)(2,1)}, u32[]{:S(2)}) copy-start(bf16[128,1536]{1,0:T(8,128)(2,1)} %tokens_ref.1) | copy-start | bytes 1179652
  0.7 96.8 %copy-start.60 = (s32[128,6]{0,1:T(8,128)S(1)}, s32[128,6]{0,1:T(8,128)}, u32[]{:S(2)}) copy-start(s32[128,6]{0,1:T(8,128)} %param.18) | copy-start | bytes 9220
  3.8 93.1 %copy-start.62 = (s32[128]{0:T(128)S(1)}, s32[128]{0:T(128)}, u32[]{:S(2)}) copy-start(s32[128]{0:T(128)} %param.17) | copy-start | bytes 1540
  96.4 30.0 %copy-start.1 = (bf16[4,2,2,2,48,1536]{5,4,3,2,1,0:T(8,128)(2,1)}, bf16[4,2,2,2,48,1536]{5,4,3,2,1,0:T(8,128)(2,1)S(1)}, u32[]{:S(2)}) copy-start(bf16[4,2,2,2,48,1536]{5,4,3,2,1,0:T(8,128)(2,1)S(1)} %get-tuple-element.68) | copy-start | bytes 14155780
  96.4 30.0 %copy-start.17 = (bf16[4,2,2,2,48,128]{5,4,3,2,1,0:T(8,128)(2,1)}, bf16[4,2,2,2,48,128]{5,4,3,2,1,0:T(8,128)(2,1)S(1)}, u32[]{:S(2)}) copy-start(bf16[4,2,2,2,48,128]{5,4,3,2,1,0:T(8,128)(2,1)S(1)} %get-tuple-element.67) | copy-start | bytes 1179652
  96.4 27.9 %copy-start.46 = (s32[1536]{0:T(1024)S(1)}, s32[1536]{0:T(1024)}, u32[]{:S(2)}) copy-start(s32[1536]{0:T(1024)} %get-tuple-element.134) | copy-start | bytes 18436
  96.4 27.9 %copy-start.58 = (f32[1536]{0:T(1024)S(1)}, f32[1536]{0:T(1024)}, u32[]{:S(2)}) copy-start(f32[1536]{0:T(1024)} %get-tuple-element.135) | copy-start | bytes 18436
  96.7 29.6 %copy-start.33 = (bf16[128,1536]{1,0:T(8,128)(2,1)S(1)}, bf16[128,1536]{1,0:T(8,128)(2,1)}, u32[]{:S(2)}) copy-start(bf16[128,1536]{1,0:T(8,128)(2,1)} %refs_4_.1) | copy-start | bytes 1179652
  97.7 28.6 %copy-start.49 = (pred[128,128]{1,0:T(8,128)(4,1)}, pred[128,128]{1,0:T(8,128)(4,1)S(1)}, u32[]{:S(2)}) copy-start(pred[128,128]{1,0:T(8,128)(4,1)S(1)} %fusion.26) | copy-start | bytes 49156
  97.8 28.5 %copy-start.64 = (bf16[128,128]{1,0:T(8,128)(2,1)}, bf16[128,128]{1,0:T(8,128)(2,1)S(1)}, u32[]{:S(2)}) copy-start(bf16[128,128]{1,0:T(8,128)(2,1)S(1)} %fusion.4) | copy-start | bytes 98308
  124.3 23.1 %copy-start.27 = (bf16[32,128]{1,0:T(8,128)(2,1)}, bf16[32,128]{1,0:T(8,128)(2,1)S(1)}, u32[]{:S(2)}) copy-start(bf16[32,128]{1,0:T(8,128)(2,1)S(1)} %get-tuple-element.72.marks_ref.refs_11_) | copy-start | bytes 24580
  129.8 70.8 %all-to-all-start = ((bf16[64,24,1536]{2,1,0:T(8,128)(2,1)}), bf16[64,24,1536]{2,1,0:T(8,128)(2,1)}, u32[]{:S(2)}, u32[]{:S(2)}) async-start(bf16[64,24,1536]{2,1,0:T(8,128)(2,1)} %bitcast.104), calls=%async_computation | async-start | bytes 9437184 | tf_op jit(solution)/shard_map/all_to_all | solution.py:1527
  146.5 14.3 %copy-start.16 = (bf16[128,1536]{1,0:T(8,128)(2,1)}, bf16[128,1536]{1,0:T(8,128)(2,1)S(1)}, u32[]{:S(2)}) copy-start(bf16[128,1536]{1,0:T(8,128)(2,1)S(1)} %convolution_convert_fusion.7.qkv_ref.refs_9_) | copy-start | bytes 1179652
  147.1 13.8 %copy-start.43 = (bf16[128,1536]{1,0:T(8,128)(2,1)}, bf16[128,1536]{1,0:T(8,128)(2,1)S(1)}, u32[]{:S(2)}) copy-start(bf16[128,1536]{1,0:T(8,128)(2,1)S(1)} %fusion.3.refs_1_) | copy-start | bytes 1179652
  147.4 13.4 %copy-start.19 = (bf16[1536,128]{1,0:T(8,128)(2,1)}, bf16[1536,128]{1,0:T(8,128)(2,1)S(1)}, u32[]{:S(2)}) copy-start(bf16[1536,128]{1,0:T(8,128)(2,1)S(1)} %fusion.16.owner_ref.refs_2_) | copy-start | bytes 1179652
  147.5 13.3 %copy-start.21 = (f32[128,128]{1,0:T(8,128)}, f32[128,128]{1,0:T(8,128)S(1)}, u32[]{:S(2)}) copy-start(f32[128,128]{1,0:T(8,128)S(1)} %broadcast_in_dim.18.segments_ref.refs_12_) | copy-start | bytes 196612
  147.5 15.2 %copy-start.3 = (bf16[4,2,2,2,48,1024]{5,4,3,2,1,0:T(8,128)(2,1)S(1)}, bf16[4,2,2,2,48,1024]{5,4,3,2,1,0:T(8,128)(2,1)}, u32[]{:S(2)}) copy-start(bf16[4,2,2,2,48,1024]{5,4,3,2,1,0:T(8,128)(2,1)} %copy-done.2) | copy-start | bytes 9437188
  160.8 7.7 %copy-start.6 = (bf16[128,1536]{1,0:T(8,128)(2,1)}, bf16[128,1536]{1,0:T(8,128)(2,1)S(1)}, u32[]{:S(2)}) copy-start(bf16[128,1536]{1,0:T(8,128)(2,1)S(1)} %get-tuple-element.74) | copy-start | bytes 1179652
  160.8 14.1 %copy-start.10 = (f32[128,1536]{1,0:T(8,128)}, f32[128,1536]{1,0:T(8,128)S(1)}, u32[]{:S(2)}) copy-start(f32[128,1536]{1,0:T(8,128)S(1)} %get-tuple-element.79.refs_5_) | copy-start | bytes 2359300
  414.8 68.4 %all-to-all-start.1 = ((bf16[64,24,1536]{2,1,0:T(8,128)(2,1)}), bf16[64,24,1536]{2,1,0:T(8,128)(2,1)}, u32[]{:S(2)}, u32[]{:S(2)}) async-start(bf16[64,24,1536]{2,1,0:T(8,128)(2,1)} %get-tuple-element.100), calls=%async_computation.1 | async-start | bytes 9437184 | tf_op jit(solution)/shard_map/all_to_all | solution.py:1527
  445.8 37.4 %copy-start.29 = (f32[128,1536]{1,0:T(8,128)S(1)}, f32[128,1536]{1,0:T(8,128)}, u32[]{:S(2)}) copy-start(f32[128,1536]{1,0:T(8,128)} %get-tuple-element.99) | copy-start | bytes 2359300
  582.4 6.7 %copy-start.54 = (f32[16,1024]{1,0:T(8,128)S(1)}, f32[16,1024]{1,0:T(8,128)}, u32[]{:S(2)}) copy-start(f32[16,1024]{1,0:T(8,128)} %get-tuple-element.113) | copy-start | bytes 196612
  582.4 7.9 %copy-start.52 = (f32[16,1024]{1,0:T(8,128)S(1)}, f32[16,1024]{1,0:T(8,128)}, u32[]{:S(2)}) copy-start(f32[16,1024]{1,0:T(8,128)} %get-tuple-element.115) | copy-start | bytes 196612
  582.4 8.6 %copy-start.51 = (f32[16,1024]{1,0:T(8,128)S(1)}, f32[16,1024]{1,0:T(8,128)}, u32[]{:S(2)}) copy-start(f32[16,1024]{1,0:T(8,128)} %get-tuple-element.116) | copy-start | bytes 196612
  (44 other events, 131.9 us)

commit v4 on v3

--- a/solution.py
+++ b/solution.py
@@ -21,17 +21,15 @@
 MESH_ID = pl.DeviceIdType.MESH
 AXES = ("z", "yl", "core", "yh", "xh", "xl")
 SIZES = (4, 2, 2, 2, 2, 2)
-EXPERT_AXES = ("z", "yl", "yh", "xh", "xl")
-COL_AXES = ("yh", "xh", "xl")
 
 PARTS = (
-    ("outt", 1536, "yzx", "zy"),
+    ("outt", 1536, "yzx", "yzx"),
     ("misc", 128, "yz", "yz"),
     ("q", 1536, "yz", "yz"),
-    ("kv", 1024, "zy", "yz"),
+    ("kv", 1024, "zy", "zy"),
     ("shg", 1024, "yz", "yz"),
     ("shu", 1024, "zy", "zy"),
-    ("shdt", 1024, "zy", "yz"),
+    ("shdt", 1024, "zy", "zy"),
 )
 GATHERED = tuple((name, width, order) for name, width, order, _ in PARTS)
 SUMMED = tuple((name, width, order) for name, width, _, order in PARTS)
@@ -697,17 +695,24 @@
     return own + theirs + near1 + near2 + ends + arrived
 
 
-SHARED_PARTS = [part for part in SUMMED if part[0].startswith("sh")]
-LAST_PARTS = [part for part in SUMMED if not part[0].startswith("sh")]
-
 def last_kernel(*refs):
-    count = len(LAST_PARTS)
+    count = len(SUMMED)
     grads = refs[:count]
     expert_from = refs[count : count + 2]
-    outs = refs[count + 2 : 2 * count + 2]
-    expert_to = refs[2 * count + 2 : 2 * count + 4]
-    scratch = refs[2 * count + 4 : 8 * count + 4]
-    swap_send, swap_recv, swap_local, send_sems, recv_sems, local_sems = refs[8 * count + 4 :]
+    rows_hbm, gates_high_ref, gates_low_ref, forward_ref = refs[count + 2 : count + 6]
+    outs = refs[count + 6 : 2 * count + 6]
+    expert_to = refs[2 * count + 6 : 2 * count + 8]
+    block_ref = refs[2 * count + 8]
+    scratch = refs[2 * count + 9 : 8 * count + 9]
+    (
+        rows_ref,
+        swap_send,
+        swap_recv,
+        swap_local,
+        send_sems,
+        recv_sems,
+        local_sems,
+    ) = refs[8 * count + 9 :]
     me = place()
     partner = {"core": 1 - me["core"], "xl": 1 - lax.axis_index("xl")}
     crossed = me["core"] != lax.axis_index("xl")
@@ -727,7 +732,7 @@
         return pltpu.make_async_copy(expert_from[slot], expert_to[slot], swap_local.at[slot])
 
     wires = Wires(send_sems, recv_sems, local_sems)
-    stages = Summing(wires, me, LAST_PARTS, grads, outs, scratch).stages()
+    stages = Summing(wires, me, SUMMED, grads, outs, scratch).stages()
     next(stages)
     next(stages)
 
@@ -741,6 +746,22 @@
         for slot in range(2):
             kept(slot).start()
 
+    rows_in = wires.copy(rows_hbm, rows_ref)
+    next(stages)
+    next(stages)
+    rows_in.wait()
+    features = block_ref.shape[1]
+    for left in range(0, features, 512):
+        columns = pl.ds(left, 512)
+
+        def mix(step, total):
+            blocks = rows_ref[pl.ds(step * 16, 16), :, columns].astype(F32)
+            rows = blocks.reshape(16 * CAP, 512).astype(BF16)
+            at = pl.ds(pl.multiple_of(step * 16 * CAP, 128), 16 * CAP)
+            return total + dot(gates_high_ref[:, at], rows) + dot(gates_low_ref[:, at], rows)
+
+        mixed = lax.fori_loop(0, EXPERTS // 16, mix, forward_ref[:, columns])
+        block_ref[:, columns] = mixed.astype(BF16)
     for _ in stages:
         pass
     wires.finish()
@@ -757,24 +778,26 @@
             kept(slot).wait()
 
 
-def sum_last(grads, expert_grads):
+def sum_last(grads, expert_grads, rows, gates_high, gates_low, forward_rows):
     anywhere = pl.BlockSpec(memory_space=pl.ANY)
     vmem = pl.BlockSpec(memory_space=pltpu.VMEM)
-    count = len(LAST_PARTS)
+    count = len(SUMMED)
     return pl.pallas_call(
         last_kernel,
-        out_shape=[jax.ShapeDtypeStruct((16, width), F32) for _, width, _ in LAST_PARTS]
-        + [jax.ShapeDtypeStruct(grad.shape, grad.dtype) for grad in expert_grads],
-        in_specs=[anywhere] * (count + 2),
-        out_specs=[vmem] * count + [anywhere] * 2,
-        scratch_shapes=summing_scratch(LAST_PARTS)
+        out_shape=[jax.ShapeDtypeStruct((16, width), F32) for _, width, _ in SUMMED]
+        + [jax.ShapeDtypeStruct(grad.shape, grad.dtype) for grad in expert_grads]
+        + [jax.ShapeDtypeStruct(forward_rows.shape, BF16)],
+        in_specs=[anywhere] * (count + 3) + [vmem] * 3,
+        out_specs=[vmem] * count + [anywhere] * 2 + [vmem],
+        scratch_shapes=summing_scratch(SUMMED)
         + [
+            pltpu.VMEM(rows.shape, BF16),
             pltpu.SemaphoreType.DMA((2,)),
             pltpu.SemaphoreType.DMA((2,)),
             pltpu.SemaphoreType.DMA((2,)),
-            pltpu.SemaphoreType.DMA((140,)),
-            pltpu.SemaphoreType.DMA((140,)),
-            pltpu.SemaphoreType.DMA((32,)),
+            pltpu.SemaphoreType.DMA((190,)),
+            pltpu.SemaphoreType.DMA((190,)),
+            pltpu.SemaphoreType.DMA((48,)),
         ],
         compiler_params=pltpu.CompilerParams(
             collective_id=1, has_side_effects=True, vmem_limit_bytes=56 * 1024 * 1024
@@ -782,7 +805,7 @@
         cost_estimate=pl.CostEstimate(
             flops=1_000_000_000, bytes_accessed=200_000_000, transcendentals=0
         ),
-    )(*grads, *expert_grads)
+    )(*grads, *expert_grads, rows, gates_high, gates_low, forward_rows)
 
 
 def col_device(col):
@@ -793,11 +816,112 @@
     return lax.axis_index("yh") * 4 + lax.axis_index("xh") * 2 + lax.axis_index("xl")
 
 
-def later_kernel(own_ref, marks_ref, out_ref, marks_out, send_sems, recv_sems, local_sem):
+VMEM_SPEC = pl.BlockSpec(memory_space=pltpu.VMEM)
+GROUP = QUERY_HEADS // KEY_VALUE_HEADS
+EXTRA = 128
+
+
+def dot(left, right, left_dim=1, right_dim=0):
+    return lax.dot_general(
+        left, right, (((left_dim,), (right_dim,)), ((), ())), preferred_element_type=F32
+    )
+
+
+def rounded_parts(value):
+    first = value.astype(BF16)
+    left = value - first.astype(F32)
+    second = left.astype(BF16)
+    return [first, second, (left - second.astype(F32)).astype(BF16)]
+
+
+def lane_column(index):
+    return (lax.broadcasted_iota(jnp.int32, (16, 128), 1) == index).astype(BF16)
+
+
+def gain_row(misc_ref, index):
+    return dot(lane_column(index), misc_ref[...], 1, 1)[:1]
+
+
+def allowed_pairs(marks_ref, segments_ref, rows, keys):
+    me = col_index()
+    shape = (rows, keys)
+    own = segments_ref[:, :1]
+    first_length = jnp.where(
+        me == 0,
+        jnp.sum((own == 0.0).astype(F32), axis=0, keepdims=True),
+        marks_ref[:1, :1].astype(F32),
+    )
+    last_start = (me * rows).astype(F32) + jnp.sum(
+        (own < 2.0).astype(F32), axis=0, keepdims=True
+    )
+    lowest = jnp.where(own == 0.0, 0.0, jnp.where(own == 1.0, first_length, last_start))
+    key = lax.broadcasted_iota(jnp.int32, shape, 1)
+    query = lax.broadcasted_iota(jnp.int32, shape, 0) + me * rows
+    return (key <= query) & (key.astype(F32) >= lowest)
+
+
+def head_columns(ref, group):
+    width = GROUP * HEAD_SIZE
+    return jnp.concatenate(
+        [
+            ref[:, group * width + head * HEAD_SIZE : group * width + (head + 1) * HEAD_SIZE]
+            for head in range(GROUP)
+        ],
+        axis=0,
+    )
+
+
+def head_weights(queries, keys, allowed):
+    scores = dot(queries, keys, 1, 1) * (HEAD_SIZE ** (-0.5))
+    scores = jnp.where(allowed, scores, -1e30)
+    shifted = jnp.exp(scores - jnp.max(scores, axis=1, keepdims=True))
+    return shifted / jnp.sum(shifted, axis=1, keepdims=True)
+
+
+GROUP_BLOCKS = 16
+MIDDLE_MIB = 52
+
+
+def blocks_of(value):
+    return value.reshape(GROUP_BLOCKS, CAP, value.shape[-1]).astype(BF16)
+
+
+def later_kernel(
+    tokens_ref,
+    misc_ref,
+    marks_ref,
+    query_ref,
+    keyval_ref,
+    slots_ref,
+    cotangent_ref,
+    out_ref,
+    marks_out,
+    normed_ref,
+    queries_ref,
+    rows_out,
+    rows_ref,
+    own_ref,
+    send_sems,
+    recv_sems,
+    local_sem,
+):
     me = col_index()
     rows = own_ref.shape[0]
     tail = marks_ref.shape[0]
     late = pl.ds(rows - tail, tail)
+    features = tokens_ref.shape[1]
+    gain = gain_row(misc_ref, EXPERTS)
+    total = jnp.zeros((rows, 1), F32)
+    for left in range(0, features, 512):
+        piece = tokens_ref[:, left : left + 512].astype(F32)
+        total = total + jnp.sum(piece * piece, axis=1, keepdims=True)
+    scale = lax.rsqrt(total / features + EPSILON)
+    for left in range(0, features, 512):
+        piece = tokens_ref[:, left : left + 512].astype(F32)
+        normed_ref[:, left : left + 512] = (piece * scale * gain[:, left : left + 512]).astype(BF16)
+    normed = normed_ref[...]
+    for left in range(0, own_ref.shape[1], 512):
+        own_ref[:, left : left + 512] = dot(normed, keyval_ref[:, left : left + 512]).astype(BF16)
     greet([col_device(rem(me + far, 8)) for far in range(1, 8)])
 
     def copies(far, first):
@@ -826,8 +950,26 @@
     for far in range(7, 0, -1):
         each(far, False, (me > 0) & (me + far < 8), lambda copy: copy.start())
         each(far, True, me == 0, lambda copy: copy.start())
-    keep = pltpu.make_async_copy(own_ref, out_ref.at[me], local_sem)
+    keep = pltpu.make_async_copy(own_ref, out_ref.at[me], local_sem.at[0])
     keep.start()
+    for left in range(0, queries_ref.shape[1], 512):
+        queries_ref[:, left : left + 512] = dot(normed, query_ref[:, left : left + 512]).astype(
+            BF16
+        )
+    tile = GROUP_BLOCKS * CAP
+
+    def fill(step, carry):
+        slots = slots_ref[pl.ds(pl.multiple_of(step * tile, 128), tile)]
+        blocks = pl.ds(step * GROUP_BLOCKS, GROUP_BLOCKS)
+        for left in range(0, features, 512):
+            rows_ref[blocks, :, left : left + 512] = blocks_of(
+                dot(slots, cotangent_ref[:, left : left + 512])
+            )
+        return carry
+
+    lax.fori_loop(0, EXPERTS // GROUP_BLOCKS, fill, 0)
+    laid = pltpu.make_async_copy(rows_ref, rows_out, local_sem.at[1])
+    laid.start()
 
     @pl.when(me == 0)
     def _():
@@ -849,116 +991,105 @@
         each(far, True, me == far, lambda copy: copy.wait_recv())
         each(far, False, (me > 0) & (me + far < 8), lambda copy: copy.wait_send())
         each(far, True, me == 0, lambda copy: copy.wait_send())
-
-
-def to_later(rows, marks):
+    laid.wait()
+
+
+def to_later(tokens, misc, marks, query_w, keyval_w, slots_down, cotangent):
     vmem = pl.BlockSpec(memory_space=pltpu.VMEM)
+    own = (tokens.shape[0], keyval_w.shape[1])
+    laid = (EXPERTS, CAP, tokens.shape[1])
     return pl.pallas_call(
         later_kernel,
         out_shape=[
-            jax.ShapeDtypeStruct((8,) + rows.shape, rows.dtype),
+            jax.ShapeDtypeStruct((8,) + own, BF16),
             jax.ShapeDtypeStruct(marks.shape, marks.dtype),
+            jax.ShapeDtypeStruct(tokens.shape, BF16),
+            jax.ShapeDtypeStruct((tokens.shape[0], query_w.shape[1]), BF16),
+            jax.ShapeDtypeStruct(laid, BF16),
         ],
-        in_specs=[vmem, vmem],
-        out_specs=[vmem, vmem],
+        in_specs=[vmem] * 7,
+        out_specs=[vmem] * 4 + [pl.BlockSpec(memory_space=pl.ANY)],
         scratch_shapes=[
+            pltpu.VMEM(laid, BF16),
+            pltpu.VMEM(own, BF16),
             pltpu.SemaphoreType.DMA((8, 2)),
             pltpu.SemaphoreType.DMA((8, 2)),
-            pltpu.SemaphoreType.DMA,
+            pltpu.SemaphoreType.DMA((2,)),
         ],
         compiler_params=pltpu.CompilerParams(
-            collective_id=2, has_side_effects=True, vmem_limit_bytes=16 * 1024 * 1024
+            collective_id=2, has_side_effects=True, vmem_limit_bytes=28 * 1024 * 1024
         ),
-        cost_estimate=pl.CostEstimate(flops=0, bytes_accessed=70_000_000, transcendentals=0),
-    )(rows, marks)
-
-
-VMEM_SPEC = pl.BlockSpec(memory_space=pltpu.VMEM)
-GROUP = QUERY_HEADS // KEY_VALUE_HEADS
-EXTRA = 128
-
-
-def dot(left, right, left_dim=1, right_dim=0):
-    return lax.dot_general(
-        left, right, (((left_dim,), (right_dim,)), ((), ())), preferred_element_type=F32
-    )
-
-
-def rounded_parts(value):
-    first = value.astype(BF16)
-    left = value - first.astype(F32)
-    second = left.astype(BF16)
-    return [first, second, (left - second.astype(F32)).astype(BF16)]
-
-
-def lane_column(index):
-    return (lax.broadcasted_iota(jnp.int32, (16, 128), 1) == index).astype(BF16)
-
-
-def gain_row(misc_ref, index):
-    return dot(lane_column(index), misc_ref[...], 1, 1)[:1]
-
-
-def allowed_pairs(marks_ref, segments_ref, rows, keys):
-    me = col_index()
-    shape = (rows, keys)
-    own = segments_ref[:, :1]
-    first_length = jnp.where(
-        me == 0,
-        jnp.sum((own == 0.0).astype(F32), axis=0, keepdims=True),
-        marks_ref[:1, :1].astype(F32),
-    )
-    last_start = (me * rows).astype(F32) + jnp.sum(
-        (own < 2.0).astype(F32), axis=0, keepdims=True
-    )
-    lowest = jnp.where(own == 0.0, 0.0, jnp.where(own == 1.0, first_length, last_start))
-    key = lax.broadcasted_iota(jnp.int32, shape, 1)
-    query = lax.broadcasted_iota(jnp.int32, shape, 0) + me * rows
-    return (key <= query) & (key.astype(F32) >= lowest)
-
-
-def head_columns(ref, group):
-    width = GROUP * HEAD_SIZE
-    return jnp.concatenate(
-        [
-            ref[:, group * width + head * HEAD_SIZE : group * width + (head + 1) * HEAD_SIZE]
-            for head in range(GROUP)
-        ],
-        axis=0,
-    )
-
-
-def head_weights(queries, keys, allowed):
-    scores = dot(queries, keys, 1, 1) * (HEAD_SIZE ** (-0.5))
-    scores = jnp.where(allowed, scores, -1e30)
-    shifted = jnp.exp(scores - jnp.max(scores, axis=1, keepdims=True))
-    return shifted / jnp.sum(shifted, axis=1, keepdims=True)
+        cost_estimate=pl.CostEstimate(
+            flops=1_000_000_000, bytes_accessed=80_000_000, transcendentals=0
+        ),
+    )(tokens, misc, marks, query_w, keyval_w, slots_down, cotangent)
 
 
 def middle_kernel(
-    qkv_ref,
+    queries_ref,
     every_ref,
     marks_ref,
     segments_ref,
     tokens_ref,
-    outt_ref,
     misc_ref,
     named_ref,
     slots_ref,
+    slots_down_ref,
     owner_ref,
+    cotangent_ref,
+    outt_hbm,
+    shgate_hbm,
+    shup_hbm,
+    shdt_hbm,
+    cotangent_rows,
     attended_ref,
     residual_ref,
     normed_ref,
     gates_ref,
-    outgoing_ref,
+    gates_high_ref,
+    gates_low_ref,
+    forward_ref,
+    grad_second_ref,
+    grad_received,
+    outgoing_hbm,
+    grad_shgate_hbm,
+    grad_shup_hbm,
+    grad_shdt_hbm,
+    outt_ref,
+    shgate_ref,
+    shup_ref,
+    shdt_ref,
+    grad_shgate,
+    grad_shup,
+    grad_shdt,
+    outgoing,
+    send_sems,
+    recv_sems,
+    local_sems,
 ):
     rows, features = tokens_ref.shape
     width = KEY_VALUE_HEADS * HEAD_SIZE
     keys_count = 8 * rows
+    spot = place()
+    chips = [chip_at(spot, offset) for offset in OFFSETS]
+    mine = chip_at(spot, (0, 0, 0))[1]
+    greet([where for where, _ in chips])
+    wires = Wires(send_sems, recv_sems, local_sems)
+    travelling = [
+        wires.remote(cotangent_rows.at[holder], grad_received.at[mine], where)
+        for where, holder in chips
+    ]
+    staying = [wires.copy(cotangent_rows.at[mine], grad_received.at[mine])]
+    outt_in = wires.copy(outt_hbm, outt_ref)
+    shared_in = [
+        wires.copy(shgate_hbm, shgate_ref),
+        wires.copy(shup_hbm, shup_ref),
+        wires.copy(shdt_hbm, shdt_ref),
+    ]
     allowed = allowed_pairs(marks_ref, segments_ref, rows, keys_count)
     allowed = jnp.concatenate([allowed.astype(F32)] * GROUP, axis=0) > 0.5
     for group in range(KEY_VALUE_HEADS):
-        queries = head_columns(qkv_ref, group)
+        queries = head_columns(queries_ref, group)
         columns = pl.ds(group * HEAD_SIZE, HEAD_SIZE)
         keys = every_ref[:, :, columns].reshape(keys_count, HEAD_SIZE)
         values = every_ref[:, :, pl.ds(width + group * HEAD_SIZE, HEAD_SIZE)].reshape(
@@ -970,6 +1101,7 @@
             at = (group * GROUP + head) * HEAD_SIZE
             attended_ref[:, at : at + HEAD_SIZE] = mixed[head * rows : (head + 1) * rows]
     attended = attended_ref[...]
+    outt_in.wait()
     total = jnp.zeros((rows, 1), F32)
     for left in range(0, features, 512):
         piece = tokens_ref[:, left : left + 512].astype(F32) + dot(
@@ -987,28 +1119,84 @@
     gates = chosen_exp / jnp.sum(chosen_exp, axis=1, keepdims=True)
     gates_ref[...] = gates
     parts = jnp.concatenate(rounded_parts(gates), axis=1)
-
-    def send_rows(step, carry):
-        at = pl.ds(pl.multiple_of(step * 256, 256), 256)
-        slots = slots_ref[at]
-        outgoing_ref[at, :features] = dot(slots, normed).astype(BF16)
+    tile = GROUP_BLOCKS * CAP
+
+    def fill(step, carry):
+        at = pl.ds(pl.multiple_of(step * tile, 128), tile)
+        blocks = pl.ds(step * GROUP_BLOCKS, GROUP_BLOCKS)
+        slots = slots_down_ref[at]
+        for left in range(0, features, 512):
+            outgoing[blocks, :, left : left + 512] = blocks_of(
+                dot(slots, normed_ref[:, left : left + 512])
+            )
         gate_parts = dot(slots, parts)
         owner = owner_ref[at].astype(F32)
-        lane = lax.broadcasted_iota(jnp.int32, (256, EXTRA), 1)
-        extra = jnp.zeros((256, EXTRA), F32)
+        lane = lax.broadcasted_iota(jnp.int32, (tile, EXTRA), 1)
+        extra = jnp.zeros((tile, EXTRA), F32)
         for part in range(3):
             column = jnp.sum(
                 gate_parts[:, part * 128 : (part + 1) * 128] * owner, axis=1, keepdims=True
             )
             extra = jnp.where(lane == part, column, extra)
-        outgoing_ref[at, features:] = extra.astype(BF16)
+        outgoing[blocks, :, features:] = blocks_of(extra)
         return carry
 
-    lax.fori_loop(0, slots_ref.shape[0] // 256, send_rows, 0)
-
-
-def middle(qkv, every, marks, segments, tokens, outt, misc, named, slots, owner):
+    lax.fori_loop(0, EXPERTS // GROUP_BLOCKS, fill, 0)
+    staying.append(wires.copy(outgoing, outgoing_hbm))
+
+    slot_gates = jnp.zeros((rows, slots_ref.shape[1]), F32)
+    for part in range(3):
+        slot_gates = slot_gates + dot(
+            parts[:, part * 128 : (part + 1) * 128], owner_ref[...], 1, 1
+        )
+    slot_gates = slot_gates * slots_ref[...].astype(F32)
+    gates_high = slot_gates.astype(BF16)
+    gates_high_ref[...] = gates_high
+    gates_low_ref[...] = (slot_gates - gates_high.astype(F32)).astype(BF16)
+
+    for copy in shared_in:
+        copy.wait()
+    cotangent = cotangent_ref[...]
+    gate_pre = dot(normed, shgate_ref[...])
+    up_pre = dot(normed, shup_ref[...])
+    sigmoid = 1.0 / (1.0 + jnp.exp(-gate_pre))
+    silu = gate_pre * sigmoid
+    hidden = (silu * up_pre).astype(BF16)
+    grad_hidden = dot(cotangent, shdt_ref[...])
+    grad_gate = (
+        grad_hidden * up_pre * sigmoid * (1.0 + gate_pre * (1.0 - sigmoid))
+    ).astype(BF16)
+    grad_up = (grad_hidden * silu).astype(BF16)
+    for left in range(0, features, 512):
+        columns = pl.ds(left, 512)
+        forward_ref[:, columns] = residual_ref[:, columns] + dot(hidden, shdt_ref[columns], 1, 1)
+        grad_second_ref[:, columns] = dot(grad_gate, shgate_ref[columns], 1, 1) + dot(
+            grad_up, shup_ref[columns], 1, 1
+        )
+        grad_shgate[columns] = dot(normed_ref[:, columns], grad_gate, 0, 0).astype(BF16)
+        grad_shup[columns] = dot(normed_ref[:, columns], grad_up, 0, 0).astype(BF16)
+        grad_shdt[columns] = dot(cotangent_ref[:, columns], hidden, 0, 0).astype(BF16)
+    staying += [
+        wires.copy(grad_shgate, grad_shgate_hbm),
+        wires.copy(grad_shup, grad_shup_hbm),
+        wires.copy(grad_shdt, grad_shdt_hbm),
+    ]
+    for copy in staying:
+        copy.wait()
+    for copy in travelling:
+        copy.wait_recv()
+    wires.finish()
+
+
+def middle(queries, every, marks, segments, tokens, misc, named, slots, slots_down, owner, cotangent,
+           cotangent_rows, outt, shgate, shup, shdt):
     rows, features = tokens.shape
+    slot_count = slots.shape[1]
+    anywhere = pl.BlockSpec(memory_space=pl.ANY)
+    inputs = (queries, every, marks, segments, tokens, misc, named, slots, slots_down, owner,
+              cotangent, outt, shgate, shup, shdt)
+    shared = [shgate.shape, shup.shape, shdt.shape]
+    wide = cotangent_rows.shape[:2] + (features + EXTRA,)
     return pl.pallas_call(
         middle_kernel,
         out_shape=[
@@ -1016,27 +1204,46 @@
             jax.ShapeDtypeStruct((rows, features), F32),
             jax.ShapeDtypeStruct((rows, features), BF16),
             jax.ShapeDtypeStruct((rows, 128), F32),
-            jax.ShapeDtypeStruct((slots.shape[0], features + EXTRA), BF16),
+            jax.ShapeDtypeStruct((rows, slot_count), BF16),
+            jax.ShapeDtypeStruct((rows, slot_count), BF16),
+            jax.ShapeDtypeStruct((rows, features), F32),
+            jax.ShapeDtypeStruct((rows, features), F32),
+            jax.ShapeDtypeStruct(cotangent_rows.shape, BF16),
+            jax.ShapeDtypeStruct(wide, BF16),
+        ]
+        + [jax.ShapeDtypeStruct(shape, BF16) for shape in shared],
+        in_specs=[VMEM_SPEC] * 11 + [anywhere] * 5,
+        out_specs=[VMEM_SPEC] * 8 + [anywhere] * 5,
+        scratch_shapes=[pltpu.VMEM(outt.shape, BF16)]
+        + [pltpu.VMEM(shape, BF16) for shape in shared + shared]
+        + [
+            pltpu.VMEM(wide, BF16),
+            pltpu.SemaphoreType.DMA((64,)),
+            pltpu.SemaphoreType.DMA((64,)),
+            pltpu.SemaphoreType.DMA((10,)),
         ],
-        in_specs=[VMEM_SPEC] * 10,
-        out_specs=[VMEM_SPEC] * 5,
-        compiler_params=pltpu.CompilerParams(vmem_limit_bytes=48 * 1024 * 1024),
+        compiler_params=pltpu.CompilerParams(
+            collective_id=5, has_side_effects=True, vmem_limit_bytes=MIDDLE_MIB * 1024 * 1024
+        ),
         cost_estimate=pl.CostEstimate(
-            flops=6_000_000_000, bytes_accessed=20_000_000, transcendentals=2_000_000
+            flops=10_000_000_000, bytes_accessed=250_000_000, transcendentals=2_000_000
         ),
-    )(qkv, every, marks, segments, tokens, outt, misc, named, slots, owner)
-
-
-GROUP_BLOCKS = 16
+    )(*inputs, cotangent_rows)
 
 
 def expert_kernel(
     outgoing_ref,
     cotangent_in,
+    weight_hbm,
+    down_hbm,
+    returned_ref,
+    rows_out,
+    own_in_hbm,
+    other_in_hbm,
+    own_down_hbm,
+    other_down_hbm,
     weight_ref,
     down_ref,
-    returned_ref,
-    rows_out,
     own_in_ref,
     other_in_ref,
     own_down_ref,
@@ -1048,8 +1255,6 @@
     hiddens,
     gated,
     rows_staged,
-    other_in,
-    other_down,
     send_sems,
     recv_sems,
     local_sems,
@@ -1059,16 +1264,19 @@
     chips = [chip_at(spot, offset) for offset in OFFSETS]
     sources = [chip_at(spot, offset, -1) for offset in OFFSETS]
     mine = chip_at(spot, (0, 0, 0))[1]
+    holders = [mine] + [holder for _, holder in sources]
+    wires = Wires(send_sems, recv_sems, local_sems)
+    weights_in = [wires.copy(weight_hbm, weight_ref), wires.copy(down_hbm, down_ref)]
     greet([where for where, _ in chips])
-    wires = Wires(send_sems, recv_sems, local_sems)
     rows_in = [wires.copy(outgoing_ref.at[mine], landed.at[0])]
     for number, (where, holder) in enumerate(chips):
         rows_in.append(wires.remote(outgoing_ref.at[holder], landed.at[number + 1], where))
-    holders = [mine] + [holder for _, holder in sources]
     brought = [
         wires.copy(cotangent_in.at[holder], cotangents.at[number])
         for number, holder in enumerate(holders)
     ]
+    for copy in weights_in:
+        copy.wait()
     count = len(holders)
     tile = GROUP_BLOCKS * CAP
     returning = []
@@ -1076,9 +1284,6 @@
     def flat(ref, first, columns):
         blocks = ref[first : first + GROUP_BLOCKS, :, columns].astype(F32)
         return blocks.reshape(tile, blocks.shape[-1]).astype(BF16)
-
-    def blocks_of(value):
-        return value.reshape(GROUP_BLOCKS, CAP, value.shape[-1]).astype(BF16)
 
     for first in range(0, count, GROUP_BLOCKS):
         for number in range(first, first + GROUP_BLOCKS):
@@ -1128,8 +1333,7 @@
                 )
     staged = []
     for index, first in enumerate(range(0, count, GROUP_BLOCKS)):
-        at = pl.ds(first * CAP, tile)
-        group_hidden = hiddens[at]
+        group_hidden = hiddens[pl.ds(first * CAP, tile)]
         slot = index % 2
         if index >= 2:
             for copy in staged[index - 2]:
@@ -1145,28 +1349,30 @@
                 for number in range(GROUP_BLOCKS)
             ]
         )
-        for left in range(0, features, 512):
-            columns = pl.ds(left, 512)
-            rows = flat(landed, first, columns)
-            own = dot(rows, grads[at, : 2 * HALF], 0, 0)
-            other = dot(rows, grads[at, 2 * HALF :], 0, 0)
-            rows = flat(cotangents, first, columns)
-            own_down = dot(gated[at, :HALF], rows, 0, 0)
-            other_part = dot(gated[at, HALF:], rows, 0, 0)
-            if index > 0:
-                own = own + own_in_ref[columns]
-                other = other + other_in[columns]
-                own_down = own_down + own_down_ref[:, columns]
-                other_part = other_part + other_down[:, columns]
-            own_in_ref[columns] = own
-            own_down_ref[:, columns] = own_down
-            if first + GROUP_BLOCKS == count:
-                other_in_ref[columns] = other.astype(BF16)
-                other_down_ref[:, columns] = other_part.astype(BF16)
-            else:
-                other_in[columns] = other
-                other_down[:, columns] = other_part
-    for copies in staged[-2:]:
+
+    def every_row(ref, columns):
+        return ref[:, :, columns].astype(F32).reshape(count * CAP, 256).astype(BF16)
+
+    def weight_gradients(step, carry):
+        columns = pl.ds(pl.multiple_of(step * 256, 256), 256)
+        rows = every_row(landed, columns)
+        own_in_ref[columns] = dot(rows, grads[:, : 2 * HALF], 0, 0)
+        other_in_ref[columns] = dot(rows, grads[:, 2 * HALF :], 0, 0).astype(BF16)
+        rows = every_row(cotangents, columns)
+        own_down_ref[:, columns] = dot(gated[:, :HALF], rows, 0, 0)
+        other_down_ref[:, columns] = dot(gated[:, HALF:], rows, 0, 0).astype(BF16)
+        return carry
+
+    lax.fori_loop(0, features // 256, weight_gradients, 0)
+    staged.append(
+        [
+            wires.copy(own_in_ref, own_in_hbm),
+            wires.copy(other_in_ref, other_in_hbm),
+            wires.copy(own_down_ref, own_down_hbm),
+            wires.copy(other_down_ref, other_down_hbm),
+        ]
+    )
+    for copies in staged[-3:]:
         for copy in copies:
             copy.wait()
     kept.wait()
@@ -1188,9 +1394,15 @@
             jax.ShapeDtypeStruct((HALF, features), F32),
             jax.ShapeDtypeStruct((HALF, features), BF16),
         ],
-        in_specs=[anywhere, anywhere, VMEM_SPEC, VMEM_SPEC],
-        out_specs=[anywhere, anywhere] + [VMEM_SPEC] * 4,
+        in_specs=[anywhere] * 4,
+        out_specs=[anywhere] * 6,
         scratch_shapes=[
+            pltpu.VMEM(weight.shape, BF16),
+            pltpu.VMEM(down.shape, BF16),
+            pltpu.VMEM((features, 2 * HALF), F32),
+            pltpu.VMEM((features, 2 * HALF), BF16),
+            pltpu.VMEM((HALF, features), F32),
+            pltpu.VMEM((HALF, features), BF16),
             pltpu.VMEM(outgoing.shape, BF16),
             pltpu.VMEM(grad_received.shape, BF16),
             pltpu.VMEM(outgoing.shape, BF16),
@@ -1198,14 +1410,12 @@
             pltpu.VMEM((count * cap, 2 * HALF), BF16),
             pltpu.VMEM((count * cap, 2 * HALF), BF16),
             pltpu.VMEM((2, GROUP_BLOCKS, cap, features), BF16),
-            pltpu.VMEM((features, 2 * HALF), F32),
-            pltpu.VMEM((HALF, features), F32),
             pltpu.SemaphoreType.DMA((128,)),
             pltpu.SemaphoreType.DMA((128,)),
-            pltpu.SemaphoreType.DMA((136,)),
+            pltpu.SemaphoreType.DMA((144,)),
         ],
         compiler_params=pltpu.CompilerParams(
-            collective_id=4, has_side_effects=True, vmem_limit_bytes=58 * 1024 * 1024
+            collective_id=4, has_side_effects=True, vmem_limit_bytes=56 * 1024 * 1024
         ),
         cost_estimate=pl.CostEstimate(
             flops=22_000_000_000, bytes_accessed=300_000_000, transcendentals=1_000_000
@@ -1307,10 +1517,11 @@
     )
 
 
+EARLY_ROWS = 20
+
+
 def rear_kernel(tail, *refs):
-    count = len(SHARED_PARTS)
     (
-        grad_back_ref,
         slots_ref,
         owner_ref,
         gates_ref,
@@ -1318,51 +1529,95 @@
         residual_ref,
         partial_ref,
         misc_ref,
-        outt_ref,
         qkv_ref,
-        every_ref,
         marks_ref,
         segments_ref,
+        attended_ref,
+        normed1_ref,
+        normed2_ref,
+        tokens_ref,
+        grad_back_hbm,
+        outt_hbm,
+        every_hbm,
+        own_in_hbm,
+        own_down_hbm,
+        query_hbm,
+        keyval_hbm,
         in_ref,
         down_ref,
-    ) = refs[:15]
-    grads = refs[15 : 15 + count]
+        rows_ref,
+    ) = refs[:24]
     (
-        grad_residual_ref,
-        grad_low_ref,
-        grad_logits_ref,
-        grad_gain_ref,
-        grad_queries_ref,
-        grad_keyvals_ref,
-        in_out,
-        down_out,
-    ) = refs[15 + count : 23 + count]
-    outs = refs[23 + count : 23 + 2 * count]
-    scratch = refs[23 + 2 * count : 23 + 8 * count]
+        grad_tokens_ref,
+        grad_outt_hbm,
+        grad_query_hbm,
+        grad_keyval_hbm,
+        grad_misc_hbm,
+        half_in_hbm,
+        half_down_hbm,
+        rows_out,
+    ) = refs[24:32]
     (
+        grad_back_ref,
+        outt_ref,
+        every_ref,
+        own_in_ref,
+        own_down_ref,
+        grad_outt_ref,
+        grad_query_ref,
+        grad_keyval_ref,
+        grad_misc_ref,
+        grad_residual,
+        grad_low,
+        grad_logits,
+        grad_gain,
         grad_attended,
+        grad_queries,
+        grad_first,
         blocks_ref,
         landed,
+        query_ref,
+        keyval_ref,
+        their_in,
+        their_down,
         sequence_send,
         sequence_recv,
         send_sems,
         recv_sems,
         local_sems,
-    ) = refs[23 + 8 * count :]
+    ) = refs[32:]
     me = col_index()
     spot = place()
-    rows = cotangent_ref.shape[0]
+    chips = [chip_at(spot, offset) for offset in OFFSETS]
+    mine = chip_at(spot, (0, 0, 0))[1]
+    rows, features = tokens_ref.shape
     late = pl.ds(rows - tail, tail)
     sibling = {"core": 1 - spot["core"]}
-    distant = [col_device(rem(me + far, 8)) for far in range(1, 8)]
-    greet(ring_neighbours(spot) + distant)
+    greet([where for where, _ in chips] + [sibling])
     wires = Wires(send_sems, recv_sems, local_sems)
-    stages = Summing(wires, spot, SHARED_PARTS, grads, outs, scratch).stages()
-    next(stages)
-    arriving = [
-        wires.remote(in_ref, in_out, sibling),
-        wires.remote(down_ref, down_out, sibling),
+    fetched = [
+        wires.copy(grad_back_hbm, grad_back_ref),
+        wires.copy(outt_hbm, outt_ref),
+        wires.copy(every_hbm, every_ref),
+        wires.copy(query_hbm, query_ref),
+        wires.copy(keyval_hbm, keyval_ref),
+        wires.copy(own_in_hbm, own_in_ref),
+        wires.copy(own_down_hbm, own_down_ref),
     ]
+    halves_in = [
+        wires.remote(in_ref, their_in, sibling),
+        wires.remote(down_ref, their_down, sibling),
+    ]
+    kept = wires.copy(rows_ref.at[mine], rows_out.at[mine])
+    returning = []
+
+    def send_rows(start, stop):
+        for where, holder in chips[start:stop]:
+            returning.append(wires.remote(rows_ref.at[holder], rows_out.at[mine], where))
+
+    send_rows(0, EARLY_ROWS)
+    for fetch in fetched[:3]:
+        fetch.wait()
     back_to_residual(
         grad_back_ref,
         slots_ref,
@@ -1373,28 +1628,23 @@
         partial_ref,
         misc_ref,
         outt_ref,
-        grad_residual_ref,
-        grad_low_ref,
-        grad_logits_ref,
-        grad_gain_ref,
+        grad_residual,
+        grad_low,
+        grad_logits,
+        grad_gain,
         grad_attended,
     )
-    next(stages)
     allowed = allowed_pairs(marks_ref, segments_ref, rows, 8 * rows)
     allowed = jnp.concatenate([allowed.astype(F32)] * GROUP, axis=0) > 0.5
-
-    def heads(group):
+    for group in range(KEY_VALUE_HEADS):
         back_heads(
-            group, allowed, qkv_ref, every_ref, grad_attended, grad_queries_ref, blocks_ref
-        )
-
-    for group in range(KEY_VALUE_HEADS):
-        heads(group)
-
-    def copy(far, first):
+            group, allowed, qkv_ref, every_ref, grad_attended, grad_queries, blocks_ref
+        )
+
+    def copy(far, first_block):
         block = rem(me + 8 - far, 8)
         source, target = blocks_ref.at[block], landed.at[far]
-        if first:
+        if first_block:
             source, target = blocks_ref.at[0, late], landed.at[far, late]
         return pltpu.make_async_remote_copy(
             src_ref=source,
@@ -1405,14 +1655,15 @@
             device_id_type=MESH_ID,
         )
 
-    def each(far, first, condition, act):
+    def each(far, first_block, condition, act):
         @pl.when(condition)
         def _():
-            act(copy(far, first))
+            act(copy(far, first_block))
 
     for far in range(7, 0, -1):
         each(far, False, me > far, lambda moved: moved.start())
         each(far, True, me == far, lambda moved: moved.start())
+    send_rows(EARLY_ROWS, 63)
 
     @pl.when(me == 0)
     def _():
@@ -1425,71 +1676,155 @@
         def _():
             landed[far] = jnp.zeros(landed.shape[1:], landed.dtype)
 
-    next(stages)
-    next(stages)
+    low, attended, queries = grad_low[...], attended_ref[...], grad_queries[...]
+    for left in range(0, features, 512):
+        columns = pl.ds(left, 512)
+        grad_outt_ref[columns] = dot(grad_low[:, columns], attended, 0, 0).astype(BF16)
+        grad_query_ref[columns] = dot(normed1_ref[:, columns], queries, 0, 0).astype(BF16)
+    stored = [
+        wires.copy(grad_outt_ref, grad_outt_hbm),
+        wires.copy(grad_query_ref, grad_query_hbm),
+    ]
+    for fetch in fetched[3:]:
+        fetch.wait()
+    for left in range(0, features, 512):
+        columns = pl.ds(left, 512)
+        grad_first[:, columns] = dot(queries, query_ref[columns], 1, 1)
+    for copy_in in halves_in:
+        copy_in.wait_recv()
+    for left in range(0, features, 512):
+        columns = pl.ds(left, 512)
+        their_in[columns] = (own_in_ref[columns] + their_in[columns].astype(F32)).astype(BF16)
+        their_down[:, columns] = (
+            own_down_ref[:, columns] + their_down[:, columns].astype(F32)
+        ).astype(BF16)
+    stored += [wires.copy(their_in, half_in_hbm), wires.copy(their_down, half_down_hbm)]
     for far in range(1, 8):
         each(far, False, (me > 0) & (me + far < 8), lambda moved: moved.wait_recv())
         each(far, True, me == 0, lambda moved: moved.wait_recv())
+    grad_keyvals = grad_low.at[:, pl.ds(0, keyval_ref.shape[1])]
     for row in range(0, rows, 16):
         at = pl.ds(row, 16)
         value = blocks_ref[me, at].astype(F32)
         for far in range(1, 8):
             value = value + landed[far, at].astype(F32)
-        grad_keyvals_ref[at] = value.astype(BF16)
-    next(stages)
-    next(stages)
-    next(stages)
+        grad_keyvals[at] = value.astype(BF16)
+    keyvals = grad_keyvals[...]
+    gain = gain_row(misc_ref, EXPERTS)
+    square, inner = jnp.zeros((rows, 1), F32), jnp.zeros((rows, 1), F32)
+    for left in range(0, features, 512):
+        columns = pl.ds(left, 512)
+        grad_keyval_ref[columns] = dot(normed1_ref[:, columns], keyvals, 0, 0).astype(BF16)
+        piece = grad_first[:, columns] + dot(keyvals, keyval_ref[columns], 1, 1)
+        grad_first[:, columns] = piece
+        residual = tokens_ref[:, columns].astype(F32)
+        square = square + jnp.sum(residual * residual, axis=1, keepdims=True)
+        inner = inner + jnp.sum(
+            piece * gain[:, left : left + 512] * residual, axis=1, keepdims=True
+        )
+    stored.append(wires.copy(grad_keyval_ref, grad_keyval_hbm))
+    scale = lax.rsqrt(square / features + EPSILON)
+    cubed = scale * scale * scale * (inner / features)
+    logits = grad_logits[...]
+    one_row = (lax.broadcasted_iota(jnp.int32, (16, 128), 0) == 0).astype(F32)
+    lane = lax.broadcasted_iota(jnp.int32, (16, 128), 1)
+    for left in range(0, features, 512):
+        columns = pl.ds(left, 512)
+        piece = grad_first[:, columns]
+        residual = tokens_ref[:, columns].astype(F32)
+        grad_tokens_ref[:, columns] = (
+            grad_residual[:, columns]
+            + scale * piece * gain[:, left : left + 512]
+            - residual * cubed
+        )
+        total = dot(normed2_ref[:, columns], logits, 0, 0)
+        rows1 = jnp.broadcast_to(
+            jnp.sum(piece * residual * scale, axis=0, keepdims=True), (16, 512)
+        )
+        rows2 = jnp.broadcast_to(grad_gain[:1, columns], (16, 512))
+        for index, gradient in ((EXPERTS, rows1), (EXPERTS + 1, rows2)):
+            spread = (one_row * (lane == index).astype(F32)).astype(BF16)
+            for part in rounded_parts(gradient):
+                total = total + dot(part, spread, 0, 0)
+        grad_misc_ref[columns] = total
+    stored.append(wires.copy(grad_misc_ref, grad_misc_hbm))
     for far in range(1, 8):
         each(far, False, me > far, lambda moved: moved.wait_send())
         each(far, True, me == far, lambda moved: moved.wait_send())
-    for moved in arriving:
+    for copy_out in stored:
+        copy_out.wait()
+    kept.wait()
+    for moved in returning:
         moved.wait_recv()
     wires.finish()
 
 
-def rear(tail, grad_back, slots, owner, gates, cotangent, residual1, partial, misc, outt, qkv, every,
-         marks, segments, expert_in, expert_down, grads):
-    rows, features = cotangent.shape
+def rear(tail, inputs, grad_back, outt, every, own_in, own_down, query_w, keyval_w, expert_in,
+         expert_down, rows_back):
+    rows, features = inputs[3].shape
     anywhere = pl.BlockSpec(memory_space=pl.ANY)
-    inputs = (grad_back, slots, owner, gates, cotangent, residual1, partial, misc, outt, qkv, every,
-              marks, segments)
     return pl.pallas_call(
         functools.partial(rear_kernel, tail),
         out_shape=[
             jax.ShapeDtypeStruct((rows, features), F32),
-            jax.ShapeDtypeStruct((rows, features), BF16),
-            jax.ShapeDtypeStruct((rows, 128), BF16),
-            jax.ShapeDtypeStruct((8, features), F32),
-            jax.ShapeDtypeStruct((rows, features), BF16),
-            jax.ShapeDtypeStruct(every.shape[1:], BF16),
+            jax.ShapeDtypeStruct((features, features), BF16),
+            jax.ShapeDtypeStruct(query_w.shape, BF16),
+            jax.ShapeDtypeStruct(keyval_w.shape, BF16),
+            jax.ShapeDtypeStruct((features, 128), F32),
             jax.ShapeDtypeStruct(expert_in.shape, BF16),
             jax.ShapeDtypeStruct(expert_down.shape, BF16),
-        ]
-        + [jax.ShapeDtypeStruct((16, width), F32) for _, width, _ in SHARED_PARTS],
-        in_specs=[VMEM_SPEC] * 13 + [anywhere] * (2 + len(SHARED_PARTS)),
-        out_specs=[VMEM_SPEC] * 6 + [anywhere] * 2 + [VMEM_SPEC] * len(SHARED_PARTS),
-        scratch_shapes=summing_scratch(SHARED_PARTS)
-        + [
+            jax.ShapeDtypeStruct(rows_back.shape, BF16),
+        ],
+        in_specs=[VMEM_SPEC] * 14 + [anywhere] * 10,
+        out_specs=[VMEM_SPEC] + [anywhere] * 7,
+        scratch_shapes=[
+            pltpu.VMEM(grad_back.shape, BF16),
+            pltpu.VMEM(outt.shape, BF16),
+            pltpu.VMEM(every.shape, BF16),
+            pltpu.VMEM(own_in.shape, F32),
+            pltpu.VMEM(own_down.shape, F32),
+            pltpu.VMEM((features, features), BF16),
+            pltpu.VMEM(query_w.shape, BF16),
+            pltpu.VMEM(keyval_w.shape, BF16),
+            pltpu.VMEM((features, 128), F32),
+            pltpu.VMEM((rows, features), F32),
             pltpu.VMEM((rows, features), BF16),
+            pltpu.VMEM((rows, 128), BF16),
+            pltpu.VMEM((8, features), F32),
+            pltpu.VMEM((rows, features), BF16),
+            pltpu.VMEM((rows, features), BF16),
+            pltpu.VMEM((rows, features), F32),
             pltpu.VMEM(every.shape, BF16),
             pltpu.VMEM(every.shape, BF16),
+            pltpu.VMEM(query_w.shape, BF16),
+            pltpu.VMEM(keyval_w.shape, BF16),
+            pltpu.VMEM(expert_in.shape, BF16),
+            pltpu.VMEM(expert_down.shape, BF16),
             pltpu.SemaphoreType.DMA((8,)),
             pltpu.SemaphoreType.DMA((8,)),
-            pltpu.SemaphoreType.DMA((140,)),
-            pltpu.SemaphoreType.DMA((140,)),
-            pltpu.SemaphoreType.DMA((32,)),
+            pltpu.SemaphoreType.DMA((66,)),
+            pltpu.SemaphoreType.DMA((66,)),
+            pltpu.SemaphoreType.DMA((16,)),
         ],
         compiler_params=pltpu.CompilerParams(
-            collective_id=3, has_side_effects=True, vmem_limit_bytes=56 * 1024 * 1024
+            collective_id=3, has_side_effects=True, vmem_limit_bytes=58 * 1024 * 1024
         ),
         cost_estimate=pl.CostEstimate(
             flops=10_000_000_000, bytes_accessed=150_000_000, transcendentals=2_000_000
         ),
-    )(*inputs, expert_in, expert_down, *grads)
-
-
-def inverse_rms(residual):
-    return lax.rsqrt(jnp.mean(residual * residual, axis=-1, keepdims=True) + EPSILON)
+    )(
+        *inputs,
+        grad_back,
+        outt,
+        every,
+        own_in,
+        own_down,
+        query_w,
+        keyval_w,
+        expert_in,
+        expert_down,
+        rows_back,
+    )
 
 
 def contract(left_side, right_side, left_dim, right_dim):
@@ -1501,30 +1836,12 @@
     )
 
 
-def gated_unit(gate_pre, up_pre):
-    return jax.nn.silu(gate_pre) * up_pre
-
-
-def norm_backward(residual, norm_scale, gain_row, grad_normed):
-    weighted = grad_normed * gain_row
-    inner_sum = jnp.mean(weighted * residual, axis=-1, keepdims=True)
-    grad_residual = (
-        norm_scale * weighted - residual * norm_scale * norm_scale * norm_scale * inner_sum
-    )
-    grad_gain = jnp.sum(grad_normed * residual * norm_scale, axis=0)
-    return (grad_residual, grad_gain)
-
-
 def expert_of(holder):
     return (holder // 8) * 8 + (holder % 2) * 4 + holder // 2 % 4
 
 
 def packed(grad):
     return grad.reshape(4, 2, 2, 2, 48, grad.shape[-1])
-
-
-def to_experts(rows):
-    return lax.all_to_all(rows, EXPERT_AXES, split_axis=0, concat_axis=0, tiled=True)
 
 
 def shards(
@@ -1567,8 +1884,6 @@
     outt_w, misc_w, query_w, keyval_w, shgate_w, shup_w, shdt_w = [
         gathered.reshape(feature_count, gathered.shape[-1]) for gathered in dense
     ]
-    gain_first = misc_w[:, EXPERTS].astype(F32)
-
     expert_ids = jnp.arange(128, dtype=jnp.int32)
     named = jnp.any(routes[:, :, None] == expert_ids[None, None, :], axis=1)
     named_low = named.astype(BF16)
@@ -1586,149 +1901,114 @@
         contract(owner, rank.astype(BF16), 1, 1) == (slot_ids % CAP + 1).astype(F32)[:, None]
     ).astype(BF16)
 
-    def dispatch(rows):
-        return rows.reshape(EXPERTS, CAP, rows.shape[-1])
-
-    sent_cotangent = dispatch(jnp.dot(slots_down, cotangent, preferred_element_type=F32).astype(BF16))
-    residual0 = tokens.astype(F32)
-    scale_first = inverse_rms(residual0)
-    first_normed = (residual0 * scale_first * gain_first).astype(BF16)
-    query_rows = jnp.dot(first_normed, query_w, preferred_element_type=F32).astype(BF16)
-    keyval_rows = jnp.dot(first_normed, keyval_w, preferred_element_type=F32).astype(BF16)
     own_segments = segments.astype(F32)
     tail = 32
     first_length = jnp.sum((segments == 0).astype(F32)).astype(BF16)
-    every, marks = to_later(
-        keyval_rows, jnp.broadcast_to(first_length, (tail, 128))
+    every, marks, first_normed, query_rows, sent_cotangent = to_later(
+        tokens,
+        misc_w,
+        jnp.broadcast_to(first_length, (tail, 128)),
+        query_w,
+        keyval_w,
+        slots_down,
+        cotangent,
     )
-    sent_cotangent, every = lax.optimization_barrier((sent_cotangent, every))
-    grad_received = to_experts(sent_cotangent)
     segment_tile = jnp.broadcast_to(own_segments[:, None], (local_rows, 128))
-    attended_rows, residual1, second_normed, gates, outgoing = middle(
+    (
+        attended_rows,
+        residual1,
+        second_normed,
+        gates,
+        gates_high,
+        gates_low,
+        forward_rows,
+        grad_second,
+        grad_received,
+        outgoing,
+        grad_shgate,
+        grad_shup,
+        grad_shdt,
+    ) = middle(
         query_rows,
         every,
         marks,
         segment_tile,
         tokens,
-        outt_w,
         misc_w,
         named.astype(F32),
+        slots,
         slots_down,
         owner,
-    )
-    shared_gate = jnp.dot(second_normed, shgate_w, preferred_element_type=F32)
-    shared_up = jnp.dot(second_normed, shup_w, preferred_element_type=F32)
-    shared_hidden = gated_unit(shared_gate, shared_up).astype(BF16)
-    shared_out = contract(shared_hidden, shdt_w, 1, 1)
-    grad_shdt = contract(cotangent, shared_hidden, 0, 0).astype(BF16)
-    grad_shared_hidden = jnp.dot(cotangent, shdt_w, preferred_element_type=F32)
-    unused_shared, pull_shared = jax.vjp(gated_unit, shared_gate, shared_up)
-    grad_shared_gate, grad_shared_up = pull_shared(grad_shared_hidden)
-    grad_shared_gate = grad_shared_gate.astype(BF16)
-    grad_shared_up = grad_shared_up.astype(BF16)
-    grad_shgate = contract(second_normed, grad_shared_gate, 0, 0).astype(BF16)
-    grad_shup = contract(second_normed, grad_shared_up, 0, 0).astype(BF16)
-    grad_second = contract(grad_shared_gate, shgate_w, 1, 1) + contract(
-        grad_shared_up, shup_w, 1, 1
-    )
-
-    forward_rows = residual1 + shared_out
-    slot_gates = slots.astype(F32) * lax.dot_general(
-        gates,
-        owner.astype(F32),
-        (((1,), (1,)), ((), ())),
-        precision=lax.Precision.HIGHEST,
-        preferred_element_type=F32,
-    )
-    gates_high = lax.reduce_precision(slot_gates, exponent_bits=8, mantissa_bits=7)
-    (
-        outgoing,
-        grad_shdt,
-        grad_shgate,
-        grad_shup,
-        grad_second,
-        forward_rows,
-        slot_gates,
-        gates_high,
-    ) = lax.optimization_barrier(
-        (
-            outgoing,
-            grad_shdt,
-            grad_shgate,
-            grad_shup,
-            grad_second,
-            forward_rows,
-            slot_gates,
-            gates_high,
-        )
+        cotangent,
+        sent_cotangent,
+        outt_w,
+        shgate_w,
+        shup_w,
+        shdt_w,
     )
     grad_back, half_out, own_in, other_in, own_down, other_down = expert(
-        dispatch(outgoing), grad_received, expert_w, expert_down
+        outgoing, grad_received, expert_w, expert_down
     )
     grad_back = grad_back.reshape(slot_count, feature_count + EXTRA)
     (
-        grad_residual1,
-        grad_attn_low,
-        grad_logits,
-        grad_gain_second,
-        grad_queries,
-        grad_keyvals,
-        their_in,
-        their_down,
-        sum_shgate,
-        sum_shup,
-        sum_shdt,
+        grad_tokens,
+        grad_outt,
+        grad_query,
+        grad_keyval,
+        grad_misc,
+        half_in,
+        half_down,
+        returned,
     ) = rear(
         tail,
+        (
+            slots,
+            owner,
+            gates,
+            cotangent,
+            residual1,
+            grad_second,
+            misc_w,
+            query_rows,
+            marks,
+            segment_tile,
+            attended_rows,
+            first_normed,
+            second_normed,
+            tokens,
+        ),
         grad_back,
-        slots,
-        owner,
-        gates,
-        cotangent,
-        residual1,
-        grad_second,
-        misc_w,
         outt_w,
-        query_rows,
         every,
-        marks,
-        segment_tile,
+        own_in,
+        own_down,
+        query_w,
+        keyval_w,
         other_in,
         other_down,
-        [packed(grad_shgate), packed(grad_shup), packed(grad_shdt)],
+        half_out,
     )
-    half_out, grad_keyvals = lax.optimization_barrier((half_out, grad_keyvals))
-    returned = to_experts(half_out).reshape(slot_count, feature_count)
-    grad_gain_second = grad_gain_second[0]
-    grad_router = contract(second_normed, grad_logits, 0, 0)
-    grad_outt = contract(grad_attn_low, attended_rows, 0, 0).astype(BF16)
-    half_in = (own_in + their_in.astype(F32)).astype(BF16)
-    half_down = (own_down + their_down.astype(F32)).astype(BF16)
-    grad_query = contract(first_normed, grad_queries, 0, 0).astype(BF16)
-    grad_keyval = contract(first_normed, grad_keyvals, 0, 0).astype(BF16)
-    grad_first = contract(grad_queries, query_w, 1, 1) + contract(grad_keyvals, keyval_w, 1, 1)
-    grad_norm_first, grad_gain_first = norm_backward(residual0, scale_first, gain_first, grad_first)
-    grad_tokens = grad_residual1 + grad_norm_first
-    grad_misc = jnp.concatenate(
+    *summed, half_in, half_down, block_out = sum_last(
         [
-            grad_router[:, :EXPERTS],
-            grad_gain_first[:, None],
-            grad_gain_second[:, None],
-            jnp.zeros((feature_count, 62), F32),
+            packed(grad)
+            for grad in (
+                grad_outt,
+                grad_misc,
+                grad_query,
+                grad_keyval,
+                grad_shgate,
+                grad_shup,
+                grad_shdt,
+            )
         ],
-        axis=1,
-    )
-    expert_mix = jnp.dot(
-        gates_high.astype(BF16), returned, preferred_element_type=F32
-    ) + jnp.dot((slot_gates - gates_high).astype(BF16), returned, preferred_element_type=F32)
-    block_out = (forward_rows + expert_mix).astype(BF16)
-    grad_misc, block_out = lax.optimization_barrier((grad_misc, block_out))
-    *summed, half_in, half_down = sum_last(
-        [packed(grad) for grad in (grad_outt, grad_misc, grad_query, grad_keyval)],
         [half_in, half_down],
+        returned,
+        gates_high,
+        gates_low,
+        forward_rows,
     )
     sum_outt, sum_misc, sum_query, sum_keyval, sum_shgate, sum_shup, sum_shdt = [
-        piece[:12] for piece in (*summed, sum_shgate, sum_shup, sum_shdt)
+        piece[:12] for piece in summed
     ]
     return (
         block_out,

time: 601 us -> 542 us (0.902)
  Pallas kernels: 421 us -> 489 us
  waiting for transfers between devices: 51.5 us -> 0 us
  matrix products: 50.1 us -> 2.71 us
  starting transfers between devices: 23.5 us -> 0 us
    pallas_call x1, Pallas kernels: 13.3 us -> 72.7 us  [middle(): pl.pallas_call(middle_kernel, out_shape=[jax.ShapeDtypeStruct((rows, feat...]
    all_to_all x2 -> x0, waiting for transfers between devices: 51.5 us -> none  [to_experts(): lax.all_to_all(rows, EXPERT_AXES, split_axis=0, concat_axis=0, tiled=True)]
    dot_general x14 -> x2, matrix products: 31.5 us -> 2.56 us  [contract(): lax.dot_general(left_side, right_side, (((left_dim,), (right_dim,)), ((),...]
    all_to_all x2 -> x0, starting transfers between devices: 23.5 us -> none  [to_experts(): lax.all_to_all(rows, EXPERT_AXES, split_axis=0, concat_axis=0, tiled=True)]
    pallas_call x1, Pallas kernels: 73.5 us -> 92.6 us  [rear(): pl.pallas_call(functools.partial(rear_kernel, tail), out_shape=[jax.Shape...]
    dot_general x9 -> x0, matrix products: 18.5 us -> none  [the longest x1 3.92 us: shards(): jnp.dot((slot_gates - gates_high).astype(BF16), returned, preferred_eleme...]
    pallas_call x1, Pallas kernels: 141 us -> 124 us  [expert(): pl.pallas_call(expert_kernel, out_shape=[jax.ShapeDtypeStruct(outgoing.sh...]
    optimization_barrier x2 -> x0, local copies, waits for them, and re-layouts: 6.19 us -> none  [the longest x1 5.04 us: shards(): lax.optimization_barrier((outgoing, grad_shdt, grad_shgate, grad_shup, gr...]
  transfers between devices with their start and end apart: 2 -> 0, of which waited for: 2 -> 0; matrix products, arithmetic and copies ran while one was open for 8% -> 0% of each run, Pallas kernels for 2% -> 0%
where the time goes in v4:
time: 542 us; the launch traced here: 535 us
  Pallas kernels  489 us (90%)
  local copies, waits for them, and re-layouts  33.6 us (6%)
  other arithmetic  8.3 us (2%)
    pallas_call x1, Pallas kernels, expert(): pl.pallas_call(expert_kernel, out_shape=[jax.ShapeDtypeStruct(outgoing.sh...  124 us
    pallas_call x1, Pallas kernels, sum_last(): pl.pallas_call(last_kernel, out_shape=[jax.ShapeDtypeStruct((16, width),...  96.1 us
    pallas_call x1, Pallas kernels, rear(): pl.pallas_call(functools.partial(rear_kernel, tail), out_shape=[jax.Shape...  92.6 us
    pallas_call x1, Pallas kernels, gather_weights(): pl.pallas_call(gather_kernel, out_shape=shapes, in_specs=[pl.BlockSpec(me...  79.3 us
    pallas_call x1, Pallas kernels, middle(): pl.pallas_call(middle_kernel, out_shape=[jax.ShapeDtypeStruct((rows, feat...  72.7 us
    unnamed x75, local copies, waits for them, and re-layouts  25.9 us
    pallas_call x1, Pallas kernels, to_later(): pl.pallas_call(later_kernel, out_shape=[jax.ShapeDtypeStruct((8,) + own,...  24.4 us

profile of v4, /device:TPU:3, one launch (start us, length us, event | category | flops | bytes accessed | tf_op | source)
XLA Modules:
  0.0 535.1 jit_solution(8071676499846265004)
XLA Ops:
  0.7 1.4 fusion.24
  7.0 1.3 fusion.1.slots_ref.slots_down_ref
  8.4 1.2 fusion.slots_ref.refs_0_
  10.6 1.1 copy-done.3
  11.8 1.1 copy-done.4
  12.9 79.3 %shard_map.263 = (bf16[4,2,2,2,48,1536]{5,4,3,2,1,0:T(8,128)(2,1)S(1)}, bf16[4,2,2,2,48,128]{5,4,3,2,1,0:T(8,128)(2,1)S(1)}, bf16[4,2,2,2,48,1536]{5,4,3,2,1,0:T...) custom-call(bf16[16,7296]{1,0:T(8,128)(2,1)S(1)} %concatenate.7.shar, ...), custom_call_target="tpu_custom_call" | custom-call | bytes 200000000 | tf_op jit(solution)/shard_map/pallas_call | solution.py:368
  92.2 2.1 copy-done.12
  94.4 1.8 copy-done.14
  96.1 1.7 copy-done.15
  97.9 1.6 copy-done.16
  99.5 1.6 copy-done.17
  101.2 1.1 copy-done.19
  102.3 24.4 %shard_map.264 = (bf16[8,128,1024]{2,1,0:T(8,128)(2,1)S(1)}, bf16[32,128]{1,0:T(8,128)(2,1)S(1)}, bf16[128,1536]{1,0:T(8,128)(2,1)S(1)}, bf16[128,1536]{1,0:T(8,128)(2,1)S(1)}, bf16[64,24,1536]{2,1,0:T(8,128)(2,1)S(1)}) custom-call(bf16[128,1536]{1,0:T(8,128)(2,1)S(1)} %copy-done.7, bf16[1536,128]{1,0:T(8,128)(2,1)S(1)} %bitcast.50, ...), custom_call_target="tpu_custom_call" | custom-call | flops 1000000000 | bytes 80000000 | tf_op jit(solution)/shard_map/pallas_call | solution.py:1001
  126.8 2.1 copy-done.13
  128.9 1.4 copy-done.18
  131.8 72.7 %shard_map.265 = (bf16[128,1536]{1,0:T(8,128)(2,1)S(1)}, f32[128,1536]{1,0:T(8,128)}, bf16[128,1536]{1,0:T(8,128)(2,1)S(1)}, f32[128,128]{1,0:T(8,128)S(1)}, bf1...) custom-call(bf16[128,1536]{1,0:T(8,128)(2,1)} %copy-done.21, ...), custom_call_target="tpu_custom_call" | custom-call | flops 10000000000 | bytes 250000000 | tf_op jit(solution)/shard_map/pallas_call | solution.py:1200
  208.2 124.2 %shard_map.266 = (bf16[64,24,1664]{2,1,0:T(8,128)(2,1)}, bf16[64,24,1536]{2,1,0:T(8,128)(2,1)}, f32[1536,512]{1,0:T(8,128)}, bf16[1536,512]{1,0:T(8,128)(2,1)}, ...) custom-call(bf16[64,24,1664]{2,1,0:T(8,128)(2,1)} %get-tuple-element.82.outgoing_ref, ...), custom_call_target="tpu_custom_call" | custom-call | flops 22000001024 | bytes 300000000 | tf_op jit(solution)/shard_map/pallas_call | solution.py:1387
  332.4 92.6 %shard_map.267 = (f32[128,1536]{1,0:T(8,128)}, bf16[1536,1536]{1,0:T(8,128)(2,1)}, bf16[1536,1536]{1,0:T(8,128)(2,1)}, bf16[1536,1024]{1,0:T(8,128)(2,1)}, f32[1...) custom-call(bf16[128,1536]{1,0:T(8,128)(2,1)} %fusion.slots_ref.refs_0_, ...), custom_call_target="tpu_custom_call" | custom-call | flops 10000000000 | bytes 150000000 | tf_op jit(solution)/shard_map/pallas_call | solution.py:1766
  425.0 96.1 %shard_map.268 = (f32[16,1536]{1,0:T(8,128)}, f32[16,128]{1,0:T(8,128)}, f32[16,1536]{1,0:T(8,128)}, f32[16,1024]{1,0:T(8,128)}, f32[16,1024]{1,0:T(8,128)}, /*i...) custom-call(bf16[4,2,2,2,48,1536]{5,4,3,2,1,0:T(8,128)(2,1)} %bitcas, ...), custom_call_target="tpu_custom_call" | custom-call | flops 1000000000 | bytes 200000000 | tf_op jit(solution)/shard_map/pallas_call | solution.py:785
  521.1 1.5 slice_reduce_fusion
  522.6 1.5 slice_bitcast_fusion.1
  524.1 1.5 slice_bitcast_fusion
  525.6 2.5 bitcast_convert_fusion
  528.2 1.9 bitcast_convert_fusion.1
  (78 shorter events, 16.0 us)
Async XLA Ops:
  0.6 101.7 %copy-start.7 = (bf16[128,1536]{1,0:T(8,128)(2,1)S(1)}, bf16[128,1536]{1,0:T(8,128)(2,1)}, u32[]{:S(2)}) copy-start(bf16[128,1536]{1,0:T(8,128)(2,1)} %refs_13_.1) | copy-start | bytes 1179652
  0.7 10.0 %copy-start.2 = (bf16[1,1536,256]{2,1,0:T(8,128)(2,1)S(1)}, bf16[1,1536,256]{2,1,0:T(8,128)(2,1)}, u32[]{:S(2)}) copy-start(bf16[1,1536,256]{2,1,0:T(8,128)(2,1)} %param.28) | copy-start | bytes 2359300
  6.0 125.8 %copy-start.11 = (f32[128,128]{1,0:T(8,128)}, f32[128,128]{1,0:T(8,128)S(1)}, u32[]{:S(2)}) copy-start(f32[128,128]{1,0:T(8,128)S(1)} %broadcast_in_dim.14.segments_ref.refs_9_) | copy-start | bytes 196612
  7.0 95.3 %copy-start.8 = (bf16[128,1536]{1,0:T(8,128)(2,1)S(1)}, bf16[128,1536]{1,0:T(8,128)(2,1)}, u32[]{:S(2)}) copy-start(bf16[128,1536]{1,0:T(8,128)(2,1)} %refs_3_.1) | copy-start | bytes 1179652
  8.4 118.4 %copy-start.10 = (bf16[1536,128]{1,0:T(8,128)(2,1)}, bf16[1536,128]{1,0:T(8,128)(2,1)S(1)}, u32[]{:S(2)}) copy-start(bf16[1536,128]{1,0:T(8,128)(2,1)S(1)} %fusion.1.slots_ref.slots_down_ref) | copy-start | bytes 1179652
  92.2 2.2 copy-start.12
  94.4 1.8 copy-start.14
  96.1 1.7 copy-start.15
  97.9 1.6 copy-start.16
  99.5 1.6 copy-start.17
  102.3 24.4 %copy-start = (bf16[4,2,2,2,48,1536]{5,4,3,2,1,0:T(8,128)(2,1)}, bf16[4,2,2,2,48,1536]{5,4,3,2,1,0:T(8,128)(2,1)S(1)}, u32[]{:S(2)}) copy-start(bf16[4,2,2,2,48,1536]{5,4,3,2,1,0:T(8,128)(2,1)S(1)} %get-tuple-element.66) | copy-start | bytes 14155780
  102.3 24.4 %copy-start.1 = (bf16[4,2,2,2,48,1024]{5,4,3,2,1,0:T(8,128)(2,1)}, bf16[4,2,2,2,48,1024]{5,4,3,2,1,0:T(8,128)(2,1)S(1)}, u32[]{:S(2)}) copy-start(bf16[4,2,2,2,48,1024]{5,4,3,2,1,0:T(8,128)(2,1)S(1)} %get-tuple-element.67) | copy-start | bytes 9437188
  102.3 24.5 %copy-start.9 = (bf16[4,2,2,2,48,128]{5,4,3,2,1,0:T(8,128)(2,1)}, bf16[4,2,2,2,48,128]{5,4,3,2,1,0:T(8,128)(2,1)S(1)}, u32[]{:S(2)}) copy-start(bf16[4,2,2,2,48,128]{5,4,3,2,1,0:T(8,128)(2,1)S(1)} %get-tuple-element.65) | copy-start | bytes 1179652
  126.8 2.1 copy-start.13
  128.9 1.4 copy-start.18
  131.8 72.7 %copy-start.22 = (bf16[32,128]{1,0:T(8,128)(2,1)}, bf16[32,128]{1,0:T(8,128)(2,1)S(1)}, u32[]{:S(2)}) copy-start(bf16[32,128]{1,0:T(8,128)(2,1)S(1)} %get-tuple-element.70.marks_ref.refs_8_) | copy-start | bytes 24580
  521.1 7.1 %copy-start.26 = (bf16[1536,512]{1,0:T(8,128)(2,1)S(1)}, bf16[1536,512]{1,0:T(8,128)(2,1)}, u32[]{:S(2)}) copy-start(bf16[1536,512]{1,0:T(8,128)(2,1)} %get-tuple-element.114) | copy-start | bytes 4718596
  525.6 4.4 copy-start.28
  528.2 2.7 copy-start.27
  528.2 3.5 copy-start.29
  528.2 4.2 copy-start.33
  528.2 4.8 copy-start.30
  528.2 5.4 %copy-start.32 = (f32[16,1024]{1,0:T(8,128)S(1)}, f32[16,1024]{1,0:T(8,128)}, u32[]{:S(2)}) copy-start(f32[16,1024]{1,0:T(8,128)} %get-tuple-element.111) | copy-start | bytes 196612
  528.2 6.0 %copy-start.31 = (f32[16,1024]{1,0:T(8,128)S(1)}, f32[16,1024]{1,0:T(8,128)}, u32[]{:S(2)}) copy-start(f32[16,1024]{1,0:T(8,128)} %get-tuple-element.112) | copy-start | bytes 196612
  (10 other events, 8.6 us)

commit v5 on v4

--- a/solution.py
+++ b/solution.py
@@ -160,231 +160,6 @@
     yl = slice(None) if "y" in axes else rem(spot["y"], 2)
     yh = slice(None) if "y" in axes else spot["y"] // 2
     return ref.at[z, yl, me["core"], yh, :, columns]
-
-
-def gather_kernel(shard_ref, gate_ref, up_ref, down_ref, *rest):
-    count = len(GATHERED)
-    outs = rest[:count]
-    expert_in, expert_out, landed = rest[count : count + 3]
-    stages = rest[count + 3 : 2 * count + 3]
-    send_sems, recv_sems, local_sems = rest[2 * count + 3 :]
-    me = place()
-    nxt = {axis: rem(me[axis] + 1, 4) for axis in "xyz"}
-    opp = {axis: rem(me[axis] + 2, 4) for axis in "xyz"}
-    prv = {axis: rem(me[axis] + 3, 4) for axis in "xyz"}
-    sibling = {"core": 1 - me["core"]}
-    partner = {"core": 1 - me["core"], "xl": 1 - lax.axis_index("xl")}
-    crossed = me["core"] != lax.axis_index("xl")
-    greet(
-        [device("x", nxt["x"]), device("x", opp["x"]), device("x", prv["x"])]
-        + [device("y", nxt["y"]), device("y", prv["y"])]
-        + [device("z", nxt["z"]), device("z", prv["z"]), sibling, partner]
-    )
-    wires = Wires(send_sems, recv_sems, local_sems)
-    runs, start = [], 0
-    for index, (name, width, order) in enumerate(GATHERED):
-        last_x = len(order) == 3
-        quarter = width // 4 if last_x else width
-        run = {
-            "out": outs[index],
-            "order": order,
-            "width": quarter,
-            "done": "",
-            "stage": stages[index],
-            "start": start,
-            "landed": landed.at[:, :, pl.ds(start, quarter)],
-            "base": me["x"] * quarter if last_x else 0,
-            "first": [],
-            "shared": [],
-        }
-
-        def piece(x):
-            if last_x:
-                return shard_ref.at[:, pl.ds(pl.multiple_of(start + x * quarter, 128), quarter)]
-            return shard_ref.at[:, pl.ds(start, quarter)]
-
-        for where in (nxt, prv, opp):
-            run["first"].append(
-                wires.remote(piece(where["x"]), run["landed"].at[me["x"]], device("x", where["x"]))
-            )
-        run["bring"] = wires.copy(piece(me["x"]), run["landed"].at[me["x"]])
-        runs.append(run)
-        start += width
-
-    whole = [
-        (gate_ref, expert_in.at[:, pl.ds(0, HALF)]),
-        (up_ref, expert_in.at[:, pl.ds(HALF, HALF)]),
-        (down_ref, expert_out.at[pl.ds(0, HALF)]),
-    ]
-
-    def moved(slot):
-        source, target = whole[slot]
-        return pltpu.make_async_remote_copy(
-            src_ref=source,
-            dst_ref=target,
-            send_sem=send_sems.at[EXPERT_SEM + slot],
-            recv_sem=recv_sems.at[EXPERT_SEM + slot],
-            device_id=partner,
-            device_id_type=MESH_ID,
-        )
-
-    def kept(slot):
-        source, target = whole[slot]
-        return pltpu.make_async_copy(source, target, local_sems.at[20 + slot])
-
-    @pl.when(crossed)
-    def _():
-        for slot in range(3):
-            moved(slot).start()
-
-    @pl.when(jnp.logical_not(crossed))
-    def _():
-        for slot in range(3):
-            kept(slot).start()
-
-    def part_columns(run, axis, value, which):
-        base = value * run["width"] if axis == "x" else run["base"]
-        left, size = 0, run["width"]
-        if which is not None:
-            first_half, second_half = halves(run["width"])
-            left, size = (0, first_half) if which == 0 else (first_half, second_half)
-        if isinstance(base, int):
-            return pl.ds(base + left, size)
-        return pl.ds(pl.multiple_of(base + left, 128), size)
-
-    def blocks(run, axis, value, which=None):
-        columns = part_columns(run, axis, value, which)
-        return block_ref(run["out"], run["done"], me, axis, value, columns)
-
-    def begin(run, axis, source=None):
-        target = blocks(run, axis, me[axis])
-        source = target if source is None else source
-        run["forth"] = wires.remote(source, target, device(axis, nxt[axis]))
-        run["back"] = wires.remote(source, target, device(axis, prv[axis]))
-
-    pick = spread_rows((48, 64), False).astype(BF16)
-    for run in runs:
-        run["bring"].wait()
-        for copy in run["first"]:
-            copy.wait_recv()
-        for left in range(0, run["width"], 512):
-            size = min(512, run["width"] - left)
-            left_in = run["start"] + left
-            piece_rows = landed[:, :, left_in : left_in + size].reshape(64, size)
-            run["stage"][:, left : left + size] = jnp.dot(
-                pick, piece_rows, preferred_element_type=F32
-            ).astype(BF16)
-        axis = run["order"][0]
-        begin(run, axis, run["stage"])
-        run["own"] = wires.copy(run["stage"], blocks(run, axis, me[axis]))
-
-    def forward(run, axis):
-        run["forth"].wait_recv()
-        source = blocks(run, axis, prv[axis], 0)
-        run["more"] = [wires.remote(source, source, device(axis, nxt[axis]))]
-        run["back"].wait_recv()
-        if halves(run["width"])[1] > 0:
-            source = blocks(run, axis, nxt[axis], 1)
-            run["more"].append(wires.remote(source, source, device(axis, prv[axis])))
-
-    def share(run, axis, value):
-        source = blocks(run, axis, value)
-        run["shared"].append(wires.remote(source, source, sibling))
-
-    def advance(run, step):
-        axis = run["order"][step]
-        for copy in run["more"]:
-            copy.wait_recv()
-        if step == len(run["order"]) - 1:
-            share(run, axis, opp[axis])
-            return
-        if step == 0:
-            run["own"].wait()
-        run["done"] = run["done"] + axis
-        following = run["order"][step + 1]
-        begin(run, following)
-        if step + 1 == len(run["order"]) - 1:
-            share(run, following, me[following])
-
-    def last_forward(run):
-        axis = run["order"][-1]
-        forward(run, axis)
-        share(run, axis, prv[axis])
-        share(run, axis, nxt[axis])
-
-    threes = [run for run in runs if len(run["order"]) == 3]
-    twos = [run for run in runs if len(run["order"]) == 2]
-    for run in runs:
-        forward(run, run["order"][0])
-    for run in runs:
-        advance(run, 0)
-    for run in threes:
-        forward(run, run["order"][1])
-    for run in threes:
-        advance(run, 1)
-    for run in twos:
-        last_forward(run)
-    for run in threes:
-        last_forward(run)
-
-    @pl.when(crossed)
-    def _():
-        for slot in range(3):
-            moved(slot).wait_recv()
-
-    @pl.when(jnp.logical_not(crossed))
-    def _():
-        for slot in range(3):
-            kept(slot).wait()
-
-    handed = [
-        wires.remote(
-            expert_in.at[:, pl.ds(0, 2 * HALF)], expert_in.at[:, pl.ds(2 * HALF, 2 * HALF)], sibling
-        ),
-        wires.remote(expert_out.at[pl.ds(0, HALF)], expert_out.at[pl.ds(HALF, HALF)], sibling),
-    ]
-    for run in twos + threes:
-        advance(run, len(run["order"]) - 1)
-    for run in runs:
-        for copy in run["shared"]:
-            copy.wait_recv()
-    for copy in handed:
-        copy.wait_recv()
-    wires.finish()
-
-    @pl.when(crossed)
-    def _():
-        for slot in range(3):
-            moved(slot).wait_send()
-
-
-def gather_weights(shard, gate_w, up_w, down_w):
-    shapes = [jax.ShapeDtypeStruct((4, 2, 2, 2, 48, width), BF16) for _, width, _ in GATHERED]
-    shapes += [
-        jax.ShapeDtypeStruct((gate_w.shape[0], 4 * HALF), BF16),
-        jax.ShapeDtypeStruct((2 * HALF, down_w.shape[1]), BF16),
-    ]
-    anywhere = pl.BlockSpec(memory_space=pl.ANY)
-    return pl.pallas_call(
-        gather_kernel,
-        out_shape=shapes,
-        in_specs=[pl.BlockSpec(memory_space=pltpu.VMEM)] + [anywhere] * 3,
-        out_specs=[anywhere] * (len(GATHERED) + 2),
-        scratch_shapes=[pltpu.VMEM((4, 16, TOTAL), BF16)]
-        + [
-            pltpu.VMEM((48, width // 4 if len(order) == 3 else width), BF16)
-            for _, width, order in GATHERED
-        ]
-        + [
-            pltpu.SemaphoreType.DMA((EXPERT_SEM + 4,)),
-            pltpu.SemaphoreType.DMA((EXPERT_SEM + 4,)),
-            pltpu.SemaphoreType.DMA((24,)),
-        ],
-        compiler_params=pltpu.CompilerParams(
-            collective_id=0, has_side_effects=True, vmem_limit_bytes=16 * 1024 * 1024
-        ),
-        cost_estimate=pl.CostEstimate(flops=0, bytes_accessed=200_000_000, transcendentals=0),
-    )(shard, gate_w, up_w, down_w)
 
 
 class Summing:
@@ -734,20 +509,7 @@
     wires = Wires(send_sems, recv_sems, local_sems)
     stages = Summing(wires, me, SUMMED, grads, outs, scratch).stages()
     next(stages)
-    next(stages)
-
-    @pl.when(crossed)
-    def _():
-        for slot in range(2):
-            moved(slot).start()
-
-    @pl.when(jnp.logical_not(crossed))
-    def _():
-        for slot in range(2):
-            kept(slot).start()
-
     rows_in = wires.copy(rows_hbm, rows_ref)
-    next(stages)
     next(stages)
     rows_in.wait()
     features = block_ref.shape[1]
@@ -762,6 +524,18 @@
 
         mixed = lax.fori_loop(0, EXPERTS // 16, mix, forward_ref[:, columns])
         block_ref[:, columns] = mixed.astype(BF16)
+    next(stages)
+
+    @pl.when(crossed)
+    def _():
+        for slot in range(2):
+            moved(slot).start()
+
+    @pl.when(jnp.logical_not(crossed))
+    def _():
+        for slot in range(2):
+            kept(slot).start()
+
     for _ in stages:
         pass
     wires.finish()
@@ -838,8 +612,8 @@
     return (lax.broadcasted_iota(jnp.int32, (16, 128), 1) == index).astype(BF16)
 
 
-def gain_row(misc_ref, index):
-    return dot(lane_column(index), misc_ref[...], 1, 1)[:1]
+def gain_row(misc, index):
+    return dot(lane_column(index), misc, 1, 1)[:1]
 
 
 def allowed_pairs(marks_ref, segments_ref, rows, keys):
@@ -879,38 +653,249 @@
 
 
 GROUP_BLOCKS = 16
-MIDDLE_MIB = 52
+MIDDLE_MIB = 46
 
 
 def blocks_of(value):
     return value.reshape(GROUP_BLOCKS, CAP, value.shape[-1]).astype(BF16)
 
 
-def later_kernel(
-    tokens_ref,
-    misc_ref,
-    marks_ref,
-    query_ref,
-    keyval_ref,
-    slots_ref,
-    cotangent_ref,
-    out_ref,
-    marks_out,
-    normed_ref,
-    queries_ref,
-    rows_out,
-    rows_ref,
-    own_ref,
-    send_sems,
-    recv_sems,
-    local_sem,
+def front_kernel(
+    shard_ref, tokens_ref, cotangent_ref, routes_ref, segments_ref, gate_ref, up_ref, down_ref, *rest
 ):
-    me = col_index()
-    rows = own_ref.shape[0]
+    count = len(GATHERED)
+    results = rest[:count]
+    (
+        expert_in,
+        expert_out,
+        every_ref,
+        marks_out,
+        normed_ref,
+        queries_ref,
+        rows_out,
+        named_ref,
+        slots_ref,
+        slots_down_ref,
+        owner_ref,
+        tile_ref,
+    ) = rest[count : count + 12]
+    rest = rest[count + 12 :]
+    outs = rest[:count]
+    landed = rest[count]
+    stages = rest[count + 1 : 2 * count + 1]
+    (
+        marks_ref,
+        rows_ref,
+        own_ref,
+        sequence_send,
+        sequence_recv,
+        send_sems,
+        recv_sems,
+        local_sems,
+    ) = rest[2 * count + 1 :]
+    me = place()
+    col = col_index()
+    rows, features = tokens_ref.shape
     tail = marks_ref.shape[0]
     late = pl.ds(rows - tail, tail)
-    features = tokens_ref.shape[1]
-    gain = gain_row(misc_ref, EXPERTS)
+    nxt = {axis: rem(me[axis] + 1, 4) for axis in "xyz"}
+    opp = {axis: rem(me[axis] + 2, 4) for axis in "xyz"}
+    prv = {axis: rem(me[axis] + 3, 4) for axis in "xyz"}
+    sibling = {"core": 1 - me["core"]}
+    partner = {"core": 1 - me["core"], "xl": 1 - lax.axis_index("xl")}
+    crossed = me["core"] != lax.axis_index("xl")
+    greet(
+        [device("x", nxt["x"]), device("x", opp["x"]), device("x", prv["x"])]
+        + [device("y", nxt["y"]), device("y", prv["y"])]
+        + [device("z", nxt["z"]), device("z", prv["z"]), sibling, partner]
+        + [col_device(rem(col + far, 8)) for far in range(1, 8)]
+    )
+    wires = Wires(send_sems, recv_sems, local_sems)
+    runs, start = [], 0
+    for index, (name, width, order) in enumerate(GATHERED):
+        last_x = len(order) == 3
+        quarter = width // 4 if last_x else width
+        run = {
+            "name": name,
+            "out": outs[index],
+            "result": results[index],
+            "order": order,
+            "width": quarter,
+            "done": "",
+            "stage": stages[index],
+            "start": start,
+            "landed": landed.at[:, :, pl.ds(start, quarter)],
+            "base": me["x"] * quarter if last_x else 0,
+            "first": [],
+            "shared": [],
+        }
+
+        def piece(x):
+            if last_x:
+                return shard_ref.at[:, pl.ds(pl.multiple_of(start + x * quarter, 128), quarter)]
+            return shard_ref.at[:, pl.ds(start, quarter)]
+
+        for where in (nxt, prv, opp):
+            run["first"].append(
+                wires.remote(piece(where["x"]), run["landed"].at[me["x"]], device("x", where["x"]))
+            )
+        run["bring"] = wires.copy(piece(me["x"]), run["landed"].at[me["x"]])
+        runs.append(run)
+        start += width
+
+    whole = [
+        (gate_ref, expert_in.at[:, pl.ds(0, HALF)]),
+        (up_ref, expert_in.at[:, pl.ds(HALF, HALF)]),
+        (down_ref, expert_out.at[pl.ds(0, HALF)]),
+    ]
+
+    def moved(slot):
+        source, target = whole[slot]
+        return pltpu.make_async_remote_copy(
+            src_ref=source,
+            dst_ref=target,
+            send_sem=send_sems.at[EXPERT_SEM + slot],
+            recv_sem=recv_sems.at[EXPERT_SEM + slot],
+            device_id=partner,
+            device_id_type=MESH_ID,
+        )
+
+    def kept(slot):
+        source, target = whole[slot]
+        return pltpu.make_async_copy(source, target, local_sems.at[28 + slot])
+
+    @pl.when(crossed)
+    def _():
+        for slot in range(3):
+            moved(slot).start()
+
+    @pl.when(jnp.logical_not(crossed))
+    def _():
+        for slot in range(3):
+            kept(slot).start()
+
+    def part_columns(run, axis, value, which):
+        base = value * run["width"] if axis == "x" else run["base"]
+        left, size = 0, run["width"]
+        if which is not None:
+            first_half, second_half = halves(run["width"])
+            left, size = (0, first_half) if which == 0 else (first_half, second_half)
+        if isinstance(base, int):
+            return pl.ds(base + left, size)
+        return pl.ds(pl.multiple_of(base + left, 128), size)
+
+    def blocks(run, axis, value, which=None):
+        columns = part_columns(run, axis, value, which)
+        return block_ref(run["out"], run["done"], me, axis, value, columns)
+
+    def begin(run, axis, source=None):
+        target = blocks(run, axis, me[axis])
+        source = target if source is None else source
+        run["forth"] = wires.remote(source, target, device(axis, nxt[axis]))
+        run["back"] = wires.remote(source, target, device(axis, prv[axis]))
+
+    pick = spread_rows((48, 64), False).astype(BF16)
+    for run in runs:
+        run["bring"].wait()
+        for copy in run["first"]:
+            copy.wait_recv()
+        for left in range(0, run["width"], 512):
+            size = min(512, run["width"] - left)
+            left_in = run["start"] + left
+            piece_rows = landed[:, :, left_in : left_in + size].reshape(64, size)
+            run["stage"][:, left : left + size] = jnp.dot(
+                pick, piece_rows, preferred_element_type=F32
+            ).astype(BF16)
+        axis = run["order"][0]
+        begin(run, axis, run["stage"])
+        run["own"] = wires.copy(run["stage"], blocks(run, axis, me[axis]))
+
+    def forward(run, axis):
+        run["forth"].wait_recv()
+        source = blocks(run, axis, prv[axis], 0)
+        run["more"] = [wires.remote(source, source, device(axis, nxt[axis]))]
+        run["back"].wait_recv()
+        if halves(run["width"])[1] > 0:
+            source = blocks(run, axis, nxt[axis], 1)
+            run["more"].append(wires.remote(source, source, device(axis, prv[axis])))
+
+    def share(run, axis, value):
+        source = blocks(run, axis, value)
+        run["shared"].append(wires.remote(source, source, sibling))
+
+    def advance(run, step):
+        axis = run["order"][step]
+        for copy in run["more"]:
+            copy.wait_recv()
+        if step == len(run["order"]) - 1:
+            share(run, axis, opp[axis])
+            return
+        if step == 0:
+            run["own"].wait()
+        run["done"] = run["done"] + axis
+        following = run["order"][step + 1]
+        begin(run, following)
+        if step + 1 == len(run["order"]) - 1:
+            share(run, following, me[following])
+
+    def last_forward(run):
+        axis = run["order"][-1]
+        forward(run, axis)
+        share(run, axis, prv[axis])
+        share(run, axis, nxt[axis])
+
+    lay_out_routes(routes_ref, named_ref, slots_ref, slots_down_ref, owner_ref)
+    lay_out_segments(segments_ref, tile_ref, marks_ref)
+    threes = [run for run in runs if len(run["order"]) == 3]
+    twos = [run for run in runs if len(run["order"]) == 2]
+    for run in runs:
+        forward(run, run["order"][0])
+    for run in runs:
+        advance(run, 0)
+    for run in threes:
+        forward(run, run["order"][1])
+    for run in threes:
+        advance(run, 1)
+    for run in twos:
+        last_forward(run)
+    for run in threes:
+        last_forward(run)
+
+    @pl.when(crossed)
+    def _():
+        for slot in range(3):
+            moved(slot).wait_recv()
+
+    @pl.when(jnp.logical_not(crossed))
+    def _():
+        for slot in range(3):
+            kept(slot).wait()
+
+    handed = [
+        wires.remote(
+            expert_in.at[:, pl.ds(0, 2 * HALF)], expert_in.at[:, pl.ds(2 * HALF, 2 * HALF)], sibling
+        ),
+        wires.remote(expert_out.at[pl.ds(0, HALF)], expert_out.at[pl.ds(HALF, HALF)], sibling),
+    ]
+    for run in twos + threes:
+        advance(run, len(run["order"]) - 1)
+    stored = []
+
+    def complete(run):
+        for copy in run["shared"]:
+            copy.wait_recv()
+        stored.append(wires.copy(run["out"], run["result"]))
+
+    early = [run for run in runs if run["name"] in ("misc", "q", "kv")]
+    for run in early:
+        complete(run)
+    weights = {run["name"]: run["out"] for run in early}
+
+    def weight_columns(name, columns):
+        value = weights[name][:, :, :, :, :, columns]
+        return value.reshape(features, value.shape[-1])
+
+    gain = gain_row(weight_columns("misc", pl.ds(0, 128)), EXPERTS)
     total = jnp.zeros((rows, 1), F32)
     for left in range(0, features, 512):
         piece = tokens_ref[:, left : left + 512].astype(F32)
@@ -921,20 +906,21 @@
         normed_ref[:, left : left + 512] = (piece * scale * gain[:, left : left + 512]).astype(BF16)
     normed = normed_ref[...]
     for left in range(0, own_ref.shape[1], 512):
-        own_ref[:, left : left + 512] = dot(normed, keyval_ref[:, left : left + 512]).astype(BF16)
-    greet([col_device(rem(me + far, 8)) for far in range(1, 8)])
+        own_ref[:, left : left + 512] = dot(normed, weight_columns("kv", pl.ds(left, 512))).astype(
+            BF16
+        )
 
     def copies(far, first):
-        there = col_device(rem(me + far, 8))
-        pairs = [(own_ref, out_ref.at[me])]
+        there = col_device(rem(col + far, 8))
+        pairs = [(own_ref, every_ref.at[col])]
         if first:
-            pairs = [(own_ref.at[late], out_ref.at[0, late]), (marks_ref, marks_out)]
+            pairs = [(own_ref.at[late], every_ref.at[0, late]), (marks_ref, marks_out)]
         return [
             pltpu.make_async_remote_copy(
                 src_ref=source,
                 dst_ref=target,
-                send_sem=send_sems.at[far, number],
-                recv_sem=recv_sems.at[far, number],
+                send_sem=sequence_send.at[far, number],
+                recv_sem=sequence_recv.at[far, number],
                 device_id=there,
                 device_id_type=MESH_ID,
             )
@@ -948,18 +934,35 @@
                 act(copy)
 
     for far in range(7, 0, -1):
-        each(far, False, (me > 0) & (me + far < 8), lambda copy: copy.start())
-        each(far, True, me == 0, lambda copy: copy.start())
-    keep = pltpu.make_async_copy(own_ref, out_ref.at[me], local_sem.at[0])
-    keep.start()
+        each(far, False, (col > 0) & (col + far < 8), lambda copy: copy.start())
+        each(far, True, col == 0, lambda copy: copy.start())
+    keep = wires.copy(own_ref, every_ref.at[col])
+
+    @pl.when(col == 0)
+    def _():
+        marks_out[...] = marks_ref[...]
+
+    @pl.when(col > 0)
+    def _():
+        every_ref[0, : rows - tail] = jnp.zeros((rows - tail, own_ref.shape[1]), own_ref.dtype)
+
+    for far in range(1, 8):
+
+        @pl.when(col + far < 8)
+        def _():
+            every_ref[col + far] = jnp.zeros(own_ref.shape, own_ref.dtype)
+
+    for run in runs:
+        if run["name"] not in weights:
+            complete(run)
     for left in range(0, queries_ref.shape[1], 512):
-        queries_ref[:, left : left + 512] = dot(normed, query_ref[:, left : left + 512]).astype(
-            BF16
-        )
+        queries_ref[:, left : left + 512] = dot(
+            normed, weight_columns("q", pl.ds(left, 512))
+        ).astype(BF16)
     tile = GROUP_BLOCKS * CAP
 
     def fill(step, carry):
-        slots = slots_ref[pl.ds(pl.multiple_of(step * tile, 128), tile)]
+        slots = slots_down_ref[pl.ds(pl.multiple_of(step * tile, 128), tile)]
         blocks = pl.ds(step * GROUP_BLOCKS, GROUP_BLOCKS)
         for left in range(0, features, 512):
             rows_ref[blocks, :, left : left + 512] = blocks_of(
@@ -968,61 +971,121 @@
         return carry
 
     lax.fori_loop(0, EXPERTS // GROUP_BLOCKS, fill, 0)
-    laid = pltpu.make_async_copy(rows_ref, rows_out, local_sem.at[1])
-    laid.start()
-
-    @pl.when(me == 0)
-    def _():
-        marks_out[...] = marks_ref[...]
-
-    @pl.when(me > 0)
-    def _():
-        out_ref[0, : rows - tail] = jnp.zeros((rows - tail, own_ref.shape[1]), own_ref.dtype)
-
-    for far in range(1, 8):
-
-        @pl.when(me + far < 8)
-        def _():
-            out_ref[me + far] = jnp.zeros(own_ref.shape, own_ref.dtype)
-
+    stored.append(wires.copy(rows_ref, rows_out))
+    for copy in handed:
+        copy.wait_recv()
     keep.wait()
     for far in range(1, 8):
-        each(far, False, me > far, lambda copy: copy.wait_recv())
-        each(far, True, me == far, lambda copy: copy.wait_recv())
-        each(far, False, (me > 0) & (me + far < 8), lambda copy: copy.wait_send())
-        each(far, True, me == 0, lambda copy: copy.wait_send())
-    laid.wait()
-
-
-def to_later(tokens, misc, marks, query_w, keyval_w, slots_down, cotangent):
-    vmem = pl.BlockSpec(memory_space=pltpu.VMEM)
-    own = (tokens.shape[0], keyval_w.shape[1])
-    laid = (EXPERTS, CAP, tokens.shape[1])
+        each(far, False, col > far, lambda copy: copy.wait_recv())
+        each(far, True, col == far, lambda copy: copy.wait_recv())
+        each(far, False, (col > 0) & (col + far < 8), lambda copy: copy.wait_send())
+        each(far, True, col == 0, lambda copy: copy.wait_send())
+    for copy in stored:
+        copy.wait()
+    wires.finish()
+
+    @pl.when(crossed)
+    def _():
+        for slot in range(3):
+            moved(slot).wait_send()
+
+
+def lay_out_routes(routes_ref, named_ref, slots_ref, slots_down_ref, owner_ref):
+    rows = routes_ref.shape[0]
+    count = EXPERTS * CAP
+    expert = lax.broadcasted_iota(jnp.int32, (rows, 128), 1)
+    named = jnp.zeros((rows, 128), F32)
+    for choice in range(TOPK):
+        named = named + (routes_ref[:, choice : choice + 1] == expert).astype(F32)
+    named_ref[...] = named
+    ahead = lax.broadcasted_iota(jnp.int32, (rows, rows), 1) <= lax.broadcasted_iota(
+        jnp.int32, (rows, rows), 0
+    )
+    rank = (dot(ahead.astype(F32).astype(BF16), named.astype(BF16)) * named).astype(BF16)
+
+    def holder_of(slot):
+        return ((slot.astype(F32) + 0.5) * (1.0 / CAP)).astype(jnp.int32)
+
+    slot = lax.broadcasted_iota(jnp.int32, (count, 128), 0)
+    holder = holder_of(slot)
+    owned = (
+        (holder & 56) + (holder & 1) * 4 + ((holder & 6) >> 1)
+        == lax.broadcasted_iota(jnp.int32, (count, 128), 1)
+    )
+    owner = owned.astype(F32).astype(BF16)
+    owner_ref[...] = owner
+    turn = (slot - holder * CAP + 1).astype(F32)
+    slots_down_ref[...] = (dot(owner, rank, 1, 1) == turn).astype(F32).astype(BF16)
+    slot = lax.broadcasted_iota(jnp.int32, (rows, count), 1)
+    turn = (slot - holder_of(slot) * CAP + 1).astype(F32)
+    slots_ref[...] = (dot(rank, owner, 1, 1) == turn).astype(F32).astype(BF16)
+
+
+def lay_out_segments(segments_ref, tile_ref, marks_ref):
+    rows = segments_ref.shape[1]
+    same = lax.broadcasted_iota(jnp.int32, (rows, rows), 0) == lax.broadcasted_iota(
+        jnp.int32, (rows, rows), 1
+    )
+    numbers = jnp.where(same, segments_ref[...].astype(F32), 0.0).astype(BF16)
+    tile = dot(numbers, jnp.ones((rows, 128), BF16))
+    tile_ref[...] = tile
+    length = jnp.sum((tile == 0.0).astype(F32), axis=0, keepdims=True)
+    marks_ref[...] = jnp.broadcast_to(length, marks_ref.shape).astype(BF16)
+
+
+def front(shard, tokens, cotangent, routes, segments, gate_w, up_w, down_w):
+    anywhere = pl.BlockSpec(memory_space=pl.ANY)
+    rows, features = tokens.shape
+    blocks = [(4, 2, 2, 2, 48, width) for _, width, _ in GATHERED]
+    own = (rows, 2 * KEY_VALUE_HEADS * HEAD_SIZE)
+    laid = (EXPERTS, CAP, features)
+    slots = EXPERTS * CAP
+    marks = (32, 128)
     return pl.pallas_call(
-        later_kernel,
-        out_shape=[
+        front_kernel,
+        out_shape=[jax.ShapeDtypeStruct(shape, BF16) for shape in blocks]
+        + [
+            jax.ShapeDtypeStruct((features, 4 * HALF), BF16),
+            jax.ShapeDtypeStruct((2 * HALF, features), BF16),
             jax.ShapeDtypeStruct((8,) + own, BF16),
-            jax.ShapeDtypeStruct(marks.shape, marks.dtype),
+            jax.ShapeDtypeStruct(marks, BF16),
             jax.ShapeDtypeStruct(tokens.shape, BF16),
-            jax.ShapeDtypeStruct((tokens.shape[0], query_w.shape[1]), BF16),
+            jax.ShapeDtypeStruct((rows, QUERY_HEADS * HEAD_SIZE), BF16),
             jax.ShapeDtypeStruct(laid, BF16),
+            jax.ShapeDtypeStruct((rows, 128), F32),
+            jax.ShapeDtypeStruct((rows, slots), BF16),
+            jax.ShapeDtypeStruct((slots, 128), BF16),
+            jax.ShapeDtypeStruct((slots, 128), BF16),
+            jax.ShapeDtypeStruct((rows, 128), F32),
         ],
-        in_specs=[vmem] * 7,
-        out_specs=[vmem] * 4 + [pl.BlockSpec(memory_space=pl.ANY)],
-        scratch_shapes=[
+        in_specs=[VMEM_SPEC] * 5 + [anywhere] * 3,
+        out_specs=[anywhere] * (len(GATHERED) + 2)
+        + [VMEM_SPEC] * 4
+        + [anywhere]
+        + [VMEM_SPEC] * 5,
+        scratch_shapes=[pltpu.VMEM(shape, BF16) for shape in blocks]
+        + [pltpu.VMEM((4, 16, TOTAL), BF16)]
+        + [
+            pltpu.VMEM((48, width // 4 if len(order) == 3 else width), BF16)
+            for _, width, order in GATHERED
+        ]
+        + [
+            pltpu.VMEM(marks, BF16),
             pltpu.VMEM(laid, BF16),
             pltpu.VMEM(own, BF16),
             pltpu.SemaphoreType.DMA((8, 2)),
             pltpu.SemaphoreType.DMA((8, 2)),
-            pltpu.SemaphoreType.DMA((2,)),
+            pltpu.SemaphoreType.DMA((EXPERT_SEM + 4,)),
+            pltpu.SemaphoreType.DMA((EXPERT_SEM + 4,)),
+            pltpu.SemaphoreType.DMA((32,)),
         ],
         compiler_params=pltpu.CompilerParams(
-            collective_id=2, has_side_effects=True, vmem_limit_bytes=28 * 1024 * 1024
+            collective_id=0, has_side_effects=True, vmem_limit_bytes=56 * 1024 * 1024
         ),
         cost_estimate=pl.CostEstimate(
-            flops=1_000_000_000, bytes_accessed=80_000_000, transcendentals=0
+            flops=2_000_000_000, bytes_accessed=250_000_000, transcendentals=0
         ),
-    )(tokens, misc, marks, query_w, keyval_w, slots_down, cotangent)
+    )(shard, tokens, cotangent, routes, segments, gate_w, up_w, down_w)
 
 
 def middle_kernel(
@@ -1110,7 +1173,7 @@
         residual_ref[:, left : left + 512] = piece
         total = total + jnp.sum(piece * piece, axis=1, keepdims=True)
     scale = lax.rsqrt(total / features + EPSILON)
-    normed_ref[...] = (residual_ref[...] * scale * gain_row(misc_ref, EXPERTS + 1)).astype(BF16)
+    normed_ref[...] = (residual_ref[...] * scale * gain_row(misc_ref[...], EXPERTS + 1)).astype(BF16)
     normed = normed_ref[...]
     logits = dot(normed, misc_ref[...])
     named = named_ref[...] > 0.5
@@ -1415,7 +1478,7 @@
             pltpu.SemaphoreType.DMA((144,)),
         ],
         compiler_params=pltpu.CompilerParams(
-            collective_id=4, has_side_effects=True, vmem_limit_bytes=56 * 1024 * 1024
+            collective_id=4, has_side_effects=True, vmem_limit_bytes=48 * 1024 * 1024
         ),
         cost_estimate=pl.CostEstimate(
             flops=22_000_000_000, bytes_accessed=300_000_000, transcendentals=1_000_000
@@ -1451,7 +1514,7 @@
         gates * (grad_gates - jnp.sum(gates * grad_gates, axis=1, keepdims=True))
     ).astype(BF16)
     grad_logits_ref[...] = grad_logits
-    gain = gain_row(misc_ref, EXPERTS + 1)
+    gain = gain_row(misc_ref[...], EXPERTS + 1)
     square, inner = jnp.zeros((rows, 1), F32), jnp.zeros((rows, 1), F32)
     for left in range(0, features, 512):
         columns = pl.ds(left, 512)
@@ -1710,7 +1773,7 @@
             value = value + landed[far, at].astype(F32)
         grad_keyvals[at] = value.astype(BF16)
     keyvals = grad_keyvals[...]
-    gain = gain_row(misc_ref, EXPERTS)
+    gain = gain_row(misc_ref[...], EXPERTS)
     square, inner = jnp.zeros((rows, 1), F32), jnp.zeros((rows, 1), F32)
     for left in range(0, features, 512):
         columns = pl.ds(left, 512)
@@ -1880,40 +1943,35 @@
         axis=1,
     )
     shard = jnp.concatenate([shard, jnp.zeros((4, TOTAL), BF16)], axis=0)
-    *dense, expert_w, expert_down = gather_weights(shard, w_exgate[0], w_exup[0], w_exdown[0])
-    outt_w, misc_w, query_w, keyval_w, shgate_w, shup_w, shdt_w = [
-        gathered.reshape(feature_count, gathered.shape[-1]) for gathered in dense
-    ]
-    expert_ids = jnp.arange(128, dtype=jnp.int32)
-    named = jnp.any(routes[:, :, None] == expert_ids[None, None, :], axis=1)
-    named_low = named.astype(BF16)
-    token_ids = jnp.arange(local_rows, dtype=jnp.int32)
-    before = (token_ids[None, :] <= token_ids[:, None]).astype(BF16)
-    rank = jnp.dot(before, named_low, preferred_element_type=F32) * named.astype(F32)
-    slot_count = EXPERTS * CAP
-    slot_ids = jnp.arange(slot_count, dtype=jnp.int32)
-    holder = slot_ids // CAP
-    slot_expert = expert_of(holder)
-    owner = (slot_expert[:, None] == expert_ids[None, :]).astype(BF16)
-    rank_wide = contract(rank.astype(BF16), owner, 1, 1)
-    slots = (rank_wide == (slot_ids % CAP + 1).astype(F32)[None, :]).astype(BF16)
-    slots_down = (
-        contract(owner, rank.astype(BF16), 1, 1) == (slot_ids % CAP + 1).astype(F32)[:, None]
-    ).astype(BF16)
-
-    own_segments = segments.astype(F32)
     tail = 32
-    first_length = jnp.sum((segments == 0).astype(F32)).astype(BF16)
-    every, marks, first_normed, query_rows, sent_cotangent = to_later(
-        tokens,
+    (
+        outt_w,
         misc_w,
-        jnp.broadcast_to(first_length, (tail, 128)),
         query_w,
         keyval_w,
+        shgate_w,
+        shup_w,
+        shdt_w,
+        expert_w,
+        expert_down,
+        every,
+        marks,
+        first_normed,
+        query_rows,
+        sent_cotangent,
+        named,
+        slots,
         slots_down,
-        cotangent,
-    )
-    segment_tile = jnp.broadcast_to(own_segments[:, None], (local_rows, 128))
+        owner,
+        segment_tile,
+    ) = front(
+        shard, tokens, cotangent, routes, segments[None, :], w_exgate[0], w_exup[0], w_exdown[0]
+    )
+    outt_w, misc_w, query_w, keyval_w, shgate_w, shup_w, shdt_w = [
+        gathered.reshape(feature_count, gathered.shape[-1])
+        for gathered in (outt_w, misc_w, query_w, keyval_w, shgate_w, shup_w, shdt_w)
+    ]
+    slot_count = EXPERTS * CAP
     (
         attended_rows,
         residual1,
@@ -1935,7 +1993,7 @@
         segment_tile,
         tokens,
         misc_w,
-        named.astype(F32),
+        named,
         slots,
         slots_down,
         owner,

time: 542 us -> 556 us (1.026)
  Pallas kernels: 489 us -> 511 us
    pallas_call x1, Pallas kernels: 124 us -> 137 us  [expert(): pl.pallas_call(expert_kernel, out_shape=[jax.ShapeDtypeStruct(outgoing.sh...]
    pallas_call x1, Pallas kernels: 96.1 us -> 105 us  [sum_last(): pl.pallas_call(last_kernel, out_shape=[jax.ShapeDtypeStruct((16, width),...]
    unnamed x75 -> x68, local copies, waits for them, and re-layouts: 25.9 us -> 23.1 us
    pallas_call x2 -> x1, Pallas kernels: 104 us -> 103 us  [front(): pl.pallas_call(front_kernel, out_shape=[jax.ShapeDtypeStruct(shape, BF16)...]
where the time goes in v5:
time: 556 us; the launch traced here: 547 us
  Pallas kernels  511 us (92%)
  local copies, waits for them, and re-layouts  30.8 us (6%)
    pallas_call x1, Pallas kernels, expert(): pl.pallas_call(expert_kernel, out_shape=[jax.ShapeDtypeStruct(outgoing.sh...  137 us
    pallas_call x1, Pallas kernels, sum_last(): pl.pallas_call(last_kernel, out_shape=[jax.ShapeDtypeStruct((16, width),...  105 us
    pallas_call x1, Pallas kernels, front(): pl.pallas_call(front_kernel, out_shape=[jax.ShapeDtypeStruct(shape, BF16)...  103 us
    pallas_call x1, Pallas kernels, rear(): pl.pallas_call(functools.partial(rear_kernel, tail), out_shape=[jax.Shape...  89.8 us
    pallas_call x1, Pallas kernels, middle(): pl.pallas_call(middle_kernel, out_shape=[jax.ShapeDtypeStruct((rows, feat...  76.2 us
    unnamed x68, local copies, waits for them, and re-layouts  23.1 us

profile of v5, /device:TPU:3, one launch (start us, length us, event | category | flops | bytes accessed | tf_op | source)
XLA Modules:
  0.0 547.3 jit_solution(2471484377111225790)
XLA Ops:
  2.1 1.4 copy.35.routes_ref
  3.6 1.0 concatenate.6
  5.3 103.3 %shard_map.263 = (bf16[4,2,2,2,48,1536]{5,4,3,2,1,0:T(8,128)(2,1)}, bf16[4,2,2,2,48,128]{5,4,3,2,1,0:T(8,128)(2,1)}, bf16[4,2,2,2,48,1536]{5,4,3,2,1,0:T(8,128)(...) custom-call(bf16[16,7296]{1,0:T(8,128)(2,1)} %concatenate.7.shard_re, ...), custom_call_target="tpu_custom_call" | custom-call | flops 2000000000 | bytes 250000000 | tf_op jit(solution)/shard_map/pallas_call | solution.py:1044
  108.6 1.0 copy-done.5
  109.6 1.0 copy-done.11
  110.6 1.0 copy-done.12
  111.6 1.0 copy-done.13
  114.1 1.0 copy-done.20
  115.9 76.2 %shard_map.264 = (bf16[128,1536]{1,0:T(8,128)(2,1)S(1)}, f32[128,1536]{1,0:T(8,128)S(1)}, bf16[128,1536]{1,0:T(8,128)(2,1)S(1)}, f32[128,128]{1,0:T(8,128)S(1)},...) custom-call(bf16[128,1536]{1,0:T(8,128)(2,1)S(1)} %copy-done.11, ...), custom_call_target="tpu_custom_call" | custom-call | flops 10000000000 | bytes 250000000 | tf_op jit(solution)/shard_map/pallas_call | solution.py:1263
  192.2 0.9 copy-done
  194.6 0.9 copy-done.8
  195.5 0.9 copy-done.9
  198.5 136.5 %shard_map.265 = (bf16[64,24,1664]{2,1,0:T(8,128)(2,1)}, bf16[64,24,1536]{2,1,0:T(8,128)(2,1)}, f32[1536,512]{1,0:T(8,128)}, bf16[1536,512]{1,0:T(8,128)(2,1)S(1...) custom-call(bf16[64,24,1664]{2,1,0:T(8,128)(2,1)} %get-tuple-element.90.outgoing_ref, ...), custom_call_target="tpu_custom_call" | custom-call | flops 22000001024 | bytes 300000000 | tf_op jit(solution)/shard_map/pallas_call | solution.py:1450
  335.0 1.1 copy-done.6
  336.1 1.1 copy-done.7
  337.3 0.9 copy-done.10
  338.2 89.8 %shard_map.266 = (f32[128,1536]{1,0:T(8,128)}, bf16[1536,1536]{1,0:T(8,128)(2,1)}, bf16[1536,1536]{1,0:T(8,128)(2,1)}, bf16[1536,1024]{1,0:T(8,128)(2,1)}, f32[1...) custom-call(bf16[128,1536]{1,0:T(8,128)(2,1)} %get-tuple-element.70.slots, ...), custom_call_target="tpu_custom_call" | custom-call | flops 10000000000 | bytes 150000000 | tf_op jit(solution)/shard_map/pallas_call | solution.py:1829
  428.0 105.1 %shard_map.267 = (f32[16,1536]{1,0:T(8,128)}, f32[16,128]{1,0:T(8,128)}, f32[16,1536]{1,0:T(8,128)}, f32[16,1024]{1,0:T(8,128)}, f32[16,1024]{1,0:T(8,128)}, /*i...) custom-call(bf16[4,2,2,2,48,1536]{5,4,3,2,1,0:T(8,128)(2,1)} %bitcas, ...), custom_call_target="tpu_custom_call" | custom-call | flops 1000000000 | bytes 200000000 | tf_op jit(solution)/shard_map/pallas_call | solution.py:559
  533.1 1.5 slice_reduce_fusion
  534.6 1.5 slice_bitcast_fusion.1
  536.1 1.5 slice_bitcast_fusion
  537.6 2.5 bitcast_convert_fusion
  540.2 1.9 bitcast_convert_fusion.1
  542.8 0.9 copy.44
  (59 shorter events, 12.2 us)
Async XLA Ops:
  5.3 103.3 %copy-start.3 = (bf16[128,1536]{1,0:T(8,128)(2,1)S(1)}, bf16[128,1536]{1,0:T(8,128)(2,1)}, u32[]{:S(2)}) copy-start(bf16[128,1536]{1,0:T(8,128)(2,1)} %refs_13_.1) | copy-start | bytes 1179652
  5.3 103.3 %copy-start.4 = (bf16[128,1536]{1,0:T(8,128)(2,1)S(1)}, bf16[128,1536]{1,0:T(8,128)(2,1)}, u32[]{:S(2)}) copy-start(bf16[128,1536]{1,0:T(8,128)(2,1)} %refs_3_.1) | copy-start | bytes 1179652
  108.6 1.0 copy-start.5
  109.6 1.0 copy-start.11
  110.6 1.0 copy-start.12
  111.6 1.0 copy-start.13
  112.6 0.8 copy-start.16
  114.1 1.0 copy-start.20
  115.1 0.8 copy-start.21
  115.9 82.5 %copy-start.19 = (bf16[512,1536]{1,0:T(8,128)(2,1)S(1)}, bf16[512,1536]{1,0:T(8,128)(2,1)}, u32[]{:S(2)}) copy-start(bf16[512,1536]{1,0:T(8,128)(2,1)} %get-tuple-element.93.down_hbm) | copy-start | bytes 4718596
  192.2 0.9 copy-start
  194.6 0.9 copy-start.8
  195.5 0.9 copy-start.9
  335.0 1.1 copy-start.6
  336.1 1.1 copy-start.7
  337.3 0.9 copy-start.10
  533.1 7.1 %copy-start.22 = (bf16[1536,512]{1,0:T(8,128)(2,1)S(1)}, bf16[1536,512]{1,0:T(8,128)(2,1)}, u32[]{:S(2)}) copy-start(bf16[1536,512]{1,0:T(8,128)(2,1)} %get-tuple-element.124) | copy-start | bytes 4718596
  537.6 4.4 copy-start.24
  540.1 2.7 copy-start.23
  540.1 3.5 copy-start.25
  540.1 4.2 copy-start.29
  540.1 4.8 copy-start.26
  540.2 5.4 copy-start.28
  540.2 6.0 %copy-start.27 = (f32[16,1024]{1,0:T(8,128)S(1)}, f32[16,1024]{1,0:T(8,128)}, u32[]{:S(2)}) copy-start(f32[16,1024]{1,0:T(8,128)} %get-tuple-element.122) | copy-start | bytes 196612
  (6 other events, 4.3 us)

commit v6 on v5

--- a/solution.py
+++ b/solution.py
@@ -509,7 +509,20 @@
     wires = Wires(send_sems, recv_sems, local_sems)
     stages = Summing(wires, me, SUMMED, grads, outs, scratch).stages()
     next(stages)
+    next(stages)
+
+    @pl.when(crossed)
+    def _():
+        for slot in range(2):
+            moved(slot).start()
+
+    @pl.when(jnp.logical_not(crossed))
+    def _():
+        for slot in range(2):
+            kept(slot).start()
+
     rows_in = wires.copy(rows_hbm, rows_ref)
+    next(stages)
     next(stages)
     rows_in.wait()
     features = block_ref.shape[1]
@@ -524,18 +537,6 @@
 
         mixed = lax.fori_loop(0, EXPERTS // 16, mix, forward_ref[:, columns])
         block_ref[:, columns] = mixed.astype(BF16)
-    next(stages)
-
-    @pl.when(crossed)
-    def _():
-        for slot in range(2):
-            moved(slot).start()
-
-    @pl.when(jnp.logical_not(crossed))
-    def _():
-        for slot in range(2):
-            kept(slot).start()
-
     for _ in stages:
         pass
     wires.finish()
@@ -653,7 +654,7 @@
 
 
 GROUP_BLOCKS = 16
-MIDDLE_MIB = 46
+MIDDLE_MIB = 52
 
 
 def blocks_of(value):
@@ -1478,7 +1479,7 @@
             pltpu.SemaphoreType.DMA((144,)),
         ],
         compiler_params=pltpu.CompilerParams(
-            collective_id=4, has_side_effects=True, vmem_limit_bytes=48 * 1024 * 1024
+            collective_id=4, has_side_effects=True, vmem_limit_bytes=56 * 1024 * 1024
         ),
         cost_estimate=pl.CostEstimate(
             flops=22_000_000_000, bytes_accessed=300_000_000, transcendentals=1_000_000

time: 556 us -> 549 us (0.987)
  local copies, waits for them, and re-layouts: 30.8 us -> 19.9 us
    pallas_call x1, Pallas kernels: 89.8 us -> 101 us  [rear(): pl.pallas_call(functools.partial(rear_kernel, tail), out_shape=[jax.Shape...]
    unnamed x68 -> x40, local copies, waits for them, and re-layouts: 23.1 us -> 12.2 us
    pallas_call x1, Pallas kernels: 105 us -> 96.7 us  [sum_last(): pl.pallas_call(last_kernel, out_shape=[jax.ShapeDtypeStruct((16, width),...]
where the time goes in v6:
time: 549 us; the launch traced here: 541 us
  Pallas kernels  516 us (94%)
  local copies, waits for them, and re-layouts  19.9 us (4%)
    pallas_call x1, Pallas kernels, expert(): pl.pallas_call(expert_kernel, out_shape=[jax.ShapeDtypeStruct(outgoing.sh...  138 us
    pallas_call x1, Pallas kernels, front(): pl.pallas_call(front_kernel, out_shape=[jax.ShapeDtypeStruct(shape, BF16)...  103 us
    pallas_call x1, Pallas kernels, rear(): pl.pallas_call(functools.partial(rear_kernel, tail), out_shape=[jax.Shape...  101 us
    pallas_call x1, Pallas kernels, sum_last(): pl.pallas_call(last_kernel, out_shape=[jax.ShapeDtypeStruct((16, width),...  96.7 us
    pallas_call x1, Pallas kernels, middle(): pl.pallas_call(middle_kernel, out_shape=[jax.ShapeDtypeStruct((rows, feat...  77.6 us
    unnamed x40, local copies, waits for them, and re-layouts  12.2 us

profile of v6, /device:TPU:3, one launch (start us, length us, event | category | flops | bytes accessed | tf_op | source)
XLA Modules:
  0.0 541.4 jit_solution(14633142351228003688)
XLA Ops:
  0.6 0.7 copy.33
  1.4 0.8 copy.34
  2.1 1.4 copy.35.routes_ref
  3.6 1.0 concatenate.6
  4.6 0.7 concatenate.7.shard_ref
  5.3 103.2 %shard_map.263 = (bf16[4,2,2,2,48,1536]{5,4,3,2,1,0:T(8,128)(2,1)}, bf16[4,2,2,2,48,128]{5,4,3,2,1,0:T(8,128)(2,1)}, bf16[4,2,2,2,48,1536]{5,4,3,2,1,0:T(8,128)(...) custom-call(bf16[16,7296]{1,0:T(8,128)(2,1)} %concatenate.7.shard_re, ...), custom_call_target="tpu_custom_call" | custom-call | flops 2000000000 | bytes 250000000 | tf_op jit(solution)/shard_map/pallas_call | solution.py:1045
  108.5 0.8 copy-done.4
  109.4 0.7 copy-done.6
  110.0 0.8 copy-done.7
  110.9 77.6 %shard_map.264 = (bf16[128,1536]{1,0:T(8,128)(2,1)S(1)}, f32[128,1536]{1,0:T(8,128)}, bf16[128,1536]{1,0:T(8,128)(2,1)S(1)}, f32[128,128]{1,0:T(8,128)S(1)}, bf1...) custom-call(bf16[128,1536]{1,0:T(8,128)(2,1)} %get-tuple-element.72., ...), custom_call_target="tpu_custom_call" | custom-call | flops 10000000000 | bytes 250000000 | tf_op jit(solution)/shard_map/pallas_call | solution.py:1264
  188.5 0.7 copy-done
  189.3 0.7 copy-done.1
  190.0 0.7 copy-done.2
  190.8 0.7 copy-done.3
  192.2 137.6 %shard_map.265 = (bf16[64,24,1664]{2,1,0:T(8,128)(2,1)}, bf16[64,24,1536]{2,1,0:T(8,128)(2,1)}, f32[1536,512]{1,0:T(8,128)}, bf16[1536,512]{1,0:T(8,128)(2,1)}, ...) custom-call(bf16[64,24,1664]{2,1,0:T(8,128)(2,1)} %get-tuple-element.90.outgoing_ref, ...), custom_call_target="tpu_custom_call" | custom-call | flops 22000001024 | bytes 300000000 | tf_op jit(solution)/shard_map/pallas_call | solution.py:1451
  329.7 101.0 %shard_map.266 = (f32[128,1536]{1,0:T(8,128)}, bf16[1536,1536]{1,0:T(8,128)(2,1)}, bf16[1536,1536]{1,0:T(8,128)(2,1)}, bf16[1536,1024]{1,0:T(8,128)(2,1)}, f32[1...) custom-call(bf16[128,1536]{1,0:T(8,128)(2,1)} %get-tuple-element.70.slots, ...), custom_call_target="tpu_custom_call" | custom-call | flops 10000000000 | bytes 150000000 | tf_op jit(solution)/shard_map/pallas_call | solution.py:1830
  430.8 96.7 %shard_map.267 = (f32[16,1536]{1,0:T(8,128)}, f32[16,128]{1,0:T(8,128)}, f32[16,1536]{1,0:T(8,128)}, f32[16,1024]{1,0:T(8,128)}, f32[16,1024]{1,0:T(8,128)}, /*i...) custom-call(bf16[4,2,2,2,48,1536]{5,4,3,2,1,0:T(8,128)(2,1)} %bitcas, ...), custom_call_target="tpu_custom_call" | custom-call | flops 1000000000 | bytes 200000000 | tf_op jit(solution)/shard_map/pallas_call | solution.py:560
  527.5 1.5 slice_reduce_fusion
  529.0 1.5 slice_bitcast_fusion.1
  530.5 1.5 slice_bitcast_fusion
  532.0 2.5 bitcast_convert_fusion
  534.6 1.9 bitcast_convert_fusion.1
  536.4 0.7 copy.43
  537.2 0.9 copy.44
  (31 shorter events, 3.8 us)
Async XLA Ops:
  108.5 0.8 copy-start.4
  109.3 0.7 copy-start.6
  110.0 0.8 copy-start.7
  188.5 0.7 copy-start
  189.3 0.7 copy-start.1
  190.0 0.7 copy-start.2
  190.8 0.7 copy-start.3
  191.5 0.6 copy-start.5
  527.5 7.1 %copy-start.8 = (bf16[1536,512]{1,0:T(8,128)(2,1)S(1)}, bf16[1536,512]{1,0:T(8,128)(2,1)}, u32[]{:S(2)}) copy-start(bf16[1536,512]{1,0:T(8,128)(2,1)} %get-tuple-element.124) | copy-start | bytes 4718596
  532.0 4.4 copy-start.10
  534.5 2.7 copy-start.9
  534.5 3.5 copy-start.11
  534.5 4.2 copy-start.15
  534.5 4.8 copy-start.12
  534.6 5.4 copy-start.14
  534.6 6.0 %copy-start.13 = (f32[16,1024]{1,0:T(8,128)S(1)}, f32[16,1024]{1,0:T(8,128)}, u32[]{:S(2)}) copy-start(f32[16,1024]{1,0:T(8,128)} %get-tuple-element.122) | copy-start | bytes 196612

commit v7 on v4

--- a/solution.py
+++ b/solution.py
@@ -879,7 +879,7 @@
 
 
 GROUP_BLOCKS = 16
-MIDDLE_MIB = 52
+MIDDLE_MIB = 61
 
 
 def blocks_of(value):
@@ -1415,7 +1415,7 @@
             pltpu.SemaphoreType.DMA((144,)),
         ],
         compiler_params=pltpu.CompilerParams(
-            collective_id=4, has_side_effects=True, vmem_limit_bytes=56 * 1024 * 1024
+            collective_id=4, has_side_effects=True, vmem_limit_bytes=61 * 1024 * 1024
         ),
         cost_estimate=pl.CostEstimate(
             flops=22_000_000_000, bytes_accessed=300_000_000, transcendentals=1_000_000
@@ -1807,7 +1807,7 @@
             pltpu.SemaphoreType.DMA((16,)),
         ],
         compiler_params=pltpu.CompilerParams(
-            collective_id=3, has_side_effects=True, vmem_limit_bytes=58 * 1024 * 1024
+            collective_id=3, has_side_effects=True, vmem_limit_bytes=61 * 1024 * 1024
         ),
         cost_estimate=pl.CostEstimate(
             flops=10_000_000_000, bytes_accessed=150_000_000, transcendentals=2_000_000

time: 542 us -> 540 us (level)
    unnamed x75 -> x63, local copies, waits for them, and re-layouts: 25.9 us -> 20.4 us
where the time goes in v7:
time: 540 us; the launch traced here: 535 us
  Pallas kernels  493 us (91%)
  local copies, waits for them, and re-layouts  28.8 us (5%)
  other arithmetic  8.99 us (2%)
    pallas_call x1, Pallas kernels, expert(): pl.pallas_call(expert_kernel, out_shape=[jax.ShapeDtypeStruct(outgoing.sh...  125 us
    pallas_call x1, Pallas kernels, sum_last(): pl.pallas_call(last_kernel, out_shape=[jax.ShapeDtypeStruct((16, width),...  96.8 us
    pallas_call x1, Pallas kernels, rear(): pl.pallas_call(functools.partial(rear_kernel, tail), out_shape=[jax.Shape...  94 us
    pallas_call x1, Pallas kernels, gather_weights(): pl.pallas_call(gather_kernel, out_shape=shapes, in_specs=[pl.BlockSpec(me...  79.3 us
    pallas_call x1, Pallas kernels, middle(): pl.pallas_call(middle_kernel, out_shape=[jax.ShapeDtypeStruct((rows, feat...  73.4 us
    pallas_call x1, Pallas kernels, to_later(): pl.pallas_call(later_kernel, out_shape=[jax.ShapeDtypeStruct((8,) + own,...  24.5 us
    unnamed x63, local copies, waits for them, and re-layouts  20.4 us

profile of v7, /device:TPU:3, one launch (start us, length us, event | category | flops | bytes accessed | tf_op | source)
XLA Modules:
  0.0 535.0 jit_solution(17339517923150069161)
XLA Ops:
  0.7 1.4 fusion.24
  7.3 1.0 concatenate.6
  8.3 1.3 fusion.1.slots_ref.slots_down_ref
  9.7 1.2 fusion.slots_ref.refs_0_
  10.9 1.0 fusion.3.owner_ref.refs_1_
  11.9 79.3 %shard_map.263 = (bf16[4,2,2,2,48,1536]{5,4,3,2,1,0:T(8,128)(2,1)S(1)}, bf16[4,2,2,2,48,128]{5,4,3,2,1,0:T(8,128)(2,1)S(1)}, bf16[4,2,2,2,48,1536]{5,4,3,2,1,0:T...) custom-call(bf16[16,7296]{1,0:T(8,128)(2,1)S(1)} %concatenate.7.shar, ...), custom_call_target="tpu_custom_call" | custom-call | bytes 200000000 | tf_op jit(solution)/shard_map/pallas_call | solution.py:368
  91.3 2.2 copy-done.9
  93.5 1.7 copy-done.11
  95.2 1.7 copy-done.12
  96.9 1.6 copy-done.13
  98.5 1.6 copy-done.14
  100.2 1.1 copy-done.16
  101.3 24.5 %shard_map.264 = (bf16[8,128,1024]{2,1,0:T(8,128)(2,1)S(1)}, bf16[32,128]{1,0:T(8,128)(2,1)S(1)}, bf16[128,1536]{1,0:T(8,128)(2,1)S(1)}, bf16[128,1536]{1,0:T(8,128)(2,1)S(1)}, bf16[64,24,1536]{2,1,0:T(8,128)(2,1)S(1)}) custom-call(bf16[128,1536]{1,0:T(8,128)(2,1)S(1)} %copy-done.5, bf16[1536,128]{1,0:T(8,128)(2,1)S(1)} %bitcast.50, ...), custom_call_target="tpu_custom_call" | custom-call | flops 1000000000 | bytes 80000000 | tf_op jit(solution)/shard_map/pallas_call | solution.py:1001
  125.9 2.1 copy-done.10
  128.0 1.4 copy-done.15
  131.5 73.4 %shard_map.265 = (bf16[128,1536]{1,0:T(8,128)(2,1)}, f32[128,1536]{1,0:T(8,128)}, bf16[128,1536]{1,0:T(8,128)(2,1)}, f32[128,128]{1,0:T(8,128)}, bf16[128,1536]{...) custom-call(bf16[128,1536]{1,0:T(8,128)(2,1)} %copy-done.18, ...), custom_call_target="tpu_custom_call" | custom-call | flops 10000000000 | bytes 250000000 | tf_op jit(solution)/shard_map/pallas_call | solution.py:1200
  204.9 125.2 %shard_map.266 = (bf16[64,24,1664]{2,1,0:T(8,128)(2,1)}, bf16[64,24,1536]{2,1,0:T(8,128)(2,1)}, f32[1536,512]{1,0:T(8,128)}, bf16[1536,512]{1,0:T(8,128)(2,1)}, ...) custom-call(bf16[64,24,1664]{2,1,0:T(8,128)(2,1)} %get-tuple-element.82.outgoing_ref, ...), custom_call_target="tpu_custom_call" | custom-call | flops 22000001024 | bytes 300000000 | tf_op jit(solution)/shard_map/pallas_call | solution.py:1387
  330.2 94.0 %shard_map.267 = (f32[128,1536]{1,0:T(8,128)}, bf16[1536,1536]{1,0:T(8,128)(2,1)}, bf16[1536,1536]{1,0:T(8,128)(2,1)}, bf16[1536,1024]{1,0:T(8,128)(2,1)}, f32[1...) custom-call(bf16[128,1536]{1,0:T(8,128)(2,1)} %fusion.slots_ref.refs_0_, ...), custom_call_target="tpu_custom_call" | custom-call | flops 10000000000 | bytes 150000000 | tf_op jit(solution)/shard_map/pallas_call | solution.py:1766
  424.2 96.8 %shard_map.268 = (f32[16,1536]{1,0:T(8,128)}, f32[16,128]{1,0:T(8,128)}, f32[16,1536]{1,0:T(8,128)}, f32[16,1024]{1,0:T(8,128)}, f32[16,1024]{1,0:T(8,128)}, /*i...) custom-call(bf16[4,2,2,2,48,1536]{5,4,3,2,1,0:T(8,128)(2,1)} %bitcas, ...), custom_call_target="tpu_custom_call" | custom-call | flops 1000000000 | bytes 200000000 | tf_op jit(solution)/shard_map/pallas_call | solution.py:785
  521.0 1.5 slice_reduce_fusion
  522.5 1.5 slice_bitcast_fusion.1
  524.0 1.5 slice_bitcast_fusion
  525.6 2.5 bitcast_convert_fusion
  528.1 1.9 bitcast_convert_fusion.1
  (66 shorter events, 12.2 us)
Async XLA Ops:
  0.6 11.3 %copy-start.4 = (bf16[1,256,1536]{2,1,0:T(8,128)(2,1)S(1)}, bf16[1,256,1536]{2,1,0:T(8,128)(2,1)}, u32[]{:S(2)}) copy-start(bf16[1,256,1536]{2,1,0:T(8,128)(2,1)} %param.30) | copy-start | bytes 2359300
  0.7 11.3 %copy-start.3 = (bf16[1,1536,256]{2,1,0:T(8,128)(2,1)S(1)}, bf16[1,1536,256]{2,1,0:T(8,128)(2,1)}, u32[]{:S(2)}) copy-start(bf16[1,1536,256]{2,1,0:T(8,128)(2,1)} %param.29) | copy-start | bytes 2359300
  0.7 11.3 %copy-start.2 = (bf16[1,1536,256]{2,1,0:T(8,128)(2,1)S(1)}, bf16[1,1536,256]{2,1,0:T(8,128)(2,1)}, u32[]{:S(2)}) copy-start(bf16[1,1536,256]{2,1,0:T(8,128)(2,1)} %param.28) | copy-start | bytes 2359300
  0.7 100.7 %copy-start.5 = (bf16[128,1536]{1,0:T(8,128)(2,1)S(1)}, bf16[128,1536]{1,0:T(8,128)(2,1)}, u32[]{:S(2)}) copy-start(bf16[128,1536]{1,0:T(8,128)(2,1)} %refs_13_.1) | copy-start | bytes 1179652
  0.7 100.6 %copy-start.6 = (bf16[128,1536]{1,0:T(8,128)(2,1)S(1)}, bf16[128,1536]{1,0:T(8,128)(2,1)}, u32[]{:S(2)}) copy-start(bf16[128,1536]{1,0:T(8,128)(2,1)} %refs_3_.1) | copy-start | bytes 1179652
  9.7 116.2 %copy-start.8 = (bf16[1536,128]{1,0:T(8,128)(2,1)}, bf16[1536,128]{1,0:T(8,128)(2,1)S(1)}, u32[]{:S(2)}) copy-start(bf16[1536,128]{1,0:T(8,128)(2,1)S(1)} %fusion.1.slots_ref.slots_down_ref) | copy-start | bytes 1179652
  91.3 2.2 copy-start.9
  93.5 1.7 copy-start.11
  95.2 1.7 copy-start.12
  96.9 1.6 copy-start.13
  98.5 1.6 copy-start.14
  101.3 24.6 %copy-start = (bf16[4,2,2,2,48,1536]{5,4,3,2,1,0:T(8,128)(2,1)}, bf16[4,2,2,2,48,1536]{5,4,3,2,1,0:T(8,128)(2,1)S(1)}, u32[]{:S(2)}) copy-start(bf16[4,2,2,2,48,1536]{5,4,3,2,1,0:T(8,128)(2,1)S(1)} %get-tuple-element.66) | copy-start | bytes 14155780
  101.3 24.6 %copy-start.1 = (bf16[4,2,2,2,48,1024]{5,4,3,2,1,0:T(8,128)(2,1)}, bf16[4,2,2,2,48,1024]{5,4,3,2,1,0:T(8,128)(2,1)S(1)}, u32[]{:S(2)}) copy-start(bf16[4,2,2,2,48,1024]{5,4,3,2,1,0:T(8,128)(2,1)S(1)} %get-tuple-element.67) | copy-start | bytes 9437188
  101.3 24.6 %copy-start.7 = (bf16[4,2,2,2,48,128]{5,4,3,2,1,0:T(8,128)(2,1)}, bf16[4,2,2,2,48,128]{5,4,3,2,1,0:T(8,128)(2,1)S(1)}, u32[]{:S(2)}) copy-start(bf16[4,2,2,2,48,128]{5,4,3,2,1,0:T(8,128)(2,1)S(1)} %get-tuple-element.65) | copy-start | bytes 1179652
  125.9 2.1 copy-start.10
  128.0 1.4 copy-start.15
  521.0 7.1 %copy-start.20 = (bf16[1536,512]{1,0:T(8,128)(2,1)S(1)}, bf16[1536,512]{1,0:T(8,128)(2,1)}, u32[]{:S(2)}) copy-start(bf16[1536,512]{1,0:T(8,128)(2,1)} %get-tuple-element.114) | copy-start | bytes 4718596
  525.5 4.4 copy-start.22
  528.1 2.7 copy-start.21
  528.1 3.5 copy-start.23
  528.1 4.2 copy-start.27
  528.1 4.8 copy-start.24
  528.1 5.4 %copy-start.26 = (f32[16,1024]{1,0:T(8,128)S(1)}, f32[16,1024]{1,0:T(8,128)}, u32[]{:S(2)}) copy-start(f32[16,1024]{1,0:T(8,128)} %get-tuple-element.111) | copy-start | bytes 196612
  528.1 6.0 %copy-start.25 = (f32[16,1024]{1,0:T(8,128)S(1)}, f32[16,1024]{1,0:T(8,128)}, u32[]{:S(2)}) copy-start(f32[16,1024]{1,0:T(8,128)} %get-tuple-element.112) | copy-start | bytes 196612
  (4 other events, 3.2 us)
